TPU v7x, 32 devices: a whole 2x2x4 slice. The times are simulated.
32 devices in a mesh: dp: 8 (over z, y), tensor: 4 (over x, core).
Axes of the slice: x: 2, y: 2, z: 4, core: 2. Of those that a mesh axis runs over, the one named last changes fastest.
Arguments:
- inputs: bfloat16 [8192, 2048], P(('dp', 'tensor')), may hold values from -6 to 6
- segment_ids: int32 [8, 1024], P('dp', 'tensor'), may hold values from 0 to 2, never falling along the last dimension, each value on 1 to 768 neighbouring positions
- expert_ids: int32 [8192, 8], P(('dp', 'tensor')), may hold values from 0 to 63, all different within a row
- gate_values: bfloat16 [8192, 8], P(('dp', 'tensor')), may hold values from 0.039794922 to 0.29882812
- attn_gain: float32 [2048], replicated, may hold values from 0.25 to 1.75
- query_gain: float32 [128], replicated, may hold values from 0.25 to 1.75
- key_gain: float32 [128], replicated, may hold values from 0.25 to 1.75
- w_query: bfloat16 [2048, 2048], P('dp', 'tensor'), may hold values from -0.125 to 0.125
- w_key: bfloat16 [2048, 2048], P('dp', 'tensor'), may hold values from -0.125 to 0.125
- w_value: bfloat16 [2048, 2048], P('dp', 'tensor'), may hold values from -0.125 to 0.125
- w_output: bfloat16 [2048, 2048], P('tensor', 'dp'), may hold values from -2 to 2
- ffn_gain: float32 [2048], replicated, may hold values from 0.25 to 1.75
- w_gate: bfloat16 [64, 2048, 1024], P('dp', None, 'tensor'), may hold values from -0.125 to 0.125
- w_up: bfloat16 [64, 2048, 1024], P('dp', None, 'tensor'), may hold values from -0.125 to 0.125
- w_down: bfloat16 [64, 1024, 2048], P('dp', 'tensor'), may hold values from -0.75 to 0.75
- cotangent: bfloat16 [8192, 2048], P(('dp', 'tensor')), may hold values from -6 to 6
Outputs:
- outputs: float32 [8192, 2048], P(('dp', 'tensor'))
- grad_inputs: float32 [8192, 2048], P(('dp', 'tensor'))
- grad_attn_gain: float32 [2048], replicated
- grad_query_gain: float32 [128], replicated
- grad_key_gain: float32 [128], replicated
- grad_w_query: float32 [2048, 2048], P('dp', 'tensor')
- grad_w_key: float32 [2048, 2048], P('dp', 'tensor')
- grad_w_value: float32 [2048, 2048], P('dp', 'tensor')
- grad_w_output: float32 [2048, 2048], P('tensor', 'dp')
- grad_ffn_gain: float32 [2048], replicated
- grad_w_gate: float32 [64, 2048, 1024], P('dp', None, 'tensor')
- grad_w_up: float32 [64, 2048, 1024], P('dp', None, 'tensor')
- grad_w_down: float32 [64, 1024, 2048], P('dp', 'tensor')
Inputs may be any that keep to these rules, and one draw needn't show every extreme that they name: `segment_ids`: within a pack the ids never fall. `expert_ids`: each token names 8 different experts.
All inputs are finite; a program needn't handle non-finite values.
Results may differ from a plain program's by a relative error of at most 0.02.
Values may be sent and summed in bfloat16 or wider, within the bound.
No kernel may reach another device: no remote copies, remote signals or barrier semaphores. Data moves between devices by JAX's collectives and lax.ppermute only.
A program may use at most 512 MiB of HBM per device.

v0:
```python
import jax
import jax.numpy as jnp
from jax import lax
from jax.sharding import PartitionSpec as P

WINDOW = 1024


EPSILON = 1e-06
THETA = 50000.0
NEG_FILL = -1e30


def matmul(left_side, right_side):
    return jnp.dot(left_side, right_side, preferred_element_type=jnp.float32)


def contract_last(left_side, right_side):
    return lax.dot_general(
        left_side, right_side, (((1,), (1,)), ((), ())), preferred_element_type=jnp.float32
    )


def contract_first(left_side, right_side):
    return lax.dot_general(
        left_side, right_side, (((0,), (0,)), ((), ())), preferred_element_type=jnp.float32
    )


def norm_parts(values):
    factor = lax.rsqrt(jnp.mean(values * values, axis=-1, keepdims=True) + EPSILON)
    return (values * factor, factor)


def norm_back(grad_out, normed, factor, gain_vec):
    scaled = grad_out * gain_vec
    return factor * (scaled - normed * jnp.mean(scaled * normed, axis=-1, keepdims=True))


def rope_tables(length, head_size):
    half_size = head_size // 2
    frequency = THETA ** (-(2.0 * jnp.arange(half_size, dtype=jnp.float32)) / head_size)
    angles = jnp.arange(length, dtype=jnp.float32)[:, None] * frequency[None, :]
    return (jnp.cos(angles)[:, None, :], jnp.sin(angles)[:, None, :])


def rotate(values, cosine, sine_tab):
    half_size = values.shape[-1] // 2
    first_half = values[..., :half_size]
    second_half = values[..., half_size:]
    return jnp.concatenate(
        [
            first_half * cosine - second_half * sine_tab,
            second_half * cosine + first_half * sine_tab,
        ],
        axis=-1,
    )


def rotate_back(grads_in, cosine, sine_tab):
    half_size = grads_in.shape[-1] // 2
    first_half = grads_in[..., :half_size]
    second_half = grads_in[..., half_size:]
    return jnp.concatenate(
        [
            first_half * cosine + second_half * sine_tab,
            second_half * cosine - first_half * sine_tab,
        ],
        axis=-1,
    )


def block_mask(segments, offset, block_rows, key_count):
    query_pos = offset + jnp.arange(block_rows)
    key_pos = jnp.arange(key_count)
    same_doc = segments[offset : offset + block_rows][:, None] == segments[None, :]
    near_pos = jnp.abs(query_pos[:, None] - key_pos[None, :]) < WINDOW // 2
    return same_doc & near_pos


def block_scores(query_block, key_low, allowed, inv_root):
    scores = (
        jnp.einsum("qhd,khd->hqk", query_block, key_low, preferred_element_type=jnp.float32)
        * inv_root
    )
    return jnp.where(allowed[None], scores, NEG_FILL)


def row_sum(term_fn, tok_rows):
    return lax.psum_scatter(
        term_fn(jnp.int32(0), lax.axis_size("tensor") * tok_rows),
        "tensor",
        scatter_dimension=0,
        tiled=True,
    )


def gather_rows(values):
    return lax.all_gather(values, "tensor", axis=0, tiled=True)


def from_experts(values):
    return lax.all_to_all(values, "dp", split_axis=1, concat_axis=1, tiled=True)


def to_experts(source_rows, slot_token, slot_gate, layout):
    picked = jnp.take(source_rows, slot_token, axis=0, mode="fill", fill_value=0)
    if slot_gate is not None:
        picked = (picked.astype(jnp.float32) * slot_gate[:, None]).astype(jnp.bfloat16)
    picked = picked.reshape(layout + (picked.shape[1],))
    return lax.all_to_all(picked, "dp", split_axis=1, concat_axis=1, tiled=True)


def pair_sum(table, weights_low, pair_slots, row_count):
    picked = jnp.take(table, pair_slots.reshape(-1), axis=0, mode="fill", fill_value=0)
    picked = picked.reshape(row_count, pair_slots.shape[1], table.shape[1])
    return jnp.einsum("rk,rkd->rd", weights_low, picked, preferred_element_type=jnp.float32)


def expert_forward(operands):
    rows_in, gate_mat, up_mat, down_mat = operands
    flat_rows = rows_in.reshape(-1, rows_in.shape[-1])
    gated = matmul(flat_rows, gate_mat)
    lifted = matmul(flat_rows, up_mat)
    hidden = (jax.nn.silu(gated) * lifted).astype(jnp.bfloat16)
    result = matmul(hidden, down_mat).astype(jnp.bfloat16)
    return (result.reshape(rows_in.shape), gated, lifted)


def expert_backward(operands):
    rows_in, grad_in, gated, lifted, gate_mat, up_mat, down_mat = operands
    flat_rows = rows_in.reshape(-1, rows_in.shape[-1])
    flat_grad = grad_in.reshape(-1, grad_in.shape[-1])
    gate_sig = jax.nn.sigmoid(gated)
    activated = jax.nn.silu(gated)
    hidden = (activated * lifted).astype(jnp.bfloat16)
    grad_hidden = contract_last(flat_grad, down_mat)
    grad_down = contract_first(hidden, flat_grad)
    grad_gated = (grad_hidden * lifted * gate_sig * (1.0 + gated * (1.0 - gate_sig))).astype(
        jnp.bfloat16
    )
    grad_lifted = (grad_hidden * activated).astype(jnp.bfloat16)
    grad_gate = contract_first(flat_rows, grad_gated)
    grad_up = contract_first(flat_rows, grad_lifted)
    grad_rows = (contract_last(grad_gated, gate_mat) + contract_last(grad_lifted, up_mat)).astype(
        jnp.bfloat16
    )
    return (grad_rows.reshape(rows_in.shape), grad_gate, grad_up, grad_down)


def shards(
    inputs,
    segment_ids,
    expert_ids,
    gate_values,
    attn_gain,
    query_gain,
    key_gain,
    w_query,
    w_key,
    w_value,
    w_output,
    ffn_gain,
    w_gate,
    w_up,
    w_down,
    cotangent,
):
    tok_rows, model_width = inputs.shape
    head_size = query_gain.shape[0]
    tensor_count = lax.axis_size("tensor")
    data_count = lax.axis_size("dp")
    local_experts = w_gate.shape[0]
    all_experts = local_experts * data_count
    top_count = expert_ids.shape[1]
    seq_len = tok_rows * tensor_count
    capacity = seq_len * top_count // all_experts
    inv_root = head_size ** (-0.5)
    inputs_f32 = inputs.astype(jnp.float32)
    normed_one, factor_one = norm_parts(inputs_f32)
    first_in = (normed_one * attn_gain).astype(jnp.bfloat16)
    pack_in, pack_cot, pack_ids, pack_gates, pack_segs = (
        lax.all_gather(first_in, "tensor", axis=0, tiled=True),
        lax.all_gather(cotangent, "tensor", axis=0, tiled=True),
        lax.all_gather(expert_ids, "tensor", axis=0, tiled=True),
        lax.all_gather(gate_values, "tensor", axis=0, tiled=True),
        lax.all_gather(segment_ids, "tensor", axis=1, tiled=True),
    )
    full_query, full_key, full_value, full_output = (
        lax.all_gather(w_query, "dp", axis=0, tiled=True),
        lax.all_gather(w_key, "dp", axis=0, tiled=True),
        lax.all_gather(w_value, "dp", axis=0, tiled=True),
        lax.all_gather(w_output, "dp", axis=1, tiled=True),
    )
    query_pre = matmul(pack_in, full_query)
    key_pre = matmul(pack_in, full_key)
    value_low = matmul(pack_in, full_value).astype(jnp.bfloat16)
    head_count = query_pre.shape[1] // head_size
    cosine, sine_tab = rope_tables(seq_len, head_size)
    query_norm, query_factor = norm_parts(query_pre.reshape(seq_len, head_count, head_size))
    key_norm, key_factor = norm_parts(key_pre.reshape(seq_len, head_count, head_size))
    query_low = rotate(query_norm * query_gain, cosine, sine_tab).astype(jnp.bfloat16)
    key_low = rotate(key_norm * key_gain, cosine, sine_tab).astype(jnp.bfloat16)
    value_heads = value_low.reshape(seq_len, head_count, head_size)
    segments = pack_segs[0]
    block_rows = min(512, seq_len)
    block_total = seq_len // block_rows
    masks = []
    mixture_parts = []
    lse_parts = []
    for block_index in range(block_total):
        offset = block_index * block_rows
        allowed = block_mask(segments, offset, block_rows, seq_len)
        masks.append(allowed)
        scores = block_scores(query_low[offset : offset + block_rows], key_low, allowed, inv_root)
        top_score = jnp.max(scores, axis=-1, keepdims=True)
        raw_weights = jnp.exp(scores - top_score)
        totals = jnp.sum(raw_weights, axis=-1, keepdims=True)
        weights_low = (raw_weights / totals).astype(jnp.bfloat16)
        mixture_parts.append(
            jnp.einsum(
                "hqk,khd->qhd", weights_low, value_heads, preferred_element_type=jnp.float32
            ).astype(jnp.bfloat16)
        )
        lse_parts.append(top_score + jnp.log(totals))
    mixture = jnp.concatenate(mixture_parts, axis=0).reshape(seq_len, head_count * head_size)

    def attn_term(offset, row_count):
        return matmul(mixture, full_output)

    middle = inputs_f32 + row_sum(attn_term, tok_rows)
    normed_two, factor_two = norm_parts(middle)
    second_in = (normed_two * ffn_gain).astype(jnp.bfloat16)
    pack_second = gather_rows(second_in)
    expert_range = jnp.arange(all_experts, dtype=jnp.int32)
    matches = pack_ids[:, :, None] == expert_range[None, None, :]
    token_counts = jnp.sum(matches.astype(jnp.float32), axis=1).astype(jnp.bfloat16)
    token_range = jnp.arange(seq_len, dtype=jnp.int32)
    earlier = (token_range[:, None] > token_range[None, :]).astype(jnp.bfloat16)
    before = matmul(earlier, token_counts)
    places = (
        jnp.sum(jnp.where(matches, before[:, None, :], 0.0), axis=2).astype(jnp.int32).reshape(-1)
    )
    flat_ids = pack_ids.reshape(-1)
    owners = flat_ids // local_experts
    local_index = flat_ids % local_experts
    dump_slot = all_experts * capacity
    slot_index = jnp.where(
        places < capacity,
        local_index * (data_count * capacity) + owners * capacity + places,
        dump_slot,
    ).astype(jnp.int32)
    pair_token = jnp.arange(seq_len * top_count) // top_count
    slot_token = (
        jnp.full((dump_slot + 1,), seq_len, jnp.int32).at[slot_index].set(pair_token)[:dump_slot]
    )
    pair_gates = pack_gates.astype(jnp.float32)
    slot_gate = (
        jnp.zeros((dump_slot + 1,), jnp.float32)
        .at[slot_index]
        .set(pair_gates.reshape(-1))[:dump_slot]
    )
    pair_slots = slot_index.reshape(seq_len, top_count)
    layout = (local_experts, data_count, capacity)
    arrived_rows = to_experts(pack_second, slot_token, None, layout)
    expert_out, gated_all, lifted_all = lax.map(
        expert_forward, (arrived_rows, w_gate, w_up, w_down)
    )
    returned = from_experts(expert_out).reshape(-1, model_width)

    def combine_term(offset, row_count):
        return pair_sum(returned, pack_gates, pair_slots, row_count)

    outputs = middle + row_sum(combine_term, tok_rows)
    grad_arrived = to_experts(pack_cot, slot_token, slot_gate, layout)
    grad_rows_all, grad_w_gate, grad_w_up, grad_w_down = lax.map(
        expert_backward, (arrived_rows, grad_arrived, gated_all, lifted_all, w_gate, w_up, w_down)
    )
    returned_grad = from_experts(grad_rows_all).reshape(-1, model_width)
    unit_gates = jnp.ones_like(pack_gates)

    def dispatch_term(offset, row_count):
        return pair_sum(returned_grad, unit_gates, pair_slots, row_count)

    grad_second = row_sum(dispatch_term, tok_rows)
    ffn_gain_part = jnp.sum(grad_second * normed_two, axis=0)
    grad_middle = cotangent.astype(jnp.float32) + norm_back(
        grad_second, normed_two, factor_two, ffn_gain
    )
    pack_grad = gather_rows(grad_middle.astype(jnp.bfloat16))
    output_part = contract_first(mixture, pack_grad)
    grad_mixture = (
        contract_last(pack_grad, full_output)
        .astype(jnp.bfloat16)
        .reshape(seq_len, head_count, head_size)
    )
    grad_query_parts = []
    grad_key_sum = jnp.zeros((seq_len, head_count, head_size), jnp.float32)
    grad_value_sum = jnp.zeros((seq_len, head_count, head_size), jnp.float32)
    for block_index in range(block_total):
        offset = block_index * block_rows
        query_block = query_low[offset : offset + block_rows]
        grad_block = grad_mixture[offset : offset + block_rows]
        scores = block_scores(query_block, key_low, masks[block_index], inv_root)
        prob_rows = jnp.exp(scores - lse_parts[block_index])
        grad_probs = jnp.einsum(
            "qhd,khd->hqk", grad_block, value_heads, preferred_element_type=jnp.float32
        )
        row_delta = jnp.sum(grad_probs * prob_rows, axis=-1, keepdims=True)
        grad_scores = (prob_rows * (grad_probs - row_delta)).astype(jnp.bfloat16)
        grad_query_parts.append(
            jnp.einsum("hqk,khd->qhd", grad_scores, key_low, preferred_element_type=jnp.float32)
            * inv_root
        )
        grad_key_sum = (
            grad_key_sum
            + jnp.einsum(
                "hqk,qhd->khd", grad_scores, query_block, preferred_element_type=jnp.float32
            )
            * inv_root
        )
        grad_value_sum = grad_value_sum + jnp.einsum(
            "hqk,qhd->khd",
            prob_rows.astype(jnp.bfloat16),
            grad_block,
            preferred_element_type=jnp.float32,
        )
    grad_query_norm = rotate_back(jnp.concatenate(grad_query_parts, axis=0), cosine, sine_tab)
    grad_key_norm = rotate_back(grad_key_sum, cosine, sine_tab)
    query_gain_part = jnp.sum(grad_query_norm * query_norm, axis=(0, 1))
    key_gain_part = jnp.sum(grad_key_norm * key_norm, axis=(0, 1))
    grad_query_pre = (
        norm_back(grad_query_norm, query_norm, query_factor, query_gain)
        .reshape(seq_len, -1)
        .astype(jnp.bfloat16)
    )
    grad_key_pre = (
        norm_back(grad_key_norm, key_norm, key_factor, key_gain)
        .reshape(seq_len, -1)
        .astype(jnp.bfloat16)
    )
    grad_value_low = grad_value_sum.reshape(seq_len, -1).astype(jnp.bfloat16)
    query_part = contract_first(pack_in, grad_query_pre)
    key_part = contract_first(pack_in, grad_key_pre)
    value_part = contract_first(pack_in, grad_value_low)

    def input_term(offset, row_count):
        total_term = contract_last(grad_query_pre, full_query)
        total_term = total_term + contract_last(grad_key_pre, full_key)
        return total_term + contract_last(grad_value_low, full_value)

    grad_first = row_sum(input_term, tok_rows)
    attn_gain_part = jnp.sum(grad_first * normed_one, axis=0)
    grad_inputs = grad_middle + norm_back(grad_first, normed_one, factor_one, attn_gain)
    grad_w_query, grad_w_key, grad_w_value, grad_w_output = (
        lax.psum_scatter(
            query_part.astype(jnp.bfloat16), "dp", scatter_dimension=0, tiled=True
        ).astype(jnp.float32),
        lax.psum_scatter(
            key_part.astype(jnp.bfloat16), "dp", scatter_dimension=0, tiled=True
        ).astype(jnp.float32),
        lax.psum_scatter(
            value_part.astype(jnp.bfloat16), "dp", scatter_dimension=0, tiled=True
        ).astype(jnp.float32),
        lax.psum_scatter(
            output_part.astype(jnp.bfloat16), "dp", scatter_dimension=1, tiled=True
        ).astype(jnp.float32),
    )
    grad_attn_gain, grad_ffn_gain, grad_query_gain, grad_key_gain = lax.psum(
        (attn_gain_part, ffn_gain_part, query_gain_part, key_gain_part), ("dp", "tensor")
    )
    return (
        outputs,
        grad_inputs,
        grad_attn_gain,
        grad_query_gain,
        grad_key_gain,
        grad_w_query,
        grad_w_key,
        grad_w_value,
        grad_w_output,
        grad_ffn_gain,
        grad_w_gate,
        grad_w_up,
        grad_w_down,
    )


def solution(mesh):
    in_specs = (
        P(("dp", "tensor"), None),
        P("dp", "tensor"),
        P(("dp", "tensor"), None),
        P(("dp", "tensor"), None),
        P(),
        P(),
        P(),
        P("dp", "tensor"),
        P("dp", "tensor"),
        P("dp", "tensor"),
        P("tensor", "dp"),
        P(),
        P("dp", None, "tensor"),
        P("dp", None, "tensor"),
        P("dp", "tensor", None),
        P(("dp", "tensor"), None),
    )
    out_specs = (
        P(("dp", "tensor"), None),
        P(("dp", "tensor"), None),
        P(),
        P(),
        P(),
        P("dp", "tensor"),
        P("dp", "tensor"),
        P("dp", "tensor"),
        P("tensor", "dp"),
        P(),
        P("dp", None, "tensor"),
        P("dp", None, "tensor"),
        P("dp", "tensor", None),
    )
    return jax.shard_map(shards, mesh=mesh, in_specs=in_specs, out_specs=out_specs, check_vma=False)
```

profile of v0, /device:TPU:0, one launch (start us, length us, event | category | flops | bytes accessed | tf_op | source)
XLA Modules:
  0.0 4033.0 jit_solution(11331437797596595188)
XLA Ops:
  24.9 37.3 all-gather.15.cloned.1.call-done
  62.2 35.1 all-gather.9.cloned.1.call-done
  105.8 42.9 %all-gather.13.cloned.1.call-done = bf16[2048,512]{1,0:T(8,128)(2,1)} async-done(((bf16[256,512]{1,0:T(8,128)(2,1)}), bf16[2048,512]{1,0:T(8,128)(2,1)}) %all-gather.13.cloned.1.call-update) | async-done | bytes 2097168 | tf_op jit(solution)/shard_map/all_gather | solution.py:190
  174.3 24.2 all-gather.11.cloned.1.call-done
  209.5 40.6 %all-gather.17.cloned.1.call-done = bf16[512,2048]{1,0:T(8,128)(2,1)} async-done(((bf16[512,256]{1,0:T(8,128)(2,1)}), bf16[512,2048]{1,0:T(8,128)(2,1)}) %all-gather.17.cloned.1.call-update) | async-done | bytes 2097168 | tf_op jit(solution)/shard_map/all_gather | solution.py:193
  257.6 70.0 %reduce-scatter.9.cloned.1.call-done = f32[256,2048]{1,0:T(8,128)} async-done(((f32[1024,2048]{1,0:T(8,128)}), f32[256,2048]{1,0:T(8,128)}) %reduce-scatter.9.cloned.1.call-update) | async-done | bytes 2097168 | tf_op jit(solution)/shard_map/reduce_scatter | solution.py:90
  339.7 30.5 scatter_custom_fusion
  370.3 64.1 %gather_fusion = bf16[8192,2048]{1,0:T(8,128)(2,1)} fusion(bf16[1024,2048]{1,0:T(8,128)(2,1)} %all-gather.19.cloned.1.call-done, s32[8192]{0:T(1024)S(1)} %fusion.109), kind=kCustom, calls=%fused_computation.clone | custom fusion | bytes 67141632 | tf_op jit(solution)/shard_map/jit(_take)/gather | solution.py:107
  434.3 22.3 broadcast_select_fusion
  456.7 22.8 copy.110
  493.1 30.5 scatter_custom_fusion.1
  524.1 64.5 %gather_fusion.2 = bf16[8192,2048]{1,0:T(8,128)(2,1)} fusion(bf16[1024,2048]{1,0:T(8,128)(2,1)} %all-gather.21.cloned.1.call-done, s32[8192]{0:T(1024)S(1)} %fusion.109), kind=kCustom, calls=%fused_computation.2.clone | custom fusion | bytes 67141632 | tf_op jit(solution)/shard_map/jit(_take)/gather | solution.py:107
  588.6 23.1 multiply_convert_fusion.4
  611.7 22.8 copy.115
  634.5 575.4 %all-to-all-done = bf16[8,8,128,2048]{3,2,0,1:T(8,128)(2,1)} async-done(((bf16[8,8,128,2048]{3,2,0,1:T(8,128)(2,1)}), bf16[8,8,128,2048]{3,2,0,1:T(8,128)(2,1)}, u32[]{:S(2)}, u32[]{:S(2)}) %all-to-all-start) | async-done | bytes 33554464 | tf_op jit(solution)/shard_map/all_to_all | solution.py:111
  1217.0 22.9 copy.111
  1250.9 114.0 %while.30 = (s32[]{:T(128)}, bf16[8,8,128,2048]{3,2,0,1:T(8,128)(2,1)}, f32[8,1024,256]{2,1,0:T(8,128)}, f32[8,1024,256]{2,1,0:T(8,128)}, bf16[8,8,128,2048]{3,2...) while((s32[]{:T(128)}, ...), condition=%wide.region_13.15_spmd, body=%wide.region_12.14_spmd.sunk | while | flops 3224895488 | bytes 38799472 | solution.py:266
  1364.9 574.4 %all-to-all-done.2 = bf16[8,8,128,2048]{3,2,0,1:T(8,128)(2,1)} async-done(((bf16[8,8,128,2048]{3,2,0,1:T(8,128)(2,1)}), bf16[8,8,128,2048]{3,2,0,1:T(8,128)(2,1)}, u32[]{:S(2)}, u32[]{:S(2)}) %all-to-all-start.2) | async-done | bytes 33554464 | tf_op jit(solution)/shard_map/all_to_all | solution.py:111
  1950.4 202.5 %while.31 = (s32[]{:T(128)}, bf16[8,8,128,2048]{3,2,0,1:T(8,128)(2,1)}, f32[8,2048,256]{2,1,0:T(8,128)}, f32[8,2048,256]{2,1,0:T(8,128)}, f32[8,256,2048]{2,1,0:...) while((s32[]{:T(128)}, ...), condition=%wide.region_17.20_spmd, body=%wide.region_16.19_spmd.sunk | while | flops 6451625984 | bytes 79693984 | solution.py:276
  2160.9 720.8 %all-to-all-done.3 = bf16[8,8,128,2048]{3,2,0,1:T(8,128)(2,1)} async-done(((bf16[8,8,128,2048]{3,2,0,1:T(8,128)(2,1)}), bf16[8,8,128,2048]{3,2,0,1:T(8,128)(2,1)}, u32[]{:S(2)}, u32[]{:S(2)}) %all-to-all-start.3) | async-done | bytes 33554464 | tf_op jit(solution)/shard_map/all_to_all | solution.py:103
  2889.0 23.0 copy.119
  2912.0 256.5 %gather_fusion.3 = bf16[8192,2048]{1,0:T(8,128)(2,1)} fusion(bf16[8192,2048]{1,0:T(8,128)(2,1)} %bitcast.291, s32[8192]{0:T(1024)S(1)} %broadcast_clamp_fusion), kind=kCustom, calls=%fused_computation.3.clone | custom fusion | bytes 67141632 | tf_op jit(solution)/shard_map/jit(_take)/gather | solution.py:115
  3168.4 14.8 fusion.39
  3190.8 69.8 %reduce-scatter.13.cloned.1.call-done = f32[256,2048]{1,0:T(8,128)} async-done(((f32[1024,2048]{1,0:T(8,128)}), f32[256,2048]{1,0:T(8,128)}) %reduce-scatter.13.cloned.1.call-update) | async-done | bytes 2097168 | tf_op jit(solution)/shard_map/reduce_scatter | solution.py:90
  3265.8 34.5 all-gather.23.cloned.1.call-done
  3393.0 233.4 %all-to-all-done.1 = bf16[8,8,128,2048]{3,2,0,1:T(8,128)(2,1)} async-done(((bf16[8,8,128,2048]{3,2,0,1:T(8,128)(2,1)}), bf16[8,8,128,2048]{3,2,0,1:T(8,128)(2,1)}, u32[]{:S(2)}, u32[]{:S(2)}) %all-to-all-start.1) | async-done | bytes 33554464 | tf_op jit(solution)/shard_map/all_to_all | solution.py:103
  3626.4 23.2 copy.113
  3649.6 219.5 %gather_fusion.1 = bf16[8192,2048]{1,0:T(8,128)(2,1)} fusion(bf16[8192,2048]{1,0:T(8,128)(2,1)} %bitcast.290, s32[8192]{0:T(1024)S(1)} %broadcast_clamp_fusion), kind=kCustom, calls=%fused_computation.1.clone | custom fusion | bytes 67141632 | tf_op jit(solution)/shard_map/jit(_take)/gather | solution.py:115
  3869.1 15.9 fusion.41
  3900.7 44.2 %reduce-scatter.15.cloned.1.call-done = f32[256,2048]{1,0:T(8,128)} async-done(((f32[1024,2048]{1,0:T(8,128)}), f32[256,2048]{1,0:T(8,128)}) %reduce-scatter.15.cloned.1.call-update) | async-done | bytes 2097168 | tf_op jit(solution)/shard_map/reduce_scatter | solution.py:90
  3947.2 40.0 all-reduce
  3987.2 32.8 reduce-scatter.11.cloned.1.call-done
  (436 shorter events, 585.4 us)
Async XLA Ops:
  7.2 55.0 %all-gather.15.cloned.1.call-start = ((), (), s32[]{:S(2)}) async-start(), calls=%async_computation.15 | async-start | bytes 2359296 | tf_op jit(solution)/shard_map/all_gather | solution.py:191
  7.9 89.4 %all-gather.9.cloned.1.call-start = ((), (), s32[]{:S(2)}) async-start(), calls=%async_computation.12 | async-start | bytes 5242880 | tf_op jit(solution)/shard_map/all_gather | solution.py:183
  12.6 136.2 %all-gather.13.cloned.1.call-start = ((), (), s32[]{:S(2)}) async-start(), calls=%async_computation.14 | async-start | bytes 2359296 | tf_op jit(solution)/shard_map/all_gather | solution.py:190
  13.3 185.2 %all-gather.11.cloned.1.call-start = ((), (), s32[]{:S(2)}) async-start(), calls=%async_computation.13 | async-start | bytes 2359296 | tf_op jit(solution)/shard_map/all_gather | solution.py:192
  13.9 236.2 %all-gather.17.cloned.1.call-start = ((), (), s32[]{:S(2)}) async-start(), calls=%async_computation.16 | async-start | bytes 2359296 | tf_op jit(solution)/shard_map/all_gather | solution.py:193
  14.5 313.1 %reduce-scatter.9.cloned.1.call-start = ((), (), s32[]{:S(2)}) async-start(), calls=%async_computation.17 | async-start | bytes 10485760 | tf_op jit(solution)/shard_map/reduce_scatter | solution.py:90
  22.5 139.2 %copy-start.27 = (f32[1024,64]{1,0:T(8,128)}, f32[1024,64]{1,0:T(8,128)S(1)}, u32[]{:S(2)}) copy-start(f32[1024,64]{1,0:T(8,128)S(1)} %get-tuple-element.257) | copy-start | bytes 786436
  22.5 139.2 %copy-start.29 = (f32[1024,64]{1,0:T(8,128)}, f32[1024,64]{1,0:T(8,128)S(1)}, u32[]{:S(2)}) copy-start(f32[1024,64]{1,0:T(8,128)S(1)} %get-tuple-element.258) | copy-start | bytes 786436
  257.5 74.5 %copy-start.69 = (s32[256,8]{0,1:T(8,128)S(1)}, s32[256,8]{0,1:T(8,128)}, u32[]{:S(2)}) copy-start(s32[256,8]{0,1:T(8,128)} %param.26) | copy-start | bytes 24580
  257.5 112.7 %all-gather.19.cloned.1.call-start = ((), (), s32[]{:S(2)}) async-start(), calls=%async_computation.18 | async-start | bytes 5242880 | tf_op jit(solution)/shard_map/all_gather | solution.py:99
  337.5 96.9 %copy-start.23 = (s32[1024,8]{1,0:T(8,128)}, s32[1024,8]{1,0:T(8,128)S(1)}, u32[]{:S(2)}) copy-start(s32[1024,8]{1,0:T(8,128)S(1)} %copy.107) | copy-start | bytes 98308
  338.8 95.5 %copy-start.25 = (s32[1024,8]{1,0:T(8,128)}, s32[1024,8]{1,0:T(8,128)S(1)}, u32[]{:S(2)}) copy-start(s32[1024,8]{1,0:T(8,128)S(1)} %copy.106) | copy-start | bytes 98308
  479.5 730.4 %all-to-all-start = ((bf16[8,8,128,2048]{3,2,0,1:T(8,128)(2,1)}), bf16[8,8,128,2048]{3,2,0,1:T(8,128)(2,1)}, u32[]{:S(2)}, u32[]{:S(2)}) async-start(bf16[8,8,128,2048]{3,2,0,1:T(8,128)(2,1)} %copy.110), calls=%async_computation.1 | async-start | bytes 67108864 | tf_op jit(solution)/shard_map/all_to_all | solution.py:111
  486.7 37.4 all-gather.21.cloned.1.call-start
  492.7 95.9 %copy-start.45 = (bf16[1024,8]{0,1:T(8,128)(2,1)}, bf16[1024,8]{0,1:T(8,128)(2,1)S(1)}, u32[]{:S(2)}) copy-start(bf16[1024,8]{0,1:T(8,128)(2,1)S(1)} %all_gather.44) | copy-start | bytes 49156
  1209.8 729.5 %all-to-all-start.2 = ((bf16[8,8,128,2048]{3,2,0,1:T(8,128)(2,1)}), bf16[8,8,128,2048]{3,2,0,1:T(8,128)(2,1)}, u32[]{:S(2)}, u32[]{:S(2)}) async-start(bf16[8,8,128,2048]{3,2,0,1:T(8,128)(2,1)} %copy.115), calls=%async_computation.4 | async-start | bytes 67108864 | tf_op jit(solution)/shard_map/all_to_all | solution.py:111
  2153.0 728.8 %all-to-all-start.3 = ((bf16[8,8,128,2048]{3,2,0,1:T(8,128)(2,1)}), bf16[8,8,128,2048]{3,2,0,1:T(8,128)(2,1)}, u32[]{:S(2)}, u32[]{:S(2)}) async-start(bf16[8,8,128,2048]{3,2,0,1:T(8,128)(2,1)} %get-tuple-element.127), calls=%async_computation.5 | async-start | bytes 67108864 | tf_op jit(solution)/shard_map/all_to_all | solution.py:103
  2160.9 1007.5 %copy-start.70 = (pred[8192]{0:T(1024)(128)(4,1)}, pred[8192]{0:T(1024)(128)(4,1)S(1)}, u32[]{:S(2)}) copy-start(pred[8192]{0:T(1024)(128)(4,1)S(1)} %get-tuple-element.223) | copy-start | bytes 24580
  2881.8 744.6 %all-to-all-start.1 = ((bf16[8,8,128,2048]{3,2,0,1:T(8,128)(2,1)}), bf16[8,8,128,2048]{3,2,0,1:T(8,128)(2,1)}, u32[]{:S(2)}, u32[]{:S(2)}) async-start(bf16[8,8,128,2048]{3,2,0,1:T(8,128)(2,1)} %get-tuple-element.124), calls=%async_computation.2 | async-start | bytes 67108864 | tf_op jit(solution)/shard_map/all_to_all | solution.py:103
  2888.9 371.7 %reduce-scatter.13.cloned.1.call-start = ((), (), s32[]{:S(2)}) async-start(), calls=%async_computation.21 | async-start | bytes 10485760 | tf_op jit(solution)/shard_map/reduce_scatter | solution.py:90
  3190.7 109.6 %all-gather.23.cloned.1.call-start = ((), (), s32[]{:S(2)}) async-start(), calls=%async_computation.22 | async-start | bytes 5242880 | tf_op jit(solution)/shard_map/all_gather | solution.py:99
  3265.8 627.4 %reduce-scatter.23.cloned.1.call-start = ((), (), s32[]{:S(2)}) async-start(), calls=%async_computation.27 | async-start | bytes 2359296 | tf_op jit(solution)/shard_map/reduce_scatter | solution.py:365
  3306.6 588.7 %reduce-scatter.21.cloned.1.call-start = ((), (), s32[]{:S(2)}) async-start(), calls=%async_computation.26 | async-start | bytes 2359296 | tf_op jit(solution)/shard_map/reduce_scatter | solution.py:362
  3326.1 571.0 %reduce-scatter.17.cloned.1.call-start = ((), (), s32[]{:S(2)}) async-start(), calls=%async_computation.24 | async-start | bytes 2359296 | tf_op jit(solution)/shard_map/reduce_scatter | solution.py:356
  3364.1 534.8 %reduce-scatter.19.cloned.1.call-start = ((), (), s32[]{:S(2)}) async-start(), calls=%async_computation.25 | async-start | bytes 2359296 | tf_op jit(solution)/shard_map/reduce_scatter | solution.py:359
  3379.4 565.5 %reduce-scatter.15.cloned.1.call-start = ((), (), s32[]{:S(2)}) async-start(), calls=%async_computation.23 | async-start | bytes 10485760 | tf_op jit(solution)/shard_map/reduce_scatter | solution.py:90
  3391.9 628.0 %reduce-scatter.11.cloned.1.call-start = ((), (), s32[]{:S(2)}) async-start(), calls=%async_computation.19 | async-start | bytes 10485760 | tf_op jit(solution)/shard_map/reduce_scatter | solution.py:90
  3649.6 219.5 %copy-start.71 = (pred[8192]{0:T(1024)(128)(4,1)S(1)}, pred[8192]{0:T(1024)(128)(4,1)}, u32[]{:S(2)}) copy-start(pred[8192]{0:T(1024)(128)(4,1)} %copy-done.70) | copy-start | bytes 24580
  3892.5 127.4 %copy-start.5 = (f32[256,2048]{1,0:T(8,128)S(1)}, f32[256,2048]{1,0:T(8,128)}, u32[]{:S(2)}) copy-start(f32[256,2048]{1,0:T(8,128)} %copy-done.3) | copy-start | bytes 6291460
  3892.5 127.4 %copy-start.49 = (f32[2048]{0:T(1024)S(1)}, f32[2048]{0:T(1024)}, u32[]{:S(2)}) copy-start(f32[2048]{0:T(1024)} %param.35) | copy-start | bytes 24580
  3892.6 127.4 %copy-start.62 = (f32[256]{0:T(256)S(1)}, f32[256]{0:T(256)}, u32[]{:S(2)}) copy-start(f32[256]{0:T(256)} %copy-done.60) | copy-start | bytes 3076
  3892.6 127.4 %copy-start.66 = (f32[256]{0:T(256)S(1)}, f32[256]{0:T(256)}, u32[]{:S(2)}) copy-start(f32[256]{0:T(256)} %copy-done.65) | copy-start | bytes 3076
  (75 other events, 1352.5 us)
Sparse Core Ops, SparseCore 0:
  10.1 51.9 all-gather.14
  64.3 32.9 all-gather.8
  99.4 49.2 all-gather.12
  150.7 47.7 all-gather.10
  200.4 49.6 all-gather.16
  257.6 69.8 reduce-scatter.8
  332.2 34.4 all-gather.18
  489.2 34.8 all-gather.20
  3190.8 69.6 reduce-scatter.12
  3265.8 34.4 all-gather.22
  3306.8 353.6 reduce-scatter.22
  3663.8 66.7 reduce-scatter.20
  3734.2 66.8 reduce-scatter.16
  3805.0 66.7 reduce-scatter.18
  3874.2 70.6 reduce-scatter.14
  3947.5 72.3 reduce-scatter.10
where the time goes:
time: 4050 us; the launch traced here: 4030 us
  waiting for transfers between devices  2540 us (63%)
  local copies, waits for them, and re-layouts  937 us (23%)
  matrix products  344 us (8%)
  other arithmetic  110 us (3%)
  blocking collectives  56.3 us (1%)
    all_to_all x2, waiting for transfers between devices, to_experts(): return lax.all_to_all(picked, 'dp', split_axis=1, concat_axis=1, tiled=True)  1150 us
    all_to_all x2, waiting for transfers between devices, from_experts(): return lax.all_to_all(values, 'dp', split_axis=1, concat_axis=1, tiled=True)  954 us
    gather x2, local copies, waits for them, and re-layouts, pair_sum(): jnp.take(table, pair_slots.reshape(-1), axis=0, mode='fill', fill_value=0)  476 us
    reduce_scatter x4, waiting for transfers between devices, row_sum(): lax.psum_scatter(term_fn(jnp.int32(0), lax.axis_size('tensor') * tok_rows...  217 us
    gather x2, local copies, waits for them, and re-layouts, to_experts(): jnp.take(source_rows, slot_token, axis=0, mode='fill', fill_value=0)  129 us
    dot_general x29, matrix products, matmul(): return jnp.dot(left_side, right_side, preferred_element_type=jnp.float32)  102 us
    dot_general x28, matrix products, contract_first(): lax.dot_general(left_side, right_side, (((0,), (0,)), ((), ())), preferre...  94.4 us
    dot_general x28, matrix products, contract_last(): lax.dot_general(left_side, right_side, (((1,), (1,)), ((), ())), preferre...  84.5 us
  transfers between devices with their start and end apart: 20, of which 15 were waited for; matrix products, arithmetic and copies ran while one was open for 26% of the time, Pallas kernels for 0%

commit v1 on v0

--- a/solution.py
+++ b/solution.py
@@ -1,6 +1,10 @@
 import jax
 import jax.numpy as jnp
+import functools
+
 from jax import lax
+from jax.experimental import pallas as pl
+from jax.experimental.pallas import tpu as pltpu
 from jax.sharding import PartitionSpec as P
 
 WINDOW = 1024
@@ -146,6 +150,374 @@
         jnp.bfloat16
     )
     return (grad_rows.reshape(rows_in.shape), grad_gate, grad_up, grad_down)
+
+
+VMEM_BYTES = 60 * 1024 * 1024
+COLUMN_CHUNK = 512
+
+
+def select_rows(places_ref, gates_ref, pick_ref, capacity):
+    expert_count, seq_len = places_ref.shape[1:]
+    slot_range = lax.broadcasted_iota(jnp.int32, (capacity, seq_len), 0)
+    for expert in range(expert_count):
+        hit = places_ref[0, expert : expert + 1, :] == slot_range
+        weight = 1.0 if gates_ref is None else gates_ref[0, expert : expert + 1, :]
+        rows = slice(expert * capacity, (expert + 1) * capacity)
+        pick_ref[rows, :] = jnp.where(hit, weight, 0.0).astype(jnp.bfloat16)
+
+
+def spread_rows(places_ref, gates_ref, pick_ref, capacity):
+    seq_len, expert_count = places_ref.shape[1:]
+    slot_range = lax.broadcasted_iota(jnp.int32, (seq_len, capacity), 1)
+    for expert in range(expert_count):
+        hit = places_ref[0, :, expert : expert + 1] == slot_range
+        weight = 1.0 if gates_ref is None else gates_ref[0, :, expert : expert + 1]
+        columns = slice(expert * capacity, (expert + 1) * capacity)
+        pick_ref[:, columns] = jnp.where(hit, weight, 0.0).astype(jnp.bfloat16)
+
+
+def rows_to_slots(pick_ref, rows_ref, slots_ref, pack, capacity):
+    width = rows_ref.shape[2]
+    expert_count = slots_ref.shape[0]
+    for start in range(0, width, COLUMN_CHUNK):
+        columns = slice(start, start + COLUMN_CHUNK)
+        picked = matmul(pick_ref[...], rows_ref[0, :, columns]).astype(jnp.bfloat16)
+        slots_ref[:, pack, :, columns] = picked.reshape(expert_count, capacity, COLUMN_CHUNK)
+
+
+def slots_to_rows(pick_ref, slots_ref, rows_ref, pack):
+    width = rows_ref.shape[2]
+    for start in range(0, width, COLUMN_CHUNK):
+        columns = slice(start, start + COLUMN_CHUNK)
+        slots = slots_ref[:, pack, :, columns].reshape(-1, COLUMN_CHUNK)
+        rows_ref[0, :, columns] = matmul(pick_ref[...], slots).astype(rows_ref.dtype)
+
+
+def cot_kernel(packs, experts, capacity, places, gates, rows, down, slots_out, hidden_out, slots, pick):
+    step = pl.program_id(0)
+
+    @pl.when(step < packs)
+    def _():
+        select_rows(places, gates, pick, capacity)
+        rows_to_slots(pick, rows, slots, step, capacity)
+
+    @pl.when(step >= packs)
+    def _():
+        block = slots[step - packs].reshape(packs * capacity, -1)
+        slots_out[0] = block
+        hidden_out[0] = contract_last(block, down[0])
+
+
+def row_kernel(
+    packs, experts, capacity, places, places_t, rows, gate, up, grad_hidden,
+    slots_out, hidden_out, gated_out, lifted_out, rows_out, slots, grads, pick, spread,
+):
+    step = pl.program_id(0)
+
+    @pl.when(step < packs)
+    def _():
+        select_rows(places, None, pick, capacity)
+        rows_to_slots(pick, rows, slots, step, capacity)
+
+    @pl.when((step >= packs) & (step < packs + experts))
+    def _():
+        expert = step - packs
+        block = slots[expert].reshape(packs * capacity, -1)
+        slots_out[0] = block
+        gated = matmul(block, gate[0])
+        lifted = matmul(block, up[0])
+        sig = 1.0 / (1.0 + jnp.exp(-gated))
+        active = gated * sig
+        hidden_out[0] = (active * lifted).astype(jnp.bfloat16)
+        above = grad_hidden[0]
+        grad_gated = (above * lifted * sig * (1.0 + gated * (1.0 - sig))).astype(jnp.bfloat16)
+        grad_lifted = (above * active).astype(jnp.bfloat16)
+        gated_out[0] = grad_gated
+        lifted_out[0] = grad_lifted
+        back = contract_last(grad_gated, gate[0]) + contract_last(grad_lifted, up[0])
+        grads[expert] = back.astype(jnp.bfloat16).reshape(packs, capacity, -1)
+
+    @pl.when(step >= packs + experts)
+    def _():
+        spread_rows(places_t, None, spread, capacity)
+        slots_to_rows(spread, grads, rows_out, step - packs - experts)
+
+
+def mix_kernel(packs, experts, capacity, places_t, gates_t, hidden, down, rows_out, results, spread):
+    step = pl.program_id(0)
+
+    @pl.when(step < experts)
+    def _():
+        result = matmul(hidden[0], down[0])
+        results[step] = result.astype(jnp.bfloat16).reshape(packs, capacity, -1)
+
+    @pl.when(step >= experts)
+    def _():
+        spread_rows(places_t, gates_t, spread, capacity)
+        slots_to_rows(spread, results, rows_out, step - experts)
+
+
+def weight_kernel(planes, *refs):
+    slots, grads, hidden, gated, lifted = (refs[i * planes : (i + 1) * planes] for i in range(5))
+    gate_out, up_out, down_out = refs[5 * planes :]
+
+    def total(left, right):
+        result = contract_first(left[0][0], right[0][0])
+        for index in range(1, planes):
+            result = result + contract_first(left[index][0], right[index][0])
+        return result
+
+    gate_out[0] = total(slots, gated)
+    up_out[0] = total(slots, lifted)
+    down_out[0] = total(hidden, grads)
+
+
+def block(shape, place):
+    tail = (0,) * (len(shape) - 1)
+    return pl.BlockSpec((1,) + tuple(shape[1:]), lambda step: (place(step),) + tail)
+
+
+def staged(first, count):
+    return lambda step: jnp.clip(step - first, 0, count - 1)
+
+
+def shape_of(shape, kind):
+    return jax.ShapeDtypeStruct(shape, kind)
+
+
+def call(kernel, steps, specs, out_specs, out_shape, scratch):
+    return pl.pallas_call(
+        kernel,
+        grid=(steps,),
+        in_specs=specs,
+        out_specs=out_specs,
+        out_shape=out_shape,
+        scratch_shapes=scratch,
+        compiler_params=pltpu.CompilerParams(
+            dimension_semantics=("arbitrary",), vmem_limit_bytes=VMEM_BYTES
+        ),
+    )
+
+
+def cot_slots(places, gates, rows, down, capacity):
+    packs, seq_len, width = rows.shape
+    experts, hidden_width, _ = down.shape
+    slot_rows = packs * capacity
+    by_pack, by_expert = staged(0, packs), staged(packs, experts)
+    out_shape = [
+        shape_of((experts, slot_rows, width), jnp.bfloat16),
+        shape_of((experts, slot_rows, hidden_width), jnp.float32),
+    ]
+    return call(
+        functools.partial(cot_kernel, packs, experts, capacity),
+        packs + experts,
+        [block(places.shape, by_pack), block(gates.shape, by_pack), block(rows.shape, by_pack), block(down.shape, by_expert)],
+        [block(out.shape, by_expert) for out in out_shape],
+        out_shape,
+        [
+            pltpu.VMEM((experts, packs, capacity, width), jnp.bfloat16),
+            pltpu.VMEM((experts * capacity, seq_len), jnp.bfloat16),
+        ],
+    )(places, gates, rows, down)
+
+
+def row_slots(places, places_t, rows, gate, up, grad_hidden, capacity):
+    packs, seq_len, width = rows.shape
+    experts, _, hidden_width = gate.shape
+    slot_rows = packs * capacity
+    first, middle, last = staged(0, packs), staged(packs, experts), staged(packs + experts, packs)
+    narrow = shape_of((experts, slot_rows, hidden_width), jnp.bfloat16)
+    out_shape = [
+        shape_of((experts, slot_rows, width), jnp.bfloat16), narrow, narrow, narrow,
+        shape_of(rows.shape, jnp.bfloat16),
+    ]
+    return call(
+        functools.partial(row_kernel, packs, experts, capacity),
+        2 * packs + experts,
+        [
+            block(places.shape, first), block(places_t.shape, last), block(rows.shape, first),
+            block(gate.shape, middle), block(up.shape, middle), block(grad_hidden.shape, middle),
+        ],
+        [block(out.shape, middle) for out in out_shape[:4]] + [block(rows.shape, last)],
+        out_shape,
+        [
+            pltpu.VMEM((experts, packs, capacity, width), jnp.bfloat16),
+            pltpu.VMEM((experts, packs, capacity, width), jnp.bfloat16),
+            pltpu.VMEM((experts * capacity, seq_len), jnp.bfloat16),
+            pltpu.VMEM((seq_len, experts * capacity), jnp.bfloat16),
+        ],
+    )(places, places_t, rows, gate, up, grad_hidden)
+
+
+def mix_rows(places_t, gates_t, hidden, down, capacity):
+    packs, seq_len, _ = places_t.shape
+    experts, _, width = down.shape
+    first, last = staged(0, experts), staged(experts, packs)
+    out = shape_of((packs, seq_len, width), jnp.bfloat16)
+    return call(
+        functools.partial(mix_kernel, packs, experts, capacity),
+        packs + experts,
+        [
+            block(places_t.shape, last), block(gates_t.shape, last),
+            block(hidden.shape, first), block(down.shape, first),
+        ],
+        block(out.shape, last),
+        out,
+        [
+            pltpu.VMEM((experts, packs, capacity, width), jnp.bfloat16),
+            pltpu.VMEM((seq_len, experts * capacity), jnp.bfloat16),
+        ],
+    )(places_t, gates_t, hidden, down)
+
+
+def weight_grads(slots, grads, hidden, gated, lifted):
+    planes = len(slots)
+    operands = [*slots, *grads, *hidden, *gated, *lifted]
+    experts, _, width = slots[0].shape
+    hidden_width = hidden[0].shape[2]
+    each = lambda step: step
+    out_shape = [
+        shape_of((experts, width, hidden_width), jnp.float32),
+        shape_of((experts, width, hidden_width), jnp.float32),
+        shape_of((experts, hidden_width, width), jnp.float32),
+    ]
+    return call(
+        functools.partial(weight_kernel, planes),
+        experts,
+        [block(operand.shape, each) for operand in operands],
+        [block(out.shape, each) for out in out_shape],
+        out_shape,
+        [],
+    )(*operands)
+
+
+def routing(all_ids, all_gates, local_experts, capacity):
+    seq_len = all_ids.shape[1]
+    first = lax.axis_index("dp") * local_experts
+    wanted = first + jnp.arange(local_experts, dtype=jnp.int32)
+    matches = all_ids[:, :, :, None] == wanted
+    member = jnp.any(matches, axis=2)
+    gates = jnp.sum(jnp.where(matches, all_gates.astype(jnp.float32)[..., None], 0.0), axis=2)
+    order = jnp.arange(seq_len, dtype=jnp.int32)
+    earlier = (order[:, None] > order[None, :]).astype(jnp.bfloat16)
+    before = jnp.einsum(
+        "ts,pse->pte", earlier, member.astype(jnp.bfloat16), preferred_element_type=jnp.float32
+    ).astype(jnp.int32)
+    return jnp.where(member & (before < capacity), before, -1), gates
+
+
+def experts_by_exchange(
+    second_in, cotangent, expert_ids, gate_values, w_gate, w_up, w_down, middle, capacity
+):
+    tok_rows, model_width = second_in.shape
+    tensor_count = lax.axis_size("tensor")
+    data_count = lax.axis_size("dp")
+    local_experts = w_gate.shape[0]
+    all_experts = local_experts * data_count
+    top_count = expert_ids.shape[1]
+    seq_len = tok_rows * tensor_count
+    pack_cot, pack_ids, pack_gates = (
+        gather_rows(cotangent), gather_rows(expert_ids), gather_rows(gate_values)
+    )
+    pack_second = gather_rows(second_in)
+    expert_range = jnp.arange(all_experts, dtype=jnp.int32)
+    matches = pack_ids[:, :, None] == expert_range[None, None, :]
+    token_counts = jnp.sum(matches.astype(jnp.float32), axis=1).astype(jnp.bfloat16)
+    token_range = jnp.arange(seq_len, dtype=jnp.int32)
+    earlier = (token_range[:, None] > token_range[None, :]).astype(jnp.bfloat16)
+    before = matmul(earlier, token_counts)
+    places = (
+        jnp.sum(jnp.where(matches, before[:, None, :], 0.0), axis=2).astype(jnp.int32).reshape(-1)
+    )
+    flat_ids = pack_ids.reshape(-1)
+    owners = flat_ids // local_experts
+    local_index = flat_ids % local_experts
+    dump_slot = all_experts * capacity
+    slot_index = jnp.where(
+        places < capacity,
+        local_index * (data_count * capacity) + owners * capacity + places,
+        dump_slot,
+    ).astype(jnp.int32)
+    pair_token = jnp.arange(seq_len * top_count) // top_count
+    slot_token = (
+        jnp.full((dump_slot + 1,), seq_len, jnp.int32).at[slot_index].set(pair_token)[:dump_slot]
+    )
+    pair_gates = pack_gates.astype(jnp.float32)
+    slot_gate = (
+        jnp.zeros((dump_slot + 1,), jnp.float32)
+        .at[slot_index]
+        .set(pair_gates.reshape(-1))[:dump_slot]
+    )
+    pair_slots = slot_index.reshape(seq_len, top_count)
+    layout = (local_experts, data_count, capacity)
+    arrived_rows = to_experts(pack_second, slot_token, None, layout)
+    expert_out, gated_all, lifted_all = lax.map(
+        expert_forward, (arrived_rows, w_gate, w_up, w_down)
+    )
+    returned = from_experts(expert_out).reshape(-1, model_width)
+
+    def combine_term(offset, row_count):
+        return pair_sum(returned, pack_gates, pair_slots, row_count)
+
+    outputs = middle + row_sum(combine_term, tok_rows)
+    grad_arrived = to_experts(pack_cot, slot_token, slot_gate, layout)
+    grad_rows_all, grad_w_gate, grad_w_up, grad_w_down = lax.map(
+        expert_backward, (arrived_rows, grad_arrived, gated_all, lifted_all, w_gate, w_up, w_down)
+    )
+    returned_grad = from_experts(grad_rows_all).reshape(-1, model_width)
+    unit_gates = jnp.ones_like(pack_gates)
+
+    def dispatch_term(offset, row_count):
+        return pair_sum(returned_grad, unit_gates, pair_slots, row_count)
+
+    grad_second = row_sum(dispatch_term, tok_rows)
+    return outputs, grad_second, grad_w_gate, grad_w_up, grad_w_down
+
+
+def experts_by_gather(
+    second_in, cotangent, expert_ids, gate_values, w_gate, w_up, w_down, middle, capacity
+):
+    tok_rows, model_width = second_in.shape
+    axes = ("dp", "tensor")
+    data_count = lax.axis_size("dp")
+    seq_len = tok_rows * lax.axis_size("tensor")
+    local_experts = w_gate.shape[0]
+
+    def everywhere(values):
+        gathered = lax.all_gather(values, axes, axis=0, tiled=True)
+        return gathered.reshape(data_count, seq_len, values.shape[1])
+
+    places_t, gates_t = routing(
+        everywhere(expert_ids), everywhere(gate_values), local_experts, capacity
+    )
+    places, gates = places_t.transpose(0, 2, 1), gates_t.transpose(0, 2, 1)
+    per_plane = 2
+    planes = data_count // per_plane
+    all_cot = everywhere(cotangent)
+    all_rows = everywhere(second_in)
+    kept = []
+    row_parts, mix_parts = [], []
+    for plane in range(planes):
+        packs = slice(plane * per_plane, (plane + 1) * per_plane)
+        grad_slots, grad_hidden = cot_slots(
+            places[packs], gates[packs], all_cot[packs], w_down, capacity
+        )
+        slots, hidden, grad_gated, grad_lifted, row_part = row_slots(
+            places[packs], places_t[packs], all_rows[packs], w_gate, w_up, grad_hidden, capacity
+        )
+        row_parts.append(row_part)
+        mix_parts.append(mix_rows(places_t[packs], gates_t[packs], hidden, w_down, capacity))
+        kept.append((slots, grad_slots, hidden, grad_gated, grad_lifted))
+
+    def scattered(parts):
+        whole = jnp.concatenate(parts, axis=0).reshape(data_count * seq_len, model_width)
+        summed = lax.psum_scatter(whole, axes, scatter_dimension=0, tiled=True)
+        return summed.astype(jnp.float32)
+
+    grad_second = scattered(row_parts)
+    outputs = middle + scattered(mix_parts)
+    grad_w_gate, grad_w_up, grad_w_down = weight_grads(*zip(*kept))
+    return outputs, grad_second, grad_w_gate, grad_w_up, grad_w_down
 
 
 def shards(
@@ -179,11 +551,8 @@
     inputs_f32 = inputs.astype(jnp.float32)
     normed_one, factor_one = norm_parts(inputs_f32)
     first_in = (normed_one * attn_gain).astype(jnp.bfloat16)
-    pack_in, pack_cot, pack_ids, pack_gates, pack_segs = (
+    pack_in, pack_segs = (
         lax.all_gather(first_in, "tensor", axis=0, tiled=True),
-        lax.all_gather(cotangent, "tensor", axis=0, tiled=True),
-        lax.all_gather(expert_ids, "tensor", axis=0, tiled=True),
-        lax.all_gather(gate_values, "tensor", axis=0, tiled=True),
         lax.all_gather(segment_ids, "tensor", axis=1, tiled=True),
     )
     full_query, full_key, full_value, full_output = (
@@ -231,58 +600,14 @@
     middle = inputs_f32 + row_sum(attn_term, tok_rows)
     normed_two, factor_two = norm_parts(middle)
     second_in = (normed_two * ffn_gain).astype(jnp.bfloat16)
-    pack_second = gather_rows(second_in)
-    expert_range = jnp.arange(all_experts, dtype=jnp.int32)
-    matches = pack_ids[:, :, None] == expert_range[None, None, :]
-    token_counts = jnp.sum(matches.astype(jnp.float32), axis=1).astype(jnp.bfloat16)
-    token_range = jnp.arange(seq_len, dtype=jnp.int32)
-    earlier = (token_range[:, None] > token_range[None, :]).astype(jnp.bfloat16)
-    before = matmul(earlier, token_counts)
-    places = (
-        jnp.sum(jnp.where(matches, before[:, None, :], 0.0), axis=2).astype(jnp.int32).reshape(-1)
-    )
-    flat_ids = pack_ids.reshape(-1)
-    owners = flat_ids // local_experts
-    local_index = flat_ids % local_experts
-    dump_slot = all_experts * capacity
-    slot_index = jnp.where(
-        places < capacity,
-        local_index * (data_count * capacity) + owners * capacity + places,
-        dump_slot,
-    ).astype(jnp.int32)
-    pair_token = jnp.arange(seq_len * top_count) // top_count
-    slot_token = (
-        jnp.full((dump_slot + 1,), seq_len, jnp.int32).at[slot_index].set(pair_token)[:dump_slot]
-    )
-    pair_gates = pack_gates.astype(jnp.float32)
-    slot_gate = (
-        jnp.zeros((dump_slot + 1,), jnp.float32)
-        .at[slot_index]
-        .set(pair_gates.reshape(-1))[:dump_slot]
-    )
-    pair_slots = slot_index.reshape(seq_len, top_count)
-    layout = (local_experts, data_count, capacity)
-    arrived_rows = to_experts(pack_second, slot_token, None, layout)
-    expert_out, gated_all, lifted_all = lax.map(
-        expert_forward, (arrived_rows, w_gate, w_up, w_down)
-    )
-    returned = from_experts(expert_out).reshape(-1, model_width)
-
-    def combine_term(offset, row_count):
-        return pair_sum(returned, pack_gates, pair_slots, row_count)
-
-    outputs = middle + row_sum(combine_term, tok_rows)
-    grad_arrived = to_experts(pack_cot, slot_token, slot_gate, layout)
-    grad_rows_all, grad_w_gate, grad_w_up, grad_w_down = lax.map(
-        expert_backward, (arrived_rows, grad_arrived, gated_all, lifted_all, w_gate, w_up, w_down)
-    )
-    returned_grad = from_experts(grad_rows_all).reshape(-1, model_width)
-    unit_gates = jnp.ones_like(pack_gates)
-
-    def dispatch_term(offset, row_count):
-        return pair_sum(returned_grad, unit_gates, pair_slots, row_count)
-
-    grad_second = row_sum(dispatch_term, tok_rows)
+    if seq_len <= local_experts * capacity:
+        outputs, grad_second, grad_w_gate, grad_w_up, grad_w_down = experts_by_gather(
+            second_in, cotangent, expert_ids, gate_values, w_gate, w_up, w_down, middle, capacity
+        )
+    else:
+        outputs, grad_second, grad_w_gate, grad_w_up, grad_w_down = experts_by_exchange(
+            second_in, cotangent, expert_ids, gate_values, w_gate, w_up, w_down, middle, capacity
+        )
     ffn_gain_part = jnp.sum(grad_second * normed_two, axis=0)
     grad_middle = cotangent.astype(jnp.float32) + norm_back(
         grad_second, normed_two, factor_two, ffn_gain

time: 4050 us -> 2060 us (0.51)
  waiting for transfers between devices: 2540 us -> 1200 us
  local copies, waits for them, and re-layouts: 937 us -> 92.4 us
  Pallas kernels: 0 us -> 383 us
  matrix products: 344 us -> 98.5 us
  blocking collectives: 56.3 us -> 142 us
    all_to_all x4 -> x0, waiting for transfers between devices: 2100 us -> none  [the longest x2 1150 us: to_experts(): return lax.all_to_all(picked, 'dp', split_axis=1, concat_axis=1, tiled=True)]
    reduce_scatter x0 -> x2, waiting for transfers between devices: none -> 653 us  [scattered(): summed = lax.psum_scatter(whole, axes, scatter_dimension=0, tiled=True)]
    gather x4 -> x0, local copies, waits for them, and re-layouts: 605 us -> none  [the longest x2 476 us: pair_sum(): jnp.take(table, pair_slots.reshape(-1), axis=0, mode='fill', fill_value=0)]
    pallas_call x0 -> x13, Pallas kernels: none -> 383 us  [the longest x4 160 us: row_slots(): call(functools.partial(row_kernel, packs, experts, capacity), 2 * packs +...]
    all_gather x1 -> x2, waiting for transfers between devices: 0.56 us -> 94.1 us  [everywhere(): gathered = lax.all_gather(values, axes, axis=0, tiled=True)]
    dot_general x29 -> x4, matrix products: 102 us -> 23.3 us  [matmul(): return jnp.dot(left_side, right_side, preferred_element_type=jnp.float32)]
    dot_general x28 -> x4, matrix products: 94.4 us -> 17.3 us  [contract_first(): lax.dot_general(left_side, right_side, (((0,), (0,)), ((), ())), preferre...]
    all_gather x2, blocking collectives: 10.4 us -> 80.9 us  [everywhere(): gathered = lax.all_gather(values, axes, axis=0, tiled=True)]
  transfers between devices with their start and end apart: 20 -> 16, of which waited for: 15 -> 13; matrix products, arithmetic and copies ran while one was open for 26% -> 9% of each run, Pallas kernels for 0% -> 11%
where the time goes in v1:
time: 2060 us; the launch traced here: 2050 us
  waiting for transfers between devices  1200 us (58%)
  Pallas kernels  383 us (19%)
  blocking collectives  142 us (7%)
  other arithmetic  112 us (5%)
  matrix products  98.5 us (5%)
  local copies, waits for them, and re-layouts  92.4 us (4%)
    reduce_scatter x2, waiting for transfers between devices, scattered(): summed = lax.psum_scatter(whole, axes, scatter_dimension=0, tiled=True)  653 us
    reduce_scatter x2, waiting for transfers between devices, row_sum(): lax.psum_scatter(term_fn(jnp.int32(0), lax.axis_size('tensor') * tok_rows...  171 us
    pallas_call x4, Pallas kernels, row_slots(): call(functools.partial(row_kernel, packs, experts, capacity), 2 * packs +...  160 us
    all_gather x2, waiting for transfers between devices, everywhere(): gathered = lax.all_gather(values, axes, axis=0, tiled=True)  94.1 us
    pallas_call x4, Pallas kernels, mix_rows(): call(functools.partial(mix_kernel, packs, experts, capacity), packs + exp...  88.8 us
    pallas_call x4, Pallas kernels, cot_slots(): call(functools.partial(cot_kernel, packs, experts, capacity), packs + exp...  86 us
    all_gather x2, blocking collectives, everywhere(): gathered = lax.all_gather(values, axes, axis=0, tiled=True)  80.9 us
    reduce_scatter x1, waiting for transfers between devices, shards(): lax.psum_scatter(output_part.astype(jnp.bfloat16), 'dp', scatter_dimensio...  57.2 us
  transfers between devices with their start and end apart: 16, of which 13 were waited for; matrix products, arithmetic and copies ran while one was open for 9% of the time, Pallas kernels for 11%

profile of v1, /device:TPU:0, one launch (start us, length us, event | category | flops | bytes accessed | tf_op | source)
XLA Modules:
  0.0 2047.9 jit_solution(2163504744724585719)
XLA Ops:
  25.4 37.6 %all-gather.13.cloned.1.call-done = bf16[2048,512]{1,0:T(8,128)(2,1)} async-done(((bf16[256,512]{1,0:T(8,128)(2,1)}), bf16[2048,512]{1,0:T(8,128)(2,1)}) %all-gather.13.cloned.1.call-update) | async-done | bytes 2097168 | tf_op jit(solution)/shard_map/all_gather | solution.py:559
  63.0 35.1 %all-gather.9.cloned.1.call-done = bf16[1024,2048]{1,0:T(8,128)(2,1)} async-done(((bf16[256,2048]{1,0:T(8,128)(2,1)}), bf16[1024,2048]{1,0:T(8,128)(2,1)}) %all-gather.9.cloned.1.call-update) | async-done | bytes 4194320 | tf_op jit(solution)/shard_map/all_gather | solution.py:555
  105.4 44.2 %all-gather.15.cloned.1.call-done = bf16[2048,512]{1,0:T(8,128)(2,1)} async-done(((bf16[256,512]{1,0:T(8,128)(2,1)}), bf16[2048,512]{1,0:T(8,128)(2,1)}) %all-gather.15.cloned.1.call-update) | async-done | bytes 2097168 | tf_op jit(solution)/shard_map/all_gather | solution.py:560
  176.5 22.9 %all-gather.11.cloned.1.call-done = bf16[2048,512]{1,0:T(8,128)(2,1)} async-done(((bf16[256,512]{1,0:T(8,128)(2,1)}), bf16[2048,512]{1,0:T(8,128)(2,1)}) %all-gather.11.cloned.1.call-update) | async-done | bytes 2097168 | tf_op jit(solution)/shard_map/all_gather | solution.py:561
  210.2 40.8 %all-gather.17.cloned.1.call-done = bf16[512,2048]{1,0:T(8,128)(2,1)} async-done(((bf16[512,256]{1,0:T(8,128)(2,1)}), bf16[512,2048]{1,0:T(8,128)(2,1)}) %all-gather.17.cloned.1.call-update) | async-done | bytes 2097168 | tf_op jit(solution)/shard_map/all_gather | solution.py:562
  259.0 99.3 %reduce-scatter.9.cloned.1.call-done = f32[256,2048]{1,0:T(8,128)} async-done(((f32[1024,2048]{1,0:T(8,128)}), f32[256,2048]{1,0:T(8,128)}) %reduce-scatter.9.cloned.1.call-update) | async-done | bytes 2097168 | tf_op jit(solution)/shard_map/reduce_scatter | solution.py:94
  361.9 42.5 %all_gather.42 = s32[8192,8]{0,1:T(8,128)S(1)} all-gather(s32[256,8]{0,1:T(8,128)S(1)} %copy-done.61), channel_id=1, replica_groups=mesh['dp'=8,'tensor'=4] {'dp','tensor'}, dimensions={0}, use_global_device_ids=true | all-gather | bytes 270336 | tf_op jit(solution)/shard_map/all_gather | solution.py:487
  415.3 38.4 %all_gather.43 = bf16[8192,8]{0,1:T(8,128)(2,1)S(1)} all-gather(bf16[256,8]{0,1:T(8,128)(2,1)S(1)} %copy-done.66), channel_id=1, replica_groups=mesh['dp'=8,'tensor'=4] {'dp','tensor'}, dimensions={0}, use_global_device_ids=true | all-gather | bytes 135168 | tf_op jit(solution)/shard_map/all_gather | solution.py:487
  475.9 23.5 %fusion.58 = (bf16[2048,2048]{1,0:T(8,128)(2,1)}, bf16[2048,2048]{1,0:T(8,128)(2,1)}, bf16[2048,2048]{1,0:T(8,128)(2,1)}, bf16[2048,2048]{1,0:T(8,128)(2,1)}) fusion(bf16[8192,2048]{1,0:T(8,128)(2,1)} %all-gather.21.cloned.1.call-done), kind=kLoop, calls=%fused_computation.144 | loop fusion | bytes 67108864 | tf_op jit(solution)/shard_map/slice | solution.py:503
  499.4 21.4 %shard_map.264 = (bf16[8,256,2048]{2,1,0:T(8,128)(2,1)}, f32[8,256,256]{2,1,0:T(8,128)}) custom-call(s32[2,8,1024]{2,1,0:T(8,128)} %copy.79.places, f32[2,8,1024]{2,1,0:T(8,128)} %get-tuple-element.126.gates, bf16[2,1024,2048]{2,1,0:T(8,128)(2,1)} %bitcast.162, bf16[8,256,2048]{2,1,0:T(8,128)(2,1)} %down.15), custom_call_target="tpu_custom_call" | custom-call | tf_op jit(solution)/shard_map/pallas_call | solution.py:311
  520.8 21.2 %shard_map.261 = (bf16[8,256,2048]{2,1,0:T(8,128)(2,1)}, f32[8,256,256]{2,1,0:T(8,128)}) custom-call(s32[2,8,1024]{2,1,0:T(8,128)} %copy.76.places, f32[2,8,1024]{2,1,0:T(8,128)} %get-tuple-element.127.gates, bf16[2,1024,2048]{2,1,0:T(8,128)(2,1)} %bitcast.161, bf16[8,256,2048]{2,1,0:T(8,128)(2,1)} %down.15), custom_call_target="tpu_custom_call" | custom-call | tf_op jit(solution)/shard_map/pallas_call | solution.py:311
  542.0 21.3 %shard_map.258 = (bf16[8,256,2048]{2,1,0:T(8,128)(2,1)}, f32[8,256,256]{2,1,0:T(8,128)}) custom-call(s32[2,8,1024]{2,1,0:T(8,128)} %copy.73.places, f32[2,8,1024]{2,1,0:T(8,128)} %get-tuple-element.128.gates, bf16[2,1024,2048]{2,1,0:T(8,128)(2,1)} %bitcast.160, bf16[8,256,2048]{2,1,0:T(8,128)(2,1)} %down.15), custom_call_target="tpu_custom_call" | custom-call | tf_op jit(solution)/shard_map/pallas_call | solution.py:311
  563.3 22.1 %shard_map.255 = (bf16[8,256,2048]{2,1,0:T(8,128)(2,1)}, f32[8,256,256]{2,1,0:T(8,128)}) custom-call(s32[2,8,1024]{2,1,0:T(8,128)} %copy.70.places, f32[2,8,1024]{2,1,0:T(8,128)} %get-tuple-element.125.gates, bf16[2,1024,2048]{2,1,0:T(8,128)(2,1)} %bitcast.159, bf16[8,256,2048]{2,1,0:T(8,128)(2,1)} %down.15), custom_call_target="tpu_custom_call" | custom-call | tf_op jit(solution)/shard_map/pallas_call | solution.py:311
  585.4 86.5 %all-gather.19.cloned.1.call-done = bf16[8192,2048]{1,0:T(8,128)(2,1)} async-done(((bf16[256,2048]{1,0:T(8,128)(2,1)}), bf16[8192,2048]{1,0:T(8,128)(2,1)}) %all-gather.19.cloned.1.call-update) | async-done | bytes 33554448 | tf_op jit(solution)/shard_map/all_gather | solution.py:487
  671.8 23.1 %fusion.59 = (bf16[2048,2048]{1,0:T(8,128)(2,1)}, bf16[2048,2048]{1,0:T(8,128)(2,1)}, bf16[2048,2048]{1,0:T(8,128)(2,1)}, bf16[2048,2048]{1,0:T(8,128)(2,1)}) fusion(bf16[8192,2048]{1,0:T(8,128)(2,1)} %all-gather.19.cloned.1.call-done), kind=kLoop, calls=%fused_computation.145 | loop fusion | bytes 67108864 | tf_op jit(solution)/shard_map/slice | solution.py:506
  695.0 39.9 %shard_map.265 = (bf16[8,256,2048]{2,1,0:T(8,128)(2,1)}, bf16[8,256,256]{2,1,0:T(8,128)(2,1)}, bf16[8,256,256]{2,1,0:T(8,128)(2,1)}, bf16[8,256,256]{2,1,0:T(8,128)(2,1)}, bf16[2,1024,2048]{2,1,0:T(8,128)(2,1)}) custom-call(s32[2,8,1024]{2,1,0:T(8,128)} %copy.79.places, s32[2,1024,8]{2,1,0:T(8,128)} %get-tuple-element.106.places_t, ...), custom_call_target="tpu_custom_call" | custom-call | tf_op jit(solution)/shard_map/pallas_call | solution.py:334
  734.9 40.0 %shard_map.262 = (bf16[8,256,2048]{2,1,0:T(8,128)(2,1)}, bf16[8,256,256]{2,1,0:T(8,128)(2,1)}, bf16[8,256,256]{2,1,0:T(8,128)(2,1)}, bf16[8,256,256]{2,1,0:T(8,128)(2,1)}, bf16[2,1024,2048]{2,1,0:T(8,128)(2,1)}) custom-call(s32[2,8,1024]{2,1,0:T(8,128)} %copy.76.places, s32[2,1024,8]{2,1,0:T(8,128)} %get-tuple-element.107.places_t, ...), custom_call_target="tpu_custom_call" | custom-call | tf_op jit(solution)/shard_map/pallas_call | solution.py:334
  774.9 39.9 %shard_map.259 = (bf16[8,256,2048]{2,1,0:T(8,128)(2,1)}, bf16[8,256,256]{2,1,0:T(8,128)(2,1)}, bf16[8,256,256]{2,1,0:T(8,128)(2,1)}, bf16[8,256,256]{2,1,0:T(8,128)(2,1)}, bf16[2,1024,2048]{2,1,0:T(8,128)(2,1)}) custom-call(s32[2,8,1024]{2,1,0:T(8,128)} %copy.73.places, s32[2,1024,8]{2,1,0:T(8,128)} %get-tuple-element.108.places_t, ...), custom_call_target="tpu_custom_call" | custom-call | tf_op jit(solution)/shard_map/pallas_call | solution.py:334
  814.7 40.2 %shard_map.256 = (bf16[8,256,2048]{2,1,0:T(8,128)(2,1)}, bf16[8,256,256]{2,1,0:T(8,128)(2,1)}, bf16[8,256,256]{2,1,0:T(8,128)(2,1)}, bf16[8,256,256]{2,1,0:T(8,128)(2,1)}, bf16[2,1024,2048]{2,1,0:T(8,128)(2,1)}) custom-call(s32[2,8,1024]{2,1,0:T(8,128)} %copy.70.places, s32[2,1024,8]{2,1,0:T(8,128)} %get-tuple-element.105.places_t, ...), custom_call_target="tpu_custom_call" | custom-call | tf_op jit(solution)/shard_map/pallas_call | solution.py:334
  855.0 22.7 %pad_maximum_fusion.1 = bf16[8,1024,2048]{2,1,0:T(8,128)(2,1)} fusion(bf16[2,1024,2048]{2,1,0:T(8,128)(2,1)} %get-tuple-element.55, bf16[2,1024,2048]{2,1,0:T(8,128)(2,1)} %get-tuple-element.54, bf16[2,1024,2048]{2,1,0:T(8,128)(2,1)} %get-tuple-element.53, bf16[2,1024,2048]{2,1,0:T(8,128)(2,1)} %get-tuple-element.52), kind=kLoop, calls=%fused_computation.1 | loop fusion | flops 50331648 | bytes 67108864 | tf_op jit(solution)/shard_map/concatenate | solution.py:513
  877.8 352.4 %reduce-scatter.13.cloned.1.call-done = bf16[256,2048]{1,0:T(8,128)(2,1)} async-done(((bf16[8192,2048]{1,0:T(8,128)(2,1)}), bf16[256,2048]{1,0:T(8,128)(2,1)}) %reduce-scatter.13.cloned.1.call-update) | async-done | bytes 1048592 | tf_op jit(solution)/shard_map/reduce_scatter | solution.py:514
  1234.8 42.1 %all-gather.23.cloned.1.call-done = bf16[1024,2048]{1,0:T(8,128)(2,1)} async-done(((bf16[256,2048]{1,0:T(8,128)(2,1)}), bf16[1024,2048]{1,0:T(8,128)(2,1)}) %all-gather.23.cloned.1.call-update) | async-done | bytes 4194320 | tf_op jit(solution)/shard_map/all_gather | solution.py:103
  1380.5 22.2 %shard_map.266 = bf16[2,1024,2048]{2,1,0:T(8,128)(2,1)} custom-call(s32[2,1024,8]{2,1,0:T(8,128)} %get-tuple-element.106.places_t, f32[2,1024,8]{2,1,0:T(8,128)} %copy.112.gates_t, bf16[8,256,256]{2,1,0:T(8,128)(2,1)} %get-tuple-element.51.hidden.refs_11_, bf16[8,256,2048]{2,1,0:T(8,128)(2,1)} %down.15), custom_call_target="tpu_custom_call" | custom-call | tf_op jit(solution)/shard_map/pallas_call | solution.py:357
  1402.6 22.1 %shard_map.263 = bf16[2,1024,2048]{2,1,0:T(8,128)(2,1)} custom-call(s32[2,1024,8]{2,1,0:T(8,128)} %get-tuple-element.107.places_t, f32[2,1024,8]{2,1,0:T(8,128)} %copy.111.gates_t, bf16[8,256,256]{2,1,0:T(8,128)(2,1)} %get-tuple-element.49.hidden.refs_10_, bf16[8,256,2048]{2,1,0:T(8,128)(2,1)} %down.15), custom_call_target="tpu_custom_call" | custom-call | tf_op jit(solution)/shard_map/pallas_call | solution.py:357
  1424.8 22.4 %shard_map.260 = bf16[2,1024,2048]{2,1,0:T(8,128)(2,1)} custom-call(s32[2,1024,8]{2,1,0:T(8,128)} %get-tuple-element.108.places_t, f32[2,1024,8]{2,1,0:T(8,128)} %copy.110.gates_t, bf16[8,256,256]{2,1,0:T(8,128)(2,1)} %get-tuple-element.47.hidden.refs_9_, bf16[8,256,2048]{2,1,0:T(8,128)(2,1)} %down.15), custom_call_target="tpu_custom_call" | custom-call | tf_op jit(solution)/shard_map/pallas_call | solution.py:357
  1447.2 22.1 %shard_map.257 = bf16[2,1024,2048]{2,1,0:T(8,128)(2,1)} custom-call(s32[2,1024,8]{2,1,0:T(8,128)} %get-tuple-element.105.places_t, f32[2,1024,8]{2,1,0:T(8,128)} %copy.109.gates_t, bf16[8,256,256]{2,1,0:T(8,128)(2,1)} %get-tuple-element.45.hidden.refs_8_, bf16[8,256,2048]{2,1,0:T(8,128)(2,1)} %down.15), custom_call_target="tpu_custom_call" | custom-call | tf_op jit(solution)/shard_map/pallas_call | solution.py:357
  1469.2 23.1 %pad_maximum_fusion = bf16[8,1024,2048]{2,1,0:T(8,128)(2,1)} fusion(bf16[2,1024,2048]{2,1,0:T(8,128)(2,1)} %shard_map.266, bf16[2,1024,2048]{2,1,0:T(8,128)(2,1)} %shard_map.263, bf16[2,1024,2048]{2,1,0:T(8,128)(2,1)} %shard_map.260, bf16[2,1024,2048]{2,1,0:T(8,128)(2,1)} %shard_map.257), kind=kLoop, calls=%fused_computation | loop fusion | flops 50331648 | bytes 67108864 | tf_op jit(solution)/shard_map/concatenate | solution.py:513
  1492.4 48.2 %shard_map.267 = (f32[8,2048,256]{2,1,0:T(8,128)}, f32[8,2048,256]{2,1,0:T(8,128)}, f32[8,256,2048]{2,1,0:T(8,128)}) custom-call(bf16[8,256,2048]{2,1,0:T(8,128)(2,1)} %get-tuple-element.56.refs_0_, bf16[8,256,2048]{2,1,0:T(8,128)(2,1)} %get-tuple-element.57.refs_1_, bf16[8,256,2048]{2,1,0:T(8,128)(2,1)} %get-tuple-element.58.refs_2_, ...), custom_call_target="tpu_custom_call" | custom-call | tf_op jit(solution)/shard_map/pallas_call | solution.py:384
  1546.2 57.2 %reduce-scatter.23.cloned.1.call-done = bf16[512,256]{1,0:T(8,128)(2,1)} async-done(((bf16[512,2048]{1,0:T(8,128)(2,1)}), bf16[512,256]{1,0:T(8,128)(2,1)}) %reduce-scatter.23.cloned.1.call-update) | async-done | bytes 262160 | tf_op jit(solution)/shard_map/reduce_scatter | solution.py:690
  1605.2 71.5 %reduce-scatter.15.cloned.1.call-done = f32[256,2048]{1,0:T(8,128)} async-done(((f32[1024,2048]{1,0:T(8,128)}), f32[256,2048]{1,0:T(8,128)}) %reduce-scatter.15.cloned.1.call-update) | async-done | bytes 2097168 | tf_op jit(solution)/shard_map/reduce_scatter | solution.py:94
  1679.1 55.4 %all-reduce = (f32[2048]{0:T(1024)}, f32[128]{0:T(128)}, f32[128]{0:T(128)}, f32[2048]{0:T(1024)}) all-reduce(f32[2048]{0:T(1024)S(1)} %get-tuple-element.77, f32[128]{0:T(128)S(1)} %bitcast_reduce_fusion.1, f32[128]{0:T(128)S(1)} %bitcast_reduce_fusion, f32[2048]{0:T(1024)S(1)} %copy-done.52), channel_id=1, replica_groups=mesh['dp'=8,'tensor'=4] {'dp','tensor'}, use_global_device_ids=true, to_apply=%region_21.22 | all-reduce | flops 4352 | bytes 34816 | tf_op jit(solution)/shard_map/psum | solution.py:694
  1734.4 300.1 %reduce-scatter.11.cloned.1.call-done = bf16[256,2048]{1,0:T(8,128)(2,1)} async-done(((bf16[8192,2048]{1,0:T(8,128)(2,1)}), bf16[256,2048]{1,0:T(8,128)(2,1)}) %reduce-scatter.11.cloned.1.call-update) | async-done | bytes 1048592 | tf_op jit(solution)/shard_map/reduce_scatter | solution.py:514
  (289 shorter events, 229.4 us)
Async XLA Ops:
  8.0 55.0 %all-gather.13.cloned.1.call-start = ((), (), s32[]{:S(2)}) async-start(), calls=%async_computation.10 | async-start | bytes 2359296 | tf_op jit(solution)/shard_map/all_gather | solution.py:559
  8.7 89.4 %all-gather.9.cloned.1.call-start = ((), (), s32[]{:S(2)}) async-start(), calls=%async_computation.8 | async-start | bytes 5242880 | tf_op jit(solution)/shard_map/all_gather | solution.py:555
  12.9 136.7 %all-gather.15.cloned.1.call-start = ((), (), s32[]{:S(2)}) async-start(), calls=%async_computation.11 | async-start | bytes 2359296 | tf_op jit(solution)/shard_map/all_gather | solution.py:560
  13.6 185.8 %all-gather.11.cloned.1.call-start = ((), (), s32[]{:S(2)}) async-start(), calls=%async_computation.9 | async-start | bytes 2359296 | tf_op jit(solution)/shard_map/all_gather | solution.py:561
  14.2 236.7 %all-gather.17.cloned.1.call-start = ((), (), s32[]{:S(2)}) async-start(), calls=%async_computation.12 | async-start | bytes 2359296 | tf_op jit(solution)/shard_map/all_gather | solution.py:562
  14.8 343.5 %reduce-scatter.9.cloned.1.call-start = ((), (), s32[]{:S(2)}) async-start(), calls=%async_computation.13 | async-start | bytes 10485760 | tf_op jit(solution)/shard_map/reduce_scatter | solution.py:94
  16.8 143.7 %copy-start.24 = (f32[1024,64]{1,0:T(8,128)}, f32[1024,64]{1,0:T(8,128)S(1)}, u32[]{:S(2)}) copy-start(f32[1024,64]{1,0:T(8,128)S(1)} %get-tuple-element.137) | copy-start | bytes 786436
  16.8 143.7 %copy-start.26 = (f32[1024,64]{1,0:T(8,128)}, f32[1024,64]{1,0:T(8,128)S(1)}, u32[]{:S(2)}) copy-start(f32[1024,64]{1,0:T(8,128)S(1)} %get-tuple-element.138) | copy-start | bytes 786436
  105.4 51.5 %copy-start.45 = (f32[1024,4]{0,1:T(4,128)}, f32[1024,4]{0,1:T(4,128)S(1)}, u32[]{:S(2)}) copy-start(f32[1024,4]{0,1:T(4,128)S(1)} %add_rsqrt_fusion.1) | copy-start | bytes 49156
  258.3 100.0 %copy-start.5 = (bf16[256,2048]{1,0:T(8,128)(2,1)S(1)}, bf16[256,2048]{1,0:T(8,128)(2,1)}, u32[]{:S(2)}) copy-start(bf16[256,2048]{1,0:T(8,128)(2,1)} %param.16) | copy-start | bytes 3145732
  258.3 217.6 %all-gather.21.cloned.1.call-start = ((), (), s32[]{:S(2)}) async-start(), calls=%async_computation.15 | async-start | bytes 34603008 | tf_op jit(solution)/shard_map/all_gather | solution.py:487
  258.9 101.4 %copy-start.47 = (f32[2048]{0:T(1024)S(1)}, f32[2048]{0:T(1024)}, u32[]{:S(2)}) copy-start(f32[2048]{0:T(1024)} %param.27) | copy-start | bytes 24580
  258.9 412.9 %all-gather.19.cloned.1.call-start = ((), (), s32[]{:S(2)}) async-start(), calls=%async_computation.14 | async-start | bytes 34603008 | tf_op jit(solution)/shard_map/all_gather | solution.py:487
  360.2 872.7 %copy-start.3 = (f32[256,2048]{1,0:T(8,128)}, f32[256,2048]{1,0:T(8,128)S(1)}, u32[]{:S(2)}) copy-start(f32[256,2048]{1,0:T(8,128)S(1)} %get-tuple-element.88) | copy-start | bytes 6291460
  360.3 872.7 %copy-start.55 = (f32[256]{0:T(256)}, f32[256]{0:T(256)S(1)}, u32[]{:S(2)}) copy-start(f32[256]{0:T(256)S(1)} %add_rsqrt_fusion.2) | copy-start | bytes 3076
  361.8 868.4 %reduce-scatter.13.cloned.1.call-start = ((), (), s32[]{:S(2)}) async-start(), calls=%async_computation.17 | async-start | bytes 34603008 | tf_op jit(solution)/shard_map/reduce_scatter | solution.py:514
  877.7 355.2 %copy-start.16 = (bf16[256,2048]{1,0:T(8,128)(2,1)S(1)}, bf16[256,2048]{1,0:T(8,128)(2,1)}, u32[]{:S(2)}) copy-start(bf16[256,2048]{1,0:T(8,128)(2,1)} %param.31) | copy-start | bytes 3145732
  877.7 399.2 %all-gather.23.cloned.1.call-start = ((), (), s32[]{:S(2)}) async-start(), calls=%async_computation.18 | async-start | bytes 5242880 | tf_op jit(solution)/shard_map/all_gather | solution.py:103
  1234.7 306.1 %reduce-scatter.17.cloned.1.call-start = ((), (), s32[]{:S(2)}) async-start(), calls=%async_computation.20 | async-start | bytes 2359296 | tf_op jit(solution)/shard_map/reduce_scatter | solution.py:681
  1321.7 220.9 %reduce-scatter.19.cloned.1.call-start = ((), (), s32[]{:S(2)}) async-start(), calls=%async_computation.21 | async-start | bytes 2359296 | tf_op jit(solution)/shard_map/reduce_scatter | solution.py:684
  1338.0 206.4 %reduce-scatter.21.cloned.1.call-start = ((), (), s32[]{:S(2)}) async-start(), calls=%async_computation.22 | async-start | bytes 2359296 | tf_op jit(solution)/shard_map/reduce_scatter | solution.py:687
  1353.4 250.1 %reduce-scatter.23.cloned.1.call-start = ((), (), s32[]{:S(2)}) async-start(), calls=%async_computation.23 | async-start | bytes 2359296 | tf_op jit(solution)/shard_map/reduce_scatter | solution.py:690
  1360.5 316.3 %reduce-scatter.15.cloned.1.call-start = ((), (), s32[]{:S(2)}) async-start(), calls=%async_computation.19 | async-start | bytes 10485760 | tf_op jit(solution)/shard_map/reduce_scatter | solution.py:94
  1374.2 660.3 %reduce-scatter.11.cloned.1.call-start = ((), (), s32[]{:S(2)}) async-start(), calls=%async_computation.16 | async-start | bytes 34603008 | tf_op jit(solution)/shard_map/reduce_scatter | solution.py:514
  1540.6 136.2 %copy-start.6 = (bf16[256,2048]{1,0:T(8,128)(2,1)S(1)}, bf16[256,2048]{1,0:T(8,128)(2,1)}, u32[]{:S(2)}) copy-start(bf16[256,2048]{1,0:T(8,128)(2,1)} %param.16) | copy-start | bytes 3145732
  1540.6 136.2 %copy-start.49 = (f32[2048]{0:T(1024)S(1)}, f32[2048]{0:T(1024)}, u32[]{:S(2)}) copy-start(f32[2048]{0:T(1024)} %param.20) | copy-start | bytes 24580
  1540.7 136.1 %copy-start.58 = (f32[256]{0:T(256)S(1)}, f32[256]{0:T(256)}, u32[]{:S(2)}) copy-start(f32[256]{0:T(256)} %copy-done.57) | copy-start | bytes 3076
  1546.2 132.8 %copy-start.52 = (f32[2048]{0:T(1024)S(1)}, f32[2048]{0:T(1024)}, u32[]{:S(2)}) copy-start(f32[2048]{0:T(1024)} %get-tuple-element.75) | copy-start | bytes 24580
  1546.2 488.3 %copy-start.4 = (f32[256,2048]{1,0:T(8,128)S(1)}, f32[256,2048]{1,0:T(8,128)}, u32[]{:S(2)}) copy-start(f32[256,2048]{1,0:T(8,128)} %copy-done.3) | copy-start | bytes 6291460
  1546.2 488.3 %copy-start.48 = (f32[2048]{0:T(1024)S(1)}, f32[2048]{0:T(1024)}, u32[]{:S(2)}) copy-start(f32[2048]{0:T(1024)} %param.27) | copy-start | bytes 24580
  1546.2 488.3 %copy-start.56 = (f32[256]{0:T(256)S(1)}, f32[256]{0:T(256)}, u32[]{:S(2)}) copy-start(f32[256]{0:T(256)} %copy-done.55) | copy-start | bytes 3076
  1546.2 488.3 %copy-start.60 = (f32[256]{0:T(256)S(1)}, f32[256]{0:T(256)}, u32[]{:S(2)}) copy-start(f32[256]{0:T(256)} %copy-done.59) | copy-start | bytes 3076
  (62 other events, 300.0 us)
Sparse Core Ops, SparseCore 0:
  11.0 51.9 all-gather.12
  65.1 32.9 all-gather.8
  100.3 49.2 all-gather.14
  151.6 47.7 all-gather.10
  201.3 49.6 all-gather.16
  258.4 99.7 reduce-scatter.8
  1234.8 42.0 all-gather.22
  1321.8 67.6 reduce-scatter.16
  1394.0 66.9 reduce-scatter.18
  1465.4 66.7 reduce-scatter.20
  1536.1 67.3 reduce-scatter.22
  1606.1 70.6 reduce-scatter.14
  1679.1 355.4 reduce-scatter.10
Sparse Core Ops, SparseCore 1:
  262.1 213.8 all-gather.20
  479.1 192.7 all-gather.18
  877.8 352.4 reduce-scatter.12

commit v2 on v1

--- a/solution.py
+++ b/solution.py
@@ -185,15 +185,20 @@
         slots_ref[:, pack, :, columns] = picked.reshape(expert_count, capacity, COLUMN_CHUNK)
 
 
-def slots_to_rows(pick_ref, slots_ref, rows_ref, pack):
-    width = rows_ref.shape[2]
+def slots_to_rows(pick_ref, slots_ref, own_ref, other_ref, pack):
+    width = own_ref.shape[3]
     for start in range(0, width, COLUMN_CHUNK):
         columns = slice(start, start + COLUMN_CHUNK)
         slots = slots_ref[:, pack, :, columns].reshape(-1, COLUMN_CHUNK)
-        rows_ref[0, :, columns] = matmul(pick_ref[...], slots).astype(rows_ref.dtype)
-
-
-def cot_kernel(packs, experts, capacity, places, gates, rows, down, slots_out, hidden_out, slots, pick):
+        rows = matmul(pick_ref[...], slots).astype(own_ref.dtype)
+        rows = rows.reshape(2, 2, own_ref.shape[2], COLUMN_CHUNK)
+        own_ref[0, :, :, columns] = rows[:, 0]
+        other_ref[0, :, :, columns] = rows[:, 1]
+
+
+def cot_kernel(
+    packs, experts, capacity, table, places, gates, rows, down, slots_out, hidden_out, slots, pick
+):
     step = pl.program_id(0)
 
     @pl.when(step < packs)
@@ -208,16 +213,44 @@
         hidden_out[0] = contract_last(block, down[0])
 
 
+def piece_copies(own, other, rows, sems, pack):
+    half_rows = own.shape[1]
+    copies = []
+    for far in range(2):
+        for core, source in enumerate((own, other)):
+            for half, index in enumerate((4 * far + pack, 2 + 4 * pack + far)):
+                start = ((far * 2 + core) * 2 + half) * half_rows
+                copies.append(
+                    pltpu.make_async_copy(
+                        source.at[index],
+                        rows.at[pack, pl.ds(start, half_rows)],
+                        sems.at[pack * 8 + len(copies)],
+                    )
+                )
+    return copies
+
+
 def row_kernel(
-    packs, experts, capacity, places, places_t, rows, gate, up, grad_hidden,
-    slots_out, hidden_out, gated_out, lifted_out, rows_out, slots, grads, pick, spread,
+    packs, experts, capacity, places, places_t, own, other, gate, up, grad_hidden,
+    slots_out, hidden_out, gated_out, lifted_out, rows_own, rows_other,
+    rows, slots, grads, pick, spread, sems,
 ):
     step = pl.program_id(0)
 
-    @pl.when(step < packs)
+    @pl.when(step == 0)
     def _():
-        select_rows(places, None, pick, capacity)
-        rows_to_slots(pick, rows, slots, step, capacity)
+        for pack in range(packs):
+            for copy in piece_copies(own, other, rows, sems, pack):
+                copy.start()
+
+    for pack in range(packs):
+
+        @pl.when(step == pack)
+        def _(pack=pack):
+            select_rows(places, None, pick, capacity)
+            for copy in piece_copies(own, other, rows, sems, pack):
+                copy.wait()
+            rows_to_slots(pick, rows.at[pl.ds(pack, 1)], slots, pack, capacity)
 
     @pl.when((step >= packs) & (step < packs + experts))
     def _():
@@ -240,10 +273,12 @@
     @pl.when(step >= packs + experts)
     def _():
         spread_rows(places_t, None, spread, capacity)
-        slots_to_rows(spread, grads, rows_out, step - packs - experts)
-
-
-def mix_kernel(packs, experts, capacity, places_t, gates_t, hidden, down, rows_out, results, spread):
+        slots_to_rows(spread, grads, rows_own, rows_other, step - packs - experts)
+
+
+def mix_kernel(
+    packs, experts, capacity, places_t, gates_t, hidden, down, rows_own, rows_other, results, spread
+):
     step = pl.program_id(0)
 
     @pl.when(step < experts)
@@ -254,7 +289,7 @@
     @pl.when(step >= experts)
     def _():
         spread_rows(places_t, gates_t, spread, capacity)
-        slots_to_rows(spread, results, rows_out, step - experts)
+        slots_to_rows(spread, results, rows_own, rows_other, step - experts)
 
 
 def weight_kernel(planes, *refs):
@@ -274,36 +309,44 @@
 
 def block(shape, place):
     tail = (0,) * (len(shape) - 1)
-    return pl.BlockSpec((1,) + tuple(shape[1:]), lambda step: (place(step),) + tail)
+    return pl.BlockSpec((1,) + tuple(shape[1:]), lambda *ids: (place(*ids),) + tail)
 
 
 def staged(first, count):
-    return lambda step: jnp.clip(step - first, 0, count - 1)
+    return lambda step, *rest: jnp.clip(step - first, 0, count - 1)
 
 
 def shape_of(shape, kind):
     return jax.ShapeDtypeStruct(shape, kind)
 
 
-def call(kernel, steps, specs, out_specs, out_shape, scratch):
+def call(kernel, steps, specs, out_specs, out_shape, scratch, flops, prefetch=0):
     return pl.pallas_call(
         kernel,
-        grid=(steps,),
-        in_specs=specs,
-        out_specs=out_specs,
+        grid_spec=pltpu.PrefetchScalarGridSpec(
+            num_scalar_prefetch=prefetch,
+            grid=(steps,),
+            in_specs=specs,
+            out_specs=out_specs,
+            scratch_shapes=scratch,
+        ),
         out_shape=out_shape,
-        scratch_shapes=scratch,
+        cost_estimate=pl.CostEstimate(
+            flops=flops, transcendentals=0, bytes_accessed=flops // 500
+        ),
         compiler_params=pltpu.CompilerParams(
             dimension_semantics=("arbitrary",), vmem_limit_bytes=VMEM_BYTES
         ),
     )
 
 
-def cot_slots(places, gates, rows, down, capacity):
-    packs, seq_len, width = rows.shape
+def cot_slots(table, places, gates, rows, down, capacity):
+    packs = table.shape[0]
+    _, seq_len, width = rows.shape
     experts, hidden_width, _ = down.shape
     slot_rows = packs * capacity
     by_pack, by_expert = staged(0, packs), staged(packs, experts)
+    listed = lambda step, numbers: numbers[by_pack(step)]
     out_shape = [
         shape_of((experts, slot_rows, width), jnp.bfloat16),
         shape_of((experts, slot_rows, hidden_width), jnp.float32),
@@ -311,49 +354,58 @@
     return call(
         functools.partial(cot_kernel, packs, experts, capacity),
         packs + experts,
-        [block(places.shape, by_pack), block(gates.shape, by_pack), block(rows.shape, by_pack), block(down.shape, by_expert)],
+        [
+            block(places.shape, listed), block(gates.shape, listed), block(rows.shape, listed),
+            block(down.shape, by_expert),
+        ],
         [block(out.shape, by_expert) for out in out_shape],
         out_shape,
         [
             pltpu.VMEM((experts, packs, capacity, width), jnp.bfloat16),
             pltpu.VMEM((experts * capacity, seq_len), jnp.bfloat16),
         ],
-    )(places, gates, rows, down)
-
-
-def row_slots(places, places_t, rows, gate, up, grad_hidden, capacity):
-    packs, seq_len, width = rows.shape
-    experts, _, hidden_width = gate.shape
+        2 * experts * slot_rows * width * (seq_len + hidden_width),
+        1,
+    )(table, places, gates, rows, down)
+
+
+def row_slots(places, places_t, own, other, gate, up, grad_hidden, capacity):
+    packs, _, seq_len = places.shape
+    experts, width, hidden_width = gate.shape
     slot_rows = packs * capacity
     first, middle, last = staged(0, packs), staged(packs, experts), staged(packs + experts, packs)
     narrow = shape_of((experts, slot_rows, hidden_width), jnp.bfloat16)
+    part = shape_of((packs, 2, seq_len // 4, width), jnp.bfloat16)
     out_shape = [
-        shape_of((experts, slot_rows, width), jnp.bfloat16), narrow, narrow, narrow,
-        shape_of(rows.shape, jnp.bfloat16),
+        shape_of((experts, slot_rows, width), jnp.bfloat16), narrow, narrow, narrow, part, part
     ]
+    anywhere = pl.BlockSpec(memory_space=pl.ANY)
     return call(
         functools.partial(row_kernel, packs, experts, capacity),
         2 * packs + experts,
         [
-            block(places.shape, first), block(places_t.shape, last), block(rows.shape, first),
+            block(places.shape, first), block(places_t.shape, last), anywhere, anywhere,
             block(gate.shape, middle), block(up.shape, middle), block(grad_hidden.shape, middle),
         ],
-        [block(out.shape, middle) for out in out_shape[:4]] + [block(rows.shape, last)],
+        [block(out.shape, middle) for out in out_shape[:4]] + [block(part.shape, last)] * 2,
         out_shape,
         [
+            pltpu.VMEM((packs, seq_len, width), jnp.bfloat16),
             pltpu.VMEM((experts, packs, capacity, width), jnp.bfloat16),
             pltpu.VMEM((experts, packs, capacity, width), jnp.bfloat16),
             pltpu.VMEM((experts * capacity, seq_len), jnp.bfloat16),
             pltpu.VMEM((seq_len, experts * capacity), jnp.bfloat16),
+            pltpu.SemaphoreType.DMA((8 * packs,)),
         ],
-    )(places, places_t, rows, gate, up, grad_hidden)
+        4 * experts * slot_rows * width * (seq_len + 2 * hidden_width),
+    )(places, places_t, own, other, gate, up, grad_hidden)
 
 
 def mix_rows(places_t, gates_t, hidden, down, capacity):
     packs, seq_len, _ = places_t.shape
-    experts, _, width = down.shape
+    experts, hidden_width, width = down.shape
     first, last = staged(0, experts), staged(experts, packs)
-    out = shape_of((packs, seq_len, width), jnp.bfloat16)
+    part = shape_of((packs, 2, seq_len // 4, width), jnp.bfloat16)
     return call(
         functools.partial(mix_kernel, packs, experts, capacity),
         packs + experts,
@@ -361,12 +413,13 @@
             block(places_t.shape, last), block(gates_t.shape, last),
             block(hidden.shape, first), block(down.shape, first),
         ],
-        block(out.shape, last),
-        out,
+        [block(part.shape, last)] * 2,
+        [part, part],
         [
             pltpu.VMEM((experts, packs, capacity, width), jnp.bfloat16),
             pltpu.VMEM((seq_len, experts * capacity), jnp.bfloat16),
         ],
+        2 * experts * packs * capacity * width * (seq_len + hidden_width),
     )(places_t, gates_t, hidden, down)
 
 
@@ -388,21 +441,153 @@
         [block(out.shape, each) for out in out_shape],
         out_shape,
         [],
+        6 * planes * slots[0].shape[1] * experts * width * hidden_width,
     )(*operands)
 
 
+def swapped(values, axis, bit):
+    count = lax.axis_size(axis)
+    return lax.ppermute(values, axis, [(i, i ^ bit) for i in range(count)])
+
+
+def far_side(values):
+    return swapped(values, "tensor", 2)
+
+
+def far_core(values):
+    return swapped(values, "tensor", 1)
+
+
+def far_pack(values):
+    return swapped(values, "dp", 1)
+
+
+def next_plane(values):
+    count = lax.axis_size("dp")
+    return lax.ppermute(values, "dp", [(i, (i + 2) % count) for i in range(count)])
+
+
+def spread_plane(values):
+    half_rows = values.shape[0] // 2
+    upper, lower = values[:half_rows], values[half_rows:]
+    near_upper = jnp.stack([upper, far_pack(upper)])
+    near_lower = jnp.stack([lower, far_side(lower)])
+    own = jnp.concatenate([near_upper, near_lower, far_side(near_upper), far_pack(near_lower)])
+    return own, far_core(own)
+
+
+def plane_order():
+    packs = lax.axis_size("dp")
+    planes = packs // 2
+    index = lax.axis_index("dp")
+    return jnp.stack(
+        [
+            ((index // 2 + planes - plane) % planes) * 2 + (index % 2 ^ near)
+            for plane in range(planes)
+            for near in range(2)
+        ]
+    )
+
+
+def laid(pieces, order):
+    whole = jnp.zeros((len(pieces),) + pieces[0].shape, pieces[0].dtype)
+    for index, piece in enumerate(pieces):
+        place = (order[index],) + (0,) * piece.ndim
+        whole = lax.dynamic_update_slice(whole, piece[None], place)
+    return whole
+
+
+def gather_packs(values):
+    pieces = []
+    for plane in range(lax.axis_size("dp") // 2):
+        values = next_plane(values) if plane else values
+        pieces += [values, far_pack(values)]
+    return laid(pieces, plane_order())
+
+
+def fold_packs(values):
+    order = plane_order()
+    take = lambda index: lax.dynamic_index_in_dim(values, order[index], 0, keepdims=False)
+    near = [added(take(2 * i), far_pack(take(2 * i + 1))) for i in range(values.shape[0] // 2)]
+    summed = near[1]
+    for part in near[2:]:
+        summed = added(next_plane(summed), part)
+    return added(next_plane(summed), near[0], jnp.float32)
+
+
+def gather_sides(values):
+    across = far_side(values)
+    pieces = [values, far_core(values), across, far_core(across)]
+    order = lax.axis_index("tensor") ^ jnp.arange(len(pieces), dtype=jnp.int32)
+    return laid(pieces, order).reshape((-1,) + values.shape[1:])
+
+
+def fold_sides(values):
+    split = values.astype(jnp.bfloat16).reshape((4, -1) + values.shape[1:])
+    take = lambda bits: lax.dynamic_index_in_dim(
+        split, lax.axis_index("tensor") ^ bits, 0, keepdims=False
+    )
+    far = added(take(2), far_core(take(3)))
+    near = added(take(0), far_core(take(1)))
+    return added(near, far_side(far), jnp.float32)
+
+
+def sum_everywhere(values):
+    for axis in ("tensor", "dp"):
+        bit = 1
+        while bit < lax.axis_size(axis):
+            values = values + swapped(values, axis, bit)
+            bit *= 2
+    return values
+
+
+def added(left, right, kind=jnp.bfloat16):
+    return (left.astype(jnp.float32) + right.astype(jnp.float32)).astype(kind)
+
+
+def fold_plane(own, other):
+    half_rows = own.shape[2] // 2
+    arrived = far_core(other)
+    upper, lower = slice(None, half_rows), slice(half_rows, None)
+    upper_near = added(own[:, 0, upper], arrived[:, 0, upper])
+    upper_far = added(own[:, 1, upper], arrived[:, 1, upper])
+    lower_near = added(own[0, :, lower], arrived[0, :, lower])
+    lower_far = added(own[1, :, lower], arrived[1, :, lower])
+    upper_near = added(upper_near, far_side(upper_far))
+    lower_near = added(lower_near, far_pack(lower_far))
+    return jnp.concatenate(
+        [
+            added(upper_near[0], far_pack(upper_near[1])),
+            added(lower_near[0], far_side(lower_near[1])),
+        ]
+    )
+
+
+def fold_all(parts):
+    summed = fold_plane(*parts[1])
+    for part in parts[2:]:
+        summed = added(next_plane(summed), fold_plane(*part))
+    return added(next_plane(summed), fold_plane(*parts[0]), jnp.float32)
+
+
 def routing(all_ids, all_gates, local_experts, capacity):
-    seq_len = all_ids.shape[1]
+    packs = lax.axis_size("dp")
     first = lax.axis_index("dp") * local_experts
     wanted = first + jnp.arange(local_experts, dtype=jnp.int32)
-    matches = all_ids[:, :, :, None] == wanted
-    member = jnp.any(matches, axis=2)
-    gates = jnp.sum(jnp.where(matches, all_gates.astype(jnp.float32)[..., None], 0.0), axis=2)
-    order = jnp.arange(seq_len, dtype=jnp.int32)
-    earlier = (order[:, None] > order[None, :]).astype(jnp.bfloat16)
-    before = jnp.einsum(
-        "ts,pse->pte", earlier, member.astype(jnp.bfloat16), preferred_element_type=jnp.float32
-    ).astype(jnp.int32)
+
+    def by_pack(values):
+        top_count, tok_rows = values.shape[1:]
+        ordered = values.reshape(packs, -1, top_count, tok_rows).transpose(0, 2, 1, 3)
+        return ordered.reshape(packs, top_count, -1)
+
+    matches = by_pack(all_ids)[:, :, None, :] == wanted[None, None, :, None]
+    pair_gates = by_pack(all_gates).astype(jnp.float32)
+    member = jnp.any(matches, axis=1)
+    gates = jnp.sum(jnp.where(matches, pair_gates[:, :, None, :], 0.0), axis=1)
+    order = jnp.arange(member.shape[2], dtype=jnp.int32)
+    earlier = (order[:, None] < order[None, :]).astype(jnp.bfloat16)
+    flat = member.reshape(packs * local_experts, -1).astype(jnp.bfloat16)
+    before = matmul(flat, earlier).astype(jnp.int32).reshape(member.shape)
     return jnp.where(member & (before < capacity), before, -1), gates
 
 
@@ -474,48 +659,43 @@
     return outputs, grad_second, grad_w_gate, grad_w_up, grad_w_down
 
 
-def experts_by_gather(
-    second_in, cotangent, expert_ids, gate_values, w_gate, w_up, w_down, middle, capacity
-):
-    tok_rows, model_width = second_in.shape
-    axes = ("dp", "tensor")
-    data_count = lax.axis_size("dp")
-    seq_len = tok_rows * lax.axis_size("tensor")
-    local_experts = w_gate.shape[0]
-
-    def everywhere(values):
-        gathered = lax.all_gather(values, axes, axis=0, tiled=True)
-        return gathered.reshape(data_count, seq_len, values.shape[1])
-
-    places_t, gates_t = routing(
-        everywhere(expert_ids), everywhere(gate_values), local_experts, capacity
-    )
-    places, gates = places_t.transpose(0, 2, 1), gates_t.transpose(0, 2, 1)
-    per_plane = 2
-    planes = data_count // per_plane
-    all_cot = everywhere(cotangent)
-    all_rows = everywhere(second_in)
+def experts_by_gather(second_in, all_cot, places, gates, w_gate, w_up, w_down, middle, capacity):
+    packs, local_experts, seq_len = places.shape
+    tensor_count = lax.axis_size("tensor")
+    planes = packs // 2
+    pack_order = plane_order()
+    side_index = lax.axis_index("tensor")
+    quarter_order = side_index ^ jnp.arange(tensor_count, dtype=jnp.int32)
+
+    def as_met(values):
+        split = values.reshape(packs, local_experts, tensor_count, -1)
+        split = jnp.take(jnp.take(split, pack_order, axis=0), quarter_order, axis=2)
+        return split.reshape(values.shape)
+
+    near_places, near_gates = as_met(places), as_met(gates)
+    places_t, gates_t = near_places.transpose(0, 2, 1), near_gates.transpose(0, 2, 1)
     kept = []
     row_parts, mix_parts = [], []
+    travelling = second_in
     for plane in range(planes):
-        packs = slice(plane * per_plane, (plane + 1) * per_plane)
+        pair = slice(plane * 2, plane * 2 + 2)
         grad_slots, grad_hidden = cot_slots(
-            places[packs], gates[packs], all_cot[packs], w_down, capacity
-        )
-        slots, hidden, grad_gated, grad_lifted, row_part = row_slots(
-            places[packs], places_t[packs], all_rows[packs], w_gate, w_up, grad_hidden, capacity
+            pack_order[pair], places, gates, all_cot, w_down, capacity
+        )
+        own, other = spread_plane(travelling)
+        if plane + 1 < planes:
+            travelling = next_plane(travelling)
+        slots, hidden, grad_gated, grad_lifted, *row_part = row_slots(
+            near_places[pair], places_t[pair], own, other, w_gate, w_up, grad_hidden, capacity
         )
         row_parts.append(row_part)
-        mix_parts.append(mix_rows(places_t[packs], gates_t[packs], hidden, w_down, capacity))
         kept.append((slots, grad_slots, hidden, grad_gated, grad_lifted))
-
-    def scattered(parts):
-        whole = jnp.concatenate(parts, axis=0).reshape(data_count * seq_len, model_width)
-        summed = lax.psum_scatter(whole, axes, scatter_dimension=0, tiled=True)
-        return summed.astype(jnp.float32)
-
-    grad_second = scattered(row_parts)
-    outputs = middle + scattered(mix_parts)
+    kept, _ = lax.optimization_barrier((kept, row_parts[-1]))
+    for plane in range(planes):
+        pair = slice(plane * 2, plane * 2 + 2)
+        mix_parts.append(mix_rows(places_t[pair], gates_t[pair], kept[plane][2], w_down, capacity))
+    grad_second, mix_parts = lax.optimization_barrier((fold_all(row_parts), mix_parts))
+    outputs = middle + fold_all(mix_parts)
     grad_w_gate, grad_w_up, grad_w_down = weight_grads(*zip(*kept))
     return outputs, grad_second, grad_w_gate, grad_w_up, grad_w_down
 
@@ -548,19 +728,45 @@
     seq_len = tok_rows * tensor_count
     capacity = seq_len * top_count // all_experts
     inv_root = head_size ** (-0.5)
+    by_gather = (
+        seq_len <= local_experts * capacity
+        and tensor_count == 4
+        and data_count > 2
+        and data_count & (data_count - 1) == 0
+    )
+    if by_gather:
+        axes = ("dp", "tensor")
+        all_ids = lax.all_gather(expert_ids.T, axes, axis=0)
+        all_gates = lax.all_gather(gate_values.T, axes, axis=0)
+        pack_segs = lax.all_gather(segment_ids, "tensor", axis=1, tiled=True)
+        inputs, cotangent, w_query, all_ids, all_gates, pack_segs = lax.optimization_barrier(
+            (inputs, cotangent, w_query, all_ids, all_gates, pack_segs)
+        )
+        all_cot = lax.all_gather(cotangent, axes, axis=0, tiled=True)
+        all_cot = all_cot.reshape(data_count, seq_len, model_width)
+        places, gates = routing(all_ids, all_gates, local_experts, capacity)
     inputs_f32 = inputs.astype(jnp.float32)
     normed_one, factor_one = norm_parts(inputs_f32)
     first_in = (normed_one * attn_gain).astype(jnp.bfloat16)
-    pack_in, pack_segs = (
-        lax.all_gather(first_in, "tensor", axis=0, tiled=True),
-        lax.all_gather(segment_ids, "tensor", axis=1, tiled=True),
-    )
-    full_query, full_key, full_value, full_output = (
-        lax.all_gather(w_query, "dp", axis=0, tiled=True),
-        lax.all_gather(w_key, "dp", axis=0, tiled=True),
-        lax.all_gather(w_value, "dp", axis=0, tiled=True),
-        lax.all_gather(w_output, "dp", axis=1, tiled=True),
-    )
+    if by_gather:
+        side_sum, side_gather = fold_sides, gather_sides
+        local_width = w_query.shape[1]
+        full_in = gather_packs(jnp.concatenate([w_query, w_key, w_value], axis=1))
+        full_in = full_in.reshape(model_width, -1)
+        full_query, full_key, full_value = (
+            full_in[:, index * local_width : (index + 1) * local_width] for index in range(3)
+        )
+        full_output = gather_packs(w_output).transpose(1, 0, 2).reshape(w_output.shape[0], -1)
+    else:
+        side_sum, side_gather = lambda term: row_sum(lambda *_: term, tok_rows), gather_rows
+        pack_segs = lax.all_gather(segment_ids, "tensor", axis=1, tiled=True)
+        full_query, full_key, full_value, full_output = (
+            lax.all_gather(w_query, "dp", axis=0, tiled=True),
+            lax.all_gather(w_key, "dp", axis=0, tiled=True),
+            lax.all_gather(w_value, "dp", axis=0, tiled=True),
+            lax.all_gather(w_output, "dp", axis=1, tiled=True),
+        )
+    pack_in = side_gather(first_in)
     query_pre = matmul(pack_in, full_query)
     key_pre = matmul(pack_in, full_key)
     value_low = matmul(pack_in, full_value).astype(jnp.bfloat16)
@@ -594,15 +800,12 @@
         lse_parts.append(top_score + jnp.log(totals))
     mixture = jnp.concatenate(mixture_parts, axis=0).reshape(seq_len, head_count * head_size)
 
-    def attn_term(offset, row_count):
-        return matmul(mixture, full_output)
-
-    middle = inputs_f32 + row_sum(attn_term, tok_rows)
+    middle = inputs_f32 + side_sum(matmul(mixture, full_output))
     normed_two, factor_two = norm_parts(middle)
     second_in = (normed_two * ffn_gain).astype(jnp.bfloat16)
-    if seq_len <= local_experts * capacity:
+    if by_gather:
         outputs, grad_second, grad_w_gate, grad_w_up, grad_w_down = experts_by_gather(
-            second_in, cotangent, expert_ids, gate_values, w_gate, w_up, w_down, middle, capacity
+            second_in, all_cot, places, gates, w_gate, w_up, w_down, middle, capacity
         )
     else:
         outputs, grad_second, grad_w_gate, grad_w_up, grad_w_down = experts_by_exchange(
@@ -612,7 +815,7 @@
     grad_middle = cotangent.astype(jnp.float32) + norm_back(
         grad_second, normed_two, factor_two, ffn_gain
     )
-    pack_grad = gather_rows(grad_middle.astype(jnp.bfloat16))
+    pack_grad = side_gather(grad_middle.astype(jnp.bfloat16))
     output_part = contract_first(mixture, pack_grad)
     grad_mixture = (
         contract_last(pack_grad, full_output)
@@ -669,31 +872,33 @@
     key_part = contract_first(pack_in, grad_key_pre)
     value_part = contract_first(pack_in, grad_value_low)
 
-    def input_term(offset, row_count):
-        total_term = contract_last(grad_query_pre, full_query)
-        total_term = total_term + contract_last(grad_key_pre, full_key)
-        return total_term + contract_last(grad_value_low, full_value)
-
-    grad_first = row_sum(input_term, tok_rows)
+    total_term = contract_last(grad_query_pre, full_query)
+    total_term = total_term + contract_last(grad_key_pre, full_key)
+    grad_first = side_sum(total_term + contract_last(grad_value_low, full_value))
     attn_gain_part = jnp.sum(grad_first * normed_one, axis=0)
     grad_inputs = grad_middle + norm_back(grad_first, normed_one, factor_one, attn_gain)
-    grad_w_query, grad_w_key, grad_w_value, grad_w_output = (
-        lax.psum_scatter(
-            query_part.astype(jnp.bfloat16), "dp", scatter_dimension=0, tiled=True
-        ).astype(jnp.float32),
-        lax.psum_scatter(
-            key_part.astype(jnp.bfloat16), "dp", scatter_dimension=0, tiled=True
-        ).astype(jnp.float32),
-        lax.psum_scatter(
-            value_part.astype(jnp.bfloat16), "dp", scatter_dimension=0, tiled=True
-        ).astype(jnp.float32),
-        lax.psum_scatter(
-            output_part.astype(jnp.bfloat16), "dp", scatter_dimension=1, tiled=True
-        ).astype(jnp.float32),
-    )
-    grad_attn_gain, grad_ffn_gain, grad_query_gain, grad_key_gain = lax.psum(
-        (attn_gain_part, ffn_gain_part, query_gain_part, key_gain_part), ("dp", "tensor")
-    )
+    gain_parts = (attn_gain_part, ffn_gain_part, query_gain_part, key_gain_part)
+    if by_gather:
+        in_part = jnp.concatenate([query_part, key_part, value_part], axis=1)
+        grad_in = fold_packs(in_part.astype(jnp.bfloat16).reshape(data_count, -1, 3 * local_width))
+        grad_w_query, grad_w_key, grad_w_value = (
+            grad_in[:, index * local_width : (index + 1) * local_width] for index in range(3)
+        )
+        by_column = output_part.astype(jnp.bfloat16).reshape(local_width, data_count, -1)
+        grad_w_output = fold_packs(by_column.transpose(1, 0, 2))
+        late = sum_everywhere(attn_gain_part)
+        early = sum_everywhere(jnp.concatenate(gain_parts[1:]))
+        splits = (model_width, model_width + head_size)
+        gain_sums = (late, *jnp.split(early, splits))
+    else:
+        grad_w_query, grad_w_key, grad_w_value, grad_w_output = (
+            lax.psum_scatter(
+                part.astype(jnp.bfloat16), "dp", scatter_dimension=along, tiled=True
+            ).astype(jnp.float32)
+            for part, along in ((query_part, 0), (key_part, 0), (value_part, 0), (output_part, 1))
+        )
+        gain_sums = lax.psum(gain_parts, ("dp", "tensor"))
+    grad_attn_gain, grad_ffn_gain, grad_query_gain, grad_key_gain = gain_sums
     return (
         outputs,
         grad_inputs,

time: 2060 us -> 1520 us (0.74)
  waiting for transfers between devices: 1200 us -> 575 us
  starting transfers between devices: 1.54 us -> 89.4 us
  local copies, waits for them, and re-layouts: 92.4 us -> 159 us
  blocking collectives: 142 us -> 86.8 us
    reduce_scatter x8 -> x0, waiting for transfers between devices: 881 us -> none  [the longest x2 653 us: scattered(): summed = lax.psum_scatter(whole, axes, scatter_dimension=0, tiled=True)]
    ppermute x0 -> x119, waiting for transfers between devices: none -> 575 us  [the longest x98 417 us: swapped(): return lax.ppermute(values, axis, [(i, i ^ bit) for i in range(count)])]
    all_gather x8 -> x1, waiting for transfers between devices: 317 us -> 0.01 us  [shards(): all_cot = lax.all_gather(cotangent, axes, axis=0, tiled=True)]
    ppermute x0 -> x119, starting transfers between devices: none -> 89.3 us  [the longest x98 77.7 us: swapped(): return lax.ppermute(values, axis, [(i, i ^ bit) for i in range(count)])]
    dynamic_update_slice x0 -> x23, local copies, waits for them, and re-layouts: none -> 68.8 us  [laid(): whole = lax.dynamic_update_slice(whole, piece[None], place)]
    psum x1 -> x0, blocking collectives: 55.4 us -> none  [shards(): lax.psum((attn_gain_part, ffn_gain_part, query_gain_part, key_gain_part),...]
    convert_element_type x7 -> x55, other arithmetic: 12.1 us -> 63.5 us  [the longest x52 61.5 us: added(): return (left.astype(jnp.float32) + right.astype(jnp.float32)).astype(kind)]
    slice x10, local copies, waits for them, and re-layouts: 60.1 us -> 9.01 us  [the longest x5 2.54 us: experts_by_gather(): near_places[pair]]
  transfers between devices with their start and end apart: 16 -> 120, of which waited for: 13 -> 61; matrix products, arithmetic and copies ran while one was open for 9% -> 18% of each run, Pallas kernels for 11% -> 26%
where the time goes in v2:
time: 1520 us; the launch traced here: 1510 us
  waiting for transfers between devices  575 us (38%)
  Pallas kernels  391 us (26%)
  local copies, waits for them, and re-layouts  159 us (10%)
  other arithmetic  107 us (7%)
  starting transfers between devices  89.4 us (6%)
  blocking collectives  86.8 us (6%)
  matrix products  80.2 us (5%)
  between operations  24.7 us (2%)
    ppermute x98, waiting for transfers between devices, swapped(): return lax.ppermute(values, axis, [(i, i ^ bit) for i in range(count)])  417 us
    pallas_call x4, Pallas kernels, row_slots(): call(functools.partial(row_kernel, packs, experts, capacity), 2 * packs +...  165 us
    ppermute x21, waiting for transfers between devices, next_plane(): lax.ppermute(values, 'dp', [(i, (i + 2) % count) for i in range(count)])  158 us
    pallas_call x4, Pallas kernels, mix_rows(): call(functools.partial(mix_kernel, packs, experts, capacity), packs + exp...  89.2 us
    pallas_call x4, Pallas kernels, cot_slots(): call(functools.partial(cot_kernel, packs, experts, capacity), packs + exp...  88.9 us
    ppermute x98, starting transfers between devices, swapped(): return lax.ppermute(values, axis, [(i, i ^ bit) for i in range(count)])  77.7 us
    dynamic_update_slice x23, local copies, waits for them, and re-layouts, laid(): whole = lax.dynamic_update_slice(whole, piece[None], place)  68.8 us
    convert_element_type x52, other arithmetic, added(): return (left.astype(jnp.float32) + right.astype(jnp.float32)).astype(kind)  61.5 us
  transfers between devices with their start and end apart: 120, of which 61 were waited for; matrix products, arithmetic and copies ran while one was open for 18% of the time, Pallas kernels for 26%

profile of v2, /device:TPU:0, one launch (start us, length us, event | category | flops | bytes accessed | tf_op | source)
XLA Modules:
  0.0 1512.8 jit_solution(2134825464637122993)
XLA Ops:
  7.3 44.3 %all-gather = s32[256,256]{1,0:T(8,128)S(1)} all-gather(s32[8,256]{1,0:T(8,128)} %bitcast.651), channel_id=2, replica_groups=mesh['dp'=8,'tensor'=4] {'dp','tensor'}, dimensions={0}, use_global_device_ids=true | all-gather | bytes 270336 | tf_op jit(solution)/shard_map/all_gather | solution.py:739
  51.6 37.2 %all-gather.1 = bf16[256,256]{1,0:T(8,128)(2,1)S(1)} all-gather(bf16[8,256]{1,0:T(8,128)(2,1)} %bitcast.652), channel_id=3, replica_groups=mesh['dp'=8,'tensor'=4] {'dp','tensor'}, dimensions={0}, use_global_device_ids=true | all-gather | bytes 135168 | tf_op jit(solution)/shard_map/all_gather | solution.py:740
  175.7 28.6 %collective-permute-done.1 = bf16[256,2048]{1,0:T(8,128)(2,1)S(1)} collective-permute-done((bf16[256,2048]{1,0:T(8,128)(2,1)}, bf16[256,2048]{1,0:T(8,128)(2,1)S(1)}, u32[]{:S(2)}, u32[]{:S(2)}) %collective-permute-start.1) | collective-permute-done | bytes 1048608 | tf_op jit(solution)/shard_map/ppermute | solution.py:450
  214.2 24.9 %collective-permute-done.8 = bf16[256,1536]{1,0:T(8,128)(2,1)} collective-permute-done((bf16[256,1536]{1,0:T(8,128)(2,1)S(1)}, bf16[256,1536]{1,0:T(8,128)(2,1)}, u32[]{:S(2)}, u32[]{:S(2)}) %collective-permute-start.8) | collective-permute-done | bytes 786464 | tf_op jit(solution)/shard_map/ppermute | solution.py:467
  253.1 21.0 %collective-permute-done.9 = bf16[256,1536]{1,0:T(8,128)(2,1)S(1)} collective-permute-done((bf16[256,1536]{1,0:T(8,128)(2,1)}, bf16[256,1536]{1,0:T(8,128)(2,1)S(1)}, u32[]{:S(2)}, u32[]{:S(2)}) %collective-permute-start.9) | collective-permute-done | bytes 786464 | tf_op jit(solution)/shard_map/ppermute | solution.py:450
  278.6 33.8 %dynamic_update_slice.83 = bf16[8,256,1536]{1,0,2:T(8,128)(2,1)} dynamic-update-slice(bf16[8,256,1536]{1,0,2:T(8,128)(2,1)} %copy.120, bf16[1,256,1536]{1,0,2:T(2,128)(2,1)S(1)} %copy.121, s32[]{:T(128)S(6)} %select_n.391, s32[]{:T(128)} %constant.421.clone.1, s32[]{:T(128)} %constant.421.clone.1) | dynamic-update-slice | bytes 1572868 | tf_op jit(solution)/shard_map/dynamic_update_slice | solution.py:496
  377.8 16.8 %collective-permute-done.19 = bf16[256,2048]{1,0:T(8,128)(2,1)} collective-permute-done((bf16[256,2048]{1,0:T(8,128)(2,1)}, bf16[256,2048]{1,0:T(8,128)(2,1)}, u32[]{:S(2)}, u32[]{:S(2)}) %collective-permute-start.19) | collective-permute-done | bytes 1048608 | tf_op jit(solution)/shard_map/ppermute | solution.py:450
  433.3 18.5 %collective-permute-done.21 = bf16[128,2048]{1,0:T(8,128)(2,1)S(1)} collective-permute-done((bf16[128,2048]{1,0:T(8,128)(2,1)S(1)}, bf16[128,2048]{1,0:T(8,128)(2,1)S(1)}, u32[]{:S(2)}, u32[]{:S(2)}) %collective-permute-start.21) | collective-permute-done | bytes 524320 | tf_op jit(solution)/shard_map/ppermute | solution.py:450
  462.0 16.1 %collective-permute-done.23 = bf16[2,128,2048]{2,1,0:T(8,128)(2,1)S(1)} collective-permute-done((bf16[2,128,2048]{2,1,0:T(8,128)(2,1)S(1)}, bf16[2,128,2048]{2,1,0:T(8,128)(2,1)S(1)}, u32[]{:S(2)}, u32[]{:S(2)}) %collective-permute-start.23) | collective-permute-done | bytes 1048608 | tf_op jit(solution)/shard_map/ppermute | solution.py:450
  523.8 17.9 %collective-permute-done.47 = bf16[2,128,2048]{2,1,0:T(8,128)(2,1)S(1)} collective-permute-done((bf16[2,128,2048]{2,1,0:T(8,128)(2,1)S(1)}, bf16[2,128,2048]{2,1,0:T(8,128)(2,1)S(1)}, u32[]{:S(2)}, u32[]{:S(2)}) %collective-permute-start.47) | collective-permute-done | bytes 1048608 | tf_op jit(solution)/shard_map/ppermute | solution.py:450
  543.8 21.9 %shard_map.255 = (bf16[8,256,2048]{2,1,0:T(8,128)(2,1)}, f32[8,256,256]{2,1,0:T(8,128)}) custom-call(s32[2]{0:T(128)} %get-tuple-element.291.table, s32[8,8,1024]{2,1,0:T(8,128)} %get-tuple-element.285.places, f32[8,8,1024]{2,1,0:T(8,128)} %copy-done.17, bf16[8,1024,2048]{2,1,0:T(8,128)(2,1)} %bitcast.573, bf16[8,256,2048]{2,1,0:T(8,128)(2,1)} %down.15), custom_call_target="tpu_custom_call" | custom-call | flops 10737418240 | bytes 21474836 | tf_op jit(solution)/shard_map/pallas_call | solution.py:354
  565.7 41.6 %shard_map.256 = (bf16[8,256,2048]{2,1,0:T(8,128)(2,1)}, bf16[8,256,256]{2,1,0:T(8,128)(2,1)}, bf16[8,256,256]{2,1,0:T(8,128)(2,1)}, bf16[8,256,256]{2,1,0:T(8,1...) custom-call(s32[2,8,1024]{2,1,0:T(8,128)} %bitcast.647, ...), custom_call_target="tpu_custom_call" | custom-call | flops 25769803776 | bytes 51539608 | tf_op jit(solution)/shard_map/pallas_call | solution.py:383
  607.9 22.4 %shard_map.257 = (bf16[8,256,2048]{2,1,0:T(8,128)(2,1)}, f32[8,256,256]{2,1,0:T(8,128)}) custom-call(s32[2]{0:T(128)} %get-tuple-element.292.table, s32[8,8,1024]{2,1,0:T(8,128)} %get-tuple-element.285.places, f32[8,8,1024]{2,1,0:T(8,128)} %copy-done.17, bf16[8,1024,2048]{2,1,0:T(8,128)(2,1)} %bitcast.574, bf16[8,256,2048]{2,1,0:T(8,128)(2,1)} %down.15), custom_call_target="tpu_custom_call" | custom-call | flops 10737418240 | bytes 21474836 | tf_op jit(solution)/shard_map/pallas_call | solution.py:354
  630.3 41.3 %shard_map.258 = (bf16[8,256,2048]{2,1,0:T(8,128)(2,1)}, bf16[8,256,256]{2,1,0:T(8,128)(2,1)}, bf16[8,256,256]{2,1,0:T(8,128)(2,1)}, bf16[8,256,256]{2,1,0:T(8,1...) custom-call(s32[2,8,1024]{2,1,0:T(8,128)} %bitcast.646, ...), custom_call_target="tpu_custom_call" | custom-call | flops 25769803776 | bytes 51539608 | tf_op jit(solution)/shard_map/pallas_call | solution.py:383
  671.7 22.1 %shard_map.259 = (bf16[8,256,2048]{2,1,0:T(8,128)(2,1)}, f32[8,256,256]{2,1,0:T(8,128)}) custom-call(s32[2]{0:T(128)} %get-tuple-element.293.table, s32[8,8,1024]{2,1,0:T(8,128)} %get-tuple-element.285.places, f32[8,8,1024]{2,1,0:T(8,128)} %copy-done.17, bf16[8,1024,2048]{2,1,0:T(8,128)(2,1)} %bitcast.575, bf16[8,256,2048]{2,1,0:T(8,128)(2,1)} %down.15), custom_call_target="tpu_custom_call" | custom-call | flops 10737418240 | bytes 21474836 | tf_op jit(solution)/shard_map/pallas_call | solution.py:354
  693.8 41.3 %shard_map.260 = (bf16[8,256,2048]{2,1,0:T(8,128)(2,1)}, bf16[8,256,256]{2,1,0:T(8,128)(2,1)}, bf16[8,256,256]{2,1,0:T(8,128)(2,1)}, bf16[8,256,256]{2,1,0:T(8,1...) custom-call(s32[2,8,1024]{2,1,0:T(8,128)} %bitcast.645, ...), custom_call_target="tpu_custom_call" | custom-call | flops 25769803776 | bytes 51539608 | tf_op jit(solution)/shard_map/pallas_call | solution.py:383
  735.7 22.4 %shard_map.261 = (bf16[8,256,2048]{2,1,0:T(8,128)(2,1)}, f32[8,256,256]{2,1,0:T(8,128)}) custom-call(s32[2]{0:T(128)} %get-tuple-element.294.table, s32[8,8,1024]{2,1,0:T(8,128)} %get-tuple-element.285.places, f32[8,8,1024]{2,1,0:T(8,128)} %copy-done.17, bf16[8,1024,2048]{2,1,0:T(8,128)(2,1)} %bitcast.576, bf16[8,256,2048]{2,1,0:T(8,128)(2,1)} %down.15), custom_call_target="tpu_custom_call" | custom-call | flops 10737418240 | bytes 21474836 | tf_op jit(solution)/shard_map/pallas_call | solution.py:354
  758.1 41.3 %shard_map.262 = (bf16[8,256,2048]{2,1,0:T(8,128)(2,1)}, bf16[8,256,256]{2,1,0:T(8,128)(2,1)}, bf16[8,256,256]{2,1,0:T(8,128)(2,1)}, bf16[8,256,256]{2,1,0:T(8,1...) custom-call(s32[2,8,1024]{2,1,0:T(8,128)} %bitcast.644, ...), custom_call_target="tpu_custom_call" | custom-call | flops 25769803776 | bytes 51539608 | tf_op jit(solution)/shard_map/pallas_call | solution.py:383
  799.5 22.3 %shard_map.263 = (bf16[2,2,256,2048]{3,2,1,0:T(8,128)(2,1)}, bf16[2,2,256,2048]{3,2,1,0:T(8,128)(2,1)}) custom-call(s32[2,1024,8]{2,1,0:T(8,128)} %get-tuple-element.206.places_t, f32[2,1024,8]{2,1,0:T(8,128)} %get-tuple-element.203.gates_t, bf16[8,256,256]{2,1,0:T(8,128)(2,1)} %get-tuple-element.129.hidden.refs_8_, bf16[8,256,2048]{2,1,0:T(8,128)(2,1)} %down.15), custom_call_target="tpu_custom_call" | custom-call | flops 10737418240 | bytes 21474836 | tf_op jit(solution)/shard_map/pallas_call | solution.py:409
  821.8 22.1 %shard_map.264 = (bf16[2,2,256,2048]{3,2,1,0:T(8,128)(2,1)}, bf16[2,2,256,2048]{3,2,1,0:T(8,128)(2,1)}) custom-call(s32[2,1024,8]{2,1,0:T(8,128)} %get-tuple-element.209.places_t, f32[2,1024,8]{2,1,0:T(8,128)} %get-tuple-element.202.gates_t, bf16[8,256,256]{2,1,0:T(8,128)(2,1)} %get-tuple-element.132.hidden.refs_9_, bf16[8,256,2048]{2,1,0:T(8,128)(2,1)} %down.15), custom_call_target="tpu_custom_call" | custom-call | flops 10737418240 | bytes 21474836 | tf_op jit(solution)/shard_map/pallas_call | solution.py:409
  843.8 22.5 %shard_map.265 = (bf16[2,2,256,2048]{3,2,1,0:T(8,128)(2,1)}, bf16[2,2,256,2048]{3,2,1,0:T(8,128)(2,1)}) custom-call(s32[2,1024,8]{2,1,0:T(8,128)} %get-tuple-element.208.places_t, f32[2,1024,8]{2,1,0:T(8,128)} %get-tuple-element.201.gates_t, bf16[8,256,256]{2,1,0:T(8,128)(2,1)} %get-tuple-element.135.hidden.refs_10_, bf16[8,256,2048]{2,1,0:T(8,128)(2,1)} %down.15), custom_call_target="tpu_custom_call" | custom-call | flops 10737418240 | bytes 21474836 | tf_op jit(solution)/shard_map/pallas_call | solution.py:409
  1005.2 21.6 %collective-permute-done.43 = bf16[256,2048]{1,0:T(8,128)(2,1)S(1)} collective-permute-done((bf16[256,2048]{1,0:T(8,128)(2,1)S(1)}, bf16[256,2048]{1,0:T(8,128)(2,1)S(1)}, u32[]{:S(2)}, u32[]{:S(2)}) %collective-permute-start.43) | collective-permute-done | bytes 1048608 | tf_op jit(solution)/shard_map/ppermute | solution.py:467
  1027.3 22.3 %shard_map.266 = (bf16[2,2,256,2048]{3,2,1,0:T(8,128)(2,1)}, bf16[2,2,256,2048]{3,2,1,0:T(8,128)(2,1)}) custom-call(s32[2,1024,8]{2,1,0:T(8,128)} %get-tuple-element.207.places_t, f32[2,1024,8]{2,1,0:T(8,128)} %get-tuple-element.200.gates_t, bf16[8,256,256]{2,1,0:T(8,128)(2,1)} %get-tuple-element.138.hidden.refs_11_, bf16[8,256,2048]{2,1,0:T(8,128)(2,1)} %down.15), custom_call_target="tpu_custom_call" | custom-call | flops 10737418240 | bytes 21474836 | tf_op jit(solution)/shard_map/pallas_call | solution.py:409
  1202.6 16.3 %collective-permute-done.118 = bf16[512,256]{1,0:T(8,128)(2,1)S(1)} collective-permute-done((bf16[512,256]{1,0:T(8,128)(2,1)S(1)}, bf16[512,256]{1,0:T(8,128)(2,1)S(1)}, u32[]{:S(2)}, u32[]{:S(2)}) %collective-permute-start.118) | collective-permute-done | bytes 262176 | tf_op jit(solution)/shard_map/ppermute | solution.py:450
  1222.2 47.7 %shard_map.267 = (f32[8,2048,256]{2,1,0:T(8,128)}, f32[8,2048,256]{2,1,0:T(8,128)}, f32[8,256,2048]{2,1,0:T(8,128)}) custom-call(bf16[8,256,2048]{2,1,0:T(8,128)(2,1)} %get-tuple-element.150.refs_0_, bf16[8,256,2048]{2,1,0:T(8,128)(2,1)} %get-tuple-element.151.refs_1_, bf16[8,256,2048]{2,1,0:T(8,128)(2,1)} %get-tuple-element.152.refs_2_, ...), custom_call_target="tpu_custom_call" | custom-call | flops 25769803776 | bytes 51539608 | tf_op jit(solution)/shard_map/pallas_call | solution.py:437
  1306.7 27.5 %collective-permute-done.97 = f32[2048]{0:T(1024)S(1)} collective-permute-done((f32[2048]{0:T(1024)S(1)}, f32[2048]{0:T(1024)S(1)}, u32[]{:S(2)}, u32[]{:S(2)}) %collective-permute-start.97) | collective-permute-done | bytes 8224 | tf_op jit(solution)/shard_map/ppermute | solution.py:450
  1352.6 16.0 %collective-permute-done.67 = bf16[2,128,2048]{2,1,0:T(8,128)(2,1)} collective-permute-done((bf16[2,128,2048]{2,1,0:T(8,128)(2,1)S(1)}, bf16[2,128,2048]{2,1,0:T(8,128)(2,1)}, u32[]{:S(2)}, u32[]{:S(2)}) %collective-permute-start.67) | collective-permute-done | bytes 1048608 | tf_op jit(solution)/shard_map/ppermute | solution.py:450
  1374.9 16.2 %collective-permute-done.73 = bf16[2,128,2048]{2,1,0:T(8,128)(2,1)} collective-permute-done((bf16[2,128,2048]{2,1,0:T(8,128)(2,1)S(1)}, bf16[2,128,2048]{2,1,0:T(8,128)(2,1)}, u32[]{:S(2)}, u32[]{:S(2)}) %collective-permute-start.73) | collective-permute-done | bytes 1048608 | tf_op jit(solution)/shard_map/ppermute | solution.py:450
  1396.8 16.8 %collective-permute-done.79 = bf16[2,128,2048]{2,1,0:T(8,128)(2,1)} collective-permute-done((bf16[2,128,2048]{2,1,0:T(8,128)(2,1)S(1)}, bf16[2,128,2048]{2,1,0:T(8,128)(2,1)}, u32[]{:S(2)}, u32[]{:S(2)}) %collective-permute-start.79) | collective-permute-done | bytes 1048608 | tf_op jit(solution)/shard_map/ppermute | solution.py:450
  1418.2 17.7 %collective-permute-done.70 = bf16[128,2048]{1,0:T(8,128)(2,1)S(1)} collective-permute-done((bf16[128,2048]{1,0:T(8,128)(2,1)S(1)}, bf16[128,2048]{1,0:T(8,128)(2,1)S(1)}, u32[]{:S(2)}, u32[]{:S(2)}) %collective-permute-start.70) | collective-permute-done | bytes 524320 | tf_op jit(solution)/shard_map/ppermute | solution.py:450
  1462.2 21.4 %collective-permute-done.77 = bf16[256,2048]{1,0:T(8,128)(2,1)S(1)} collective-permute-done((bf16[256,2048]{1,0:T(8,128)(2,1)S(1)}, bf16[256,2048]{1,0:T(8,128)(2,1)S(1)}, u32[]{:S(2)}, u32[]{:S(2)}) %collective-permute-start.77) | collective-permute-done | bytes 1048608 | tf_op jit(solution)/shard_map/ppermute | solution.py:467
  1486.0 15.8 %collective-permute-done.83 = bf16[256,2048]{1,0:T(8,128)(2,1)S(1)} collective-permute-done((bf16[256,2048]{1,0:T(8,128)(2,1)S(1)}, bf16[256,2048]{1,0:T(8,128)(2,1)S(1)}, u32[]{:S(2)}, u32[]{:S(2)}) %collective-permute-start.83) | collective-permute-done | bytes 1048608 | tf_op jit(solution)/shard_map/ppermute | solution.py:467
  (697 shorter events, 668.6 us)
Async XLA Ops:
  7.2 536.6 %all-gather.4.cloned.1.call-start = ((), (), s32[]{:S(2)}) async-start(), calls=%async_computation | async-start | bytes 34603008 | tf_op jit(solution)/shard_map/all_gather | solution.py:745
  95.1 76.4 %collective-permute-start.3 = (bf16[256,1536]{1,0:T(8,128)(2,1)S(1)}, bf16[256,1536]{1,0:T(8,128)(2,1)}, u32[]{:S(2)}, u32[]{:S(2)}) collective-permute-start(bf16[256,1536]{1,0:T(8,128)(2,1)S(1)} %constant_dynamic-update-slice_fusion), channel_id=1, source_target_pairs={{0,4},{4,0},{8,12},{12,8},{16,20},{20,16},{24,28},{28,24},{1,5},{5... | collective-permute-start | bytes 2359304 | tf_op jit(solution)/shard_map/ppermute | solution.py:450
  95.2 74.6 %collective-permute-start.4 = (bf16[256,1536]{1,0:T(8,128)(2,1)S(1)}, bf16[256,1536]{1,0:T(8,128)(2,1)}, u32[]{:S(2)}, u32[]{:S(2)}) collective-permute-start(bf16[256,1536]{1,0:T(8,128)(2,1)S(1)} %constant_dynamic-update-slice_fusion), channel_id=1, source_target_pairs={{0,8},{4,12},{8,16},{12,20},{16,24},{20,28},{24,0},{28,4},{1,9},{5... | collective-permute-start | bytes 2359304 | tf_op jit(solution)/shard_map/ppermute | solution.py:467
  95.4 46.6 %collective-permute-start.10 = (bf16[512,256]{0,1:T(8,128)(2,1)S(1)}, bf16[512,256]{0,1:T(8,128)(2,1)}, u32[]{:S(2)}, u32[]{:S(2)}) collective-permute-start(bf16[512,256]{0,1:T(8,128)(2,1)S(1)} %copy.126), channel_id=1, source_target_pairs={{0,4},{4,0},{8,12},{12,8},{16,20},{20,16},{24,28},{28,24},{1,5},{5... | collective-permute-start | bytes 786440 | tf_op jit(solution)/shard_map/ppermute | solution.py:450
  104.5 99.7 %collective-permute-start = (bf16[256,2048]{1,0:T(8,128)(2,1)}, bf16[256,2048]{1,0:T(8,128)(2,1)}, u32[]{:S(2)}, u32[]{:S(2)}) collective-permute-start(bf16[256,2048]{1,0:T(8,128)(2,1)} %get-tuple-element.183), channel_id=1, source_target_pairs={{0,1},{1,0},{2,3},{3,2},{4,5},{5,4},{6,7},{7,6},{8,9},{9,8},{10,11... | collective-permute-start | bytes 3145736 | tf_op jit(solution)/shard_map/ppermute | solution.py:450
  455.8 302.4 %collective-permute-start.60 = (bf16[8,128,2048]{2,1,0:T(8,128)(2,1)}, bf16[8,128,2048]{2,1,0:T(8,128)(2,1)}, u32[]{:S(2)}, u32[]{:S(2)}) collective-permute-start(bf16[8,128,2048]{2,1,0:T(8,128)(2,1)} %constant_dynamic-update-slice_fusion.21.own), channel_id=1, source_target_pairs={{0,1},{1,0},{2,3},{3,2},{4,5},{5,4},{6,7},{7,6},{8,9},{9,8},{10,11... | collective-permute-start | bytes 12582920 | tf_op jit(solution)/shard_map/ppermute | solution.py:450
  480.2 85.5 %collective-permute-start.25 = (bf16[8,128,2048]{2,1,0:T(8,128)(2,1)}, bf16[8,128,2048]{2,1,0:T(8,128)(2,1)}, u32[]{:S(2)}, u32[]{:S(2)}) collective-permute-start(bf16[8,128,2048]{2,1,0:T(8,128)(2,1)} %constant_dynamic-update-slice_fusion.3.own), channel_id=1, source_target_pairs={{0,1},{1,0},{2,3},{3,2},{4,5},{5,4},{6,7},{7,6},{8,9},{9,8},{10,11... | collective-permute-start | bytes 12582920 | tf_op jit(solution)/shard_map/ppermute | solution.py:450
  514.7 115.6 %collective-permute-start.37 = (bf16[8,128,2048]{2,1,0:T(8,128)(2,1)}, bf16[8,128,2048]{2,1,0:T(8,128)(2,1)}, u32[]{:S(2)}, u32[]{:S(2)}) collective-permute-start(bf16[8,128,2048]{2,1,0:T(8,128)(2,1)} %constant_dynamic-update-slice_fusion.9.own), channel_id=1, source_target_pairs={{0,1},{1,0},{2,3},{3,2},{4,5},{5,4},{6,7},{7,6},{8,9},{9,8},{10,11... | collective-permute-start | bytes 12582920 | tf_op jit(solution)/shard_map/ppermute | solution.py:450
  543.8 150.0 %collective-permute-start.49 = (bf16[8,128,2048]{2,1,0:T(8,128)(2,1)}, bf16[8,128,2048]{2,1,0:T(8,128)(2,1)}, u32[]{:S(2)}, u32[]{:S(2)}) collective-permute-start(bf16[8,128,2048]{2,1,0:T(8,128)(2,1)} %constant_dynamic-update-slice_fusion.15.own), channel_id=1, source_target_pairs={{0,1},{1,0},{2,3},{3,2},{4,5},{5,4},{6,7},{7,6},{8,9},{9,8},{10,11... | collective-permute-start | bytes 12582920 | tf_op jit(solution)/shard_map/ppermute | solution.py:450
  607.3 259.0 %collective-permute-start.26 = (bf16[2,2,256,2048]{3,2,1,0:T(8,128)(2,1)}, bf16[2,2,256,2048]{3,2,1,0:T(8,128)(2,1)}, u32[]{:S(2)}, u32[]{:S(2)}) collective-permute-start(bf16[2,2,256,2048]{3,2,1,0:T(8,128)(2,1)} %get-tuple-element.99), channel_id=1, source_target_pairs={{0,1},{1,0},{2,3},{3,2},{4,5},{5,4},{6,7},{7,6},{8,9},{9,8},{10,11... | collective-permute-start | bytes 12582920 | tf_op jit(solution)/shard_map/ppermute | solution.py:450
  671.6 200.4 %collective-permute-start.38 = (bf16[2,2,256,2048]{3,2,1,0:T(8,128)(2,1)}, bf16[2,2,256,2048]{3,2,1,0:T(8,128)(2,1)}, u32[]{:S(2)}, u32[]{:S(2)}) collective-permute-start(bf16[2,2,256,2048]{3,2,1,0:T(8,128)(2,1)} %get-tuple-element.102), channel_id=1, source_target_pairs={{0,1},{1,0},{2,3},{3,2},{4,5},{5,4},{6,7},{7,6},{8,9},{9,8},{10,11... | collective-permute-start | bytes 12582920 | tf_op jit(solution)/shard_map/ppermute | solution.py:450
  735.2 141.4 %collective-permute-start.50 = (bf16[2,2,256,2048]{3,2,1,0:T(8,128)(2,1)}, bf16[2,2,256,2048]{3,2,1,0:T(8,128)(2,1)}, u32[]{:S(2)}, u32[]{:S(2)}) collective-permute-start(bf16[2,2,256,2048]{3,2,1,0:T(8,128)(2,1)} %get-tuple-element.105), channel_id=1, source_target_pairs={{0,1},{1,0},{2,3},{3,2},{4,5},{5,4},{6,7},{7,6},{8,9},{9,8},{10,11... | collective-permute-start | bytes 12582920 | tf_op jit(solution)/shard_map/ppermute | solution.py:450
  799.4 82.1 %collective-permute-start.61 = (bf16[2,2,256,2048]{3,2,1,0:T(8,128)(2,1)}, bf16[2,2,256,2048]{3,2,1,0:T(8,128)(2,1)}, u32[]{:S(2)}, u32[]{:S(2)}) collective-permute-start(bf16[2,2,256,2048]{3,2,1,0:T(8,128)(2,1)} %get-tuple-element.108), channel_id=1, source_target_pairs={{0,1},{1,0},{2,3},{3,2},{4,5},{5,4},{6,7},{7,6},{8,9},{9,8},{10,11... | collective-permute-start | bytes 12582920 | tf_op jit(solution)/shard_map/ppermute | solution.py:450
  881.5 57.9 %collective-permute-start.51 = (bf16[2,128,2048]{2,1,0:T(8,128)(2,1)S(1)}, bf16[2,128,2048]{2,1,0:T(8,128)(2,1)S(1)}, u32[]{:S(2)}, u32[]{:S(2)}) collective-permute-start(bf16[2,128,2048]{2,1,0:T(8,128)(2,1)S(1)} %fusion.76), channel_id=1, source_target_pairs={{0,2},{1,3},{2,0},{3,1},{4,6},{5,7},{6,4},{7,5},{8,10},{9,11},{10,... | collective-permute-start | bytes 3145736 | tf_op jit(solution)/shard_map/ppermute | solution.py:450
  894.5 47.9 %collective-permute-start.53 = (bf16[2,128,2048]{2,1,0:T(8,128)(2,1)S(1)}, bf16[2,128,2048]{2,1,0:T(8,128)(2,1)S(1)}, u32[]{:S(2)}, u32[]{:S(2)}) collective-permute-start(bf16[2,128,2048]{2,1,0:T(8,128)(2,1)S(1)} %fusion.78), channel_id=1, source_target_pairs={{0,4},{4,0},{8,12},{12,8},{16,20},{20,16},{24,28},{28,24},{1,5},{5... | collective-permute-start | bytes 3145736 | tf_op jit(solution)/shard_map/ppermute | solution.py:450
  897.4 64.5 %collective-permute-start.62 = (bf16[2,128,2048]{2,1,0:T(8,128)(2,1)S(1)}, bf16[2,128,2048]{2,1,0:T(8,128)(2,1)S(1)}, u32[]{:S(2)}, u32[]{:S(2)}) collective-permute-start(bf16[2,128,2048]{2,1,0:T(8,128)(2,1)S(1)} %fusion.80), channel_id=1, source_target_pairs={{0,2},{1,3},{2,0},{3,1},{4,6},{5,7},{6,4},{7,5},{8,10},{9,11},{10,... | collective-permute-start | bytes 3145736 | tf_op jit(solution)/shard_map/ppermute | solution.py:450
  916.9 47.9 %collective-permute-start.64 = (bf16[2,128,2048]{2,1,0:T(8,128)(2,1)S(1)}, bf16[2,128,2048]{2,1,0:T(8,128)(2,1)S(1)}, u32[]{:S(2)}, u32[]{:S(2)}) collective-permute-start(bf16[2,128,2048]{2,1,0:T(8,128)(2,1)S(1)} %fusion.82), channel_id=1, source_target_pairs={{0,4},{4,0},{8,12},{12,8},{16,20},{20,16},{24,28},{28,24},{1,5},{5... | collective-permute-start | bytes 3145736 | tf_op jit(solution)/shard_map/ppermute | solution.py:450
  919.9 53.2 %collective-permute-start.30 = (bf16[128,2048]{1,0:T(8,128)(2,1)S(1)}, bf16[128,2048]{1,0:T(8,128)(2,1)S(1)}, u32[]{:S(2)}, u32[]{:S(2)}) collective-permute-start(bf16[128,2048]{1,0:T(8,128)(2,1)S(1)} %slice_bitcast_fusion.37), channel_id=1, source_target_pairs={{0,2},{1,3},{2,0},{3,1},{4,6},{5,7},{6,4},{7,5},{8,10},{9,11},{10,... | collective-permute-start | bytes 1572872 | tf_op jit(solution)/shard_map/ppermute | solution.py:450
  984.4 65.2 %collective-permute-start.65 = (bf16[128,2048]{1,0:T(8,128)(2,1)}, bf16[128,2048]{1,0:T(8,128)(2,1)S(1)}, u32[]{:S(2)}, u32[]{:S(2)}) collective-permute-start(bf16[128,2048]{1,0:T(8,128)(2,1)} %slice_bitcast_fusion.25), channel_id=1, source_target_pairs={{0,2},{1,3},{2,0},{3,1},{4,6},{5,7},{6,4},{7,5},{8,10},{9,11},{10,... | collective-permute-start | bytes 1572872 | tf_op jit(solution)/shard_map/ppermute | solution.py:450
  1136.7 63.9 %collective-permute-start.93 = (bf16[256,2048]{1,0:T(8,128)(2,1)S(1)}, bf16[256,2048]{1,0:T(8,128)(2,1)S(1)}, u32[]{:S(2)}, u32[]{:S(2)}) collective-permute-start(bf16[256,2048]{1,0:T(8,128)(2,1)S(1)} %get-tuple-element.191), channel_id=1, source_target_pairs={{0,1},{1,0},{2,3},{3,2},{4,5},{5,4},{6,7},{7,6},{8,9},{9,8},{10,11... | collective-permute-start | bytes 3145736 | tf_op jit(solution)/shard_map/ppermute | solution.py:450
  1193.3 84.7 %collective-permute-start.84 = (bf16[2,2,256,2048]{3,2,1,0:T(8,128)(2,1)}, bf16[2,2,256,2048]{3,2,1,0:T(8,128)(2,1)}, u32[]{:S(2)}, u32[]{:S(2)}) collective-permute-start(bf16[2,2,256,2048]{3,2,1,0:T(8,128)(2,1)} %get-tuple-element.148), channel_id=1, source_target_pairs={{0,1},{1,0},{2,3},{3,2},{4,5},{5,4},{6,7},{7,6},{8,9},{9,8},{10,11... | collective-permute-start | bytes 12582920 | tf_op jit(solution)/shard_map/ppermute | solution.py:450
  1218.9 63.6 %collective-permute-start.66 = (bf16[2,2,256,2048]{3,2,1,0:T(8,128)(2,1)}, bf16[2,2,256,2048]{3,2,1,0:T(8,128)(2,1)}, u32[]{:S(2)}, u32[]{:S(2)}) collective-permute-start(bf16[2,2,256,2048]{3,2,1,0:T(8,128)(2,1)} %get-tuple-element.142), channel_id=1, source_target_pairs={{0,1},{1,0},{2,3},{3,2},{4,5},{5,4},{6,7},{7,6},{8,9},{9,8},{10,11... | collective-permute-start | bytes 12582920 | tf_op jit(solution)/shard_map/ppermute | solution.py:450
  1218.9 68.5 %collective-permute-start.72 = (bf16[2,2,256,2048]{3,2,1,0:T(8,128)(2,1)}, bf16[2,2,256,2048]{3,2,1,0:T(8,128)(2,1)}, u32[]{:S(2)}, u32[]{:S(2)}) collective-permute-start(bf16[2,2,256,2048]{3,2,1,0:T(8,128)(2,1)} %get-tuple-element.144), channel_id=1, source_target_pairs={{0,1},{1,0},{2,3},{3,2},{4,5},{5,4},{6,7},{7,6},{8,9},{9,8},{10,11... | collective-permute-start | bytes 12582920 | tf_op jit(solution)/shard_map/ppermute | solution.py:450
  1219.5 53.5 %collective-permute-start.106 = (bf16[256,1536]{1,0:T(8,128)(2,1)}, bf16[256,1536]{1,0:T(8,128)(2,1)}, u32[]{:S(2)}, u32[]{:S(2)}) collective-permute-start(bf16[256,1536]{1,0:T(8,128)(2,1)} %fusion.54), channel_id=1, source_target_pairs={{0,8},{4,12},{8,16},{12,20},{16,24},{20,28},{24,0},{28,4},{1,9},{5... | collective-permute-start | bytes 2359304 | tf_op jit(solution)/shard_map/ppermute | solution.py:467
  1221.1 53.5 %collective-permute-start.94 = (bf16[256,2048]{1,0:T(8,128)(2,1)S(1)}, bf16[256,2048]{1,0:T(8,128)(2,1)S(1)}, u32[]{:S(2)}, u32[]{:S(2)}) collective-permute-start(bf16[256,2048]{1,0:T(8,128)(2,1)S(1)} %fusion.25), channel_id=1, source_target_pairs={{0,2},{1,3},{2,0},{3,1},{4,6},{5,7},{6,4},{7,5},{8,10},{9,11},{10,... | collective-permute-start | bytes 3145736 | tf_op jit(solution)/shard_map/ppermute | solution.py:450
  1277.9 66.1 %collective-permute-start.111 = (bf16[256,1536]{1,0:T(8,128)(2,1)S(1)}, bf16[256,1536]{1,0:T(8,128)(2,1)S(1)}, u32[]{:S(2)}, u32[]{:S(2)}) collective-permute-start(bf16[256,1536]{1,0:T(8,128)(2,1)S(1)} %copy-done.58), channel_id=1, source_target_pairs={{0,4},{4,0},{8,12},{12,8},{16,20},{20,16},{24,28},{28,24},{1,5},{5... | collective-permute-start | bytes 2359304 | tf_op jit(solution)/shard_map/ppermute | solution.py:450
  1292.9 54.1 %collective-permute-start.85 = (bf16[2,128,2048]{2,1,0:T(8,128)(2,1)S(1)}, bf16[2,128,2048]{2,1,0:T(8,128)(2,1)S(1)}, u32[]{:S(2)}, u32[]{:S(2)}) collective-permute-start(bf16[2,128,2048]{2,1,0:T(8,128)(2,1)S(1)} %fusion.96), channel_id=1, source_target_pairs={{0,2},{1,3},{2,0},{3,1},{4,6},{5,7},{6,4},{7,5},{8,10},{9,11},{10,... | collective-permute-start | bytes 3145736 | tf_op jit(solution)/shard_map/ppermute | solution.py:450
  1295.1 53.4 %collective-permute-start.87 = (bf16[2,128,2048]{2,1,0:T(8,128)(2,1)S(1)}, bf16[2,128,2048]{2,1,0:T(8,128)(2,1)S(1)}, u32[]{:S(2)}, u32[]{:S(2)}) collective-permute-start(bf16[2,128,2048]{2,1,0:T(8,128)(2,1)S(1)} %fusion.98), channel_id=1, source_target_pairs={{0,4},{4,0},{8,12},{12,8},{16,20},{20,16},{24,28},{28,24},{1,5},{5... | collective-permute-start | bytes 3145736 | tf_op jit(solution)/shard_map/ppermute | solution.py:450
  1344.6 46.4 %collective-permute-start.73 = (bf16[2,128,2048]{2,1,0:T(8,128)(2,1)S(1)}, bf16[2,128,2048]{2,1,0:T(8,128)(2,1)}, u32[]{:S(2)}, u32[]{:S(2)}) collective-permute-start(bf16[2,128,2048]{2,1,0:T(8,128)(2,1)S(1)} %fusion.88), channel_id=1, source_target_pairs={{0,2},{1,3},{2,0},{3,1},{4,6},{5,7},{6,4},{7,5},{8,10},{9,11},{10,... | collective-permute-start | bytes 3145736 | tf_op jit(solution)/shard_map/ppermute | solution.py:450
  1348.6 65.0 %collective-permute-start.79 = (bf16[2,128,2048]{2,1,0:T(8,128)(2,1)S(1)}, bf16[2,128,2048]{2,1,0:T(8,128)(2,1)}, u32[]{:S(2)}, u32[]{:S(2)}) collective-permute-start(bf16[2,128,2048]{2,1,0:T(8,128)(2,1)S(1)} %fusion.92), channel_id=1, source_target_pairs={{0,2},{1,3},{2,0},{3,1},{4,6},{5,7},{6,4},{7,5},{8,10},{9,11},{10,... | collective-permute-start | bytes 3145736 | tf_op jit(solution)/shard_map/ppermute | solution.py:450
  1368.6 46.5 %collective-permute-start.81 = (bf16[2,128,2048]{2,1,0:T(8,128)(2,1)S(1)}, bf16[2,128,2048]{2,1,0:T(8,128)(2,1)S(1)}, u32[]{:S(2)}, u32[]{:S(2)}) collective-permute-start(bf16[2,128,2048]{2,1,0:T(8,128)(2,1)S(1)} %fusion.94), channel_id=1, source_target_pairs={{0,4},{4,0},{8,12},{12,8},{16,20},{20,16},{24,28},{28,24},{1,5},{5... | collective-permute-start | bytes 3145736 | tf_op jit(solution)/shard_map/ppermute | solution.py:450
  1370.3 115.5 %collective-permute-start.88 = (bf16[128,2048]{1,0:T(8,128)(2,1)S(1)}, bf16[128,2048]{1,0:T(8,128)(2,1)S(1)}, u32[]{:S(2)}, u32[]{:S(2)}) collective-permute-start(bf16[128,2048]{1,0:T(8,128)(2,1)S(1)} %slice_bitcast_fusion.9), channel_id=1, source_target_pairs={{0,2},{1,3},{2,0},{3,1},{4,6},{5,7},{6,4},{7,5},{8,10},{9,11},{10,... | collective-permute-start | bytes 1572872 | tf_op jit(solution)/shard_map/ppermute | solution.py:450
  (190 other events, 3299.2 us)
Sparse Core Ops, SparseCore 0:
  94.2 258.4 all-gather.3

commit v3 on v2

--- a/solution.py
+++ b/solution.py
@@ -489,20 +489,43 @@
     )
 
 
-def laid(pieces, order):
-    whole = jnp.zeros((len(pieces),) + pieces[0].shape, pieces[0].dtype)
+def place_kernel(by_column, order, *refs):
+    *pieces, whole, sems = refs
+    copies = []
     for index, piece in enumerate(pieces):
-        place = (order[index],) + (0,) * piece.ndim
-        whole = lax.dynamic_update_slice(whole, piece[None], place)
-    return whole
-
-
-def gather_packs(values):
+        target = whole.at[order[index]]
+        if by_column:
+            width = piece.shape[1]
+            target = whole.at[:, pl.ds(pl.multiple_of(order[index] * width, 128), width)]
+        copies.append(pltpu.make_async_copy(piece, target, sems.at[index]))
+        copies[-1].start()
+    for copy in copies:
+        copy.wait()
+
+
+def laid(pieces, order, by_column=False):
+    count = len(pieces)
+    rows, columns = pieces[0].shape
+    shape = (rows, count * columns) if by_column else (count, rows, columns)
+    anywhere = pl.BlockSpec(memory_space=pl.ANY)
+    return call(
+        functools.partial(place_kernel, by_column),
+        1,
+        [anywhere] * count,
+        anywhere,
+        shape_of(shape, pieces[0].dtype),
+        [pltpu.SemaphoreType.DMA((count,))],
+        1000,
+        1,
+    )(order, *pieces)
+
+
+def gather_packs(values, by_column=False):
     pieces = []
     for plane in range(lax.axis_size("dp") // 2):
         values = next_plane(values) if plane else values
         pieces += [values, far_pack(values)]
-    return laid(pieces, plane_order())
+    return laid(pieces, plane_order(), by_column)
 
 
 def fold_packs(values):
@@ -545,29 +568,51 @@
     return (left.astype(jnp.float32) + right.astype(jnp.float32)).astype(kind)
 
 
-def fold_plane(own, other):
+def fold_first(own, arrived):
     half_rows = own.shape[2] // 2
-    arrived = far_core(other)
     upper, lower = slice(None, half_rows), slice(half_rows, None)
-    upper_near = added(own[:, 0, upper], arrived[:, 0, upper])
-    upper_far = added(own[:, 1, upper], arrived[:, 1, upper])
-    lower_near = added(own[0, :, lower], arrived[0, :, lower])
-    lower_far = added(own[1, :, lower], arrived[1, :, lower])
-    upper_near = added(upper_near, far_side(upper_far))
-    lower_near = added(lower_near, far_pack(lower_far))
+    return (
+        added(own[:, 0, upper], arrived[:, 0, upper]),
+        added(own[0, :, lower], arrived[0, :, lower]),
+        added(own[:, 1, upper], arrived[:, 1, upper]),
+        added(own[1, :, lower], arrived[1, :, lower]),
+    )
+
+
+def fold_second(upper, lower, upper_far, lower_far):
+    upper = added(upper, far_side(upper_far))
+    lower = added(lower, far_pack(lower_far))
+    return upper[0], lower[0], upper[1], lower[1]
+
+
+def fold_third(upper, lower, upper_far, lower_far):
     return jnp.concatenate(
-        [
-            added(upper_near[0], far_pack(upper_near[1])),
-            added(lower_near[0], far_side(lower_near[1])),
-        ]
-    )
-
-
-def fold_all(parts):
-    summed = fold_plane(*parts[1])
-    for part in parts[2:]:
-        summed = added(next_plane(summed), fold_plane(*part))
-    return added(next_plane(summed), fold_plane(*parts[0]), jnp.float32)
+        [added(upper, far_pack(upper_far)), added(lower, far_side(lower_far))]
+    )
+
+
+def tied(small, values):
+    return lax.optimization_barrier((small, values))
+
+
+def gather_tables(expert_ids, gate_values, segment_ids):
+    top_count = expert_ids.shape[1]
+    tables = jnp.concatenate(
+        [expert_ids.T.astype(jnp.bfloat16), gate_values.T, segment_ids.astype(jnp.bfloat16)]
+    )[None]
+    for axis in ("tensor", "dp"):
+        bit = 1
+        while bit < lax.axis_size(axis):
+            tables = jnp.concatenate([tables, swapped(tables, axis, bit)])
+            bit *= 2
+        if axis == "tensor":
+            sides = jnp.arange(tables.shape[0], dtype=jnp.int32) ^ lax.axis_index("tensor")
+            segments = jnp.take(tables[:, -1], sides, axis=0).reshape(-1)
+    devices = jnp.arange(tables.shape[0], dtype=jnp.int32)
+    own = lax.axis_index("dp") * lax.axis_size("tensor") + lax.axis_index("tensor")
+    tables = jnp.take(tables, devices ^ own, axis=0)
+    all_ids, all_gates = tables[:, :top_count], tables[:, top_count : 2 * top_count]
+    return all_ids.astype(jnp.int32), all_gates, segments.astype(jnp.int32)
 
 
 def routing(all_ids, all_gates, local_experts, capacity):
@@ -659,7 +704,41 @@
     return outputs, grad_second, grad_w_gate, grad_w_up, grad_w_down
 
 
-def experts_by_gather(second_in, all_cot, places, gates, w_gate, w_up, w_down, middle, capacity):
+class Folding:
+    def __init__(self, order):
+        self.order, self.waiting = order, {}
+        self.summed, self.count, self.total = None, 0, None
+
+    def begin(self, plane, own, other):
+        self.waiting[plane] = (0, (own, far_core(other)))
+
+    def step(self, small):
+        made = {}
+        for plane, (stage, values) in self.waiting.items():
+            if stage < 3:
+                made[plane] = (fold_first, fold_second, fold_third)[stage](*values)
+        ready = {plane: values for plane, (stage, values) in self.waiting.items() if stage == 3}
+        following = self.order[self.count] if self.count < len(self.order) else None
+        passed = None
+        if following in ready:
+            last = self.count + 1 == len(self.order)
+            kind = jnp.float32 if last else jnp.bfloat16
+            passed = ready[following]
+            if self.summed is not None:
+                passed = added(next_plane(self.summed), passed, kind)
+            del self.waiting[following]
+            self.count += 1
+            if last:
+                self.total = passed
+        small, (made, passed) = tied(small, (made, passed))
+        for plane, values in made.items():
+            self.waiting[plane] = (self.waiting[plane][0] + 1, values)
+        if passed is not None:
+            self.summed = passed
+        return small
+
+
+def experts_by_gather(second_in, all_cot, places, gates, w_gate, w_up, w_down, capacity):
     packs, local_experts, seq_len = places.shape
     tensor_count = lax.axis_size("tensor")
     planes = packs // 2
@@ -674,30 +753,31 @@
 
     near_places, near_gates = as_met(places), as_met(gates)
     places_t, gates_t = near_places.transpose(0, 2, 1), near_gates.transpose(0, 2, 1)
-    kept = []
-    row_parts, mix_parts = [], []
-    travelling = second_in
+    pieces, travelling = [], second_in
     for plane in range(planes):
-        pair = slice(plane * 2, plane * 2 + 2)
+        travelling = next_plane(travelling) if plane else travelling
+        pieces.append(spread_plane(travelling))
+    pairs = [slice(plane * 2, plane * 2 + 2) for plane in range(planes)]
+    order = [*range(1, planes), 0]
+    kept, folding, mixing = {}, Folding(order), Folding(order)
+    for plane in range(planes):
+        pair = pairs[plane]
         grad_slots, grad_hidden = cot_slots(
             pack_order[pair], places, gates, all_cot, w_down, capacity
         )
-        own, other = spread_plane(travelling)
-        if plane + 1 < planes:
-            travelling = next_plane(travelling)
-        slots, hidden, grad_gated, grad_lifted, *row_part = row_slots(
-            near_places[pair], places_t[pair], own, other, w_gate, w_up, grad_hidden, capacity
-        )
-        row_parts.append(row_part)
-        kept.append((slots, grad_slots, hidden, grad_gated, grad_lifted))
-    kept, _ = lax.optimization_barrier((kept, row_parts[-1]))
-    for plane in range(planes):
-        pair = slice(plane * 2, plane * 2 + 2)
-        mix_parts.append(mix_rows(places_t[pair], gates_t[pair], kept[plane][2], w_down, capacity))
-    grad_second, mix_parts = lax.optimization_barrier((fold_all(row_parts), mix_parts))
-    outputs = middle + fold_all(mix_parts)
-    grad_w_gate, grad_w_up, grad_w_down = weight_grads(*zip(*kept))
-    return outputs, grad_second, grad_w_gate, grad_w_up, grad_w_down
+        near = folding.step(near_places[pair]) if plane > 1 else near_places[pair]
+        slots, hidden, grad_gated, grad_lifted, *part = row_slots(
+            near, places_t[pair], *pieces[plane], w_gate, w_up, grad_hidden, capacity
+        )
+        folding.begin(plane, *part)
+        kept[plane] = (slots, grad_slots, hidden, grad_gated, grad_lifted)
+    for plane in order:
+        near_t = folding.step(places_t[pairs[plane]])
+        part = mix_rows(near_t, gates_t[pairs[plane]], kept[plane][2], w_down, capacity)
+        mixing.begin(plane, *part)
+    while folding.total is None:
+        folding.step(pack_order)
+    return folding.total, mixing, [kept[plane] for plane in range(planes)]
 
 
 def shards(
@@ -733,15 +813,11 @@
         and tensor_count == 4
         and data_count > 2
         and data_count & (data_count - 1) == 0
+        and all_experts <= 256
     )
     if by_gather:
         axes = ("dp", "tensor")
-        all_ids = lax.all_gather(expert_ids.T, axes, axis=0)
-        all_gates = lax.all_gather(gate_values.T, axes, axis=0)
-        pack_segs = lax.all_gather(segment_ids, "tensor", axis=1, tiled=True)
-        inputs, cotangent, w_query, all_ids, all_gates, pack_segs = lax.optimization_barrier(
-            (inputs, cotangent, w_query, all_ids, all_gates, pack_segs)
-        )
+        all_ids, all_gates, segments = gather_tables(expert_ids, gate_values, segment_ids)
         all_cot = lax.all_gather(cotangent, axes, axis=0, tiled=True)
         all_cot = all_cot.reshape(data_count, seq_len, model_width)
         places, gates = routing(all_ids, all_gates, local_experts, capacity)
@@ -756,10 +832,10 @@
         full_query, full_key, full_value = (
             full_in[:, index * local_width : (index + 1) * local_width] for index in range(3)
         )
-        full_output = gather_packs(w_output).transpose(1, 0, 2).reshape(w_output.shape[0], -1)
+        full_output = gather_packs(w_output, True)
     else:
         side_sum, side_gather = lambda term: row_sum(lambda *_: term, tok_rows), gather_rows
-        pack_segs = lax.all_gather(segment_ids, "tensor", axis=1, tiled=True)
+        segments = lax.all_gather(segment_ids, "tensor", axis=1, tiled=True)[0]
         full_query, full_key, full_value, full_output = (
             lax.all_gather(w_query, "dp", axis=0, tiled=True),
             lax.all_gather(w_key, "dp", axis=0, tiled=True),
@@ -777,7 +853,6 @@
     query_low = rotate(query_norm * query_gain, cosine, sine_tab).astype(jnp.bfloat16)
     key_low = rotate(key_norm * key_gain, cosine, sine_tab).astype(jnp.bfloat16)
     value_heads = value_low.reshape(seq_len, head_count, head_size)
-    segments = pack_segs[0]
     block_rows = min(512, seq_len)
     block_total = seq_len // block_rows
     masks = []
@@ -804,30 +879,33 @@
     normed_two, factor_two = norm_parts(middle)
     second_in = (normed_two * ffn_gain).astype(jnp.bfloat16)
     if by_gather:
-        outputs, grad_second, grad_w_gate, grad_w_up, grad_w_down = experts_by_gather(
-            second_in, all_cot, places, gates, w_gate, w_up, w_down, middle, capacity
-        )
+        grad_second, mixing, kept = experts_by_gather(
+            second_in, all_cot, places, gates, w_gate, w_up, w_down, capacity
+        )
+        mix_step = mixing.step
     else:
         outputs, grad_second, grad_w_gate, grad_w_up, grad_w_down = experts_by_exchange(
             second_in, cotangent, expert_ids, gate_values, w_gate, w_up, w_down, middle, capacity
         )
+        mix_step = lambda values: values
     ffn_gain_part = jnp.sum(grad_second * normed_two, axis=0)
     grad_middle = cotangent.astype(jnp.float32) + norm_back(
         grad_second, normed_two, factor_two, ffn_gain
     )
-    pack_grad = side_gather(grad_middle.astype(jnp.bfloat16))
+    pack_grad = mix_step(side_gather(grad_middle.astype(jnp.bfloat16)))
     output_part = contract_first(mixture, pack_grad)
     grad_mixture = (
         contract_last(pack_grad, full_output)
         .astype(jnp.bfloat16)
         .reshape(seq_len, head_count, head_size)
     )
+    grad_mixture = mix_step(grad_mixture)
     grad_query_parts = []
     grad_key_sum = jnp.zeros((seq_len, head_count, head_size), jnp.float32)
     grad_value_sum = jnp.zeros((seq_len, head_count, head_size), jnp.float32)
     for block_index in range(block_total):
         offset = block_index * block_rows
-        query_block = query_low[offset : offset + block_rows]
+        query_block = mix_step(query_low[offset : offset + block_rows])
         grad_block = grad_mixture[offset : offset + block_rows]
         scores = block_scores(query_block, key_low, masks[block_index], inv_root)
         prob_rows = jnp.exp(scores - lse_parts[block_index])
@@ -857,6 +935,7 @@
     grad_key_norm = rotate_back(grad_key_sum, cosine, sine_tab)
     query_gain_part = jnp.sum(grad_query_norm * query_norm, axis=(0, 1))
     key_gain_part = jnp.sum(grad_key_norm * key_norm, axis=(0, 1))
+    grad_query_norm = mix_step(grad_query_norm)
     grad_query_pre = (
         norm_back(grad_query_norm, query_norm, query_factor, query_gain)
         .reshape(seq_len, -1)
@@ -886,6 +965,11 @@
         )
         by_column = output_part.astype(jnp.bfloat16).reshape(local_width, data_count, -1)
         grad_w_output = fold_packs(by_column.transpose(1, 0, 2))
+        kept, _ = lax.optimization_barrier((kept, in_part))
+        grad_w_gate, grad_w_up, grad_w_down = weight_grads(*zip(*kept))
+        while mixing.total is None:
+            mixing.step(attn_gain)
+        outputs = middle + mixing.total
         late = sum_everywhere(attn_gain_part)
         early = sum_everywhere(jnp.concatenate(gain_parts[1:]))
         splits = (model_width, model_width + head_size)

time: 1520 us -> 1940 us (1.28)
  Pallas kernels: 391 us -> 907 us
  blocking collectives: 86.8 us -> 0 us
  other arithmetic: 107 us -> 154 us
  local copies, waits for them, and re-layouts: 159 us -> 115 us
  waiting for transfers between devices: 575 us -> 537 us
  starting transfers between devices: 89.4 us -> 112 us
    pallas_call x0 -> x4, Pallas kernels: none -> 516 us  [laid(): call(functools.partial(place_kernel, by_column), 1, [anywhere] * count, a...]
    all_gather x3 -> x0, blocking collectives: 86.8 us -> none  [the longest x1 44.3 us: shards(): all_ids = lax.all_gather(expert_ids.T, axes, axis=0)]
    dynamic_update_slice x23 -> x0, local copies, waits for them, and re-layouts: 68.8 us -> none  [laid(): whole = lax.dynamic_update_slice(whole, piece[None], place)]
    convert_element_type x52 -> x67, other arithmetic: 61.5 us -> 95.7 us  [added(): return (left.astype(jnp.float32) + right.astype(jnp.float32)).astype(kind)]
    ppermute x98 -> x103, waiting for transfers between devices: 417 us -> 392 us  [swapped(): return lax.ppermute(values, axis, [(i, i ^ bit) for i in range(count)])]
    ppermute x21, starting transfers between devices: 11.7 us -> 31.4 us  [next_plane(): lax.ppermute(values, 'dp', [(i, (i + 2) % count) for i in range(count)])]
    ppermute x98 -> x103, starting transfers between devices: 77.7 us -> 80.4 us  [swapped(): return lax.ppermute(values, axis, [(i, i ^ bit) for i in range(count)])]
  transfers between devices with their start and end apart: 120 -> 125, of which waited for: 61 -> 54; matrix products, arithmetic and copies ran while one was open for 18% -> 17% of each run, Pallas kernels for 26% -> 47%
where the time goes in v3:
time: 1940 us; the launch traced here: 1930 us
  Pallas kernels  907 us (47%)
  waiting for transfers between devices  537 us (28%)
  other arithmetic  154 us (8%)
  local copies, waits for them, and re-layouts  115 us (6%)
  starting transfers between devices  112 us (6%)
  matrix products  84.2 us (4%)
    pallas_call x4, Pallas kernels, laid(): call(functools.partial(place_kernel, by_column), 1, [anywhere] * count, a...  516 us
    ppermute x103, waiting for transfers between devices, swapped(): return lax.ppermute(values, axis, [(i, i ^ bit) for i in range(count)])  392 us
    pallas_call x4, Pallas kernels, row_slots(): call(functools.partial(row_kernel, packs, experts, capacity), 2 * packs +...  167 us
    ppermute x21, waiting for transfers between devices, next_plane(): lax.ppermute(values, 'dp', [(i, (i + 2) % count) for i in range(count)])  144 us
    convert_element_type x67, other arithmetic, added(): return (left.astype(jnp.float32) + right.astype(jnp.float32)).astype(kind)  95.7 us
    pallas_call x4, Pallas kernels, mix_rows(): call(functools.partial(mix_kernel, packs, experts, capacity), packs + exp...  89.4 us
    pallas_call x4, Pallas kernels, cot_slots(): call(functools.partial(cot_kernel, packs, experts, capacity), packs + exp...  88.1 us
    ppermute x103, starting transfers between devices, swapped(): return lax.ppermute(values, axis, [(i, i ^ bit) for i in range(count)])  80.4 us
  transfers between devices with their start and end apart: 125, of which 54 were waited for; matrix products, arithmetic and copies ran while one was open for 17% of the time, Pallas kernels for 47%

profile of v3, /device:TPU:0, one launch (start us, length us, event | category | flops | bytes accessed | tf_op | source)
XLA Modules:
  0.0 1925.9 jit_solution(17113218682808905848)
XLA Ops:
  25.7 26.1 %collective-permute-done.4.refs_2_ = bf16[256,1536]{1,0:T(8,128)(2,1)} collective-permute-done((bf16[256,1536]{1,0:T(8,128)(2,1)}, bf16[256,1536]{1,0:T(8,128)(2,1)}, u32[]{:S(2)}, u32[]{:S(2)}) %collective-permute-start.4) | collective-permute-done | bytes 786464 | tf_op jit(solution)/shard_map/ppermute | solution.py:467
  83.2 24.4 %collective-permute-done.24 = bf16[16,17,256]{2,0,1:T(8,128)(2,1)} collective-permute-done((bf16[16,17,256]{2,0,1:T(8,128)(2,1)}, bf16[16,17,256]{2,0,1:T(8,128)(2,1)}, u32[]{:S(2)}, u32[]{:S(2)}) %collective-permute-start.24) | collective-permute-done | bytes 139296 | tf_op jit(solution)/shard_map/ppermute | solution.py:450
  117.0 40.8 %collective-permute-done.17.refs_6_ = bf16[512,256]{1,0:T(8,128)(2,1)} collective-permute-done((bf16[512,256]{1,0:T(8,128)(2,1)}, bf16[512,256]{1,0:T(8,128)(2,1)}, u32[]{:S(2)}, u32[]{:S(2)}) %collective-permute-start.17) | collective-permute-done | bytes 262176 | tf_op jit(solution)/shard_map/ppermute | solution.py:467
  181.3 65.4 %shard_map.257 = bf16[512,2048]{1,0:T(8,128)(2,1)} custom-call(s32[8]{0:T(128)} %copy-done.119, bf16[512,256]{1,0:T(8,128)(2,1)} %refs_0_.1, bf16[512,256]{1,0:T(8,128)(2,1)} %collective-permute-done.12.refs_1_, bf16[512,256]{1,0:T(8,128)(2,1)} %collective-permute-done.13.refs_2_, bf16[512,256]{1,0:T(8,128)(2,1)} %collective-permute-done.14.refs_3_, ...), custom_call_target="tpu_custom_call" | custom-call | flops 1000 | bytes 2 | tf_op jit(solution)/shard_map/pallas_call | solution.py:511
  246.6 128.9 %shard_map.255 = bf16[4,256,2048]{2,1,0:T(8,128)(2,1)} custom-call(s32[4]{0:T(128)} %iota_xor_fusion.order, bf16[256,2048]{1,0:T(8,128)(2,1)} %copy-done.42, bf16[256,2048]{1,0:T(8,128)(2,1)} %copy-done.69, bf16[256,2048]{1,0:T(8,128)(2,1)} %collective-permute-done.1.refs_2_, bf16[256,2048]{1,0:T(8,128)(2,1)} %collective-permute-done.2.refs_3_), custom_call_target="tpu_custom_call" | custom-call | flops 1000 | bytes 2 | tf_op jit(solution)/shard_map/pallas_call | solution.py:511
  375.6 192.4 %shard_map.256 = bf16[8,256,1536]{2,1,0:T(8,128)(2,1)} custom-call(s32[8]{0:T(128)} %copy-done.119, bf16[256,1536]{1,0:T(8,128)(2,1)} %constant_dynamic-update-slice_fusion.refs_0_, bf16[256,1536]{1,0:T(8,128)(2,1)} %collective-permute-done.3.refs_1_, bf16[256,1536]{1,0:T(8,128)(2,1)} %collective-permute-done.4.refs_2_, ...), custom_call_target="tpu_custom_call" | custom-call | flops 1000 | bytes 2 | tf_op jit(solution)/shard_map/pallas_call | solution.py:511
  633.1 16.6 collective-permute-done.21
  715.4 17.0 collective-permute-done.34
  776.9 21.9 %shard_map.258 = (bf16[8,256,2048]{2,1,0:T(8,128)(2,1)}, f32[8,256,256]{2,1,0:T(8,128)}) custom-call(s32[2]{0:T(128)} %get-tuple-element.467.table, s32[8,8,1024]{2,1,0:T(8,128)} %get-tuple-element.461.places, f32[8,8,1024]{2,1,0:T(8,128)} %fusion.25.gates, bf16[8,1024,2048]{2,1,0:T(8,128)(2,1)} %bitcast.426, bf16[8,256,2048]{2,1,0:T(8,128)(2,1)} %down.15), custom_call_target="tpu_custom_call" | custom-call | flops 10737418240 | bytes 21474836 | tf_op jit(solution)/shard_map/pallas_call | solution.py:354
  798.8 41.5 %shard_map.259 = (bf16[8,256,2048]{2,1,0:T(8,128)(2,1)}, bf16[8,256,256]{2,1,0:T(8,128)(2,1)}, bf16[8,256,256]{2,1,0:T(8,128)(2,1)}, bf16[8,256,256]{2,1,0:T(8,1...) custom-call(s32[2,8,1024]{2,1,0:T(8,128)} %bitcast.493, ...), custom_call_target="tpu_custom_call" | custom-call | flops 25769803776 | bytes 51539608 | tf_op jit(solution)/shard_map/pallas_call | solution.py:383
  840.4 21.9 %shard_map.260 = (bf16[8,256,2048]{2,1,0:T(8,128)(2,1)}, f32[8,256,256]{2,1,0:T(8,128)}) custom-call(s32[2]{0:T(128)} %get-tuple-element.468.table, s32[8,8,1024]{2,1,0:T(8,128)} %get-tuple-element.461.places, f32[8,8,1024]{2,1,0:T(8,128)} %fusion.25.gates, bf16[8,1024,2048]{2,1,0:T(8,128)(2,1)} %bitcast.427, bf16[8,256,2048]{2,1,0:T(8,128)(2,1)} %down.15), custom_call_target="tpu_custom_call" | custom-call | flops 10737418240 | bytes 21474836 | tf_op jit(solution)/shard_map/pallas_call | solution.py:354
  862.3 41.8 %shard_map.261 = (bf16[8,256,2048]{2,1,0:T(8,128)(2,1)}, bf16[8,256,256]{2,1,0:T(8,128)(2,1)}, bf16[8,256,256]{2,1,0:T(8,128)(2,1)}, bf16[8,256,256]{2,1,0:T(8,1...) custom-call(s32[2,8,1024]{2,1,0:T(8,128)} %bitcast.492, ...), custom_call_target="tpu_custom_call" | custom-call | flops 25769803776 | bytes 51539608 | tf_op jit(solution)/shard_map/pallas_call | solution.py:383
  910.1 19.8 %collective-permute-done.59 = bf16[2,128,2048]{2,1,0:T(8,128)(2,1)S(1)} collective-permute-done((bf16[2,128,2048]{2,1,0:T(8,128)(2,1)S(1)}, bf16[2,128,2048]{2,1,0:T(8,128)(2,1)S(1)}, u32[]{:S(2)}, u32[]{:S(2)}) %collective-permute-start.59) | collective-permute-done | bytes 1048608 | tf_op jit(solution)/shard_map/ppermute | solution.py:450
  931.0 22.1 %shard_map.262 = (bf16[8,256,2048]{2,1,0:T(8,128)(2,1)}, f32[8,256,256]{2,1,0:T(8,128)}) custom-call(s32[2]{0:T(128)} %get-tuple-element.469.table, s32[8,8,1024]{2,1,0:T(8,128)} %get-tuple-element.461.places, f32[8,8,1024]{2,1,0:T(8,128)} %fusion.25.gates, bf16[8,1024,2048]{2,1,0:T(8,128)(2,1)} %bitcast.428, bf16[8,256,2048]{2,1,0:T(8,128)(2,1)} %down.15), custom_call_target="tpu_custom_call" | custom-call | flops 10737418240 | bytes 21474836 | tf_op jit(solution)/shard_map/pallas_call | solution.py:354
  971.5 41.4 %shard_map.263 = (bf16[8,256,2048]{2,1,0:T(8,128)(2,1)}, bf16[8,256,256]{2,1,0:T(8,128)(2,1)}, bf16[8,256,256]{2,1,0:T(8,128)(2,1)}, bf16[8,256,256]{2,1,0:T(8,1...) custom-call(s32[2,8,1024]{2,1,0:T(8,128)} %bitcast.491, ...), custom_call_target="tpu_custom_call" | custom-call | flops 25769803776 | bytes 51539608 | tf_op jit(solution)/shard_map/pallas_call | solution.py:383
  1013.0 22.1 %shard_map.264 = (bf16[8,256,2048]{2,1,0:T(8,128)(2,1)}, f32[8,256,256]{2,1,0:T(8,128)}) custom-call(s32[2]{0:T(128)} %get-tuple-element.470.table, s32[8,8,1024]{2,1,0:T(8,128)} %get-tuple-element.461.places, f32[8,8,1024]{2,1,0:T(8,128)} %fusion.25.gates, bf16[8,1024,2048]{2,1,0:T(8,128)(2,1)} %bitcast.429, bf16[8,256,2048]{2,1,0:T(8,128)(2,1)} %down.15), custom_call_target="tpu_custom_call" | custom-call | flops 10737418240 | bytes 21474836 | tf_op jit(solution)/shard_map/pallas_call | solution.py:354
  1042.1 18.7 collective-permute-done.40
  1076.9 41.9 %shard_map.265 = (bf16[8,256,2048]{2,1,0:T(8,128)(2,1)}, bf16[8,256,256]{2,1,0:T(8,128)(2,1)}, bf16[8,256,256]{2,1,0:T(8,128)(2,1)}, bf16[8,256,256]{2,1,0:T(8,1...) custom-call(s32[2,8,1024]{2,1,0:T(8,128)} %bitcast.490, ...), custom_call_target="tpu_custom_call" | custom-call | flops 25769803776 | bytes 51539608 | tf_op jit(solution)/shard_map/pallas_call | solution.py:383
  1128.5 17.5 collective-permute-done.54
  1171.2 16.5 collective-permute-done.64
  1206.2 21.4 %collective-permute-done.68 = bf16[256,2048]{1,0:T(8,128)(2,1)S(1)} collective-permute-done((bf16[256,2048]{1,0:T(8,128)(2,1)}, bf16[256,2048]{1,0:T(8,128)(2,1)S(1)}, u32[]{:S(2)}, u32[]{:S(2)}) %collective-permute-start.68) | collective-permute-done | bytes 1048608 | tf_op jit(solution)/shard_map/ppermute | solution.py:467
  1228.0 22.4 %shard_map.268 = (bf16[2,2,256,2048]{3,2,1,0:T(8,128)(2,1)}, bf16[2,2,256,2048]{3,2,1,0:T(8,128)(2,1)}) custom-call(s32[2,1024,8]{2,1,0:T(8,128)} %get-tuple-element.222.places_t, f32[2,1024,8]{2,1,0:T(8,128)} %get-tuple-element.356.gates_t, bf16[8,256,256]{2,1,0:T(8,128)(2,1)} %get-tuple-element.303.hidden.refs_9_, bf16[8,256,2048]{2,1,0:T(8,128)(2,1)} %down.15), custom_call_target="tpu_custom_call" | custom-call | flops 10737418240 | bytes 21474836 | tf_op jit(solution)/shard_map/pallas_call | solution.py:409
  1250.4 22.1 %shard_map.269 = (bf16[2,2,256,2048]{3,2,1,0:T(8,128)(2,1)}, bf16[2,2,256,2048]{3,2,1,0:T(8,128)(2,1)}) custom-call(s32[2,1024,8]{2,1,0:T(8,128)} %get-tuple-element.226.places_t, f32[2,1024,8]{2,1,0:T(8,128)} %get-tuple-element.355.gates_t, bf16[8,256,256]{2,1,0:T(8,128)(2,1)} %get-tuple-element.304.hidden.refs_10_, bf16[8,256,2048]{2,1,0:T(8,128)(2,1)} %down.15), custom_call_target="tpu_custom_call" | custom-call | flops 10737418240 | bytes 21474836 | tf_op jit(solution)/shard_map/pallas_call | solution.py:409
  1275.9 22.5 %shard_map.270 = (bf16[2,2,256,2048]{3,2,1,0:T(8,128)(2,1)}, bf16[2,2,256,2048]{3,2,1,0:T(8,128)(2,1)}) custom-call(s32[2,1024,8]{2,1,0:T(8,128)} %get-tuple-element.230.places_t, f32[2,1024,8]{2,1,0:T(8,128)} %get-tuple-element.354.gates_t, bf16[8,256,256]{2,1,0:T(8,128)(2,1)} %get-tuple-element.305.hidden.refs_11_, bf16[8,256,2048]{2,1,0:T(8,128)(2,1)} %down.15), custom_call_target="tpu_custom_call" | custom-call | flops 10737418240 | bytes 21474836 | tf_op jit(solution)/shard_map/pallas_call | solution.py:409
  1298.4 22.4 %shard_map.267 = (bf16[2,2,256,2048]{3,2,1,0:T(8,128)(2,1)}, bf16[2,2,256,2048]{3,2,1,0:T(8,128)(2,1)}) custom-call(s32[2,1024,8]{2,1,0:T(8,128)} %get-tuple-element.218.places_t, f32[2,1024,8]{2,1,0:T(8,128)} %get-tuple-element.357.gates_t, bf16[8,256,256]{2,1,0:T(8,128)(2,1)} %get-tuple-element.302.hidden.refs_8_, bf16[8,256,2048]{2,1,0:T(8,128)(2,1)} %down.15), custom_call_target="tpu_custom_call" | custom-call | flops 10737418240 | bytes 21474836 | tf_op jit(solution)/shard_map/pallas_call | solution.py:409
  1360.3 128.9 %shard_map.266 = bf16[4,256,2048]{2,1,0:T(8,128)(2,1)} custom-call(s32[4]{0:T(128)} %iota_xor_fusion.order, bf16[256,2048]{1,0:T(8,128)(2,1)} %copy-done.50, bf16[256,2048]{1,0:T(8,128)(2,1)} %copy-done.73, bf16[256,2048]{1,0:T(8,128)(2,1)} %copy-done.74, bf16[256,2048]{1,0:T(8,128)(2,1)} %collective-permute-done.73.refs_3_), custom_call_target="tpu_custom_call" | custom-call | flops 1000 | bytes 2 | tf_op jit(solution)/shard_map/pallas_call | solution.py:511
  1532.0 18.0 collective-permute-done.80
  1554.7 17.7 collective-permute-done.82
  1575.2 18.9 collective-permute-done.84
  1750.7 47.7 %shard_map.271 = (f32[8,2048,256]{2,1,0:T(8,128)}, f32[8,2048,256]{2,1,0:T(8,128)}, f32[8,256,2048]{2,1,0:T(8,128)}) custom-call(bf16[8,256,2048]{2,1,0:T(8,128)(2,1)} %get-tuple-element.294.refs_0_, bf16[8,256,2048]{2,1,0:T(8,128)(2,1)} %get-tuple-element.295.refs_1_, bf16[8,256,2048]{2,1,0:T(8,128)(2,1)} %get-tuple-element.296.refs_2_, ...), custom_call_target="tpu_custom_call" | custom-call | flops 25769803776 | bytes 51539608 | tf_op jit(solution)/shard_map/pallas_call | solution.py:437
  1810.9 16.7 collective-permute-done.95
  1836.3 35.4 %collective-permute-done.109 = f32[2304]{0:T(1024)S(1)} collective-permute-done((f32[2304]{0:T(1024)S(1)}, f32[2304]{0:T(1024)S(1)}, u32[]{:S(2)}, u32[]{:S(2)}) %collective-permute-start.109) | collective-permute-done | bytes 9248 | tf_op jit(solution)/shard_map/ppermute | solution.py:450
  (787 shorter events, 675.9 us)
Async XLA Ops:
  7.2 769.7 %all-gather.2.cloned.1.call-start = ((), (), s32[]{:S(2)}) async-start(), calls=%async_computation | async-start | bytes 34603008 | tf_op jit(solution)/shard_map/all_gather | solution.py:821
  8.0 73.9 %collective-permute-start.12 = (bf16[512,256]{1,0:T(8,128)(2,1)}, bf16[512,256]{1,0:T(8,128)(2,1)}, u32[]{:S(2)}, u32[]{:S(2)}) collective-permute-start(bf16[512,256]{1,0:T(8,128)(2,1)} %refs_0_.1), channel_id=1, source_target_pairs={{0,4},{4,0},{8,12},{12,8},{16,20},{20,16},{24,28},{28,24},{1,5},{5... | collective-permute-start | bytes 786440 | tf_op jit(solution)/shard_map/ppermute | solution.py:450
  11.0 68.6 %collective-permute-start.13 = (bf16[512,256]{1,0:T(8,128)(2,1)}, bf16[512,256]{1,0:T(8,128)(2,1)}, u32[]{:S(2)}, u32[]{:S(2)}) collective-permute-start(bf16[512,256]{1,0:T(8,128)(2,1)} %refs_0_.1), channel_id=1, source_target_pairs={{0,8},{4,12},{8,16},{12,20},{16,24},{20,28},{24,0},{28,4},{1,9},{5... | collective-permute-start | bytes 786440 | tf_op jit(solution)/shard_map/ppermute | solution.py:467
  14.5 144.8 %collective-permute-start.1 = (bf16[256,2048]{1,0:T(8,128)(2,1)S(1)}, bf16[256,2048]{1,0:T(8,128)(2,1)}, u32[]{:S(2)}, u32[]{:S(2)}) collective-permute-start(bf16[256,2048]{1,0:T(8,128)(2,1)S(1)} %fusion.26.refs_0_), channel_id=1, source_target_pairs={{0,2},{1,3},{2,0},{3,1},{4,6},{5,7},{6,4},{7,5},{8,10},{9,11},{10,... | collective-permute-start | bytes 3145736 | tf_op jit(solution)/shard_map/ppermute | solution.py:450
  79.6 80.5 %collective-permute-start = (bf16[256,2048]{1,0:T(8,128)(2,1)S(1)}, bf16[256,2048]{1,0:T(8,128)(2,1)S(1)}, u32[]{:S(2)}, u32[]{:S(2)}) collective-permute-start(bf16[256,2048]{1,0:T(8,128)(2,1)S(1)} %fusion.26.refs_0_), channel_id=1, source_target_pairs={{0,1},{1,0},{2,3},{3,2},{4,5},{5,4},{6,7},{7,6},{8,9},{9,8},{10,11... | collective-permute-start | bytes 3145736 | tf_op jit(solution)/shard_map/ppermute | solution.py:450
  107.6 63.6 %collective-permute-start.8 = (bf16[256,1536]{1,0:T(8,128)(2,1)}, bf16[256,1536]{1,0:T(8,128)(2,1)}, u32[]{:S(2)}, u32[]{:S(2)}) collective-permute-start(bf16[256,1536]{1,0:T(8,128)(2,1)} %collective-permute-done.6.refs_4_), channel_id=1, source_target_pairs={{0,8},{4,12},{8,16},{12,20},{16,24},{20,28},{24,0},{28,4},{1,9},{5... | collective-permute-start | bytes 2359304 | tf_op jit(solution)/shard_map/ppermute | solution.py:467
  159.3 87.3 %collective-permute-start.2 = (bf16[256,2048]{1,0:T(8,128)(2,1)}, bf16[256,2048]{1,0:T(8,128)(2,1)}, u32[]{:S(2)}, u32[]{:S(2)}) collective-permute-start(bf16[256,2048]{1,0:T(8,128)(2,1)} %collective-permute-done.1.refs_2_), channel_id=1, source_target_pairs={{0,1},{1,0},{2,3},{3,2},{4,5},{5,4},{6,7},{7,6},{8,9},{9,8},{10,11... | collective-permute-start | bytes 3145736 | tf_op jit(solution)/shard_map/ppermute | solution.py:450
  159.4 216.1 %collective-permute-start.3 = (bf16[256,1536]{1,0:T(8,128)(2,1)}, bf16[256,1536]{1,0:T(8,128)(2,1)}, u32[]{:S(2)}, u32[]{:S(2)}) collective-permute-start(bf16[256,1536]{1,0:T(8,128)(2,1)} %constant_dynamic-update-slice_fusion.refs_0_), channel_id=1, source_target_pairs={{0,4},{4,0},{8,12},{12,8},{16,20},{20,16},{24,28},{28,24},{1,5},{5... | collective-permute-start | bytes 2359304 | tf_op jit(solution)/shard_map/ppermute | solution.py:450
  160.0 215.5 %collective-permute-start.5 = (bf16[256,1536]{1,0:T(8,128)(2,1)}, bf16[256,1536]{1,0:T(8,128)(2,1)}, u32[]{:S(2)}, u32[]{:S(2)}) collective-permute-start(bf16[256,1536]{1,0:T(8,128)(2,1)} %collective-permute-done.4.refs_2_), channel_id=1, source_target_pairs={{0,4},{4,0},{8,12},{12,8},{16,20},{20,16},{24,28},{28,24},{1,5},{5... | collective-permute-start | bytes 2359304 | tf_op jit(solution)/shard_map/ppermute | solution.py:450
  168.8 206.7 %collective-permute-start.7 = (bf16[256,1536]{1,0:T(8,128)(2,1)}, bf16[256,1536]{1,0:T(8,128)(2,1)}, u32[]{:S(2)}, u32[]{:S(2)}) collective-permute-start(bf16[256,1536]{1,0:T(8,128)(2,1)} %collective-permute-done.6.refs_4_), channel_id=1, source_target_pairs={{0,4},{4,0},{8,12},{12,8},{16,20},{20,16},{24,28},{28,24},{1,5},{5... | collective-permute-start | bytes 2359304 | tf_op jit(solution)/shard_map/ppermute | solution.py:450
  171.2 204.4 %collective-permute-start.9 = (bf16[256,1536]{1,0:T(8,128)(2,1)}, bf16[256,1536]{1,0:T(8,128)(2,1)}, u32[]{:S(2)}, u32[]{:S(2)}) collective-permute-start(bf16[256,1536]{1,0:T(8,128)(2,1)} %collective-permute-done.8.refs_6_), channel_id=1, source_target_pairs={{0,4},{4,0},{8,12},{12,8},{16,20},{20,16},{24,28},{28,24},{1,5},{5... | collective-permute-start | bytes 2359304 | tf_op jit(solution)/shard_map/ppermute | solution.py:450
  701.2 97.6 %collective-permute-start.29 = (bf16[8,128,2048]{2,1,0:T(8,128)(2,1)}, bf16[8,128,2048]{2,1,0:T(8,128)(2,1)}, u32[]{:S(2)}, u32[]{:S(2)}) collective-permute-start(bf16[8,128,2048]{2,1,0:T(8,128)(2,1)} %constant_dynamic-update-slice_fusion.3.own), channel_id=1, source_target_pairs={{0,1},{1,0},{2,3},{3,2},{4,5},{5,4},{6,7},{7,6},{8,9},{9,8},{10,11... | collective-permute-start | bytes 12582920 | tf_op jit(solution)/shard_map/ppermute | solution.py:450
  736.9 125.4 %collective-permute-start.36 = (bf16[8,128,2048]{2,1,0:T(8,128)(2,1)}, bf16[8,128,2048]{2,1,0:T(8,128)(2,1)}, u32[]{:S(2)}, u32[]{:S(2)}) collective-permute-start(bf16[8,128,2048]{2,1,0:T(8,128)(2,1)} %constant_dynamic-update-slice_fusion.9.own), channel_id=1, source_target_pairs={{0,1},{1,0},{2,3},{3,2},{4,5},{5,4},{6,7},{7,6},{8,9},{9,8},{10,11... | collective-permute-start | bytes 12582920 | tf_op jit(solution)/shard_map/ppermute | solution.py:450
  763.4 141.2 %collective-permute-start.57 = (bf16[128,2048]{1,0:T(8,128)(2,1)S(1)}, bf16[128,2048]{1,0:T(8,128)(2,1)S(1)}, u32[]{:S(2)}, u32[]{:S(2)}) collective-permute-start(bf16[128,2048]{1,0:T(8,128)(2,1)S(1)} %get-tuple-element.407), channel_id=1, source_target_pairs={{0,2},{1,3},{2,0},{3,1},{4,6},{5,7},{6,4},{7,5},{8,10},{9,11},{10,... | collective-permute-start | bytes 1572872 | tf_op jit(solution)/shard_map/ppermute | solution.py:450
  768.8 202.7 %collective-permute-start.47 = (bf16[8,128,2048]{2,1,0:T(8,128)(2,1)}, bf16[8,128,2048]{2,1,0:T(8,128)(2,1)}, u32[]{:S(2)}, u32[]{:S(2)}) collective-permute-start(bf16[8,128,2048]{2,1,0:T(8,128)(2,1)} %constant_dynamic-update-slice_fusion.15.own), channel_id=1, source_target_pairs={{0,1},{1,0},{2,3},{3,2},{4,5},{5,4},{6,7},{7,6},{8,9},{9,8},{10,11... | collective-permute-start | bytes 12582920 | tf_op jit(solution)/shard_map/ppermute | solution.py:450
  776.4 131.4 %collective-permute-start.58 = (bf16[2,128,2048]{2,1,0:T(8,128)(2,1)}, bf16[2,128,2048]{2,1,0:T(8,128)(2,1)}, u32[]{:S(2)}, u32[]{:S(2)}) collective-permute-start(bf16[2,128,2048]{2,1,0:T(8,128)(2,1)} %pad_maximum_fusion.14), channel_id=1, source_target_pairs={{0,2},{1,3},{2,0},{3,1},{4,6},{5,7},{6,4},{7,5},{8,10},{9,11},{10,... | collective-permute-start | bytes 3145736 | tf_op jit(solution)/shard_map/ppermute | solution.py:450
  840.3 112.8 %collective-permute-start.30 = (bf16[2,2,256,2048]{3,2,1,0:T(8,128)(2,1)}, bf16[2,2,256,2048]{3,2,1,0:T(8,128)(2,1)}, u32[]{:S(2)}, u32[]{:S(2)}) collective-permute-start(bf16[2,2,256,2048]{3,2,1,0:T(8,128)(2,1)} %get-tuple-element.167), channel_id=1, source_target_pairs={{0,1},{1,0},{2,3},{3,2},{4,5},{5,4},{6,7},{7,6},{8,9},{9,8},{10,11... | collective-permute-start | bytes 12582920 | tf_op jit(solution)/shard_map/ppermute | solution.py:450
  931.0 145.4 %collective-permute-start.60 = (bf16[8,128,2048]{2,1,0:T(8,128)(2,1)}, bf16[8,128,2048]{2,1,0:T(8,128)(2,1)}, u32[]{:S(2)}, u32[]{:S(2)}) collective-permute-start(bf16[8,128,2048]{2,1,0:T(8,128)(2,1)} %constant_dynamic-update-slice_fusion.21.own), channel_id=1, source_target_pairs={{0,1},{1,0},{2,3},{3,2},{4,5},{5,4},{6,7},{7,6},{8,9},{9,8},{10,11... | collective-permute-start | bytes 12582920 | tf_op jit(solution)/shard_map/ppermute | solution.py:450
  969.5 66.1 %collective-permute-start.38 = (bf16[2,128,2048]{2,1,0:T(8,128)(2,1)}, bf16[2,128,2048]{2,1,0:T(8,128)(2,1)}, u32[]{:S(2)}, u32[]{:S(2)}) collective-permute-start(bf16[2,128,2048]{2,1,0:T(8,128)(2,1)} %fusion.69), channel_id=1, source_target_pairs={{0,2},{1,3},{2,0},{3,1},{4,6},{5,7},{6,4},{7,5},{8,10},{9,11},{10,... | collective-permute-start | bytes 3145736 | tf_op jit(solution)/shard_map/ppermute | solution.py:450
  971.0 67.8 %collective-permute-start.39 = (bf16[2,128,2048]{2,1,0:T(8,128)(2,1)}, bf16[2,128,2048]{2,1,0:T(8,128)(2,1)}, u32[]{:S(2)}, u32[]{:S(2)}) collective-permute-start(bf16[2,128,2048]{2,1,0:T(8,128)(2,1)} %get-tuple-element.174), channel_id=1, source_target_pairs={{0,4},{4,0},{8,12},{12,8},{16,20},{20,16},{24,28},{28,24},{1,5},{5... | collective-permute-start | bytes 3145736 | tf_op jit(solution)/shard_map/ppermute | solution.py:450
  1250.4 75.4 %collective-permute-start.75 = (bf16[2,2,256,2048]{3,2,1,0:T(8,128)(2,1)}, bf16[2,2,256,2048]{3,2,1,0:T(8,128)(2,1)}, u32[]{:S(2)}, u32[]{:S(2)}) collective-permute-start(bf16[2,2,256,2048]{3,2,1,0:T(8,128)(2,1)} %get-tuple-element.225), channel_id=1, source_target_pairs={{0,1},{1,0},{2,3},{3,2},{4,5},{5,4},{6,7},{7,6},{8,9},{9,8},{10,11... | collective-permute-start | bytes 12582920 | tf_op jit(solution)/shard_map/ppermute | solution.py:450
  1272.6 78.8 %collective-permute-start.76 = (bf16[2,2,256,2048]{3,2,1,0:T(8,128)(2,1)}, bf16[2,2,256,2048]{3,2,1,0:T(8,128)(2,1)}, u32[]{:S(2)}, u32[]{:S(2)}) collective-permute-start(bf16[2,2,256,2048]{3,2,1,0:T(8,128)(2,1)} %get-tuple-element.229), channel_id=1, source_target_pairs={{0,1},{1,0},{2,3},{3,2},{4,5},{5,4},{6,7},{7,6},{8,9},{9,8},{10,11... | collective-permute-start | bytes 12582920 | tf_op jit(solution)/shard_map/ppermute | solution.py:450
  1298.4 190.8 %collective-permute-start.77 = (bf16[2,2,256,2048]{3,2,1,0:T(8,128)(2,1)}, bf16[2,2,256,2048]{3,2,1,0:T(8,128)(2,1)}, u32[]{:S(2)}, u32[]{:S(2)}) collective-permute-start(bf16[2,2,256,2048]{3,2,1,0:T(8,128)(2,1)} %get-tuple-element.233), channel_id=1, source_target_pairs={{0,1},{1,0},{2,3},{3,2},{4,5},{5,4},{6,7},{7,6},{8,9},{9,8},{10,11... | collective-permute-start | bytes 12582920 | tf_op jit(solution)/shard_map/ppermute | solution.py:450
  1320.8 174.3 %collective-permute-start.74 = (bf16[2,2,256,2048]{3,2,1,0:T(8,128)(2,1)}, bf16[2,2,256,2048]{3,2,1,0:T(8,128)(2,1)}, u32[]{:S(2)}, u32[]{:S(2)}) collective-permute-start(bf16[2,2,256,2048]{3,2,1,0:T(8,128)(2,1)} %get-tuple-element.221), channel_id=1, source_target_pairs={{0,1},{1,0},{2,3},{3,2},{4,5},{5,4},{6,7},{7,6},{8,9},{9,8},{10,11... | collective-permute-start | bytes 12582920 | tf_op jit(solution)/shard_map/ppermute | solution.py:450
  1505.5 66.9 %collective-permute-start.82 = (bf16[2,128,2048]{2,1,0:T(8,128)(2,1)S(1)}, bf16[2,128,2048]{2,1,0:T(8,128)(2,1)S(1)}, u32[]{:S(2)}, u32[]{:S(2)}) collective-permute-start(bf16[2,128,2048]{2,1,0:T(8,128)(2,1)S(1)} %copy-done.70), channel_id=1, source_target_pairs={{0,2},{1,3},{2,0},{3,1},{4,6},{5,7},{6,4},{7,5},{8,10},{9,11},{10,... | collective-permute-start | bytes 3145736 | tf_op jit(solution)/shard_map/ppermute | solution.py:450
  1529.3 64.8 %collective-permute-start.84 = (bf16[2,128,2048]{2,1,0:T(8,128)(2,1)S(1)}, bf16[2,128,2048]{2,1,0:T(8,128)(2,1)S(1)}, u32[]{:S(2)}, u32[]{:S(2)}) collective-permute-start(bf16[2,128,2048]{2,1,0:T(8,128)(2,1)S(1)} %get-tuple-element.248), channel_id=1, source_target_pairs={{0,2},{1,3},{2,0},{3,1},{4,6},{5,7},{6,4},{7,5},{8,10},{9,11},{10,... | collective-permute-start | bytes 3145736 | tf_op jit(solution)/shard_map/ppermute | solution.py:450
  1599.3 137.7 %collective-permute-start.119 = (bf16[512,256]{1,0:T(8,128)(2,1)}, bf16[512,256]{1,0:T(8,128)(2,1)S(1)}, u32[]{:S(2)}, u32[]{:S(2)}) collective-permute-start(bf16[512,256]{1,0:T(8,128)(2,1)} %bitcast.424), channel_id=1, source_target_pairs={{0,4},{4,0},{8,12},{12,8},{16,20},{20,16},{24,28},{28,24},{1,5},{5... | collective-permute-start | bytes 786440 | tf_op jit(solution)/shard_map/ppermute | solution.py:450
  1602.1 136.3 %collective-permute-start.118 = (bf16[512,256]{1,0:T(8,128)(2,1)}, bf16[512,256]{1,0:T(8,128)(2,1)}, u32[]{:S(2)}, u32[]{:S(2)}) collective-permute-start(bf16[512,256]{1,0:T(8,128)(2,1)} %fusion.104), channel_id=1, source_target_pairs={{0,8},{4,12},{8,16},{12,20},{16,24},{20,28},{24,0},{28,4},{1,9},{5... | collective-permute-start | bytes 786440 | tf_op jit(solution)/shard_map/ppermute | solution.py:467
  1744.2 62.7 %collective-permute-start.97 = (bf16[256,2048]{1,0:T(8,128)(2,1)}, bf16[256,2048]{1,0:T(8,128)(2,1)}, u32[]{:S(2)}, u32[]{:S(2)}) collective-permute-start(bf16[256,2048]{1,0:T(8,128)(2,1)} %get-tuple-element.352), channel_id=1, source_target_pairs={{0,1},{1,0},{2,3},{3,2},{4,5},{5,4},{6,7},{7,6},{8,9},{9,8},{10,11... | collective-permute-start | bytes 3145736 | tf_op jit(solution)/shard_map/ppermute | solution.py:450
  1807.0 88.1 %collective-permute-start.114 = (bf16[256,1536]{1,0:T(8,128)(2,1)S(1)}, bf16[256,1536]{1,0:T(8,128)(2,1)S(1)}, u32[]{:S(2)}, u32[]{:S(2)}) collective-permute-start(bf16[256,1536]{1,0:T(8,128)(2,1)S(1)} %copy-done.81), channel_id=1, source_target_pairs={{0,4},{4,0},{8,12},{12,8},{16,20},{20,16},{24,28},{28,24},{1,5},{5... | collective-permute-start | bytes 2359304 | tf_op jit(solution)/shard_map/ppermute | solution.py:450
  1807.6 87.4 %collective-permute-start.113 = (bf16[256,1536]{1,0:T(8,128)(2,1)S(1)}, bf16[256,1536]{1,0:T(8,128)(2,1)S(1)}, u32[]{:S(2)}, u32[]{:S(2)}) collective-permute-start(bf16[256,1536]{1,0:T(8,128)(2,1)S(1)} %add_convert_fusion.55), channel_id=1, source_target_pairs={{0,8},{4,12},{8,16},{12,20},{16,24},{20,28},{24,0},{28,4},{1,9},{5... | collective-permute-start | bytes 2359304 | tf_op jit(solution)/shard_map/ppermute | solution.py:467
  1829.2 67.3 %collective-permute-start.96 = (bf16[256,2048]{1,0:T(8,128)(2,1)S(1)}, bf16[256,2048]{1,0:T(8,128)(2,1)S(1)}, u32[]{:S(2)}, u32[]{:S(2)}) collective-permute-start(bf16[256,2048]{1,0:T(8,128)(2,1)S(1)} %add_convert_fusion.2), channel_id=1, source_target_pairs={{0,8},{4,12},{8,16},{12,20},{16,24},{20,28},{24,0},{28,4},{1,9},{5... | collective-permute-start | bytes 3145736 | tf_op jit(solution)/shard_map/ppermute | solution.py:467
  (228 other events, 6785.1 us)
Sparse Core Ops, SparseCore 0:
  10.9 312.4 all-gather.1

commit v4 on v3

--- a/solution.py
+++ b/solution.py
@@ -467,13 +467,15 @@
     return lax.ppermute(values, "dp", [(i, (i + 2) % count) for i in range(count)])
 
 
-def spread_plane(values):
+def spread_plane(values, beside):
     half_rows = values.shape[0] // 2
     upper, lower = values[:half_rows], values[half_rows:]
     near_upper = jnp.stack([upper, far_pack(upper)])
     near_lower = jnp.stack([lower, far_side(lower)])
-    own = jnp.concatenate([near_upper, near_lower, far_side(near_upper), far_pack(near_lower)])
-    return own, far_core(own)
+    near, made = beside((near_upper, near_lower))
+    own = jnp.concatenate([*near, far_side(near[0]), far_pack(near[1])])
+    own, made = lax.optimization_barrier((own, made))
+    return own, far_core(own), made
 
 
 def plane_order():
@@ -493,7 +495,7 @@
     *pieces, whole, sems = refs
     copies = []
     for index, piece in enumerate(pieces):
-        target = whole.at[order[index]]
+        target = None if by_column else whole.at[order[index]]
         if by_column:
             width = piece.shape[1]
             target = whole.at[:, pl.ds(pl.multiple_of(order[index] * width, 128), width)]
@@ -512,7 +514,7 @@
         functools.partial(place_kernel, by_column),
         1,
         [anywhere] * count,
-        anywhere,
+        pl.BlockSpec(memory_space=pltpu.VMEM),
         shape_of(shape, pieces[0].dtype),
         [pltpu.SemaphoreType.DMA((count,))],
         1000,
@@ -706,11 +708,11 @@
 
 class Folding:
     def __init__(self, order):
-        self.order, self.waiting = order, {}
+        self.order, self.waiting, self.fresh = order, {}, {}
         self.summed, self.count, self.total = None, 0, None
 
     def begin(self, plane, own, other):
-        self.waiting[plane] = (0, (own, far_core(other)))
+        self.fresh[plane] = (0, (own, far_core(other)))
 
     def step(self, small):
         made = {}
@@ -731,6 +733,8 @@
             if last:
                 self.total = passed
         small, (made, passed) = tied(small, (made, passed))
+        self.waiting.update(self.fresh)
+        self.fresh = {}
         for plane, values in made.items():
             self.waiting[plane] = (self.waiting[plane][0] + 1, values)
         if passed is not None:
@@ -756,18 +760,21 @@
     pieces, travelling = [], second_in
     for plane in range(planes):
         travelling = next_plane(travelling) if plane else travelling
-        pieces.append(spread_plane(travelling))
+
+        def beside(near, listed=pack_order[plane * 2 : plane * 2 + 2]):
+            listed, near = tied(listed, near)
+            return near, cot_slots(listed, places, gates, all_cot, w_down, capacity)
+
+        pieces.append(spread_plane(travelling, beside))
     pairs = [slice(plane * 2, plane * 2 + 2) for plane in range(planes)]
     order = [*range(1, planes), 0]
     kept, folding, mixing = {}, Folding(order), Folding(order)
     for plane in range(planes):
         pair = pairs[plane]
-        grad_slots, grad_hidden = cot_slots(
-            pack_order[pair], places, gates, all_cot, w_down, capacity
-        )
+        own, other, (grad_slots, grad_hidden) = pieces[plane]
         near = folding.step(near_places[pair]) if plane > 1 else near_places[pair]
         slots, hidden, grad_gated, grad_lifted, *part = row_slots(
-            near, places_t[pair], *pieces[plane], w_gate, w_up, grad_hidden, capacity
+            near, places_t[pair], own, other, w_gate, w_up, grad_hidden, capacity
         )
         folding.begin(plane, *part)
         kept[plane] = (slots, grad_slots, hidden, grad_gated, grad_lifted)
@@ -899,13 +906,14 @@
         .astype(jnp.bfloat16)
         .reshape(seq_len, head_count, head_size)
     )
-    grad_mixture = mix_step(grad_mixture)
     grad_query_parts = []
     grad_key_sum = jnp.zeros((seq_len, head_count, head_size), jnp.float32)
     grad_value_sum = jnp.zeros((seq_len, head_count, head_size), jnp.float32)
     for block_index in range(block_total):
         offset = block_index * block_rows
-        query_block = mix_step(query_low[offset : offset + block_rows])
+        query_block = query_low[offset : offset + block_rows]
+        if block_index:
+            query_block = mix_step(query_block)
         grad_block = grad_mixture[offset : offset + block_rows]
         scores = block_scores(query_block, key_low, masks[block_index], inv_root)
         prob_rows = jnp.exp(scores - lse_parts[block_index])

time: 1940 us -> 1420 us (0.73)
  Pallas kernels: 907 us -> 412 us
  other arithmetic: 154 us -> 190 us
  waiting for transfers between devices: 537 us -> 503 us
  local copies, waits for them, and re-layouts: 115 us -> 88 us
    pallas_call x4, Pallas kernels: 516 us -> 20.4 us  [laid(): call(functools.partial(place_kernel, by_column), 1, [anywhere] * count, p...]
  transfers between devices with their start and end apart: 125 -> 125, of which waited for: 54 -> 48; matrix products, arithmetic and copies ran while one was open for 17% -> 23% of each run, Pallas kernels for 47% -> 29%
where the time goes in v4:
time: 1420 us; the launch traced here: 1410 us
  waiting for transfers between devices  503 us (35%)
  Pallas kernels  412 us (29%)
  other arithmetic  190 us (13%)
  starting transfers between devices  121 us (9%)
  local copies, waits for them, and re-layouts  88 us (6%)
  matrix products  77.9 us (5%)
  between operations  17 us (1%)
    ppermute x103, waiting for transfers between devices, swapped(): return lax.ppermute(values, axis, [(i, i ^ bit) for i in range(count)])  374 us
    pallas_call x4, Pallas kernels, row_slots(): call(functools.partial(row_kernel, packs, experts, capacity), 2 * packs +...  166 us
    ppermute x21, waiting for transfers between devices, next_plane(): lax.ppermute(values, 'dp', [(i, (i + 2) % count) for i in range(count)])  129 us
    convert_element_type x67, other arithmetic, added(): return (left.astype(jnp.float32) + right.astype(jnp.float32)).astype(kind)  110 us
    ppermute x103, starting transfers between devices, swapped(): return lax.ppermute(values, axis, [(i, i ^ bit) for i in range(count)])  92.3 us
    pallas_call x4, Pallas kernels, mix_rows(): call(functools.partial(mix_kernel, packs, experts, capacity), packs + exp...  89.4 us
    pallas_call x4, Pallas kernels, cot_slots(): call(functools.partial(cot_kernel, packs, experts, capacity), packs + exp...  88.6 us
    pallas_call x1, Pallas kernels, weight_grads(): call(functools.partial(weight_kernel, planes), experts, [block(operand.sh...  47.7 us
  transfers between devices with their start and end apart: 125, of which 48 were waited for; matrix products, arithmetic and copies ran while one was open for 23% of the time, Pallas kernels for 29%

profile of v4, /device:TPU:0, one launch (start us, length us, event | category | flops | bytes accessed | tf_op | source)
XLA Modules:
  0.0 1409.1 jit_solution(6059360892202466087)
XLA Ops:
  23.1 28.6 %collective-permute-done.4.refs_2_ = bf16[256,1536]{1,0:T(8,128)(2,1)} collective-permute-done((bf16[256,1536]{1,0:T(8,128)(2,1)}, bf16[256,1536]{1,0:T(8,128)(2,1)}, u32[]{:S(2)}, u32[]{:S(2)}) %collective-permute-start.4) | collective-permute-done | bytes 786464 | tf_op jit(solution)/shard_map/ppermute | solution.py:467
  84.1 23.1 %collective-permute-done.24 = bf16[16,17,256]{2,0,1:T(8,128)(2,1)S(1)} collective-permute-done((bf16[16,17,256]{2,0,1:T(8,128)(2,1)}, bf16[16,17,256]{2,0,1:T(8,128)(2,1)S(1)}, u32[]{:S(2)}, u32[]{:S(2)}) %collective-permute-start.24) | collective-permute-done | bytes 139296 | tf_op jit(solution)/shard_map/ppermute | solution.py:450
  116.9 13.2 collective-permute-done.17.refs_6_
  140.3 17.5 %collective-permute-done.8.refs_6_ = bf16[256,1536]{1,0:T(8,128)(2,1)} collective-permute-done((bf16[256,1536]{1,0:T(8,128)(2,1)}, bf16[256,1536]{1,0:T(8,128)(2,1)}, u32[]{:S(2)}, u32[]{:S(2)}) %collective-permute-start.8) | collective-permute-done | bytes 786464 | tf_op jit(solution)/shard_map/ppermute | solution.py:467
  180.6 33.7 %collective-permute-done.7.refs_5_ = bf16[256,1536]{1,0:T(8,128)(2,1)} collective-permute-done((bf16[256,1536]{1,0:T(8,128)(2,1)}, bf16[256,1536]{1,0:T(8,128)(2,1)}, u32[]{:S(2)}, u32[]{:S(2)}) %collective-permute-start.7) | collective-permute-done | bytes 786464 | tf_op jit(solution)/shard_map/ppermute | solution.py:450
  214.3 31.7 %collective-permute-done.9.refs_7_ = bf16[256,1536]{1,0:T(8,128)(2,1)} collective-permute-done((bf16[256,1536]{1,0:T(8,128)(2,1)}, bf16[256,1536]{1,0:T(8,128)(2,1)}, u32[]{:S(2)}, u32[]{:S(2)}) %collective-permute-start.9) | collective-permute-done | bytes 786464 | tf_op jit(solution)/shard_map/ppermute | solution.py:450
  320.7 16.9 %collective-permute-done.21 = bf16[256,2048]{1,0:T(8,128)(2,1)} collective-permute-done((bf16[256,2048]{1,0:T(8,128)(2,1)}, bf16[256,2048]{1,0:T(8,128)(2,1)}, u32[]{:S(2)}, u32[]{:S(2)}) %collective-permute-start.21) | collective-permute-done | bytes 1048608 | tf_op jit(solution)/shard_map/ppermute | solution.py:450
  359.7 13.1 collective-permute-done.31
  412.7 12.1 collective-permute-done.55
  426.7 21.9 %shard_map.258 = (bf16[8,256,2048]{2,1,0:T(8,128)(2,1)}, f32[8,256,256]{2,1,0:T(8,128)}) custom-call(s32[2]{0:T(128)} %pad_add_fusion.table, s32[8,8,1024]{2,1,0:T(8,128)} %get-tuple-element.501.places, f32[8,8,1024]{2,1,0:T(8,128)} %copy-done.15, bf16[8,1024,2048]{2,1,0:T(8,128)(2,1)} %bitcast.412, bf16[8,256,2048]{2,1,0:T(8,128)(2,1)} %down.15), custom_call_target="tpu_custom_call" | custom-call | flops 10737418240 | bytes 21474836 | tf_op jit(solution)/shard_map/pallas_call | solution.py:354
  471.1 22.0 %shard_map.260 = (bf16[8,256,2048]{2,1,0:T(8,128)(2,1)}, f32[8,256,256]{2,1,0:T(8,128)}) custom-call(s32[2]{0:T(128)} %pad_add_fusion.1.table, s32[8,8,1024]{2,1,0:T(8,128)} %get-tuple-element.501.places, f32[8,8,1024]{2,1,0:T(8,128)} %copy-done.15, bf16[8,1024,2048]{2,1,0:T(8,128)(2,1)} %bitcast.413, bf16[8,256,2048]{2,1,0:T(8,128)(2,1)} %down.15), custom_call_target="tpu_custom_call" | custom-call | flops 10737418240 | bytes 21474836 | tf_op jit(solution)/shard_map/pallas_call | solution.py:354
  515.5 22.3 %shard_map.262 = (bf16[8,256,2048]{2,1,0:T(8,128)(2,1)}, f32[8,256,256]{2,1,0:T(8,128)}) custom-call(s32[2]{0:T(128)} %pad_add_fusion.2.table, s32[8,8,1024]{2,1,0:T(8,128)} %get-tuple-element.501.places, f32[8,8,1024]{2,1,0:T(8,128)} %copy-done.15, bf16[8,1024,2048]{2,1,0:T(8,128)(2,1)} %bitcast.414, bf16[8,256,2048]{2,1,0:T(8,128)(2,1)} %down.15), custom_call_target="tpu_custom_call" | custom-call | flops 10737418240 | bytes 21474836 | tf_op jit(solution)/shard_map/pallas_call | solution.py:354
  537.8 41.3 %shard_map.259 = (bf16[8,256,2048]{2,1,0:T(8,128)(2,1)}, bf16[8,256,256]{2,1,0:T(8,128)(2,1)}, bf16[8,256,256]{2,1,0:T(8,128)(2,1)}, bf16[8,256,256]{2,1,0:T(8,1...) custom-call(s32[2,8,1024]{2,1,0:T(8,128)} %bitcast.480, ...), custom_call_target="tpu_custom_call" | custom-call | flops 25769803776 | bytes 51539608 | tf_op jit(solution)/shard_map/pallas_call | solution.py:383
  579.7 41.6 %shard_map.261 = (bf16[8,256,2048]{2,1,0:T(8,128)(2,1)}, bf16[8,256,256]{2,1,0:T(8,128)(2,1)}, bf16[8,256,256]{2,1,0:T(8,128)(2,1)}, bf16[8,256,256]{2,1,0:T(8,1...) custom-call(s32[2,8,1024]{2,1,0:T(8,128)} %bitcast.479, ...), custom_call_target="tpu_custom_call" | custom-call | flops 25769803776 | bytes 51539608 | tf_op jit(solution)/shard_map/pallas_call | solution.py:383
  621.4 22.3 %shard_map.264 = (bf16[8,256,2048]{2,1,0:T(8,128)(2,1)}, f32[8,256,256]{2,1,0:T(8,128)}) custom-call(s32[2]{0:T(128)} %pad_add_fusion.3.table, s32[8,8,1024]{2,1,0:T(8,128)} %get-tuple-element.501.places, f32[8,8,1024]{2,1,0:T(8,128)} %copy-done.15, bf16[8,1024,2048]{2,1,0:T(8,128)(2,1)} %bitcast.415, bf16[8,256,2048]{2,1,0:T(8,128)(2,1)} %down.15), custom_call_target="tpu_custom_call" | custom-call | flops 10737418240 | bytes 21474836 | tf_op jit(solution)/shard_map/pallas_call | solution.py:354
  644.2 41.4 %shard_map.263 = (bf16[8,256,2048]{2,1,0:T(8,128)(2,1)}, bf16[8,256,256]{2,1,0:T(8,128)(2,1)}, bf16[8,256,256]{2,1,0:T(8,128)(2,1)}, bf16[8,256,256]{2,1,0:T(8,1...) custom-call(s32[2,8,1024]{2,1,0:T(8,128)} %bitcast.478, ...), custom_call_target="tpu_custom_call" | custom-call | flops 25769803776 | bytes 51539608 | tf_op jit(solution)/shard_map/pallas_call | solution.py:383
  706.5 41.6 %shard_map.265 = (bf16[8,256,2048]{2,1,0:T(8,128)(2,1)}, bf16[8,256,256]{2,1,0:T(8,128)(2,1)}, bf16[8,256,256]{2,1,0:T(8,128)(2,1)}, bf16[8,256,256]{2,1,0:T(8,1...) custom-call(s32[2,8,1024]{2,1,0:T(8,128)} %bitcast.477, ...), custom_call_target="tpu_custom_call" | custom-call | flops 25769803776 | bytes 51539608 | tf_op jit(solution)/shard_map/pallas_call | solution.py:383
  771.3 22.5 %shard_map.268 = (bf16[2,2,256,2048]{3,2,1,0:T(8,128)(2,1)}, bf16[2,2,256,2048]{3,2,1,0:T(8,128)(2,1)}) custom-call(s32[2,1024,8]{2,1,0:T(8,128)} %get-tuple-element.265.places_t, f32[2,1024,8]{2,1,0:T(8,128)} %get-tuple-element.396.gates_t, bf16[8,256,256]{2,1,0:T(8,128)(2,1)} %get-tuple-element.343.hidden.refs_9_, bf16[8,256,2048]{2,1,0:T(8,128)(2,1)} %down.15), custom_call_target="tpu_custom_call" | custom-call | flops 10737418240 | bytes 21474836 | tf_op jit(solution)/shard_map/pallas_call | solution.py:409
  801.8 16.7 %collective-permute-done.53 = bf16[2,128,2048]{2,1,0:T(8,128)(2,1)S(1)} collective-permute-done((bf16[2,128,2048]{2,1,0:T(8,128)(2,1)}, bf16[2,128,2048]{2,1,0:T(8,128)(2,1)S(1)}, u32[]{:S(2)}, u32[]{:S(2)}) %collective-permute-start.53) | collective-permute-done | bytes 1048608 | tf_op jit(solution)/shard_map/ppermute | solution.py:450
  833.9 22.1 %shard_map.269 = (bf16[2,2,256,2048]{3,2,1,0:T(8,128)(2,1)}, bf16[2,2,256,2048]{3,2,1,0:T(8,128)(2,1)}) custom-call(s32[2,1024,8]{2,1,0:T(8,128)} %get-tuple-element.269.places_t, f32[2,1024,8]{2,1,0:T(8,128)} %get-tuple-element.395.gates_t, bf16[8,256,256]{2,1,0:T(8,128)(2,1)} %get-tuple-element.344.hidden.refs_10_, bf16[8,256,2048]{2,1,0:T(8,128)(2,1)} %down.15), custom_call_target="tpu_custom_call" | custom-call | flops 10737418240 | bytes 21474836 | tf_op jit(solution)/shard_map/pallas_call | solution.py:409
  872.9 22.3 %shard_map.270 = (bf16[2,2,256,2048]{3,2,1,0:T(8,128)(2,1)}, bf16[2,2,256,2048]{3,2,1,0:T(8,128)(2,1)}) custom-call(s32[2,1024,8]{2,1,0:T(8,128)} %get-tuple-element.273.places_t, f32[2,1024,8]{2,1,0:T(8,128)} %get-tuple-element.394.gates_t, bf16[8,256,256]{2,1,0:T(8,128)(2,1)} %get-tuple-element.345.hidden.refs_11_, bf16[8,256,2048]{2,1,0:T(8,128)(2,1)} %down.15), custom_call_target="tpu_custom_call" | custom-call | flops 10737418240 | bytes 21474836 | tf_op jit(solution)/shard_map/pallas_call | solution.py:409
  906.6 19.6 %collective-permute-done.69 = bf16[256,2048]{1,0:T(8,128)(2,1)S(1)} collective-permute-done((bf16[256,2048]{1,0:T(8,128)(2,1)S(1)}, bf16[256,2048]{1,0:T(8,128)(2,1)S(1)}, u32[]{:S(2)}, u32[]{:S(2)}) %collective-permute-start.69) | collective-permute-done | bytes 1048608 | tf_op jit(solution)/shard_map/ppermute | solution.py:467
  930.2 22.5 %shard_map.267 = (bf16[2,2,256,2048]{3,2,1,0:T(8,128)(2,1)}, bf16[2,2,256,2048]{3,2,1,0:T(8,128)(2,1)}) custom-call(s32[2,1024,8]{2,1,0:T(8,128)} %get-tuple-element.261.places_t, f32[2,1024,8]{2,1,0:T(8,128)} %get-tuple-element.397.gates_t, bf16[8,256,256]{2,1,0:T(8,128)(2,1)} %get-tuple-element.342.hidden.refs_8_, bf16[8,256,2048]{2,1,0:T(8,128)(2,1)} %down.15), custom_call_target="tpu_custom_call" | custom-call | flops 10737418240 | bytes 21474836 | tf_op jit(solution)/shard_map/pallas_call | solution.py:409
  968.3 16.0 %collective-permute-done.72.refs_2_ = bf16[256,2048]{1,0:T(8,128)(2,1)S(1)} collective-permute-done((bf16[256,2048]{1,0:T(8,128)(2,1)S(1)}, bf16[256,2048]{1,0:T(8,128)(2,1)S(1)}, u32[]{:S(2)}, u32[]{:S(2)}) %collective-permute-start.72) | collective-permute-done | bytes 1048608 | tf_op jit(solution)/shard_map/ppermute | solution.py:450
  1108.0 14.4 %collective-permute-done.83 = bf16[2,128,2048]{2,1,0:T(8,128)(2,1)S(1)} collective-permute-done((bf16[2,128,2048]{2,1,0:T(8,128)(2,1)S(1)}, bf16[2,128,2048]{2,1,0:T(8,128)(2,1)S(1)}, u32[]{:S(2)}, u32[]{:S(2)}) %collective-permute-start.83) | collective-permute-done | bytes 1048608 | tf_op jit(solution)/shard_map/ppermute | solution.py:450
  1129.2 15.3 %collective-permute-done.85 = bf16[2,128,2048]{2,1,0:T(8,128)(2,1)S(1)} collective-permute-done((bf16[2,128,2048]{2,1,0:T(8,128)(2,1)S(1)}, bf16[2,128,2048]{2,1,0:T(8,128)(2,1)S(1)}, u32[]{:S(2)}, u32[]{:S(2)}) %collective-permute-start.85) | collective-permute-done | bytes 1048608 | tf_op jit(solution)/shard_map/ppermute | solution.py:450
  1204.5 11.3 collective-permute-done.93
  1230.7 14.9 %collective-permute-done.110 = bf16[256,1536]{1,0:T(8,128)(2,1)S(1)} collective-permute-done((bf16[256,1536]{1,0:T(8,128)(2,1)S(1)}, bf16[256,1536]{1,0:T(8,128)(2,1)S(1)}, u32[]{:S(2)}, u32[]{:S(2)}) %collective-permute-start.110) | collective-permute-done | bytes 786464 | tf_op jit(solution)/shard_map/ppermute | solution.py:450
  1249.9 11.6 collective-permute-done.107
  1272.5 16.5 %collective-permute-done.94 = bf16[256,2048]{1,0:T(8,128)(2,1)S(1)} collective-permute-done((bf16[256,2048]{1,0:T(8,128)(2,1)S(1)}, bf16[256,2048]{1,0:T(8,128)(2,1)S(1)}, u32[]{:S(2)}, u32[]{:S(2)}) %collective-permute-start.94) | collective-permute-done | bytes 1048608 | tf_op jit(solution)/shard_map/ppermute | solution.py:467
  1293.0 47.7 %shard_map.271 = (f32[8,2048,256]{2,1,0:T(8,128)}, f32[8,2048,256]{2,1,0:T(8,128)}, f32[8,256,2048]{2,1,0:T(8,128)}) custom-call(bf16[8,256,2048]{2,1,0:T(8,128)(2,1)} %get-tuple-element.334.refs_0_, bf16[8,256,2048]{2,1,0:T(8,128)(2,1)} %get-tuple-element.335.refs_1_, bf16[8,256,2048]{2,1,0:T(8,128)(2,1)} %get-tuple-element.336.refs_2_, ...), custom_call_target="tpu_custom_call" | custom-call | flops 25769803776 | bytes 51539608 | tf_op jit(solution)/shard_map/pallas_call | solution.py:437
  1358.5 34.5 %collective-permute-done.104 = f32[2048]{0:T(1024)S(1)} collective-permute-done((f32[2048]{0:T(1024)S(1)}, f32[2048]{0:T(1024)S(1)}, u32[]{:S(2)}, u32[]{:S(2)}) %collective-permute-start.104) | collective-permute-done | bytes 8224 | tf_op jit(solution)/shard_map/ppermute | solution.py:450
  (805 shorter events, 640.2 us)
Async XLA Ops:
  7.2 419.4 %all-gather.2.cloned.1.call-start = ((), (), s32[]{:S(2)}) async-start(), calls=%async_computation | async-start | bytes 34603008 | tf_op jit(solution)/shard_map/all_gather | solution.py:828
  8.0 73.6 %collective-permute-start.12 = (bf16[512,256]{1,0:T(8,128)(2,1)}, bf16[512,256]{1,0:T(8,128)(2,1)S(1)}, u32[]{:S(2)}, u32[]{:S(2)}) collective-permute-start(bf16[512,256]{1,0:T(8,128)(2,1)} %refs_0_.1), channel_id=1, source_target_pairs={{0,4},{4,0},{8,12},{12,8},{16,20},{20,16},{24,28},{28,24},{1,5},{5... | collective-permute-start | bytes 786440 | tf_op jit(solution)/shard_map/ppermute | solution.py:450
  11.0 68.5 %collective-permute-start.13 = (bf16[512,256]{1,0:T(8,128)(2,1)}, bf16[512,256]{1,0:T(8,128)(2,1)S(1)}, u32[]{:S(2)}, u32[]{:S(2)}) collective-permute-start(bf16[512,256]{1,0:T(8,128)(2,1)} %refs_0_.1), channel_id=1, source_target_pairs={{0,8},{4,12},{8,16},{12,20},{16,24},{20,28},{24,0},{28,4},{1,9},{5... | collective-permute-start | bytes 786440 | tf_op jit(solution)/shard_map/ppermute | solution.py:467
  14.5 116.8 %collective-permute-start.1 = (bf16[256,2048]{1,0:T(8,128)(2,1)S(1)}, bf16[256,2048]{1,0:T(8,128)(2,1)}, u32[]{:S(2)}, u32[]{:S(2)}) collective-permute-start(bf16[256,2048]{1,0:T(8,128)(2,1)S(1)} %fusion.22.refs_0_), channel_id=1, source_target_pairs={{0,2},{1,3},{2,0},{3,1},{4,6},{5,7},{6,4},{7,5},{8,10},{9,11},{10,... | collective-permute-start | bytes 3145736 | tf_op jit(solution)/shard_map/ppermute | solution.py:450
  51.7 61.8 %collective-permute-start.6 = (bf16[256,1536]{1,0:T(8,128)(2,1)}, bf16[256,1536]{1,0:T(8,128)(2,1)}, u32[]{:S(2)}, u32[]{:S(2)}) collective-permute-start(bf16[256,1536]{1,0:T(8,128)(2,1)} %collective-permute-done.4.refs_2_), channel_id=1, source_target_pairs={{0,8},{4,12},{8,16},{12,20},{16,24},{20,28},{24,0},{28,4},{1,9},{5... | collective-permute-start | bytes 2359304 | tf_op jit(solution)/shard_map/ppermute | solution.py:467
  139.5 74.8 %collective-permute-start.7 = (bf16[256,1536]{1,0:T(8,128)(2,1)}, bf16[256,1536]{1,0:T(8,128)(2,1)}, u32[]{:S(2)}, u32[]{:S(2)}) collective-permute-start(bf16[256,1536]{1,0:T(8,128)(2,1)} %collective-permute-done.6.refs_4_), channel_id=1, source_target_pairs={{0,4},{4,0},{8,12},{12,8},{16,20},{20,16},{24,28},{28,24},{1,5},{5... | collective-permute-start | bytes 2359304 | tf_op jit(solution)/shard_map/ppermute | solution.py:450
  157.8 88.2 %collective-permute-start.9 = (bf16[256,1536]{1,0:T(8,128)(2,1)}, bf16[256,1536]{1,0:T(8,128)(2,1)}, u32[]{:S(2)}, u32[]{:S(2)}) collective-permute-start(bf16[256,1536]{1,0:T(8,128)(2,1)} %collective-permute-done.8.refs_6_), channel_id=1, source_target_pairs={{0,4},{4,0},{8,12},{12,8},{16,20},{20,16},{24,28},{28,24},{1,5},{5... | collective-permute-start | bytes 2359304 | tf_op jit(solution)/shard_map/ppermute | solution.py:450
  448.6 89.2 %collective-permute-start.29 = (bf16[8,128,2048]{2,1,0:T(8,128)(2,1)}, bf16[8,128,2048]{2,1,0:T(8,128)(2,1)}, u32[]{:S(2)}, u32[]{:S(2)}) collective-permute-start(bf16[8,128,2048]{2,1,0:T(8,128)(2,1)} %pad_maximum_fusion.1.own), channel_id=1, source_target_pairs={{0,1},{1,0},{2,3},{3,2},{4,5},{5,4},{6,7},{7,6},{8,9},{9,8},{10,11... | collective-permute-start | bytes 12582920 | tf_op jit(solution)/shard_map/ppermute | solution.py:450
  493.1 86.6 %collective-permute-start.36 = (bf16[8,128,2048]{2,1,0:T(8,128)(2,1)}, bf16[8,128,2048]{2,1,0:T(8,128)(2,1)}, u32[]{:S(2)}, u32[]{:S(2)}) collective-permute-start(bf16[8,128,2048]{2,1,0:T(8,128)(2,1)} %pad_maximum_fusion.2.own), channel_id=1, source_target_pairs={{0,1},{1,0},{2,3},{3,2},{4,5},{5,4},{6,7},{7,6},{8,9},{9,8},{10,11... | collective-permute-start | bytes 12582920 | tf_op jit(solution)/shard_map/ppermute | solution.py:450
  537.8 106.4 %collective-permute-start.47 = (bf16[8,128,2048]{2,1,0:T(8,128)(2,1)}, bf16[8,128,2048]{2,1,0:T(8,128)(2,1)}, u32[]{:S(2)}, u32[]{:S(2)}) collective-permute-start(bf16[8,128,2048]{2,1,0:T(8,128)(2,1)} %pad_maximum_fusion.3.own), channel_id=1, source_target_pairs={{0,1},{1,0},{2,3},{3,2},{4,5},{5,4},{6,7},{7,6},{8,9},{9,8},{10,11... | collective-permute-start | bytes 12582920 | tf_op jit(solution)/shard_map/ppermute | solution.py:450
  579.2 106.6 %collective-permute-start.30 = (bf16[2,2,256,2048]{3,2,1,0:T(8,128)(2,1)}, bf16[2,2,256,2048]{3,2,1,0:T(8,128)(2,1)}, u32[]{:S(2)}, u32[]{:S(2)}) collective-permute-start(bf16[2,2,256,2048]{3,2,1,0:T(8,128)(2,1)} %get-tuple-element.193), channel_id=1, source_target_pairs={{0,1},{1,0},{2,3},{3,2},{4,5},{5,4},{6,7},{7,6},{8,9},{9,8},{10,11... | collective-permute-start | bytes 12582920 | tf_op jit(solution)/shard_map/ppermute | solution.py:450
  621.3 69.5 %collective-permute-start.37 = (bf16[2,2,256,2048]{3,2,1,0:T(8,128)(2,1)}, bf16[2,2,256,2048]{3,2,1,0:T(8,128)(2,1)}, u32[]{:S(2)}, u32[]{:S(2)}) collective-permute-start(bf16[2,2,256,2048]{3,2,1,0:T(8,128)(2,1)} %get-tuple-element.202), channel_id=1, source_target_pairs={{0,1},{1,0},{2,3},{3,2},{4,5},{5,4},{6,7},{7,6},{8,9},{9,8},{10,11... | collective-permute-start | bytes 12582920 | tf_op jit(solution)/shard_map/ppermute | solution.py:450
  643.7 62.4 %collective-permute-start.60 = (bf16[8,128,2048]{2,1,0:T(8,128)(2,1)}, bf16[8,128,2048]{2,1,0:T(8,128)(2,1)}, u32[]{:S(2)}, u32[]{:S(2)}) collective-permute-start(bf16[8,128,2048]{2,1,0:T(8,128)(2,1)} %pad_maximum_fusion.4.own), channel_id=1, source_target_pairs={{0,1},{1,0},{2,3},{3,2},{4,5},{5,4},{6,7},{7,6},{8,9},{9,8},{10,11... | collective-permute-start | bytes 12582920 | tf_op jit(solution)/shard_map/ppermute | solution.py:450
  685.6 62.5 %collective-permute-start.48 = (bf16[2,2,256,2048]{3,2,1,0:T(8,128)(2,1)}, bf16[2,2,256,2048]{3,2,1,0:T(8,128)(2,1)}, u32[]{:S(2)}, u32[]{:S(2)}) collective-permute-start(bf16[2,2,256,2048]{3,2,1,0:T(8,128)(2,1)} %get-tuple-element.219), channel_id=1, source_target_pairs={{0,1},{1,0},{2,3},{3,2},{4,5},{5,4},{6,7},{7,6},{8,9},{9,8},{10,11... | collective-permute-start | bytes 12582920 | tf_op jit(solution)/shard_map/ppermute | solution.py:450
  702.5 54.6 %collective-permute-start.38 = (bf16[2,128,2048]{2,1,0:T(8,128)(2,1)}, bf16[2,128,2048]{2,1,0:T(8,128)(2,1)}, u32[]{:S(2)}, u32[]{:S(2)}) collective-permute-start(bf16[2,128,2048]{2,1,0:T(8,128)(2,1)} %fusion.65), channel_id=1, source_target_pairs={{0,2},{1,3},{2,0},{3,1},{4,6},{5,7},{6,4},{7,5},{8,10},{9,11},{10,... | collective-permute-start | bytes 3145736 | tf_op jit(solution)/shard_map/ppermute | solution.py:450
  703.7 55.9 %collective-permute-start.39 = (bf16[2,128,2048]{2,1,0:T(8,128)(2,1)}, bf16[2,128,2048]{2,1,0:T(8,128)(2,1)}, u32[]{:S(2)}, u32[]{:S(2)}) collective-permute-start(bf16[2,128,2048]{2,1,0:T(8,128)(2,1)} %get-tuple-element.206), channel_id=1, source_target_pairs={{0,4},{4,0},{8,12},{12,8},{16,20},{20,16},{24,28},{28,24},{1,5},{5... | collective-permute-start | bytes 3145736 | tf_op jit(solution)/shard_map/ppermute | solution.py:450
  705.3 56.8 %collective-permute-start.40 = (bf16[2,128,2048]{2,1,0:T(8,128)(2,1)}, bf16[2,128,2048]{2,1,0:T(8,128)(2,1)}, u32[]{:S(2)}, u32[]{:S(2)}) collective-permute-start(bf16[2,128,2048]{2,1,0:T(8,128)(2,1)} %fusion.69), channel_id=1, source_target_pairs={{0,2},{1,3},{2,0},{3,1},{4,6},{5,7},{6,4},{7,5},{8,10},{9,11},{10,... | collective-permute-start | bytes 3145736 | tf_op jit(solution)/shard_map/ppermute | solution.py:450
  706.1 58.6 %collective-permute-start.41 = (bf16[2,128,2048]{2,1,0:T(8,128)(2,1)}, bf16[2,128,2048]{2,1,0:T(8,128)(2,1)}, u32[]{:S(2)}, u32[]{:S(2)}) collective-permute-start(bf16[2,128,2048]{2,1,0:T(8,128)(2,1)} %get-tuple-element.210), channel_id=1, source_target_pairs={{0,4},{4,0},{8,12},{12,8},{16,20},{20,16},{24,28},{28,24},{1,5},{5... | collective-permute-start | bytes 3145736 | tf_op jit(solution)/shard_map/ppermute | solution.py:450
  748.2 73.8 %collective-permute-start.61 = (bf16[2,2,256,2048]{3,2,1,0:T(8,128)(2,1)}, bf16[2,2,256,2048]{3,2,1,0:T(8,128)(2,1)}, u32[]{:S(2)}, u32[]{:S(2)}) collective-permute-start(bf16[2,2,256,2048]{3,2,1,0:T(8,128)(2,1)} %get-tuple-element.241), channel_id=1, source_target_pairs={{0,1},{1,0},{2,3},{3,2},{4,5},{5,4},{6,7},{7,6},{8,9},{9,8},{10,11... | collective-permute-start | bytes 12582920 | tf_op jit(solution)/shard_map/ppermute | solution.py:450
  799.1 101.2 %collective-permute-start.75 = (bf16[2,2,256,2048]{3,2,1,0:T(8,128)(2,1)}, bf16[2,2,256,2048]{3,2,1,0:T(8,128)(2,1)}, u32[]{:S(2)}, u32[]{:S(2)}) collective-permute-start(bf16[2,2,256,2048]{3,2,1,0:T(8,128)(2,1)} %get-tuple-element.268), channel_id=1, source_target_pairs={{0,1},{1,0},{2,3},{3,2},{4,5},{5,4},{6,7},{7,6},{8,9},{9,8},{10,11... | collective-permute-start | bytes 12582920 | tf_op jit(solution)/shard_map/ppermute | solution.py:450
  856.0 103.3 %collective-permute-start.76 = (bf16[2,2,256,2048]{3,2,1,0:T(8,128)(2,1)}, bf16[2,2,256,2048]{3,2,1,0:T(8,128)(2,1)}, u32[]{:S(2)}, u32[]{:S(2)}) collective-permute-start(bf16[2,2,256,2048]{3,2,1,0:T(8,128)(2,1)} %get-tuple-element.272), channel_id=1, source_target_pairs={{0,1},{1,0},{2,3},{3,2},{4,5},{5,4},{6,7},{7,6},{8,9},{9,8},{10,11... | collective-permute-start | bytes 12582920 | tf_op jit(solution)/shard_map/ppermute | solution.py:450
  895.2 89.1 %collective-permute-start.77 = (bf16[2,2,256,2048]{3,2,1,0:T(8,128)(2,1)}, bf16[2,2,256,2048]{3,2,1,0:T(8,128)(2,1)}, u32[]{:S(2)}, u32[]{:S(2)}) collective-permute-start(bf16[2,2,256,2048]{3,2,1,0:T(8,128)(2,1)} %get-tuple-element.276), channel_id=1, source_target_pairs={{0,1},{1,0},{2,3},{3,2},{4,5},{5,4},{6,7},{7,6},{8,9},{9,8},{10,11... | collective-permute-start | bytes 12582920 | tf_op jit(solution)/shard_map/ppermute | solution.py:450
  952.7 63.8 %collective-permute-start.74 = (bf16[2,2,256,2048]{3,2,1,0:T(8,128)(2,1)}, bf16[2,2,256,2048]{3,2,1,0:T(8,128)(2,1)}, u32[]{:S(2)}, u32[]{:S(2)}) collective-permute-start(bf16[2,2,256,2048]{3,2,1,0:T(8,128)(2,1)} %get-tuple-element.264), channel_id=1, source_target_pairs={{0,1},{1,0},{2,3},{3,2},{4,5},{5,4},{6,7},{7,6},{8,9},{9,8},{10,11... | collective-permute-start | bytes 12582920 | tf_op jit(solution)/shard_map/ppermute | solution.py:450
  1084.4 60.1 %collective-permute-start.85 = (bf16[2,128,2048]{2,1,0:T(8,128)(2,1)S(1)}, bf16[2,128,2048]{2,1,0:T(8,128)(2,1)S(1)}, u32[]{:S(2)}, u32[]{:S(2)}) collective-permute-start(bf16[2,128,2048]{2,1,0:T(8,128)(2,1)S(1)} %copy-done.86), channel_id=1, source_target_pairs={{0,4},{4,0},{8,12},{12,8},{16,20},{20,16},{24,28},{28,24},{1,5},{5... | collective-permute-start | bytes 3145736 | tf_op jit(solution)/shard_map/ppermute | solution.py:450
  1099.8 147.6 %collective-permute-start.121 = (bf16[512,256]{1,0:T(8,128)(2,1)}, bf16[512,256]{1,0:T(8,128)(2,1)}, u32[]{:S(2)}, u32[]{:S(2)}) collective-permute-start(bf16[512,256]{1,0:T(8,128)(2,1)} %bitcast.409), channel_id=1, source_target_pairs={{0,4},{4,0},{8,12},{12,8},{16,20},{20,16},{24,28},{28,24},{1,5},{5... | collective-permute-start | bytes 786440 | tf_op jit(solution)/shard_map/ppermute | solution.py:450
  1106.1 141.8 %collective-permute-start.120 = (bf16[512,256]{1,0:T(8,128)(2,1)}, bf16[512,256]{1,0:T(8,128)(2,1)}, u32[]{:S(2)}, u32[]{:S(2)}) collective-permute-start(bf16[512,256]{1,0:T(8,128)(2,1)} %add_convert_fusion.75), channel_id=1, source_target_pairs={{0,8},{4,12},{8,16},{12,20},{16,24},{20,28},{24,0},{28,4},{1,9},{5... | collective-permute-start | bytes 786440 | tf_op jit(solution)/shard_map/ppermute | solution.py:467
  1204.3 59.9 %collective-permute-start.97 = (bf16[256,2048]{1,0:T(8,128)(2,1)S(1)}, bf16[256,2048]{1,0:T(8,128)(2,1)S(1)}, u32[]{:S(2)}, u32[]{:S(2)}) collective-permute-start(bf16[256,2048]{1,0:T(8,128)(2,1)S(1)} %get-tuple-element.392), channel_id=1, source_target_pairs={{0,1},{1,0},{2,3},{3,2},{4,5},{5,4},{6,7},{7,6},{8,9},{9,8},{10,11... | collective-permute-start | bytes 3145736 | tf_op jit(solution)/shard_map/ppermute | solution.py:450
  1264.2 76.5 %collective-permute-start.123 = (bf16[512,256]{1,0:T(8,128)(2,1)S(1)}, bf16[512,256]{1,0:T(8,128)(2,1)}, u32[]{:S(2)}, u32[]{:S(2)}) collective-permute-start(bf16[512,256]{1,0:T(8,128)(2,1)S(1)} %bitcast.472), channel_id=1, source_target_pairs={{0,4},{4,0},{8,12},{12,8},{16,20},{20,16},{24,28},{28,24},{1,5},{5... | collective-permute-start | bytes 786440 | tf_op jit(solution)/shard_map/ppermute | solution.py:450
  1265.9 78.1 %collective-permute-start.122 = (bf16[512,256]{1,0:T(8,128)(2,1)}, bf16[512,256]{1,0:T(8,128)(2,1)}, u32[]{:S(2)}, u32[]{:S(2)}) collective-permute-start(bf16[512,256]{1,0:T(8,128)(2,1)} %add_convert_fusion.74), channel_id=1, source_target_pairs={{0,8},{4,12},{8,16},{12,20},{16,24},{20,28},{24,0},{28,4},{1,9},{5... | collective-permute-start | bytes 786440 | tf_op jit(solution)/shard_map/ppermute | solution.py:467
  1269.1 80.2 %collective-permute-start.114 = (bf16[256,1536]{1,0:T(8,128)(2,1)}, bf16[256,1536]{1,0:T(8,128)(2,1)}, u32[]{:S(2)}, u32[]{:S(2)}) collective-permute-start(bf16[256,1536]{1,0:T(8,128)(2,1)} %get-tuple-element.387), channel_id=1, source_target_pairs={{0,4},{4,0},{8,12},{12,8},{16,20},{20,16},{24,28},{28,24},{1,5},{5... | collective-permute-start | bytes 2359304 | tf_op jit(solution)/shard_map/ppermute | solution.py:450
  1291.9 57.4 %collective-permute-start.113 = (bf16[256,1536]{1,0:T(8,128)(2,1)}, bf16[256,1536]{1,0:T(8,128)(2,1)}, u32[]{:S(2)}, u32[]{:S(2)}) collective-permute-start(bf16[256,1536]{1,0:T(8,128)(2,1)} %add_convert_fusion.55), channel_id=1, source_target_pairs={{0,8},{4,12},{8,16},{12,20},{16,24},{20,28},{24,0},{28,4},{1,9},{5... | collective-permute-start | bytes 2359304 | tf_op jit(solution)/shard_map/ppermute | solution.py:467
  1292.6 62.8 %collective-permute-start.95 = (bf16[256,2048]{1,0:T(8,128)(2,1)}, bf16[256,2048]{1,0:T(8,128)(2,1)}, u32[]{:S(2)}, u32[]{:S(2)}) collective-permute-start(bf16[256,2048]{1,0:T(8,128)(2,1)} %add_convert_fusion.3), channel_id=1, source_target_pairs={{0,8},{4,12},{8,16},{12,20},{16,24},{20,28},{24,0},{28,4},{1,9},{5... | collective-permute-start | bytes 3145736 | tf_op jit(solution)/shard_map/ppermute | solution.py:467
  (246 other events, 5382.8 us)
Sparse Core Ops, SparseCore 0:
  10.9 295.1 all-gather.1

commit v5 on v4

--- a/solution.py
+++ b/solution.py
@@ -1,6 +1,7 @@
 import jax
 import jax.numpy as jnp
 import functools
+import math
 
 from jax import lax
 from jax.experimental import pallas as pl
@@ -154,26 +155,21 @@
 
 VMEM_BYTES = 60 * 1024 * 1024
 COLUMN_CHUNK = 512
+GROUP = 2
 
 
 def select_rows(places_ref, gates_ref, pick_ref, capacity):
     expert_count, seq_len = places_ref.shape[1:]
-    slot_range = lax.broadcasted_iota(jnp.int32, (capacity, seq_len), 0)
+    slot_range = lax.broadcasted_iota(jnp.int32, (capacity, seq_len), 0).astype(jnp.bfloat16)
+    nothing = jnp.zeros((capacity, seq_len), jnp.bfloat16)
     for expert in range(expert_count):
         hit = places_ref[0, expert : expert + 1, :] == slot_range
-        weight = 1.0 if gates_ref is None else gates_ref[0, expert : expert + 1, :]
+        if gates_ref is None:
+            weight = jnp.ones((capacity, seq_len), jnp.bfloat16)
+        else:
+            weight = jnp.broadcast_to(gates_ref[0, expert : expert + 1, :], (capacity, seq_len))
         rows = slice(expert * capacity, (expert + 1) * capacity)
-        pick_ref[rows, :] = jnp.where(hit, weight, 0.0).astype(jnp.bfloat16)
-
-
-def spread_rows(places_ref, gates_ref, pick_ref, capacity):
-    seq_len, expert_count = places_ref.shape[1:]
-    slot_range = lax.broadcasted_iota(jnp.int32, (seq_len, capacity), 1)
-    for expert in range(expert_count):
-        hit = places_ref[0, :, expert : expert + 1] == slot_range
-        weight = 1.0 if gates_ref is None else gates_ref[0, :, expert : expert + 1]
-        columns = slice(expert * capacity, (expert + 1) * capacity)
-        pick_ref[:, columns] = jnp.where(hit, weight, 0.0).astype(jnp.bfloat16)
+        pick_ref[rows, :] = jnp.where(hit, weight, nothing)
 
 
 def rows_to_slots(pick_ref, rows_ref, slots_ref, pack, capacity):
@@ -190,14 +186,14 @@
     for start in range(0, width, COLUMN_CHUNK):
         columns = slice(start, start + COLUMN_CHUNK)
         slots = slots_ref[:, pack, :, columns].reshape(-1, COLUMN_CHUNK)
-        rows = matmul(pick_ref[...], slots).astype(own_ref.dtype)
+        rows = contract_first(pick_ref[...], slots).astype(own_ref.dtype)
         rows = rows.reshape(2, 2, own_ref.shape[2], COLUMN_CHUNK)
         own_ref[0, :, :, columns] = rows[:, 0]
         other_ref[0, :, :, columns] = rows[:, 1]
 
 
 def cot_kernel(
-    packs, experts, capacity, table, places, gates, rows, down, slots_out, hidden_out, slots, pick
+    packs, steps, capacity, table, places, gates, rows, down, slots_out, hidden_out, slots, pick
 ):
     step = pl.program_id(0)
 
@@ -208,9 +204,10 @@
 
     @pl.when(step >= packs)
     def _():
-        block = slots[step - packs].reshape(packs * capacity, -1)
-        slots_out[0] = block
-        hidden_out[0] = contract_last(block, down[0])
+        for member in range(down.shape[0]):
+            block = slots[(step - packs) * down.shape[0] + member].reshape(packs * capacity, -1)
+            slots_out[member] = block
+            hidden_out[member] = contract_last(block, down[member])
 
 
 def piece_copies(own, other, rows, sems, pack):
@@ -231,85 +228,84 @@
 
 
 def row_kernel(
-    packs, experts, capacity, places, places_t, own, other, gate, up, grad_hidden,
-    slots_out, hidden_out, gated_out, lifted_out, rows_own, rows_other,
-    rows, slots, grads, pick, spread, sems,
+    packs, steps, capacity, places, own, other, both, grad_hidden,
+    slots_out, hidden_out, grads_out, rows_own, rows_other,
+    rows, slots, grads, pick, sems,
 ):
     step = pl.program_id(0)
+    half = hidden_out.shape[2]
 
     @pl.when(step == 0)
     def _():
         for pack in range(packs):
             for copy in piece_copies(own, other, rows, sems, pack):
                 copy.start()
+        for pack in range(packs):
+            select_rows(places.at[pl.ds(pack, 1)], None, pick.at[pack], capacity)
 
     for pack in range(packs):
 
         @pl.when(step == pack)
         def _(pack=pack):
-            select_rows(places, None, pick, capacity)
             for copy in piece_copies(own, other, rows, sems, pack):
                 copy.wait()
-            rows_to_slots(pick, rows.at[pl.ds(pack, 1)], slots, pack, capacity)
-
-    @pl.when((step >= packs) & (step < packs + experts))
+            rows_to_slots(pick.at[pack], rows.at[pl.ds(pack, 1)], slots, pack, capacity)
+
+    @pl.when((step >= packs) & (step < packs + steps))
     def _():
-        expert = step - packs
-        block = slots[expert].reshape(packs * capacity, -1)
-        slots_out[0] = block
-        gated = matmul(block, gate[0])
-        lifted = matmul(block, up[0])
-        sig = 1.0 / (1.0 + jnp.exp(-gated))
-        active = gated * sig
-        hidden_out[0] = (active * lifted).astype(jnp.bfloat16)
-        above = grad_hidden[0]
-        grad_gated = (above * lifted * sig * (1.0 + gated * (1.0 - sig))).astype(jnp.bfloat16)
-        grad_lifted = (above * active).astype(jnp.bfloat16)
-        gated_out[0] = grad_gated
-        lifted_out[0] = grad_lifted
-        back = contract_last(grad_gated, gate[0]) + contract_last(grad_lifted, up[0])
-        grads[expert] = back.astype(jnp.bfloat16).reshape(packs, capacity, -1)
-
-    @pl.when(step >= packs + experts)
+        for member in range(both.shape[0]):
+            expert = (step - packs) * both.shape[0] + member
+            block = slots[expert].reshape(packs * capacity, -1)
+            slots_out[member] = block
+            product = matmul(block, both[member])
+            gated, lifted = product[:, :half], product[:, half:]
+            sig = 1.0 / (1.0 + jnp.exp(-gated))
+            active = gated * sig
+            hidden_out[member] = (active * lifted).astype(jnp.bfloat16)
+            above = grad_hidden[member]
+            grad_gated = above * lifted * sig * (1.0 + gated * (1.0 - sig))
+            joined = jnp.concatenate([grad_gated, above * active], axis=1).astype(jnp.bfloat16)
+            grads_out[member] = joined
+            back = contract_last(joined, both[member])
+            grads[expert] = back.astype(jnp.bfloat16).reshape(packs, capacity, -1)
+
+    for pack in range(packs):
+
+        @pl.when(step == packs + steps + pack)
+        def _(pack=pack):
+            slots_to_rows(pick.at[pack], grads, rows_own, rows_other, pack)
+
+
+def mix_kernel(packs, steps, capacity, places, gates, hidden, down, rows_own, rows_other, results, pick):
+    step = pl.program_id(0)
+
+    @pl.when(step < steps)
     def _():
-        spread_rows(places_t, None, spread, capacity)
-        slots_to_rows(spread, grads, rows_own, rows_other, step - packs - experts)
-
-
-def mix_kernel(
-    packs, experts, capacity, places_t, gates_t, hidden, down, rows_own, rows_other, results, spread
-):
-    step = pl.program_id(0)
-
-    @pl.when(step < experts)
+        for member in range(down.shape[0]):
+            result = matmul(hidden[member], down[member]).astype(jnp.bfloat16)
+            results[step * down.shape[0] + member] = result.reshape(packs, capacity, -1)
+
+    @pl.when(step >= steps)
     def _():
-        result = matmul(hidden[0], down[0])
-        results[step] = result.astype(jnp.bfloat16).reshape(packs, capacity, -1)
-
-    @pl.when(step >= experts)
-    def _():
-        spread_rows(places_t, gates_t, spread, capacity)
-        slots_to_rows(spread, results, rows_own, rows_other, step - experts)
+        select_rows(places, gates, pick, capacity)
+        slots_to_rows(pick, results, rows_own, rows_other, step - steps)
 
 
 def weight_kernel(planes, *refs):
-    slots, grads, hidden, gated, lifted = (refs[i * planes : (i + 1) * planes] for i in range(5))
-    gate_out, up_out, down_out = refs[5 * planes :]
-
-    def total(left, right):
-        result = contract_first(left[0][0], right[0][0])
-        for index in range(1, planes):
-            result = result + contract_first(left[index][0], right[index][0])
-        return result
-
-    gate_out[0] = total(slots, gated)
-    up_out[0] = total(slots, lifted)
-    down_out[0] = total(hidden, grads)
-
-
-def block(shape, place):
+    slots, grads, hidden, above = (
+        jnp.concatenate([ref[0] for ref in refs[i * planes : (i + 1) * planes]]) for i in range(4)
+    )
+    gate_out, up_out, down_out = refs[-3:]
+    half = gate_out.shape[2]
+    both = contract_first(slots, above)
+    gate_out[0] = both[:, :half]
+    up_out[0] = both[:, half:]
+    down_out[0] = contract_first(hidden, grads)
+
+
+def block(shape, place, count=1):
     tail = (0,) * (len(shape) - 1)
-    return pl.BlockSpec((1,) + tuple(shape[1:]), lambda *ids: (place(*ids),) + tail)
+    return pl.BlockSpec((count,) + tuple(shape[1:]), lambda *ids: (place(*ids),) + tail)
 
 
 def staged(first, count):
@@ -320,7 +316,7 @@
     return jax.ShapeDtypeStruct(shape, kind)
 
 
-def call(kernel, steps, specs, out_specs, out_shape, scratch, flops, prefetch=0):
+def call(kernel, steps, specs, out_specs, out_shape, scratch, flops, prefetch=0, aliases={}):
     return pl.pallas_call(
         kernel,
         grid_spec=pltpu.PrefetchScalarGridSpec(
@@ -331,6 +327,7 @@
             scratch_shapes=scratch,
         ),
         out_shape=out_shape,
+        input_output_aliases=aliases,
         cost_estimate=pl.CostEstimate(
             flops=flops, transcendentals=0, bytes_accessed=flops // 500
         ),
@@ -345,20 +342,22 @@
     _, seq_len, width = rows.shape
     experts, hidden_width, _ = down.shape
     slot_rows = packs * capacity
-    by_pack, by_expert = staged(0, packs), staged(packs, experts)
+    group = math.gcd(experts, GROUP)
+    steps = experts // group
+    by_pack, by_expert = staged(0, packs), staged(packs, steps)
     listed = lambda step, numbers: numbers[by_pack(step)]
     out_shape = [
         shape_of((experts, slot_rows, width), jnp.bfloat16),
         shape_of((experts, slot_rows, hidden_width), jnp.float32),
     ]
     return call(
-        functools.partial(cot_kernel, packs, experts, capacity),
-        packs + experts,
+        functools.partial(cot_kernel, packs, steps, capacity),
+        packs + steps,
         [
             block(places.shape, listed), block(gates.shape, listed), block(rows.shape, listed),
-            block(down.shape, by_expert),
+            block(down.shape, by_expert, group),
         ],
-        [block(out.shape, by_expert) for out in out_shape],
+        [block(out.shape, by_expert, group) for out in out_shape],
         out_shape,
         [
             pltpu.VMEM((experts, packs, capacity, width), jnp.bfloat16),
@@ -369,66 +368,71 @@
     )(table, places, gates, rows, down)
 
 
-def row_slots(places, places_t, own, other, gate, up, grad_hidden, capacity):
+def row_slots(places, own, other, both, grad_hidden, capacity):
     packs, _, seq_len = places.shape
-    experts, width, hidden_width = gate.shape
+    experts, width, hidden_width = both.shape
     slot_rows = packs * capacity
-    first, middle, last = staged(0, packs), staged(packs, experts), staged(packs + experts, packs)
-    narrow = shape_of((experts, slot_rows, hidden_width), jnp.bfloat16)
+    group = math.gcd(experts, GROUP)
+    steps = experts // group
+    middle, last = staged(packs, steps), staged(packs + steps, packs)
     part = shape_of((packs, 2, seq_len // 4, width), jnp.bfloat16)
     out_shape = [
-        shape_of((experts, slot_rows, width), jnp.bfloat16), narrow, narrow, narrow, part, part
+        shape_of((experts, slot_rows, width), jnp.bfloat16),
+        shape_of((experts, slot_rows, hidden_width // 2), jnp.bfloat16),
+        shape_of((experts, slot_rows, hidden_width), jnp.bfloat16),
+        part, part,
     ]
     anywhere = pl.BlockSpec(memory_space=pl.ANY)
     return call(
-        functools.partial(row_kernel, packs, experts, capacity),
-        2 * packs + experts,
+        functools.partial(row_kernel, packs, steps, capacity),
+        2 * packs + steps,
         [
-            block(places.shape, first), block(places_t.shape, last), anywhere, anywhere,
-            block(gate.shape, middle), block(up.shape, middle), block(grad_hidden.shape, middle),
+            block(places.shape, lambda step: 0, packs), anywhere, anywhere,
+            block(both.shape, middle, group), block(grad_hidden.shape, middle, group),
         ],
-        [block(out.shape, middle) for out in out_shape[:4]] + [block(part.shape, last)] * 2,
+        [block(out.shape, middle, group) for out in out_shape[:3]] + [block(part.shape, last)] * 2,
         out_shape,
         [
             pltpu.VMEM((packs, seq_len, width), jnp.bfloat16),
             pltpu.VMEM((experts, packs, capacity, width), jnp.bfloat16),
             pltpu.VMEM((experts, packs, capacity, width), jnp.bfloat16),
-            pltpu.VMEM((experts * capacity, seq_len), jnp.bfloat16),
-            pltpu.VMEM((seq_len, experts * capacity), jnp.bfloat16),
+            pltpu.VMEM((packs, experts * capacity, seq_len), jnp.bfloat16),
             pltpu.SemaphoreType.DMA((8 * packs,)),
         ],
-        4 * experts * slot_rows * width * (seq_len + 2 * hidden_width),
-    )(places, places_t, own, other, gate, up, grad_hidden)
-
-
-def mix_rows(places_t, gates_t, hidden, down, capacity):
-    packs, seq_len, _ = places_t.shape
+        4 * experts * slot_rows * width * (seq_len + hidden_width),
+    )(places, own, other, both, grad_hidden)
+
+
+def mix_rows(places, gates, hidden, down, capacity):
+    packs, _, seq_len = places.shape
     experts, hidden_width, width = down.shape
-    first, last = staged(0, experts), staged(experts, packs)
+    group = math.gcd(experts, GROUP)
+    steps = experts // group
+    first, last = staged(0, steps), staged(steps, packs)
     part = shape_of((packs, 2, seq_len // 4, width), jnp.bfloat16)
     return call(
-        functools.partial(mix_kernel, packs, experts, capacity),
-        packs + experts,
+        functools.partial(mix_kernel, packs, steps, capacity),
+        packs + steps,
         [
-            block(places_t.shape, last), block(gates_t.shape, last),
-            block(hidden.shape, first), block(down.shape, first),
+            block(places.shape, last), block(gates.shape, last),
+            block(hidden.shape, first, group), block(down.shape, first, group),
         ],
         [block(part.shape, last)] * 2,
         [part, part],
         [
             pltpu.VMEM((experts, packs, capacity, width), jnp.bfloat16),
-            pltpu.VMEM((seq_len, experts * capacity), jnp.bfloat16),
+            pltpu.VMEM((experts * capacity, seq_len), jnp.bfloat16),
         ],
         2 * experts * packs * capacity * width * (seq_len + hidden_width),
-    )(places_t, gates_t, hidden, down)
-
-
-def weight_grads(slots, grads, hidden, gated, lifted):
+    )(places, gates, hidden, down)
+
+
+def weight_grads(first, count, slots, grads, hidden, above, earlier=()):
     planes = len(slots)
-    operands = [*slots, *grads, *hidden, *gated, *lifted]
+    operands = [*slots, *grads, *hidden, *above]
     experts, _, width = slots[0].shape
     hidden_width = hidden[0].shape[2]
-    each = lambda step: step
+    each = lambda step: step + first
     out_shape = [
         shape_of((experts, width, hidden_width), jnp.float32),
         shape_of((experts, width, hidden_width), jnp.float32),
@@ -436,13 +440,15 @@
     ]
     return call(
         functools.partial(weight_kernel, planes),
-        experts,
-        [block(operand.shape, each) for operand in operands],
+        count,
+        [block(operand.shape, each) for operand in operands]
+        + [pl.BlockSpec(memory_space=pl.ANY)] * len(earlier),
         [block(out.shape, each) for out in out_shape],
         out_shape,
         [],
-        6 * planes * slots[0].shape[1] * experts * width * hidden_width,
-    )(*operands)
+        6 * planes * slots[0].shape[1] * count * width * hidden_width,
+        aliases={len(operands) + index: index for index in range(len(earlier))},
+    )(*operands, *earlier)
 
 
 def swapped(values, axis, bit):
@@ -635,7 +641,8 @@
     earlier = (order[:, None] < order[None, :]).astype(jnp.bfloat16)
     flat = member.reshape(packs * local_experts, -1).astype(jnp.bfloat16)
     before = matmul(flat, earlier).astype(jnp.int32).reshape(member.shape)
-    return jnp.where(member & (before < capacity), before, -1), gates
+    places = jnp.where(member & (before < capacity), before, -1)
+    return places.astype(jnp.bfloat16), gates.astype(jnp.bfloat16)
 
 
 def experts_by_exchange(
@@ -709,7 +716,7 @@
 class Folding:
     def __init__(self, order):
         self.order, self.waiting, self.fresh = order, {}, {}
-        self.summed, self.count, self.total = None, 0, None
+        self.summed, self.count = None, 0
 
     def begin(self, plane, own, other):
         self.fresh[plane] = (0, (own, far_core(other)))
@@ -720,18 +727,11 @@
             if stage < 3:
                 made[plane] = (fold_first, fold_second, fold_third)[stage](*values)
         ready = {plane: values for plane, (stage, values) in self.waiting.items() if stage == 3}
-        following = self.order[self.count] if self.count < len(self.order) else None
         passed = None
-        if following in ready:
-            last = self.count + 1 == len(self.order)
-            kind = jnp.float32 if last else jnp.bfloat16
-            passed = ready[following]
-            if self.summed is not None:
-                passed = added(next_plane(self.summed), passed, kind)
-            del self.waiting[following]
+        if self.order[self.count] in ready:
+            passed = self.passed_on(ready[self.order[self.count]])
+            del self.waiting[self.order[self.count]]
             self.count += 1
-            if last:
-                self.total = passed
         small, (made, passed) = tied(small, (made, passed))
         self.waiting.update(self.fresh)
         self.fresh = {}
@@ -741,6 +741,20 @@
             self.summed = passed
         return small
 
+    def passed_on(self, values):
+        kind = jnp.float32 if self.count + 1 == len(self.order) else jnp.bfloat16
+        return values if self.summed is None else added(next_plane(self.summed), values, kind)
+
+    def finish(self):
+        self.waiting.update(self.fresh)
+        for plane in self.order[self.count :]:
+            stage, values = self.waiting[plane]
+            for fold in (fold_first, fold_second, fold_third)[stage:]:
+                values = fold(*values)
+            self.summed = self.passed_on(values)
+            self.count += 1
+        return self.summed
+
 
 def experts_by_gather(second_in, all_cot, places, gates, w_gate, w_up, w_down, capacity):
     packs, local_experts, seq_len = places.shape
@@ -756,7 +770,7 @@
         return split.reshape(values.shape)
 
     near_places, near_gates = as_met(places), as_met(gates)
-    places_t, gates_t = near_places.transpose(0, 2, 1), near_gates.transpose(0, 2, 1)
+    w_both = jnp.concatenate([w_gate, w_up], axis=2)
     pieces, travelling = [], second_in
     for plane in range(planes):
         travelling = next_plane(travelling) if plane else travelling
@@ -772,19 +786,15 @@
     for plane in range(planes):
         pair = pairs[plane]
         own, other, (grad_slots, grad_hidden) = pieces[plane]
-        near = folding.step(near_places[pair]) if plane > 1 else near_places[pair]
-        slots, hidden, grad_gated, grad_lifted, *part = row_slots(
-            near, places_t[pair], own, other, w_gate, w_up, grad_hidden, capacity
-        )
+        near = folding.step(near_places[pair]) if plane else near_places[pair]
+        slots, hidden, above, *part = row_slots(near, own, other, w_both, grad_hidden, capacity)
         folding.begin(plane, *part)
-        kept[plane] = (slots, grad_slots, hidden, grad_gated, grad_lifted)
+        kept[plane] = (slots, grad_slots, hidden, above)
     for plane in order:
-        near_t = folding.step(places_t[pairs[plane]])
-        part = mix_rows(near_t, gates_t[pairs[plane]], kept[plane][2], w_down, capacity)
+        near = folding.step(near_places[pairs[plane]])
+        part = mix_rows(near, near_gates[pairs[plane]], kept[plane][2], w_down, capacity)
         mixing.begin(plane, *part)
-    while folding.total is None:
-        folding.step(pack_order)
-    return folding.total, mixing, [kept[plane] for plane in range(planes)]
+    return folding.finish(), mixing, [kept[plane] for plane in range(planes)]
 
 
 def shards(
@@ -825,8 +835,6 @@
     if by_gather:
         axes = ("dp", "tensor")
         all_ids, all_gates, segments = gather_tables(expert_ids, gate_values, segment_ids)
-        all_cot = lax.all_gather(cotangent, axes, axis=0, tiled=True)
-        all_cot = all_cot.reshape(data_count, seq_len, model_width)
         places, gates = routing(all_ids, all_gates, local_experts, capacity)
     inputs_f32 = inputs.astype(jnp.float32)
     normed_one, factor_one = norm_parts(inputs_f32)
@@ -835,6 +843,9 @@
         side_sum, side_gather = fold_sides, gather_sides
         local_width = w_query.shape[1]
         full_in = gather_packs(jnp.concatenate([w_query, w_key, w_value], axis=1))
+        full_in, cotangent = tied(full_in, cotangent)
+        all_cot = lax.all_gather(cotangent, axes, axis=0, tiled=True)
+        all_cot = all_cot.reshape(data_count, seq_len, model_width)
         full_in = full_in.reshape(model_width, -1)
         full_query, full_key, full_value = (
             full_in[:, index * local_width : (index + 1) * local_width] for index in range(3)
@@ -899,7 +910,17 @@
     grad_middle = cotangent.astype(jnp.float32) + norm_back(
         grad_second, normed_two, factor_two, ffn_gain
     )
-    pack_grad = mix_step(side_gather(grad_middle.astype(jnp.bfloat16)))
+    grad_attended = grad_middle.astype(jnp.bfloat16)
+    if by_gather:
+        kept, grad_attended = tied(kept, grad_attended)
+        part_size = math.gcd(local_experts, GROUP)
+        weight_parts = ()
+        for first in range(0, local_experts // 2, part_size):
+            weight_parts = weight_grads(first, part_size, *zip(*kept), weight_parts)
+        weight_parts, pack_grad = tied(weight_parts, side_gather(grad_attended))
+    else:
+        pack_grad = side_gather(grad_attended)
+    pack_grad = mix_step(pack_grad)
     output_part = contract_first(mixture, pack_grad)
     grad_mixture = (
         contract_last(pack_grad, full_output)
@@ -973,11 +994,11 @@
         )
         by_column = output_part.astype(jnp.bfloat16).reshape(local_width, data_count, -1)
         grad_w_output = fold_packs(by_column.transpose(1, 0, 2))
-        kept, _ = lax.optimization_barrier((kept, in_part))
-        grad_w_gate, grad_w_up, grad_w_down = weight_grads(*zip(*kept))
-        while mixing.total is None:
-            mixing.step(attn_gain)
-        outputs = middle + mixing.total
+        kept, _ = tied(kept, in_part)
+        for first in range(local_experts // 2 // part_size * part_size, local_experts, part_size):
+            weight_parts = weight_grads(first, part_size, *zip(*kept), weight_parts)
+        grad_w_gate, grad_w_up, grad_w_down = weight_parts
+        outputs = middle + mixing.finish()
         late = sum_everywhere(attn_gain_part)
         early = sum_everywhere(jnp.concatenate(gain_parts[1:]))
         splits = (model_width, model_width + head_size)

time: 1420 us -> 1410 us (level)
  waiting for transfers between devices: 503 us -> 586 us
  Pallas kernels: 412 us -> 375 us
  other arithmetic: 190 us -> 163 us
  starting transfers between devices: 121 us -> 98.3 us
    ppermute x21, waiting for transfers between devices: 129 us -> 197 us  [next_plane(): lax.ppermute(values, 'dp', [(i, (i + 2) % count) for i in range(count)])]
    pallas_call x13 -> x16, Pallas kernels: 392 us -> 356 us  [the longest x4 152 us: row_slots(): call(functools.partial(row_kernel, packs, steps, capacity), 2 * packs + s...]
    ppermute x21, starting transfers between devices: 28.9 us -> 10.4 us  [next_plane(): lax.ppermute(values, 'dp', [(i, (i + 2) % count) for i in range(count)])]
    ppermute x103, waiting for transfers between devices: 374 us -> 390 us  [swapped(): return lax.ppermute(values, axis, [(i, i ^ bit) for i in range(count)])]
  transfers between devices with their start and end apart: 125 -> 125, of which waited for: 48 -> 56; matrix products, arithmetic and copies ran while one was open for 23% -> 20% of each run, Pallas kernels for 29% -> 26%
where the time goes in v5:
time: 1410 us
  waiting for transfers between devices  586 us (42%)
  Pallas kernels  375 us (27%)
  other arithmetic  163 us (12%)
  starting transfers between devices  98.3 us (7%)
  local copies, waits for them, and re-layouts  88.5 us (6%)
  matrix products  77.1 us (5%)
  between operations  17.4 us (1%)
    ppermute x103, waiting for transfers between devices, swapped(): return lax.ppermute(values, axis, [(i, i ^ bit) for i in range(count)])  390 us
    ppermute x21, waiting for transfers between devices, next_plane(): lax.ppermute(values, 'dp', [(i, (i + 2) % count) for i in range(count)])  197 us
    pallas_call x4, Pallas kernels, row_slots(): call(functools.partial(row_kernel, packs, steps, capacity), 2 * packs + s...  152 us
    convert_element_type x67, other arithmetic, added(): return (left.astype(jnp.float32) + right.astype(jnp.float32)).astype(kind)  99.4 us
    ppermute x103, starting transfers between devices, swapped(): return lax.ppermute(values, axis, [(i, i ^ bit) for i in range(count)])  87.9 us
    pallas_call x4, Pallas kernels, cot_slots(): call(functools.partial(cot_kernel, packs, steps, capacity), packs + steps...  81.7 us
    pallas_call x4, Pallas kernels, mix_rows(): call(functools.partial(mix_kernel, packs, steps, capacity), packs + steps...  68.7 us
    pallas_call x4, Pallas kernels, weight_grads(): call(functools.partial(weight_kernel, planes), count, [block(operand.shap...  52.8 us
  transfers between devices with their start and end apart: 125, of which 56 were waited for; matrix products, arithmetic and copies ran while one was open for 20% of the time, Pallas kernels for 26%

profile of v5, /device:TPU:0, one launch (start us, length us, event | category | flops | bytes accessed | tf_op | source)
XLA Modules:
  0.0 1406.1 jit_solution(11090896969007018340)
XLA Ops:
  13.2 19.6 %collective-permute-done.4.refs_2_ = bf16[256,1536]{1,0:T(8,128)(2,1)S(1)} collective-permute-done((bf16[256,1536]{1,0:T(8,128)(2,1)S(1)}, bf16[256,1536]{1,0:T(8,128)(2,1)S(1)}, u32[]{:S(2)}, u32[]{:S(2)}) %collective-permute-start.4) | collective-permute-done | bytes 786464 | tf_op jit(solution)/shard_map/ppermute | solution.py:473
  32.8 20.5 %collective-permute-done.6.refs_4_ = bf16[256,1536]{1,0:T(8,128)(2,1)S(1)} collective-permute-done((bf16[256,1536]{1,0:T(8,128)(2,1)S(1)}, bf16[256,1536]{1,0:T(8,128)(2,1)S(1)}, u32[]{:S(2)}, u32[]{:S(2)}) %collective-permute-start.6) | collective-permute-done | bytes 786464 | tf_op jit(solution)/shard_map/ppermute | solution.py:473
  56.6 16.4 %collective-permute-done.8.refs_6_ = bf16[256,1536]{1,0:T(8,128)(2,1)} collective-permute-done((bf16[256,1536]{1,0:T(8,128)(2,1)S(1)}, bf16[256,1536]{1,0:T(8,128)(2,1)}, u32[]{:S(2)}, u32[]{:S(2)}) %collective-permute-start.8) | collective-permute-done | bytes 786464 | tf_op jit(solution)/shard_map/ppermute | solution.py:473
  74.7 16.1 %collective-permute-done.5.refs_3_ = bf16[256,1536]{1,0:T(8,128)(2,1)} collective-permute-done((bf16[256,1536]{1,0:T(8,128)(2,1)S(1)}, bf16[256,1536]{1,0:T(8,128)(2,1)}, u32[]{:S(2)}, u32[]{:S(2)}) %collective-permute-start.5) | collective-permute-done | bytes 786464 | tf_op jit(solution)/shard_map/ppermute | solution.py:456
  90.8 16.9 %collective-permute-done.7.refs_5_ = bf16[256,1536]{1,0:T(8,128)(2,1)} collective-permute-done((bf16[256,1536]{1,0:T(8,128)(2,1)S(1)}, bf16[256,1536]{1,0:T(8,128)(2,1)}, u32[]{:S(2)}, u32[]{:S(2)}) %collective-permute-start.7) | collective-permute-done | bytes 786464 | tf_op jit(solution)/shard_map/ppermute | solution.py:456
  107.6 14.2 %collective-permute-done.9.refs_7_ = bf16[256,1536]{1,0:T(8,128)(2,1)} collective-permute-done((bf16[256,1536]{1,0:T(8,128)(2,1)}, bf16[256,1536]{1,0:T(8,128)(2,1)}, u32[]{:S(2)}, u32[]{:S(2)}) %collective-permute-start.9) | collective-permute-done | bytes 786464 | tf_op jit(solution)/shard_map/ppermute | solution.py:456
  141.7 20.8 %collective-permute-done.11 = bf16[2,17,256]{2,0,1:T(2,128)(2,1)S(1)} collective-permute-done((bf16[2,17,256]{2,0,1:T(2,128)(2,1)S(1)}, bf16[2,17,256]{2,0,1:T(2,128)(2,1)S(1)}, u32[]{:S(2)}, u32[]{:S(2)}) %collective-permute-start.11) | collective-permute-done | bytes 17440 | tf_op jit(solution)/shard_map/ppermute | solution.py:456
  278.6 19.4 %collective-permute-done.24 = bf16[16,17,256]{2,0,1:T(8,128)(2,1)S(1)} collective-permute-done((bf16[16,17,256]{2,0,1:T(8,128)(2,1)S(1)}, bf16[16,17,256]{2,0,1:T(8,128)(2,1)S(1)}, u32[]{:S(2)}, u32[]{:S(2)}) %collective-permute-start.24) | collective-permute-done | bytes 139296 | tf_op jit(solution)/shard_map/ppermute | solution.py:456
  299.2 18.3 %collective-permute-done.21 = bf16[256,2048]{1,0:T(8,128)(2,1)} collective-permute-done((bf16[256,2048]{1,0:T(8,128)(2,1)}, bf16[256,2048]{1,0:T(8,128)(2,1)}, u32[]{:S(2)}, u32[]{:S(2)}) %collective-permute-start.21) | collective-permute-done | bytes 1048608 | tf_op jit(solution)/shard_map/ppermute | solution.py:456
  339.2 32.3 %collective-permute-done.30 = bf16[256,2048]{1,0:T(8,128)(2,1)} collective-permute-done((bf16[256,2048]{1,0:T(8,128)(2,1)S(1)}, bf16[256,2048]{1,0:T(8,128)(2,1)}, u32[]{:S(2)}, u32[]{:S(2)}) %collective-permute-start.30) | collective-permute-done | bytes 1048608 | tf_op jit(solution)/shard_map/ppermute | solution.py:473
  404.2 20.4 %shard_map.258 = (bf16[8,256,2048]{2,1,0:T(8,128)(2,1)}, f32[8,256,256]{2,1,0:T(8,128)}) custom-call(s32[2]{0:T(128)} %pad_add_fusion.table, bf16[8,8,1024]{2,1,0:T(8,128)(2,1)} %get-tuple-element.539.places, bf16[8,8,1024]{2,1,0:T(8,128)(2,1)} %copy-done.28, bf16[8,1024,2048]{2,1,0:T(8,128)(2,1)} %bitcast.410, bf16[8,256,2048]{2,1,0:T(8,128)(2,1)} %down.15), custom_call_target="tpu_custom_call" | custom-call | flops 10737418240 | bytes 21474836 | tf_op jit(solution)/shard_map/pallas_call | solution.py:353
  458.0 20.4 %shard_map.260 = (bf16[8,256,2048]{2,1,0:T(8,128)(2,1)}, f32[8,256,256]{2,1,0:T(8,128)}) custom-call(s32[2]{0:T(128)} %pad_add_fusion.1.table, bf16[8,8,1024]{2,1,0:T(8,128)(2,1)} %get-tuple-element.539.places, bf16[8,8,1024]{2,1,0:T(8,128)(2,1)} %copy-done.28, bf16[8,1024,2048]{2,1,0:T(8,128)(2,1)} %bitcast.411, bf16[8,256,2048]{2,1,0:T(8,128)(2,1)} %down.15), custom_call_target="tpu_custom_call" | custom-call | flops 10737418240 | bytes 21474836 | tf_op jit(solution)/shard_map/pallas_call | solution.py:353
  500.6 38.1 %shard_map.259 = (bf16[8,256,2048]{2,1,0:T(8,128)(2,1)}, bf16[8,256,256]{2,1,0:T(8,128)(2,1)}, bf16[8,256,512]{2,1,0:T(8,128)(2,1)}, bf16[2,2,256,2048]{3,2,1,0:T(8,128)(2,1)}, bf16[2,2,256,2048]{3,2,1,0:T(8,128)(2,1)}) custom-call(bf16[2,8,1024]{2,1,0:T(8,128)(2,1)} %bitcast.472, bf16[8,128,2048]{2,1,0:T(8,128)(2,1)} %pad_maximum_fusion.1.own, ...), custom_call_target="tpu_custom_call" | custom-call | flops 25769803776 | bytes 51539608 | tf_op jit(solution)/shard_map/pallas_call | solution.py:386
  538.8 20.5 %shard_map.262 = (bf16[8,256,2048]{2,1,0:T(8,128)(2,1)}, f32[8,256,256]{2,1,0:T(8,128)}) custom-call(s32[2]{0:T(128)} %pad_add_fusion.2.table, bf16[8,8,1024]{2,1,0:T(8,128)(2,1)} %get-tuple-element.539.places, bf16[8,8,1024]{2,1,0:T(8,128)(2,1)} %copy-done.28, bf16[8,1024,2048]{2,1,0:T(8,128)(2,1)} %bitcast.412, bf16[8,256,2048]{2,1,0:T(8,128)(2,1)} %down.15), custom_call_target="tpu_custom_call" | custom-call | flops 10737418240 | bytes 21474836 | tf_op jit(solution)/shard_map/pallas_call | solution.py:353
  559.7 38.3 %shard_map.261 = (bf16[8,256,2048]{2,1,0:T(8,128)(2,1)}, bf16[8,256,256]{2,1,0:T(8,128)(2,1)}, bf16[8,256,512]{2,1,0:T(8,128)(2,1)}, bf16[2,2,256,2048]{3,2,1,0:T(8,128)(2,1)}, bf16[2,2,256,2048]{3,2,1,0:T(8,128)(2,1)}) custom-call(bf16[2,8,1024]{2,1,0:T(8,128)(2,1)} %bitcast.478, bf16[8,128,2048]{2,1,0:T(8,128)(2,1)} %pad_maximum_fusion.2.own, ...), custom_call_target="tpu_custom_call" | custom-call | flops 25769803776 | bytes 51539608 | tf_op jit(solution)/shard_map/pallas_call | solution.py:386
  598.1 20.4 %shard_map.264 = (bf16[8,256,2048]{2,1,0:T(8,128)(2,1)}, f32[8,256,256]{2,1,0:T(8,128)}) custom-call(s32[2]{0:T(128)} %pad_add_fusion.3.table, bf16[8,8,1024]{2,1,0:T(8,128)(2,1)} %get-tuple-element.539.places, bf16[8,8,1024]{2,1,0:T(8,128)(2,1)} %copy-done.28, bf16[8,1024,2048]{2,1,0:T(8,128)(2,1)} %bitcast.413, bf16[8,256,2048]{2,1,0:T(8,128)(2,1)} %down.15), custom_call_target="tpu_custom_call" | custom-call | flops 10737418240 | bytes 21474836 | tf_op jit(solution)/shard_map/pallas_call | solution.py:353
  630.8 37.8 %shard_map.263 = (bf16[8,256,2048]{2,1,0:T(8,128)(2,1)}, bf16[8,256,256]{2,1,0:T(8,128)(2,1)}, bf16[8,256,512]{2,1,0:T(8,128)(2,1)}, bf16[2,2,256,2048]{3,2,1,0:T(8,128)(2,1)}, bf16[2,2,256,2048]{3,2,1,0:T(8,128)(2,1)}) custom-call(bf16[2,8,1024]{2,1,0:T(8,128)(2,1)} %bitcast.476, bf16[8,128,2048]{2,1,0:T(8,128)(2,1)} %pad_maximum_fusion.3.own, ...), custom_call_target="tpu_custom_call" | custom-call | flops 25769803776 | bytes 51539608 | tf_op jit(solution)/shard_map/pallas_call | solution.py:386
  686.2 38.2 %shard_map.265 = (bf16[8,256,2048]{2,1,0:T(8,128)(2,1)}, bf16[8,256,256]{2,1,0:T(8,128)(2,1)}, bf16[8,256,512]{2,1,0:T(8,128)(2,1)}, bf16[2,2,256,2048]{3,2,1,0:T(8,128)(2,1)}, bf16[2,2,256,2048]{3,2,1,0:T(8,128)(2,1)}) custom-call(bf16[2,8,1024]{2,1,0:T(8,128)(2,1)} %bitcast.474, bf16[8,128,2048]{2,1,0:T(8,128)(2,1)} %pad_maximum_fusion.4.own, ...), custom_call_target="tpu_custom_call" | custom-call | flops 25769803776 | bytes 51539608 | tf_op jit(solution)/shard_map/pallas_call | solution.py:386
  797.0 17.2 %shard_map.270 = (bf16[2,2,256,2048]{3,2,1,0:T(8,128)(2,1)}, bf16[2,2,256,2048]{3,2,1,0:T(8,128)(2,1)}) custom-call(bf16[2,8,1024]{2,1,0:T(8,128)(2,1)} %bitcast.479, bf16[2,8,1024]{2,1,0:T(8,128)(2,1)} %bitcast.483, bf16[8,256,256]{2,1,0:T(8,128)(2,1)} %get-tuple-element.377.refs_9_.hidden, bf16[8,256,2048]{2,1,0:T(8,128)(2,1)} %down.15), custom_call_target="tpu_custom_call" | custom-call | flops 10737418240 | bytes 21474836 | tf_op jit(solution)/shard_map/pallas_call | solution.py:413
  817.5 22.5 %collective-permute-done.64 = bf16[2,128,2048]{2,1,0:T(8,128)(2,1)S(1)} collective-permute-done((bf16[2,128,2048]{2,1,0:T(8,128)(2,1)}, bf16[2,128,2048]{2,1,0:T(8,128)(2,1)S(1)}, u32[]{:S(2)}, u32[]{:S(2)}) %collective-permute-start.64) | collective-permute-done | bytes 1048608 | tf_op jit(solution)/shard_map/ppermute | solution.py:456
  844.6 17.0 %shard_map.271 = (bf16[2,2,256,2048]{3,2,1,0:T(8,128)(2,1)}, bf16[2,2,256,2048]{3,2,1,0:T(8,128)(2,1)}) custom-call(bf16[2,8,1024]{2,1,0:T(8,128)(2,1)} %bitcast.477, bf16[2,8,1024]{2,1,0:T(8,128)(2,1)} %bitcast.482, bf16[8,256,256]{2,1,0:T(8,128)(2,1)} %get-tuple-element.378.refs_10_.hidden, bf16[8,256,2048]{2,1,0:T(8,128)(2,1)} %down.15), custom_call_target="tpu_custom_call" | custom-call | flops 10737418240 | bytes 21474836 | tf_op jit(solution)/shard_map/pallas_call | solution.py:413
  863.8 25.7 %collective-permute-done.68 = bf16[256,2048]{1,0:T(8,128)(2,1)S(1)} collective-permute-done((bf16[256,2048]{1,0:T(8,128)(2,1)}, bf16[256,2048]{1,0:T(8,128)(2,1)S(1)}, u32[]{:S(2)}, u32[]{:S(2)}) %collective-permute-start.68) | collective-permute-done | bytes 1048608 | tf_op jit(solution)/shard_map/ppermute | solution.py:473
  890.9 17.4 %shard_map.272 = (bf16[2,2,256,2048]{3,2,1,0:T(8,128)(2,1)}, bf16[2,2,256,2048]{3,2,1,0:T(8,128)(2,1)}) custom-call(bf16[2,8,1024]{2,1,0:T(8,128)(2,1)} %bitcast.475, bf16[2,8,1024]{2,1,0:T(8,128)(2,1)} %bitcast.481, bf16[8,256,256]{2,1,0:T(8,128)(2,1)} %get-tuple-element.379.refs_11_.hidden, bf16[8,256,2048]{2,1,0:T(8,128)(2,1)} %down.15), custom_call_target="tpu_custom_call" | custom-call | flops 10737418240 | bytes 21474836 | tf_op jit(solution)/shard_map/pallas_call | solution.py:413
  908.3 17.0 %shard_map.269 = (bf16[2,2,256,2048]{3,2,1,0:T(8,128)(2,1)}, bf16[2,2,256,2048]{3,2,1,0:T(8,128)(2,1)}) custom-call(bf16[2,8,1024]{2,1,0:T(8,128)(2,1)} %bitcast.473, bf16[2,8,1024]{2,1,0:T(8,128)(2,1)} %bitcast.480, bf16[8,256,256]{2,1,0:T(8,128)(2,1)} %get-tuple-element.376.refs_8_.hidden, bf16[8,256,2048]{2,1,0:T(8,128)(2,1)} %down.15), custom_call_target="tpu_custom_call" | custom-call | flops 10737418240 | bytes 21474836 | tf_op jit(solution)/shard_map/pallas_call | solution.py:413
  936.7 16.7 %collective-permute-done.70 = bf16[256,2048]{1,0:T(8,128)(2,1)S(1)} collective-permute-done((bf16[256,2048]{1,0:T(8,128)(2,1)S(1)}, bf16[256,2048]{1,0:T(8,128)(2,1)S(1)}, u32[]{:S(2)}, u32[]{:S(2)}) %collective-permute-start.70) | collective-permute-done | bytes 1048608 | tf_op jit(solution)/shard_map/ppermute | solution.py:473
  1066.6 13.2 shard_map.273
  1149.8 16.5 %collective-permute-done.83 = bf16[2,128,2048]{2,1,0:T(8,128)(2,1)S(1)} collective-permute-done((bf16[2,128,2048]{2,1,0:T(8,128)(2,1)S(1)}, bf16[2,128,2048]{2,1,0:T(8,128)(2,1)S(1)}, u32[]{:S(2)}, u32[]{:S(2)}) %collective-permute-start.83) | collective-permute-done | bytes 1048608 | tf_op jit(solution)/shard_map/ppermute | solution.py:456
  1169.1 15.5 %collective-permute-done.85 = bf16[2,128,2048]{2,1,0:T(8,128)(2,1)S(1)} collective-permute-done((bf16[2,128,2048]{2,1,0:T(8,128)(2,1)S(1)}, bf16[2,128,2048]{2,1,0:T(8,128)(2,1)S(1)}, u32[]{:S(2)}, u32[]{:S(2)}) %collective-permute-start.85) | collective-permute-done | bytes 1048608 | tf_op jit(solution)/shard_map/ppermute | solution.py:456
  1252.6 20.4 %collective-permute-done.110 = bf16[256,1536]{1,0:T(8,128)(2,1)S(1)} collective-permute-done((bf16[256,1536]{1,0:T(8,128)(2,1)S(1)}, bf16[256,1536]{1,0:T(8,128)(2,1)S(1)}, u32[]{:S(2)}, u32[]{:S(2)}) %collective-permute-start.110) | collective-permute-done | bytes 786464 | tf_op jit(solution)/shard_map/ppermute | solution.py:456
  1291.3 15.0 %collective-permute-done.111 = bf16[256,1536]{1,0:T(8,128)(2,1)S(1)} collective-permute-done((bf16[256,1536]{1,0:T(8,128)(2,1)S(1)}, bf16[256,1536]{1,0:T(8,128)(2,1)S(1)}, u32[]{:S(2)}, u32[]{:S(2)}) %collective-permute-start.111) | collective-permute-done | bytes 786464 | tf_op jit(solution)/shard_map/ppermute | solution.py:473
  1330.2 22.1 %collective-permute-done.103 = f32[2048]{0:T(1024)S(1)} collective-permute-done((f32[2048]{0:T(1024)S(1)}, f32[2048]{0:T(1024)S(1)}, u32[]{:S(2)}, u32[]{:S(2)}) %collective-permute-start.103) | collective-permute-done | bytes 8224 | tf_op jit(solution)/shard_map/ppermute | solution.py:456
  1353.3 37.8 %collective-permute-done.104 = f32[2048]{0:T(1024)S(1)} collective-permute-done((f32[2048]{0:T(1024)S(1)}, f32[2048]{0:T(1024)S(1)}, u32[]{:S(2)}, u32[]{:S(2)}) %collective-permute-start.104) | collective-permute-done | bytes 8224 | tf_op jit(solution)/shard_map/ppermute | solution.py:456
  (799 shorter events, 685.7 us)
Async XLA Ops:
  7.2 397.0 %all-gather.2.cloned.1.call-start = ((), (), s32[]{:S(2)}) async-start(), calls=%async_computation | async-start | bytes 34603008 | tf_op jit(solution)/shard_map/all_gather | solution.py:847
  55.4 52.3 %collective-permute-start.7 = (bf16[256,1536]{1,0:T(8,128)(2,1)S(1)}, bf16[256,1536]{1,0:T(8,128)(2,1)}, u32[]{:S(2)}, u32[]{:S(2)}) collective-permute-start(bf16[256,1536]{1,0:T(8,128)(2,1)S(1)} %collective-permute-done.6.refs_4_), channel_id=1, source_target_pairs={{0,4},{4,0},{8,12},{12,8},{16,20},{20,16},{24,28},{28,24},{1,5},{5... | collective-permute-start | bytes 2359304 | tf_op jit(solution)/shard_map/ppermute | solution.py:456
  73.0 48.8 %collective-permute-start.9 = (bf16[256,1536]{1,0:T(8,128)(2,1)}, bf16[256,1536]{1,0:T(8,128)(2,1)}, u32[]{:S(2)}, u32[]{:S(2)}) collective-permute-start(bf16[256,1536]{1,0:T(8,128)(2,1)} %collective-permute-done.8.refs_6_), channel_id=1, source_target_pairs={{0,4},{4,0},{8,12},{12,8},{16,20},{20,16},{24,28},{28,24},{1,5},{5... | collective-permute-start | bytes 2359304 | tf_op jit(solution)/shard_map/ppermute | solution.py:456
  129.0 65.1 %collective-permute-start = (bf16[256,2048]{1,0:T(8,128)(2,1)S(1)}, bf16[256,2048]{1,0:T(8,128)(2,1)}, u32[]{:S(2)}, u32[]{:S(2)}) collective-permute-start(bf16[256,2048]{1,0:T(8,128)(2,1)S(1)} %fusion.22.refs_0_), channel_id=1, source_target_pairs={{0,1},{1,0},{2,3},{3,2},{4,5},{5,4},{6,7},{7,6},{8,9},{9,8},{10,11... | collective-permute-start | bytes 3145736 | tf_op jit(solution)/shard_map/ppermute | solution.py:456
  270.0 47.5 %collective-permute-start.21 = (bf16[256,2048]{1,0:T(8,128)(2,1)}, bf16[256,2048]{1,0:T(8,128)(2,1)}, u32[]{:S(2)}, u32[]{:S(2)}) collective-permute-start(bf16[256,2048]{1,0:T(8,128)(2,1)} %fusion.31), channel_id=1, source_target_pairs={{0,2},{1,3},{2,0},{3,1},{4,6},{5,7},{6,4},{7,5},{8,10},{9,11},{10,... | collective-permute-start | bytes 3145736 | tf_op jit(solution)/shard_map/ppermute | solution.py:456
  321.5 50.1 %collective-permute-start.30 = (bf16[256,2048]{1,0:T(8,128)(2,1)S(1)}, bf16[256,2048]{1,0:T(8,128)(2,1)}, u32[]{:S(2)}, u32[]{:S(2)}) collective-permute-start(bf16[256,2048]{1,0:T(8,128)(2,1)S(1)} %multiply_convert_fusion.4), channel_id=1, source_target_pairs={{0,8},{4,12},{8,16},{12,20},{16,24},{20,28},{24,0},{28,4},{1,9},{5... | collective-permute-start | bytes 3145736 | tf_op jit(solution)/shard_map/ppermute | solution.py:473
  338.1 54.8 %collective-permute-start.28 = (bf16[2,128,2048]{2,1,0:T(8,128)(2,1)S(1)}, bf16[2,128,2048]{2,1,0:T(8,128)(2,1)}, u32[]{:S(2)}, u32[]{:S(2)}) collective-permute-start(bf16[2,128,2048]{2,1,0:T(8,128)(2,1)S(1)} %pad_maximum_fusion.11), channel_id=1, source_target_pairs={{0,4},{4,0},{8,12},{12,8},{16,20},{20,16},{24,28},{28,24},{1,5},{5... | collective-permute-start | bytes 3145736 | tf_op jit(solution)/shard_map/ppermute | solution.py:456
  338.8 54.1 %collective-permute-start.27 = (bf16[2,128,2048]{2,1,0:T(8,128)(2,1)S(1)}, bf16[2,128,2048]{2,1,0:T(8,128)(2,1)}, u32[]{:S(2)}, u32[]{:S(2)}) collective-permute-start(bf16[2,128,2048]{2,1,0:T(8,128)(2,1)S(1)} %pad_maximum_fusion.10), channel_id=1, source_target_pairs={{0,2},{1,3},{2,0},{3,1},{4,6},{5,7},{6,4},{7,5},{8,10},{9,11},{10,... | collective-permute-start | bytes 3145736 | tf_op jit(solution)/shard_map/ppermute | solution.py:456
  424.6 76.0 %collective-permute-start.29 = (bf16[8,128,2048]{2,1,0:T(8,128)(2,1)}, bf16[8,128,2048]{2,1,0:T(8,128)(2,1)}, u32[]{:S(2)}, u32[]{:S(2)}) collective-permute-start(bf16[8,128,2048]{2,1,0:T(8,128)(2,1)} %pad_maximum_fusion.1.own), channel_id=1, source_target_pairs={{0,1},{1,0},{2,3},{3,2},{4,5},{5,4},{6,7},{7,6},{8,9},{9,8},{10,11... | collective-permute-start | bytes 12582920 | tf_op jit(solution)/shard_map/ppermute | solution.py:456
  478.5 81.3 %collective-permute-start.35 = (bf16[8,128,2048]{2,1,0:T(8,128)(2,1)}, bf16[8,128,2048]{2,1,0:T(8,128)(2,1)}, u32[]{:S(2)}, u32[]{:S(2)}) collective-permute-start(bf16[8,128,2048]{2,1,0:T(8,128)(2,1)} %pad_maximum_fusion.2.own), channel_id=1, source_target_pairs={{0,1},{1,0},{2,3},{3,2},{4,5},{5,4},{6,7},{7,6},{8,9},{9,8},{10,11... | collective-permute-start | bytes 12582920 | tf_op jit(solution)/shard_map/ppermute | solution.py:456
  538.7 80.3 %collective-permute-start.36 = (bf16[2,2,256,2048]{3,2,1,0:T(8,128)(2,1)}, bf16[2,2,256,2048]{3,2,1,0:T(8,128)(2,1)}, u32[]{:S(2)}, u32[]{:S(2)}) collective-permute-start(bf16[2,2,256,2048]{3,2,1,0:T(8,128)(2,1)} %get-tuple-element.229), channel_id=1, source_target_pairs={{0,1},{1,0},{2,3},{3,2},{4,5},{5,4},{6,7},{7,6},{8,9},{9,8},{10,11... | collective-permute-start | bytes 12582920 | tf_op jit(solution)/shard_map/ppermute | solution.py:456
  559.2 71.6 %collective-permute-start.42 = (bf16[8,128,2048]{2,1,0:T(8,128)(2,1)}, bf16[8,128,2048]{2,1,0:T(8,128)(2,1)}, u32[]{:S(2)}, u32[]{:S(2)}) collective-permute-start(bf16[8,128,2048]{2,1,0:T(8,128)(2,1)} %pad_maximum_fusion.3.own), channel_id=1, source_target_pairs={{0,1},{1,0},{2,3},{3,2},{4,5},{5,4},{6,7},{7,6},{8,9},{9,8},{10,11... | collective-permute-start | bytes 12582920 | tf_op jit(solution)/shard_map/ppermute | solution.py:456
  598.0 70.7 %collective-permute-start.45 = (bf16[2,2,256,2048]{3,2,1,0:T(8,128)(2,1)}, bf16[2,2,256,2048]{3,2,1,0:T(8,128)(2,1)}, u32[]{:S(2)}, u32[]{:S(2)}) collective-permute-start(bf16[2,2,256,2048]{3,2,1,0:T(8,128)(2,1)} %get-tuple-element.247), channel_id=1, source_target_pairs={{0,1},{1,0},{2,3},{3,2},{4,5},{5,4},{6,7},{7,6},{8,9},{9,8},{10,11... | collective-permute-start | bytes 12582920 | tf_op jit(solution)/shard_map/ppermute | solution.py:456
  618.5 66.3 %collective-permute-start.51 = (bf16[8,128,2048]{2,1,0:T(8,128)(2,1)}, bf16[8,128,2048]{2,1,0:T(8,128)(2,1)}, u32[]{:S(2)}, u32[]{:S(2)}) collective-permute-start(bf16[8,128,2048]{2,1,0:T(8,128)(2,1)} %pad_maximum_fusion.4.own), channel_id=1, source_target_pairs={{0,1},{1,0},{2,3},{3,2},{4,5},{5,4},{6,7},{7,6},{8,9},{9,8},{10,11... | collective-permute-start | bytes 12582920 | tf_op jit(solution)/shard_map/ppermute | solution.py:456
  627.7 49.4 %collective-permute-start.43 = (bf16[2,128,2048]{2,1,0:T(8,128)(2,1)}, bf16[2,128,2048]{2,1,0:T(8,128)(2,1)}, u32[]{:S(2)}, u32[]{:S(2)}) collective-permute-start(bf16[2,128,2048]{2,1,0:T(8,128)(2,1)} %fusion.62), channel_id=1, source_target_pairs={{0,2},{1,3},{2,0},{3,1},{4,6},{5,7},{6,4},{7,5},{8,10},{9,11},{10,... | collective-permute-start | bytes 3145736 | tf_op jit(solution)/shard_map/ppermute | solution.py:456
  629.4 50.2 %collective-permute-start.44 = (bf16[2,128,2048]{2,1,0:T(8,128)(2,1)}, bf16[2,128,2048]{2,1,0:T(8,128)(2,1)}, u32[]{:S(2)}, u32[]{:S(2)}) collective-permute-start(bf16[2,128,2048]{2,1,0:T(8,128)(2,1)} %get-tuple-element.245), channel_id=1, source_target_pairs={{0,4},{4,0},{8,12},{12,8},{16,20},{20,16},{24,28},{28,24},{1,5},{5... | collective-permute-start | bytes 3145736 | tf_op jit(solution)/shard_map/ppermute | solution.py:456
  668.6 63.2 %collective-permute-start.56 = (bf16[2,2,256,2048]{3,2,1,0:T(8,128)(2,1)}, bf16[2,2,256,2048]{3,2,1,0:T(8,128)(2,1)}, u32[]{:S(2)}, u32[]{:S(2)}) collective-permute-start(bf16[2,2,256,2048]{3,2,1,0:T(8,128)(2,1)} %get-tuple-element.269), channel_id=1, source_target_pairs={{0,1},{1,0},{2,3},{3,2},{4,5},{5,4},{6,7},{7,6},{8,9},{9,8},{10,11... | collective-permute-start | bytes 12582920 | tf_op jit(solution)/shard_map/ppermute | solution.py:456
  724.5 62.4 %collective-permute-start.61 = (bf16[2,2,256,2048]{3,2,1,0:T(8,128)(2,1)}, bf16[2,2,256,2048]{3,2,1,0:T(8,128)(2,1)}, u32[]{:S(2)}, u32[]{:S(2)}) collective-permute-start(bf16[2,2,256,2048]{3,2,1,0:T(8,128)(2,1)} %get-tuple-element.279), channel_id=1, source_target_pairs={{0,1},{1,0},{2,3},{3,2},{4,5},{5,4},{6,7},{7,6},{8,9},{9,8},{10,11... | collective-permute-start | bytes 12582920 | tf_op jit(solution)/shard_map/ppermute | solution.py:456
  814.2 112.7 %collective-permute-start.75 = (bf16[2,2,256,2048]{3,2,1,0:T(8,128)(2,1)}, bf16[2,2,256,2048]{3,2,1,0:T(8,128)(2,1)}, u32[]{:S(2)}, u32[]{:S(2)}) collective-permute-start(bf16[2,2,256,2048]{3,2,1,0:T(8,128)(2,1)} %get-tuple-element.327), channel_id=1, source_target_pairs={{0,1},{1,0},{2,3},{3,2},{4,5},{5,4},{6,7},{7,6},{8,9},{9,8},{10,11... | collective-permute-start | bytes 12582920 | tf_op jit(solution)/shard_map/ppermute | solution.py:456
  861.7 95.7 %collective-permute-start.76 = (bf16[2,2,256,2048]{3,2,1,0:T(8,128)(2,1)}, bf16[2,2,256,2048]{3,2,1,0:T(8,128)(2,1)}, u32[]{:S(2)}, u32[]{:S(2)}) collective-permute-start(bf16[2,2,256,2048]{3,2,1,0:T(8,128)(2,1)} %get-tuple-element.330), channel_id=1, source_target_pairs={{0,1},{1,0},{2,3},{3,2},{4,5},{5,4},{6,7},{7,6},{8,9},{9,8},{10,11... | collective-permute-start | bytes 12582920 | tf_op jit(solution)/shard_map/ppermute | solution.py:456
  908.3 84.8 %collective-permute-start.77 = (bf16[2,2,256,2048]{3,2,1,0:T(8,128)(2,1)}, bf16[2,2,256,2048]{3,2,1,0:T(8,128)(2,1)}, u32[]{:S(2)}, u32[]{:S(2)}) collective-permute-start(bf16[2,2,256,2048]{3,2,1,0:T(8,128)(2,1)} %get-tuple-element.333), channel_id=1, source_target_pairs={{0,1},{1,0},{2,3},{3,2},{4,5},{5,4},{6,7},{7,6},{8,9},{9,8},{10,11... | collective-permute-start | bytes 12582920 | tf_op jit(solution)/shard_map/ppermute | solution.py:456
  925.3 101.5 %collective-permute-start.74 = (bf16[2,2,256,2048]{3,2,1,0:T(8,128)(2,1)}, bf16[2,2,256,2048]{3,2,1,0:T(8,128)(2,1)}, u32[]{:S(2)}, u32[]{:S(2)}) collective-permute-start(bf16[2,2,256,2048]{3,2,1,0:T(8,128)(2,1)} %get-tuple-element.324), channel_id=1, source_target_pairs={{0,1},{1,0},{2,3},{3,2},{4,5},{5,4},{6,7},{7,6},{8,9},{9,8},{10,11... | collective-permute-start | bytes 12582920 | tf_op jit(solution)/shard_map/ppermute | solution.py:456
  955.7 45.6 %collective-permute-start.71 = (bf16[256,2048]{1,0:T(8,128)(2,1)S(1)}, bf16[256,2048]{1,0:T(8,128)(2,1)S(1)}, u32[]{:S(2)}, u32[]{:S(2)}) collective-permute-start(bf16[256,2048]{1,0:T(8,128)(2,1)S(1)} %fusion.116.refs_0_), channel_id=1, source_target_pairs={{0,1},{1,0},{2,3},{3,2},{4,5},{5,4},{6,7},{7,6},{8,9},{9,8},{10,11... | collective-permute-start | bytes 3145736 | tf_op jit(solution)/shard_map/ppermute | solution.py:456
  1045.4 79.2 %collective-permute-start.78 = (bf16[2,128,2048]{2,1,0:T(8,128)(2,1)}, bf16[2,128,2048]{2,1,0:T(8,128)(2,1)}, u32[]{:S(2)}, u32[]{:S(2)}) collective-permute-start(bf16[2,128,2048]{2,1,0:T(8,128)(2,1)} %fusion.78), channel_id=1, source_target_pairs={{0,2},{1,3},{2,0},{3,1},{4,6},{5,7},{6,4},{7,5},{8,10},{9,11},{10,... | collective-permute-start | bytes 3145736 | tf_op jit(solution)/shard_map/ppermute | solution.py:456
  1046.9 81.9 %collective-permute-start.79 = (bf16[2,128,2048]{2,1,0:T(8,128)(2,1)}, bf16[2,128,2048]{2,1,0:T(8,128)(2,1)}, u32[]{:S(2)}, u32[]{:S(2)}) collective-permute-start(bf16[2,128,2048]{2,1,0:T(8,128)(2,1)} %get-tuple-element.338), channel_id=1, source_target_pairs={{0,4},{4,0},{8,12},{12,8},{16,20},{20,16},{24,28},{28,24},{1,5},{5... | collective-permute-start | bytes 3145736 | tf_op jit(solution)/shard_map/ppermute | solution.py:456
  1047.6 84.5 %collective-permute-start.80 = (bf16[2,128,2048]{2,1,0:T(8,128)(2,1)}, bf16[2,128,2048]{2,1,0:T(8,128)(2,1)}, u32[]{:S(2)}, u32[]{:S(2)}) collective-permute-start(bf16[2,128,2048]{2,1,0:T(8,128)(2,1)} %fusion.82), channel_id=1, source_target_pairs={{0,2},{1,3},{2,0},{3,1},{4,6},{5,7},{6,4},{7,5},{8,10},{9,11},{10,... | collective-permute-start | bytes 3145736 | tf_op jit(solution)/shard_map/ppermute | solution.py:456
  1132.1 52.6 %collective-permute-start.85 = (bf16[2,128,2048]{2,1,0:T(8,128)(2,1)S(1)}, bf16[2,128,2048]{2,1,0:T(8,128)(2,1)S(1)}, u32[]{:S(2)}, u32[]{:S(2)}) collective-permute-start(bf16[2,128,2048]{2,1,0:T(8,128)(2,1)S(1)} %copy-done.92), channel_id=1, source_target_pairs={{0,4},{4,0},{8,12},{12,8},{16,20},{20,16},{24,28},{28,24},{1,5},{5... | collective-permute-start | bytes 3145736 | tf_op jit(solution)/shard_map/ppermute | solution.py:456
  1202.9 47.4 %collective-permute-start.98 = (bf16[256,2048]{1,0:T(8,128)(2,1)S(1)}, bf16[256,2048]{1,0:T(8,128)(2,1)S(1)}, u32[]{:S(2)}, u32[]{:S(2)}) collective-permute-start(bf16[256,2048]{1,0:T(8,128)(2,1)S(1)} %get-tuple-element.429), channel_id=1, source_target_pairs={{0,1},{1,0},{2,3},{3,2},{4,5},{5,4},{6,7},{7,6},{8,9},{9,8},{10,11... | collective-permute-start | bytes 3145736 | tf_op jit(solution)/shard_map/ppermute | solution.py:456
  1203.2 72.9 %collective-permute-start.97 = (bf16[256,2048]{1,0:T(8,128)(2,1)S(1)}, bf16[256,2048]{1,0:T(8,128)(2,1)S(1)}, u32[]{:S(2)}, u32[]{:S(2)}) collective-permute-start(bf16[256,2048]{1,0:T(8,128)(2,1)S(1)} %get-tuple-element.428), channel_id=1, source_target_pairs={{0,1},{1,0},{2,3},{3,2},{4,5},{5,4},{6,7},{7,6},{8,9},{9,8},{10,11... | collective-permute-start | bytes 3145736 | tf_op jit(solution)/shard_map/ppermute | solution.py:456
  1277.8 52.3 %collective-permute-start.92 = (bf16[128,2048]{1,0:T(8,128)(2,1)S(1)}, bf16[128,2048]{1,0:T(8,128)(2,1)S(1)}, u32[]{:S(2)}, u32[]{:S(2)}) collective-permute-start(bf16[128,2048]{1,0:T(8,128)(2,1)S(1)} %copy-done.99), channel_id=1, source_target_pairs={{0,4},{4,0},{8,12},{12,8},{16,20},{20,16},{24,28},{28,24},{1,5},{5... | collective-permute-start | bytes 1572872 | tf_op jit(solution)/shard_map/ppermute | solution.py:456
  1316.1 75.6 %collective-permute-start.116 = (bf16[256,1536]{1,0:T(8,128)(2,1)S(1)}, bf16[256,1536]{1,0:T(8,128)(2,1)S(1)}, u32[]{:S(2)}, u32[]{:S(2)}) collective-permute-start(bf16[256,1536]{1,0:T(8,128)(2,1)S(1)} %get-tuple-element.422), channel_id=1, source_target_pairs={{0,4},{4,0},{8,12},{12,8},{16,20},{20,16},{24,28},{28,24},{1,5},{5... | collective-permute-start | bytes 2359304 | tf_op jit(solution)/shard_map/ppermute | solution.py:456
  1330.0 61.7 %collective-permute-start.115 = (bf16[256,1536]{1,0:T(8,128)(2,1)S(1)}, bf16[256,1536]{1,0:T(8,128)(2,1)S(1)}, u32[]{:S(2)}, u32[]{:S(2)}) collective-permute-start(bf16[256,1536]{1,0:T(8,128)(2,1)S(1)} %add_convert_fusion.54), channel_id=1, source_target_pairs={{0,8},{4,12},{8,16},{12,20},{16,24},{20,28},{24,0},{28,4},{1,9},{5... | collective-permute-start | bytes 2359304 | tf_op jit(solution)/shard_map/ppermute | solution.py:473
  (242 other events, 4199.5 us)
Sparse Core Ops, SparseCore 0:
  128.2 248.0 all-gather.1

commit v6 on v5

--- a/solution.py
+++ b/solution.py
@@ -9,6 +9,8 @@
 from jax.sharding import PartitionSpec as P
 
 WINDOW = 1024
+DP = ("plane", "pack")
+TENSOR = ("side", "core")
 
 
 EPSILON = 1e-06
@@ -93,19 +95,19 @@
 
 def row_sum(term_fn, tok_rows):
     return lax.psum_scatter(
-        term_fn(jnp.int32(0), lax.axis_size("tensor") * tok_rows),
-        "tensor",
+        term_fn(jnp.int32(0), lax.axis_size(TENSOR) * tok_rows),
+        TENSOR,
         scatter_dimension=0,
         tiled=True,
     )
 
 
 def gather_rows(values):
-    return lax.all_gather(values, "tensor", axis=0, tiled=True)
+    return lax.all_gather(values, TENSOR, axis=0, tiled=True)
 
 
 def from_experts(values):
-    return lax.all_to_all(values, "dp", split_axis=1, concat_axis=1, tiled=True)
+    return lax.all_to_all(values, DP, split_axis=1, concat_axis=1, tiled=True)
 
 
 def to_experts(source_rows, slot_token, slot_gate, layout):
@@ -113,7 +115,7 @@
     if slot_gate is not None:
         picked = (picked.astype(jnp.float32) * slot_gate[:, None]).astype(jnp.bfloat16)
     picked = picked.reshape(layout + (picked.shape[1],))
-    return lax.all_to_all(picked, "dp", split_axis=1, concat_axis=1, tiled=True)
+    return lax.all_to_all(picked, DP, split_axis=1, concat_axis=1, tiled=True)
 
 
 def pair_sum(table, weights_low, pair_slots, row_count):
@@ -276,7 +278,8 @@
             slots_to_rows(pick.at[pack], grads, rows_own, rows_other, pack)
 
 
-def mix_kernel(packs, steps, capacity, places, gates, hidden, down, rows_own, rows_other, results, pick):
+def mix_kernel(packs, steps, capacity, table, places, gates, hidden, down, *refs):
+    rows_own, rows_other, results, pick = refs[-4:]
     step = pl.program_id(0)
 
     @pl.when(step < steps)
@@ -288,7 +291,8 @@
     @pl.when(step >= steps)
     def _():
         select_rows(places, gates, pick, capacity)
-        slots_to_rows(pick, results, rows_own, rows_other, step - steps)
+        pack = (step - steps) ^ table[1]
+        slots_to_rows(pick, results, rows_own.at[0], rows_other.at[0], pack)
 
 
 def weight_kernel(planes, *refs):
@@ -403,31 +407,37 @@
     )(places, own, other, both, grad_hidden)
 
 
-def mix_rows(places, gates, hidden, down, capacity):
+def mix_rows(table, places, gates, hidden, down, planes, capacity, earlier=()):
     packs, _, seq_len = places.shape
     experts, hidden_width, width = down.shape
     group = math.gcd(experts, GROUP)
     steps = experts // group
     first, last = staged(0, steps), staged(steps, packs)
-    part = shape_of((packs, 2, seq_len // 4, width), jnp.bfloat16)
+    part = shape_of((planes, packs, 2, seq_len // 4, width), jnp.bfloat16)
+    out_spec = pl.BlockSpec(
+        (1, 1) + part.shape[2:], lambda step, numbers: (numbers[0], last(step), 0, 0, 0)
+    )
     return call(
         functools.partial(mix_kernel, packs, steps, capacity),
         packs + steps,
         [
             block(places.shape, last), block(gates.shape, last),
             block(hidden.shape, first, group), block(down.shape, first, group),
-        ],
-        [block(part.shape, last)] * 2,
+        ]
+        + [pl.BlockSpec(memory_space=pl.ANY)] * len(earlier),
+        [out_spec] * 2,
         [part, part],
         [
             pltpu.VMEM((experts, packs, capacity, width), jnp.bfloat16),
             pltpu.VMEM((experts * capacity, seq_len), jnp.bfloat16),
         ],
         2 * experts * packs * capacity * width * (seq_len + hidden_width),
-    )(places, gates, hidden, down)
-
-
-def weight_grads(first, count, slots, grads, hidden, above, earlier=()):
+        1,
+        aliases={5 + index: index for index in range(len(earlier))},
+    )(table, places, gates, hidden, down, *earlier)
+
+
+def weight_grads(first, count, slots, hidden, grads, above, earlier=()):
     planes = len(slots)
     operands = [*slots, *grads, *hidden, *above]
     experts, _, width = slots[0].shape
@@ -457,20 +467,20 @@
 
 
 def far_side(values):
-    return swapped(values, "tensor", 2)
+    return swapped(values, TENSOR, 2)
 
 
 def far_core(values):
-    return swapped(values, "tensor", 1)
+    return swapped(values, TENSOR, 1)
 
 
 def far_pack(values):
-    return swapped(values, "dp", 1)
+    return swapped(values, DP, 1)
 
 
 def next_plane(values):
-    count = lax.axis_size("dp")
-    return lax.ppermute(values, "dp", [(i, (i + 2) % count) for i in range(count)])
+    count = lax.axis_size(DP)
+    return lax.ppermute(values, DP, [(i, (i + 2) % count) for i in range(count)])
 
 
 def spread_plane(values, beside):
@@ -485,9 +495,9 @@
 
 
 def plane_order():
-    packs = lax.axis_size("dp")
+    packs = lax.axis_size(DP)
     planes = packs // 2
-    index = lax.axis_index("dp")
+    index = lax.axis_index(DP)
     return jnp.stack(
         [
             ((index // 2 + planes - plane) % planes) * 2 + (index % 2 ^ near)
@@ -530,9 +540,12 @@
 
 def gather_packs(values, by_column=False):
     pieces = []
-    for plane in range(lax.axis_size("dp") // 2):
-        values = next_plane(values) if plane else values
-        pieces += [values, far_pack(values)]
+    planes = lax.axis_size("plane")
+    for plane in range(planes):
+        moved = [far_pack(values), next_plane(values) if plane + 1 < planes else ()]
+        across, following = lax.optimization_barrier(moved)
+        pieces += [values, across]
+        values = following
     return laid(pieces, plane_order(), by_column)
 
 
@@ -546,25 +559,44 @@
     return added(next_plane(summed), near[0], jnp.float32)
 
 
+def laid_sides(pieces):
+    order = lax.axis_index(TENSOR) ^ jnp.arange(len(pieces), dtype=jnp.int32)
+    return laid(pieces, order).reshape((-1,) + pieces[0].shape[1:])
+
+
 def gather_sides(values):
     across = far_side(values)
-    pieces = [values, far_core(values), across, far_core(across)]
-    order = lax.axis_index("tensor") ^ jnp.arange(len(pieces), dtype=jnp.int32)
-    return laid(pieces, order).reshape((-1,) + values.shape[1:])
+    return laid_sides([values, far_core(values), across, far_core(across)])
 
 
 def fold_sides(values):
     split = values.astype(jnp.bfloat16).reshape((4, -1) + values.shape[1:])
     take = lambda bits: lax.dynamic_index_in_dim(
-        split, lax.axis_index("tensor") ^ bits, 0, keepdims=False
+        split, lax.axis_index(TENSOR) ^ bits, 0, keepdims=False
     )
     far = added(take(2), far_core(take(3)))
     near = added(take(0), far_core(take(1)))
     return added(near, far_side(far), jnp.float32)
 
 
+def gather_both(weights, rows):
+    pieces, row_pieces, values = [], [rows], weights
+    planes = lax.axis_size("plane")
+    for plane in range(planes):
+        moved = [far_pack(values), next_plane(values) if plane + 1 < planes else ()]
+        if plane == 0:
+            moved += [far_core(rows), far_side(rows)]
+        if plane == 1:
+            moved += [far_core(row_pieces[2])]
+        across, following, *arrived = lax.optimization_barrier(moved)
+        pieces += [values, across]
+        row_pieces += arrived
+        values = following
+    return laid(pieces, plane_order()), laid_sides(row_pieces)
+
+
 def sum_everywhere(values):
-    for axis in ("tensor", "dp"):
+    for axis in (TENSOR, DP):
         bit = 1
         while bit < lax.axis_size(axis):
             values = values + swapped(values, axis, bit)
@@ -608,24 +640,24 @@
     tables = jnp.concatenate(
         [expert_ids.T.astype(jnp.bfloat16), gate_values.T, segment_ids.astype(jnp.bfloat16)]
     )[None]
-    for axis in ("tensor", "dp"):
+    for axis in (TENSOR, DP):
         bit = 1
         while bit < lax.axis_size(axis):
             tables = jnp.concatenate([tables, swapped(tables, axis, bit)])
             bit *= 2
-        if axis == "tensor":
-            sides = jnp.arange(tables.shape[0], dtype=jnp.int32) ^ lax.axis_index("tensor")
+        if axis == TENSOR:
+            sides = jnp.arange(tables.shape[0], dtype=jnp.int32) ^ lax.axis_index(TENSOR)
             segments = jnp.take(tables[:, -1], sides, axis=0).reshape(-1)
     devices = jnp.arange(tables.shape[0], dtype=jnp.int32)
-    own = lax.axis_index("dp") * lax.axis_size("tensor") + lax.axis_index("tensor")
+    own = lax.axis_index(DP) * lax.axis_size(TENSOR) + lax.axis_index(TENSOR)
     tables = jnp.take(tables, devices ^ own, axis=0)
     all_ids, all_gates = tables[:, :top_count], tables[:, top_count : 2 * top_count]
     return all_ids.astype(jnp.int32), all_gates, segments.astype(jnp.int32)
 
 
 def routing(all_ids, all_gates, local_experts, capacity):
-    packs = lax.axis_size("dp")
-    first = lax.axis_index("dp") * local_experts
+    packs = lax.axis_size(DP)
+    first = lax.axis_index(DP) * local_experts
     wanted = first + jnp.arange(local_experts, dtype=jnp.int32)
 
     def by_pack(values):
@@ -649,8 +681,8 @@
     second_in, cotangent, expert_ids, gate_values, w_gate, w_up, w_down, middle, capacity
 ):
     tok_rows, model_width = second_in.shape
-    tensor_count = lax.axis_size("tensor")
-    data_count = lax.axis_size("dp")
+    tensor_count = lax.axis_size(TENSOR)
+    data_count = lax.axis_size(DP)
     local_experts = w_gate.shape[0]
     all_experts = local_experts * data_count
     top_count = expert_ids.shape[1]
@@ -758,18 +790,23 @@
 
 def experts_by_gather(second_in, all_cot, places, gates, w_gate, w_up, w_down, capacity):
     packs, local_experts, seq_len = places.shape
-    tensor_count = lax.axis_size("tensor")
+    tensor_count = lax.axis_size(TENSOR)
     planes = packs // 2
     pack_order = plane_order()
-    side_index = lax.axis_index("tensor")
+    side_index = lax.axis_index(TENSOR)
     quarter_order = side_index ^ jnp.arange(tensor_count, dtype=jnp.int32)
 
-    def as_met(values):
+    def as_met(values, by_pack, by_quarter):
         split = values.reshape(packs, local_experts, tensor_count, -1)
-        split = jnp.take(jnp.take(split, pack_order, axis=0), quarter_order, axis=2)
+        split = jnp.take(jnp.take(split, by_pack, axis=0), by_quarter, axis=2)
         return split.reshape(values.shape)
 
-    near_places, near_gates = as_met(places), as_met(gates)
+    near_places = as_met(places, pack_order, quarter_order)
+    plane_index = pack_order[::2] // 2
+    whole_order = (plane_index[:, None] * 2 + jnp.arange(2, dtype=jnp.int32)).reshape(-1)
+    core_order = lax.axis_index("core") ^ jnp.arange(tensor_count, dtype=jnp.int32)
+    mix_places = as_met(places, whole_order, core_order)
+    mix_gates = as_met(gates, whole_order, core_order)
     w_both = jnp.concatenate([w_gate, w_up], axis=2)
     pieces, travelling = [], second_in
     for plane in range(planes):
@@ -782,19 +819,27 @@
         pieces.append(spread_plane(travelling, beside))
     pairs = [slice(plane * 2, plane * 2 + 2) for plane in range(planes)]
     order = [*range(1, planes), 0]
-    kept, folding, mixing = {}, Folding(order), Folding(order)
+    kept, folding = {}, Folding(order)
     for plane in range(planes):
         pair = pairs[plane]
         own, other, (grad_slots, grad_hidden) = pieces[plane]
         near = folding.step(near_places[pair]) if plane else near_places[pair]
         slots, hidden, above, *part = row_slots(near, own, other, w_both, grad_hidden, capacity)
         folding.begin(plane, *part)
-        kept[plane] = (slots, grad_slots, hidden, above)
-    for plane in order:
-        near = folding.step(near_places[pairs[plane]])
-        part = mix_rows(near, near_gates[pairs[plane]], kept[plane][2], w_down, capacity)
-        mixing.begin(plane, *part)
-    return folding.finish(), mixing, [kept[plane] for plane in range(planes)]
+        kept[plane] = (slots, hidden, grad_slots, above)
+    mixed = ()
+    for index, plane in enumerate(order):
+        pair = pairs[plane]
+        near = mix_places[pair] if index % 2 else folding.step(mix_places[pair])
+        table = jnp.stack([plane_index[plane], lax.axis_index("pack")])
+        mixed = mix_rows(
+            table, near, mix_gates[pair], kept[plane][1], w_down, planes, capacity, mixed
+        )
+    own, other = mixed
+    whole = added(own, far_core(other)).reshape(planes, -1, own.shape[-1])
+    whole = lax.psum_scatter(whole, ("pack", "side"), scatter_dimension=1, tiled=True)
+    whole = lax.psum_scatter(whole, "plane", scatter_dimension=0, tiled=True)
+    return folding.finish(), whole[0].astype(jnp.float32), [kept[plane] for plane in range(planes)]
 
 
 def shards(
@@ -817,8 +862,8 @@
 ):
     tok_rows, model_width = inputs.shape
     head_size = query_gain.shape[0]
-    tensor_count = lax.axis_size("tensor")
-    data_count = lax.axis_size("dp")
+    tensor_count = lax.axis_size(TENSOR)
+    data_count = lax.axis_size(DP)
     local_experts = w_gate.shape[0]
     all_experts = local_experts * data_count
     top_count = expert_ids.shape[1]
@@ -833,7 +878,7 @@
         and all_experts <= 256
     )
     if by_gather:
-        axes = ("dp", "tensor")
+        axes = (*DP, *TENSOR)
         all_ids, all_gates, segments = gather_tables(expert_ids, gate_values, segment_ids)
         places, gates = routing(all_ids, all_gates, local_experts, capacity)
     inputs_f32 = inputs.astype(jnp.float32)
@@ -842,8 +887,9 @@
     if by_gather:
         side_sum, side_gather = fold_sides, gather_sides
         local_width = w_query.shape[1]
-        full_in = gather_packs(jnp.concatenate([w_query, w_key, w_value], axis=1))
-        full_in, cotangent = tied(full_in, cotangent)
+        w_in = jnp.concatenate([w_query, w_key, w_value], axis=1)
+        full_in, pack_in = gather_both(w_in, first_in)
+        full_in, cotangent, w_output = lax.optimization_barrier((full_in, cotangent, w_output))
         all_cot = lax.all_gather(cotangent, axes, axis=0, tiled=True)
         all_cot = all_cot.reshape(data_count, seq_len, model_width)
         full_in = full_in.reshape(model_width, -1)
@@ -853,14 +899,14 @@
         full_output = gather_packs(w_output, True)
     else:
         side_sum, side_gather = lambda term: row_sum(lambda *_: term, tok_rows), gather_rows
-        segments = lax.all_gather(segment_ids, "tensor", axis=1, tiled=True)[0]
+        segments = lax.all_gather(segment_ids, TENSOR, axis=1, tiled=True)[0]
         full_query, full_key, full_value, full_output = (
-            lax.all_gather(w_query, "dp", axis=0, tiled=True),
-            lax.all_gather(w_key, "dp", axis=0, tiled=True),
-            lax.all_gather(w_value, "dp", axis=0, tiled=True),
-            lax.all_gather(w_output, "dp", axis=1, tiled=True),
+            lax.all_gather(w_query, DP, axis=0, tiled=True),
+            lax.all_gather(w_key, DP, axis=0, tiled=True),
+            lax.all_gather(w_value, DP, axis=0, tiled=True),
+            lax.all_gather(w_output, DP, axis=1, tiled=True),
         )
-    pack_in = side_gather(first_in)
+        pack_in = side_gather(first_in)
     query_pre = matmul(pack_in, full_query)
     key_pre = matmul(pack_in, full_key)
     value_low = matmul(pack_in, full_value).astype(jnp.bfloat16)
@@ -897,15 +943,13 @@
     normed_two, factor_two = norm_parts(middle)
     second_in = (normed_two * ffn_gain).astype(jnp.bfloat16)
     if by_gather:
-        grad_second, mixing, kept = experts_by_gather(
+        grad_second, mixed, kept = experts_by_gather(
             second_in, all_cot, places, gates, w_gate, w_up, w_down, capacity
         )
-        mix_step = mixing.step
     else:
         outputs, grad_second, grad_w_gate, grad_w_up, grad_w_down = experts_by_exchange(
             second_in, cotangent, expert_ids, gate_values, w_gate, w_up, w_down, middle, capacity
         )
-        mix_step = lambda values: values
     ffn_gain_part = jnp.sum(grad_second * normed_two, axis=0)
     grad_middle = cotangent.astype(jnp.float32) + norm_back(
         grad_second, normed_two, factor_two, ffn_gain
@@ -920,7 +964,6 @@
         weight_parts, pack_grad = tied(weight_parts, side_gather(grad_attended))
     else:
         pack_grad = side_gather(grad_attended)
-    pack_grad = mix_step(pack_grad)
     output_part = contract_first(mixture, pack_grad)
     grad_mixture = (
         contract_last(pack_grad, full_output)
@@ -933,8 +976,6 @@
     for block_index in range(block_total):
         offset = block_index * block_rows
         query_block = query_low[offset : offset + block_rows]
-        if block_index:
-            query_block = mix_step(query_block)
         grad_block = grad_mixture[offset : offset + block_rows]
         scores = block_scores(query_block, key_low, masks[block_index], inv_root)
         prob_rows = jnp.exp(scores - lse_parts[block_index])
@@ -964,7 +1005,6 @@
     grad_key_norm = rotate_back(grad_key_sum, cosine, sine_tab)
     query_gain_part = jnp.sum(grad_query_norm * query_norm, axis=(0, 1))
     key_gain_part = jnp.sum(grad_key_norm * key_norm, axis=(0, 1))
-    grad_query_norm = mix_step(grad_query_norm)
     grad_query_pre = (
         norm_back(grad_query_norm, query_norm, query_factor, query_gain)
         .reshape(seq_len, -1)
@@ -998,7 +1038,7 @@
         for first in range(local_experts // 2 // part_size * part_size, local_experts, part_size):
             weight_parts = weight_grads(first, part_size, *zip(*kept), weight_parts)
         grad_w_gate, grad_w_up, grad_w_down = weight_parts
-        outputs = middle + mixing.finish()
+        outputs = middle + mixed
         late = sum_everywhere(attn_gain_part)
         early = sum_everywhere(jnp.concatenate(gain_parts[1:]))
         splits = (model_width, model_width + head_size)
@@ -1006,11 +1046,11 @@
     else:
         grad_w_query, grad_w_key, grad_w_value, grad_w_output = (
             lax.psum_scatter(
-                part.astype(jnp.bfloat16), "dp", scatter_dimension=along, tiled=True
+                part.astype(jnp.bfloat16), DP, scatter_dimension=along, tiled=True
             ).astype(jnp.float32)
             for part, along in ((query_part, 0), (key_part, 0), (value_part, 0), (output_part, 1))
         )
-        gain_sums = lax.psum(gain_parts, ("dp", "tensor"))
+        gain_sums = lax.psum(gain_parts, (*DP, *TENSOR))
     grad_attn_gain, grad_ffn_gain, grad_query_gain, grad_key_gain = gain_sums
     return (
         outputs,
@@ -1030,37 +1070,41 @@
 
 
 def solution(mesh):
+    rows, columns = mesh.devices.shape
+    split = jax.sharding.Mesh(
+        mesh.devices.reshape(rows // 2, 2, columns // 2, 2), (*DP, *TENSOR)
+    )
     in_specs = (
-        P(("dp", "tensor"), None),
-        P("dp", "tensor"),
-        P(("dp", "tensor"), None),
-        P(("dp", "tensor"), None),
+        P((*DP, *TENSOR), None),
+        P(DP, TENSOR),
+        P((*DP, *TENSOR), None),
+        P((*DP, *TENSOR), None),
         P(),
         P(),
         P(),
-        P("dp", "tensor"),
-        P("dp", "tensor"),
-        P("dp", "tensor"),
-        P("tensor", "dp"),
+        P(DP, TENSOR),
+        P(DP, TENSOR),
+        P(DP, TENSOR),
+        P(TENSOR, DP),
         P(),
-        P("dp", None, "tensor"),
-        P("dp", None, "tensor"),
-        P("dp", "tensor", None),
-        P(("dp", "tensor"), None),
+        P(DP, None, TENSOR),
+        P(DP, None, TENSOR),
+        P(DP, TENSOR, None),
+        P((*DP, *TENSOR), None),
     )
     out_specs = (
-        P(("dp", "tensor"), None),
-        P(("dp", "tensor"), None),
+        P((*DP, *TENSOR), None),
+        P((*DP, *TENSOR), None),
         P(),
         P(),
         P(),
-        P("dp", "tensor"),
-        P("dp", "tensor"),
-        P("dp", "tensor"),
-        P("tensor", "dp"),
+        P(DP, TENSOR),
+        P(DP, TENSOR),
+        P(DP, TENSOR),
+        P(TENSOR, DP),
         P(),
-        P("dp", None, "tensor"),
-        P("dp", None, "tensor"),
-        P("dp", "tensor", None),
-    )
-    return jax.shard_map(shards, mesh=mesh, in_specs=in_specs, out_specs=out_specs, check_vma=False)
+        P(DP, None, TENSOR),
+        P(DP, None, TENSOR),
+        P(DP, TENSOR, None),
+    )
+    return jax.shard_map(shards, mesh=split, in_specs=in_specs, out_specs=out_specs, check_vma=False)

time: 1410 us -> 1320 us (0.936)
  waiting for transfers between devices: 586 us -> 508 us
  starting transfers between devices: 98.3 us -> 83.3 us
    ppermute x21 -> x18, waiting for transfers between devices: 197 us -> 111 us  [next_plane(): lax.ppermute(values, DP, [(i, (i + 2) % count) for i in range(count)])]
    convert_element_type x67 -> x39, other arithmetic: 99.4 us -> 78 us  [added(): return (left.astype(jnp.float32) + right.astype(jnp.float32)).astype(kind)]
    ppermute x103 -> x84, starting transfers between devices: 87.9 us -> 68.6 us  [swapped(): return lax.ppermute(values, axis, [(i, i ^ bit) for i in range(count)])]
    ppermute x103 -> x84, waiting for transfers between devices: 390 us -> 397 us  [swapped(): return lax.ppermute(values, axis, [(i, i ^ bit) for i in range(count)])]
  transfers between devices with their start and end apart: 125 -> 105, of which waited for: 56 -> 44; matrix products, arithmetic and copies ran while one was open for 20% -> 21% of each run, Pallas kernels for 26% -> 26%
where the time goes in v6:
time: 1320 us; the launch traced here: 1310 us
  waiting for transfers between devices  508 us (38%)
  Pallas kernels  378 us (29%)
  other arithmetic  153 us (12%)
  local copies, waits for them, and re-layouts  91.8 us (7%)
  starting transfers between devices  83.3 us (6%)
  matrix products  79.7 us (6%)
  between operations  16.3 us (1%)
    ppermute x84, waiting for transfers between devices, swapped(): return lax.ppermute(values, axis, [(i, i ^ bit) for i in range(count)])  397 us
    pallas_call x4, Pallas kernels, row_slots(): call(functools.partial(row_kernel, packs, steps, capacity), 2 * packs + s...  152 us
    ppermute x18, waiting for transfers between devices, next_plane(): lax.ppermute(values, DP, [(i, (i + 2) % count) for i in range(count)])  111 us
    pallas_call x4, Pallas kernels, cot_slots(): call(functools.partial(cot_kernel, packs, steps, capacity), packs + steps...  81.5 us
    convert_element_type x39, other arithmetic, added(): return (left.astype(jnp.float32) + right.astype(jnp.float32)).astype(kind)  78 us
    pallas_call x4, Pallas kernels, mix_rows(): call(functools.partial(mix_kernel, packs, steps, capacity), packs + steps...  71 us
    ppermute x84, starting transfers between devices, swapped(): return lax.ppermute(values, axis, [(i, i ^ bit) for i in range(count)])  68.6 us
    pallas_call x4, Pallas kernels, weight_grads(): call(functools.partial(weight_kernel, planes), count, [block(operand.shap...  53.1 us
  transfers between devices with their start and end apart: 105, of which 44 were waited for; matrix products, arithmetic and copies ran while one was open for 21% of the time, Pallas kernels for 26%

profile of v6, /device:TPU:0, one launch (start us, length us, event | category | flops | bytes accessed | tf_op | source)
XLA Modules:
  0.0 1309.0 jit_solution(13719459824855980645)
XLA Ops:
  16.8 16.5 %collective-permute-done.refs_1_ = bf16[256,1536]{1,0:T(8,128)(2,1)S(1)} collective-permute-done((bf16[256,1536]{1,0:T(8,128)(2,1)S(1)}, bf16[256,1536]{1,0:T(8,128)(2,1)S(1)}, u32[]{:S(2)}, u32[]{:S(2)}) %collective-permute-start) | collective-permute-done | bytes 786464 | tf_op jit(solution)/shard_map/ppermute | solution.py:466
  41.6 15.9 %collective-permute-done.4.refs_3_ = bf16[256,1536]{1,0:T(8,128)(2,1)S(1)} collective-permute-done((bf16[256,1536]{1,0:T(8,128)(2,1)S(1)}, bf16[256,1536]{1,0:T(8,128)(2,1)S(1)}, u32[]{:S(2)}, u32[]{:S(2)}) %collective-permute-start.4) | collective-permute-done | bytes 786464 | tf_op jit(solution)/shard_map/ppermute | solution.py:466
  62.5 17.4 %collective-permute-done.7.refs_5_ = bf16[256,1536]{1,0:T(8,128)(2,1)S(1)} collective-permute-done((bf16[256,1536]{1,0:T(8,128)(2,1)S(1)}, bf16[256,1536]{1,0:T(8,128)(2,1)S(1)}, u32[]{:S(2)}, u32[]{:S(2)}) %collective-permute-start.7) | collective-permute-done | bytes 786464 | tf_op jit(solution)/shard_map/ppermute | solution.py:466
  84.2 15.3 %collective-permute-done.9.refs_7_ = bf16[256,1536]{1,0:T(8,128)(2,1)} collective-permute-done((bf16[256,1536]{1,0:T(8,128)(2,1)}, bf16[256,1536]{1,0:T(8,128)(2,1)}, u32[]{:S(2)}, u32[]{:S(2)}) %collective-permute-start.9) | collective-permute-done | bytes 786464 | tf_op jit(solution)/shard_map/ppermute | solution.py:466
  245.7 14.1 %collective-permute-done.24 = bf16[16,17,256]{2,0,1:T(8,128)(2,1)S(1)} collective-permute-done((bf16[16,17,256]{2,0,1:T(8,128)(2,1)S(1)}, bf16[16,17,256]{2,0,1:T(8,128)(2,1)S(1)}, u32[]{:S(2)}, u32[]{:S(2)}) %collective-permute-start.24) | collective-permute-done | bytes 139296 | tf_op jit(solution)/shard_map/ppermute | solution.py:466
  267.7 24.4 %collective-permute-done.21 = bf16[256,2048]{1,0:T(8,128)(2,1)} collective-permute-done((bf16[256,2048]{1,0:T(8,128)(2,1)}, bf16[256,2048]{1,0:T(8,128)(2,1)}, u32[]{:S(2)}, u32[]{:S(2)}) %collective-permute-start.21) | collective-permute-done | bytes 1048608 | tf_op jit(solution)/shard_map/ppermute | solution.py:466
  317.2 14.5 %collective-permute-done.33 = bf16[256,2048]{1,0:T(8,128)(2,1)} collective-permute-done((bf16[256,2048]{1,0:T(8,128)(2,1)S(1)}, bf16[256,2048]{1,0:T(8,128)(2,1)}, u32[]{:S(2)}, u32[]{:S(2)}) %collective-permute-start.33) | collective-permute-done | bytes 1048608 | tf_op jit(solution)/shard_map/ppermute | solution.py:483
  367.0 20.4 %shard_map.258 = (bf16[8,256,2048]{2,1,0:T(8,128)(2,1)}, f32[8,256,256]{2,1,0:T(8,128)}) custom-call(s32[2]{0:T(128)} %pad_add_fusion.1.table, bf16[8,8,1024]{2,1,0:T(8,128)(2,1)} %get-tuple-element.463.places, bf16[8,8,1024]{2,1,0:T(8,128)(2,1)} %copy-done.17, bf16[8,1024,2048]{2,1,0:T(8,128)(2,1)} %bitcast.340, bf16[8,256,2048]{2,1,0:T(8,128)(2,1)} %down.15), custom_call_target="tpu_custom_call" | custom-call | flops 10737418240 | bytes 21474836 | tf_op jit(solution)/shard_map/pallas_call | solution.py:357
  395.7 31.1 %collective-permute-done.46 = bf16[128,2048]{1,0:T(8,128)(2,1)S(1)} collective-permute-done((bf16[128,2048]{1,0:T(8,128)(2,1)S(1)}, bf16[128,2048]{1,0:T(8,128)(2,1)S(1)}, u32[]{:S(2)}, u32[]{:S(2)}) %collective-permute-start.46) | collective-permute-done | bytes 524320 | tf_op jit(solution)/shard_map/ppermute | solution.py:466
  431.7 31.0 %collective-permute-done.57 = bf16[128,2048]{1,0:T(8,128)(2,1)S(1)} collective-permute-done((bf16[128,2048]{1,0:T(8,128)(2,1)S(1)}, bf16[128,2048]{1,0:T(8,128)(2,1)S(1)}, u32[]{:S(2)}, u32[]{:S(2)}) %collective-permute-start.57) | collective-permute-done | bytes 524320 | tf_op jit(solution)/shard_map/ppermute | solution.py:466
  466.2 20.4 %shard_map.260 = (bf16[8,256,2048]{2,1,0:T(8,128)(2,1)}, f32[8,256,256]{2,1,0:T(8,128)}) custom-call(s32[2]{0:T(128)} %pad_add_fusion.3.table, bf16[8,8,1024]{2,1,0:T(8,128)(2,1)} %get-tuple-element.463.places, bf16[8,8,1024]{2,1,0:T(8,128)(2,1)} %copy-done.17, bf16[8,1024,2048]{2,1,0:T(8,128)(2,1)} %bitcast.341, bf16[8,256,2048]{2,1,0:T(8,128)(2,1)} %down.15), custom_call_target="tpu_custom_call" | custom-call | flops 10737418240 | bytes 21474836 | tf_op jit(solution)/shard_map/pallas_call | solution.py:357
  501.7 37.8 %shard_map.259 = (bf16[8,256,2048]{2,1,0:T(8,128)(2,1)}, bf16[8,256,256]{2,1,0:T(8,128)(2,1)}, bf16[8,256,512]{2,1,0:T(8,128)(2,1)}, bf16[2,2,256,2048]{3,2,1,0:T(8,128)(2,1)}, bf16[2,2,256,2048]{3,2,1,0:T(8,128)(2,1)}) custom-call(bf16[2,8,1024]{2,1,0:T(8,128)(2,1)} %bitcast.414, bf16[8,128,2048]{2,1,0:T(8,128)(2,1)} %pad_maximum_fusion.1.own, ...), custom_call_target="tpu_custom_call" | custom-call | flops 25769803776 | bytes 51539608 | tf_op jit(solution)/shard_map/pallas_call | solution.py:390
  540.0 20.4 %shard_map.262 = (bf16[8,256,2048]{2,1,0:T(8,128)(2,1)}, f32[8,256,256]{2,1,0:T(8,128)}) custom-call(s32[2]{0:T(128)} %pad_add_fusion.4.table, bf16[8,8,1024]{2,1,0:T(8,128)(2,1)} %get-tuple-element.463.places, bf16[8,8,1024]{2,1,0:T(8,128)(2,1)} %copy-done.17, bf16[8,1024,2048]{2,1,0:T(8,128)(2,1)} %bitcast.342, bf16[8,256,2048]{2,1,0:T(8,128)(2,1)} %down.15), custom_call_target="tpu_custom_call" | custom-call | flops 10737418240 | bytes 21474836 | tf_op jit(solution)/shard_map/pallas_call | solution.py:357
  560.4 38.2 %shard_map.261 = (bf16[8,256,2048]{2,1,0:T(8,128)(2,1)}, bf16[8,256,256]{2,1,0:T(8,128)(2,1)}, bf16[8,256,512]{2,1,0:T(8,128)(2,1)}, bf16[2,2,256,2048]{3,2,1,0:T(8,128)(2,1)}, bf16[2,2,256,2048]{3,2,1,0:T(8,128)(2,1)}) custom-call(bf16[2,8,1024]{2,1,0:T(8,128)(2,1)} %bitcast.413, bf16[8,128,2048]{2,1,0:T(8,128)(2,1)} %pad_maximum_fusion.2.own, ...), custom_call_target="tpu_custom_call" | custom-call | flops 25769803776 | bytes 51539608 | tf_op jit(solution)/shard_map/pallas_call | solution.py:390
  599.2 20.4 %shard_map.264 = (bf16[8,256,2048]{2,1,0:T(8,128)(2,1)}, f32[8,256,256]{2,1,0:T(8,128)}) custom-call(s32[2]{0:T(128)} %pad_add_fusion.5.table, bf16[8,8,1024]{2,1,0:T(8,128)(2,1)} %get-tuple-element.463.places, bf16[8,8,1024]{2,1,0:T(8,128)(2,1)} %copy-done.17, bf16[8,1024,2048]{2,1,0:T(8,128)(2,1)} %bitcast.343, bf16[8,256,2048]{2,1,0:T(8,128)(2,1)} %down.15), custom_call_target="tpu_custom_call" | custom-call | flops 10737418240 | bytes 21474836 | tf_op jit(solution)/shard_map/pallas_call | solution.py:357
  630.1 37.9 %shard_map.263 = (bf16[8,256,2048]{2,1,0:T(8,128)(2,1)}, bf16[8,256,256]{2,1,0:T(8,128)(2,1)}, bf16[8,256,512]{2,1,0:T(8,128)(2,1)}, bf16[2,2,256,2048]{3,2,1,0:T(8,128)(2,1)}, bf16[2,2,256,2048]{3,2,1,0:T(8,128)(2,1)}) custom-call(bf16[2,8,1024]{2,1,0:T(8,128)(2,1)} %bitcast.412, bf16[8,128,2048]{2,1,0:T(8,128)(2,1)} %pad_maximum_fusion.3.own, ...), custom_call_target="tpu_custom_call" | custom-call | flops 25769803776 | bytes 51539608 | tf_op jit(solution)/shard_map/pallas_call | solution.py:390
  685.6 38.1 %shard_map.265 = (bf16[8,256,2048]{2,1,0:T(8,128)(2,1)}, bf16[8,256,256]{2,1,0:T(8,128)(2,1)}, bf16[8,256,512]{2,1,0:T(8,128)(2,1)}, bf16[2,2,256,2048]{3,2,1,0:T(8,128)(2,1)}, bf16[2,2,256,2048]{3,2,1,0:T(8,128)(2,1)}) custom-call(bf16[2,8,1024]{2,1,0:T(8,128)(2,1)} %bitcast.411, bf16[8,128,2048]{2,1,0:T(8,128)(2,1)} %pad_maximum_fusion.4.own, ...), custom_call_target="tpu_custom_call" | custom-call | flops 25769803776 | bytes 51539608 | tf_op jit(solution)/shard_map/pallas_call | solution.py:390
  742.5 17.7 %shard_map.266 = (bf16[4,2,2,256,2048]{4,3,2,1,0:T(8,128)(2,1)}, bf16[4,2,2,256,2048]{4,3,2,1,0:T(8,128)(2,1)}) custom-call(s32[2]{0:T(128)} %pad_add_fusion.7.table, bf16[2,8,1024]{2,1,0:T(8,128)(2,1)} %bitcast.409, bf16[2,8,1024]{2,1,0:T(8,128)(2,1)} %bitcast.410, bf16[8,256,256]{2,1,0:T(8,128)(2,1)} %get-tuple-element.321.hidden.refs_9_, ...), custom_call_target="tpu_custom_call" | custom-call | flops 10737418240 | bytes 21474836 | tf_op jit(solution)/shard_map/pallas_call | solution.py:420
  760.2 17.9 %shard_map.267 = (bf16[4,2,2,256,2048]{4,3,2,1,0:T(8,128)(2,1)}, bf16[4,2,2,256,2048]{4,3,2,1,0:T(8,128)(2,1)}) custom-call(s32[2]{0:T(128)} %pad_add_fusion.6.table, bf16[2,8,1024]{2,1,0:T(8,128)(2,1)} %bitcast.407, bf16[2,8,1024]{2,1,0:T(8,128)(2,1)} %bitcast.408, ...), custom_call_target="tpu_custom_call", output_to_operand_aliasing={{0}: (5, {}), {1}: (6, {})} | custom-call | flops 10737418240 | bytes 21474836 | tf_op jit(solution)/shard_map/pallas_call | solution.py:420
  794.6 17.7 %shard_map.268 = (bf16[4,2,2,256,2048]{4,3,2,1,0:T(8,128)(2,1)}, bf16[4,2,2,256,2048]{4,3,2,1,0:T(8,128)(2,1)}) custom-call(s32[2]{0:T(128)} %pad_add_fusion.2.table, bf16[2,8,1024]{2,1,0:T(8,128)(2,1)} %bitcast.405, bf16[2,8,1024]{2,1,0:T(8,128)(2,1)} %bitcast.406, ...), custom_call_target="tpu_custom_call", output_to_operand_aliasing={{0}: (5, {}), {1}: (6, {})} | custom-call | flops 10737418240 | bytes 21474836 | tf_op jit(solution)/shard_map/pallas_call | solution.py:420
  812.4 17.7 %shard_map.269 = (bf16[4,2,2,256,2048]{4,3,2,1,0:T(8,128)(2,1)}, bf16[4,2,2,256,2048]{4,3,2,1,0:T(8,128)(2,1)}) custom-call(s32[2]{0:T(128)} %pad_add_fusion.table, bf16[2,8,1024]{2,1,0:T(8,128)(2,1)} %bitcast.403, bf16[2,8,1024]{2,1,0:T(8,128)(2,1)} %bitcast.404, ...), custom_call_target="tpu_custom_call", output_to_operand_aliasing={{0}: (5, {}), {1}: (6, {})} | custom-call | flops 10737418240 | bytes 21474836 | tf_op jit(solution)/shard_map/pallas_call | solution.py:420
  830.1 25.4 %collective-permute-done.62 = bf16[4,2,2,256,2048]{4,3,2,1,0:T(8,128)(2,1)S(1)} collective-permute-done((bf16[4,2,2,256,2048]{4,3,2,1,0:T(8,128)(2,1)}, bf16[4,2,2,256,2048]{4,3,2,1,0:T(8,128)(2,1)S(1)}, u32[]{:S(2)}, u32[]{:S(2)}) %collective-permute-start.62) | collective-permute-done | bytes 16777248 | tf_op jit(solution)/shard_map/ppermute | solution.py:466
  855.5 16.2 %add_convert_fusion = bf16[4,2,2,256,2048]{4,3,2,1,0:T(8,128)(2,1)} fusion(bf16[4,2,2,256,2048]{4,3,2,1,0:T(8,128)(2,1)S(1)} %collective-permute-done.62, bf16[4,2,2,256,2048]{4,3,2,1,0:T(8,128)(2,1)} %get-tuple-element.264), kind=kLoop, calls=%fused_computation.8 | loop fusion | flops 33554432 | bytes 50331648 | tf_op jit(solution)/shard_map/convert_element_type | solution.py:608
  876.3 16.0 %collective-permute-done.65 = bf16[128,2048]{1,0:T(8,128)(2,1)S(1)} collective-permute-done((bf16[128,2048]{1,0:T(8,128)(2,1)}, bf16[128,2048]{1,0:T(8,128)(2,1)S(1)}, u32[]{:S(2)}, u32[]{:S(2)}) %collective-permute-start.65) | collective-permute-done | bytes 524320 | tf_op jit(solution)/shard_map/ppermute | solution.py:466
  900.5 38.5 %collective-permute-done.69 = bf16[2,128,2048]{2,1,0:T(8,128)(2,1)S(1)} collective-permute-done((bf16[2,128,2048]{2,1,0:T(8,128)(2,1)}, bf16[2,128,2048]{2,1,0:T(8,128)(2,1)S(1)}, u32[]{:S(2)}, u32[]{:S(2)}) %collective-permute-start.69) | collective-permute-done | bytes 1048608 | tf_op jit(solution)/shard_map/ppermute | solution.py:466
  943.5 20.6 %collective-permute-done.70 = bf16[128,2048]{1,0:T(8,128)(2,1)S(1)} collective-permute-done((bf16[128,2048]{1,0:T(8,128)(2,1)S(1)}, bf16[128,2048]{1,0:T(8,128)(2,1)S(1)}, u32[]{:S(2)}, u32[]{:S(2)}) %collective-permute-start.70) | collective-permute-done | bytes 524320 | tf_op jit(solution)/shard_map/ppermute | solution.py:466
  966.7 23.7 %collective-permute-done.71 = bf16[256,2048]{1,0:T(8,128)(2,1)S(1)} collective-permute-done((bf16[256,2048]{1,0:T(8,128)(2,1)S(1)}, bf16[256,2048]{1,0:T(8,128)(2,1)S(1)}, u32[]{:S(2)}, u32[]{:S(2)}) %collective-permute-start.71) | collective-permute-done | bytes 1048608 | tf_op jit(solution)/shard_map/ppermute | solution.py:483
  999.6 32.4 %collective-permute-done.73.refs_2_ = bf16[256,2048]{1,0:T(8,128)(2,1)S(1)} collective-permute-done((bf16[256,2048]{1,0:T(8,128)(2,1)S(1)}, bf16[256,2048]{1,0:T(8,128)(2,1)S(1)}, u32[]{:S(2)}, u32[]{:S(2)}) %collective-permute-start.73) | collective-permute-done | bytes 1048608 | tf_op jit(solution)/shard_map/ppermute | solution.py:466
  1032.0 13.5 %shard_map.270 = (f32[8,2048,256]{2,1,0:T(8,128)}, f32[8,2048,256]{2,1,0:T(8,128)}, f32[8,256,2048]{2,1,0:T(8,128)}) custom-call(bf16[8,256,2048]{2,1,0:T(8,128)(2,1)} %get-tuple-element.312.refs_0_, bf16[8,256,2048]{2,1,0:T(8,128)(2,1)} %get-tuple-element.313.refs_1_, bf16[8,256,2048]{2,1,0:T(8,128)(2,1)} %get-tuple-element.314.refs_2_, ...), custom_call_target="tpu_custom_call" | custom-call | flops 6442450944 | bytes 12884901 | tf_op jit(solution)/shard_map/pallas_call | solution.py:451
  1045.5 13.5 %shard_map.271 = (f32[8,2048,256]{2,1,0:T(8,128)}, f32[8,2048,256]{2,1,0:T(8,128)}, f32[8,256,2048]{2,1,0:T(8,128)}) custom-call(bf16[8,256,2048]{2,1,0:T(8,128)(2,1)} %get-tuple-element.312.refs_0_, bf16[8,256,2048]{2,1,0:T(8,128)(2,1)} %get-tuple-element.313.refs_1_, ...), custom_call_target="tpu_custom_call", output_to_operand_aliasing={{0}: (16, {}), {1}: (17, {}), {2}: (18, {})} | custom-call | flops 6442450944 | bytes 12884901 | tf_op jit(solution)/shard_map/pallas_call | solution.py:451
  1153.2 21.3 %collective-permute-done.85 = f32[2304]{0:T(1024)S(1)} collective-permute-done((f32[2304]{0:T(1024)S(1)}, f32[2304]{0:T(1024)S(1)}, u32[]{:S(2)}, u32[]{:S(2)}) %collective-permute-start.85) | collective-permute-done | bytes 9248 | tf_op jit(solution)/shard_map/ppermute | solution.py:466
  1201.3 14.9 %collective-permute-done.89 = bf16[256,1536]{1,0:T(8,128)(2,1)} collective-permute-done((bf16[256,1536]{1,0:T(8,128)(2,1)}, bf16[256,1536]{1,0:T(8,128)(2,1)}, u32[]{:S(2)}, u32[]{:S(2)}) %collective-permute-start.89) | collective-permute-done | bytes 786464 | tf_op jit(solution)/shard_map/ppermute | solution.py:483
  (667 shorter events, 571.9 us)
Async XLA Ops:
  7.2 359.8 %all-gather.2.cloned.1.call-start = ((), (), s32[]{:S(2)}) async-start(), calls=%async_computation.2 | async-start | bytes 34603008 | tf_op jit(solution)/shard_map/all_gather | solution.py:893
  105.7 1024.5 %reduce-scatter.3.cloned.1.call-start = ((), (), s32[]{:S(2)}) async-start(), calls=%async_computation.3 | async-start | bytes 20971520 | tf_op jit(solution)/shard_map/reduce_scatter | solution.py:840
  337.7 49.7 %collective-permute-start.35 = (bf16[128,2048]{1,0:T(8,128)(2,1)}, bf16[128,2048]{1,0:T(8,128)(2,1)}, u32[]{:S(2)}, u32[]{:S(2)}) collective-permute-start(bf16[128,2048]{1,0:T(8,128)(2,1)} %get-tuple-element.409), channel_id=1, source_target_pairs={{0,2},{1,3},{2,0},{3,1},{4,6},{5,7},{6,4},{7,5},{8,10},{9,11},{10,... | collective-permute-start | bytes 1572872 | tf_op jit(solution)/shard_map/ppermute | solution.py:466
  387.4 114.3 %collective-permute-start.29 = (bf16[8,128,2048]{2,1,0:T(8,128)(2,1)}, bf16[8,128,2048]{2,1,0:T(8,128)(2,1)}, u32[]{:S(2)}, u32[]{:S(2)}) collective-permute-start(bf16[8,128,2048]{2,1,0:T(8,128)(2,1)} %pad_maximum_fusion.1.own), channel_id=1, source_target_pairs={{0,1},{1,0},{2,3},{3,2},{4,5},{5,4},{6,7},{7,6},{8,9},{9,8},{10,11... | collective-permute-start | bytes 12582920 | tf_op jit(solution)/shard_map/ppermute | solution.py:466
  426.9 59.7 %collective-permute-start.48 = (bf16[2,128,2048]{2,1,0:T(8,128)(2,1)S(1)}, bf16[2,128,2048]{2,1,0:T(8,128)(2,1)}, u32[]{:S(2)}, u32[]{:S(2)}) collective-permute-start(bf16[2,128,2048]{2,1,0:T(8,128)(2,1)S(1)} %pad_maximum_fusion.16), channel_id=1, source_target_pairs={{0,4},{4,0},{8,12},{12,8},{16,20},{20,16},{24,28},{28,24},{1,5},{5... | collective-permute-start | bytes 3145736 | tf_op jit(solution)/shard_map/ppermute | solution.py:466
  427.3 66.7 %collective-permute-start.47 = (bf16[2,128,2048]{2,1,0:T(8,128)(2,1)S(1)}, bf16[2,128,2048]{2,1,0:T(8,128)(2,1)}, u32[]{:S(2)}, u32[]{:S(2)}) collective-permute-start(bf16[2,128,2048]{2,1,0:T(8,128)(2,1)S(1)} %pad_maximum_fusion.15), channel_id=1, source_target_pairs={{0,2},{1,3},{2,0},{3,1},{4,6},{5,7},{6,4},{7,5},{8,10},{9,11},{10,... | collective-permute-start | bytes 3145736 | tf_op jit(solution)/shard_map/ppermute | solution.py:466
  486.6 73.8 %collective-permute-start.38 = (bf16[8,128,2048]{2,1,0:T(8,128)(2,1)}, bf16[8,128,2048]{2,1,0:T(8,128)(2,1)}, u32[]{:S(2)}, u32[]{:S(2)}) collective-permute-start(bf16[8,128,2048]{2,1,0:T(8,128)(2,1)} %pad_maximum_fusion.2.own), channel_id=1, source_target_pairs={{0,1},{1,0},{2,3},{3,2},{4,5},{5,4},{6,7},{7,6},{8,9},{9,8},{10,11... | collective-permute-start | bytes 12582920 | tf_op jit(solution)/shard_map/ppermute | solution.py:466
  539.5 80.1 %collective-permute-start.30 = (bf16[2,2,256,2048]{3,2,1,0:T(8,128)(2,1)}, bf16[2,2,256,2048]{3,2,1,0:T(8,128)(2,1)}, u32[]{:S(2)}, u32[]{:S(2)}) collective-permute-start(bf16[2,2,256,2048]{3,2,1,0:T(8,128)(2,1)} %get-tuple-element.203), channel_id=1, source_target_pairs={{0,1},{1,0},{2,3},{3,2},{4,5},{5,4},{6,7},{7,6},{8,9},{9,8},{10,11... | collective-permute-start | bytes 12582920 | tf_op jit(solution)/shard_map/ppermute | solution.py:466
  560.4 69.7 %collective-permute-start.49 = (bf16[8,128,2048]{2,1,0:T(8,128)(2,1)}, bf16[8,128,2048]{2,1,0:T(8,128)(2,1)}, u32[]{:S(2)}, u32[]{:S(2)}) collective-permute-start(bf16[8,128,2048]{2,1,0:T(8,128)(2,1)} %pad_maximum_fusion.3.own), channel_id=1, source_target_pairs={{0,1},{1,0},{2,3},{3,2},{4,5},{5,4},{6,7},{7,6},{8,9},{9,8},{10,11... | collective-permute-start | bytes 12582920 | tf_op jit(solution)/shard_map/ppermute | solution.py:466
  598.7 69.5 %collective-permute-start.39 = (bf16[2,2,256,2048]{3,2,1,0:T(8,128)(2,1)}, bf16[2,2,256,2048]{3,2,1,0:T(8,128)(2,1)}, u32[]{:S(2)}, u32[]{:S(2)}) collective-permute-start(bf16[2,2,256,2048]{3,2,1,0:T(8,128)(2,1)} %get-tuple-element.216), channel_id=1, source_target_pairs={{0,1},{1,0},{2,3},{3,2},{4,5},{5,4},{6,7},{7,6},{8,9},{9,8},{10,11... | collective-permute-start | bytes 12582920 | tf_op jit(solution)/shard_map/ppermute | solution.py:466
  619.6 65.7 %collective-permute-start.60 = (bf16[8,128,2048]{2,1,0:T(8,128)(2,1)}, bf16[8,128,2048]{2,1,0:T(8,128)(2,1)}, u32[]{:S(2)}, u32[]{:S(2)}) collective-permute-start(bf16[8,128,2048]{2,1,0:T(8,128)(2,1)} %pad_maximum_fusion.4.own), channel_id=1, source_target_pairs={{0,1},{1,0},{2,3},{3,2},{4,5},{5,4},{6,7},{7,6},{8,9},{9,8},{10,11... | collective-permute-start | bytes 12582920 | tf_op jit(solution)/shard_map/ppermute | solution.py:466
  628.3 48.2 %collective-permute-start.31 = (bf16[2,128,2048]{2,1,0:T(8,128)(2,1)}, bf16[2,128,2048]{2,1,0:T(8,128)(2,1)}, u32[]{:S(2)}, u32[]{:S(2)}) collective-permute-start(bf16[2,128,2048]{2,1,0:T(8,128)(2,1)} %fusion.58), channel_id=1, source_target_pairs={{0,2},{1,3},{2,0},{3,1},{4,6},{5,7},{6,4},{7,5},{8,10},{9,11},{10,... | collective-permute-start | bytes 3145736 | tf_op jit(solution)/shard_map/ppermute | solution.py:466
  629.7 49.4 %collective-permute-start.32 = (bf16[2,128,2048]{2,1,0:T(8,128)(2,1)}, bf16[2,128,2048]{2,1,0:T(8,128)(2,1)}, u32[]{:S(2)}, u32[]{:S(2)}) collective-permute-start(bf16[2,128,2048]{2,1,0:T(8,128)(2,1)} %get-tuple-element.207), channel_id=1, source_target_pairs={{0,4},{4,0},{8,12},{12,8},{16,20},{20,16},{24,28},{28,24},{1,5},{5... | collective-permute-start | bytes 3145736 | tf_op jit(solution)/shard_map/ppermute | solution.py:466
  668.0 62.8 %collective-permute-start.50 = (bf16[2,2,256,2048]{3,2,1,0:T(8,128)(2,1)}, bf16[2,2,256,2048]{3,2,1,0:T(8,128)(2,1)}, u32[]{:S(2)}, u32[]{:S(2)}) collective-permute-start(bf16[2,2,256,2048]{3,2,1,0:T(8,128)(2,1)} %get-tuple-element.234), channel_id=1, source_target_pairs={{0,1},{1,0},{2,3},{3,2},{4,5},{5,4},{6,7},{7,6},{8,9},{9,8},{10,11... | collective-permute-start | bytes 12582920 | tf_op jit(solution)/shard_map/ppermute | solution.py:466
  681.6 42.1 %collective-permute-start.41 = (bf16[128,2048]{1,0:T(8,128)(2,1)}, bf16[128,2048]{1,0:T(8,128)(2,1)}, u32[]{:S(2)}, u32[]{:S(2)}) collective-permute-start(bf16[128,2048]{1,0:T(8,128)(2,1)} %get-tuple-element.220), channel_id=1, source_target_pairs={{0,2},{1,3},{2,0},{3,1},{4,6},{5,7},{6,4},{7,5},{8,10},{9,11},{10,... | collective-permute-start | bytes 1572872 | tf_op jit(solution)/shard_map/ppermute | solution.py:466
  682.2 42.8 %collective-permute-start.40 = (bf16[128,2048]{1,0:T(8,128)(2,1)}, bf16[128,2048]{1,0:T(8,128)(2,1)S(1)}, u32[]{:S(2)}, u32[]{:S(2)}) collective-permute-start(bf16[128,2048]{1,0:T(8,128)(2,1)} %get-tuple-element.218), channel_id=1, source_target_pairs={{0,4},{4,0},{8,12},{12,8},{16,20},{20,16},{24,28},{28,24},{1,5},{5... | collective-permute-start | bytes 1572872 | tf_op jit(solution)/shard_map/ppermute | solution.py:466
  683.8 41.4 %collective-permute-start.42 = (bf16[2,128,2048]{2,1,0:T(8,128)(2,1)}, bf16[2,128,2048]{2,1,0:T(8,128)(2,1)}, u32[]{:S(2)}, u32[]{:S(2)}) collective-permute-start(bf16[2,128,2048]{2,1,0:T(8,128)(2,1)} %fusion.62), channel_id=1, source_target_pairs={{0,2},{1,3},{2,0},{3,1},{4,6},{5,7},{6,4},{7,5},{8,10},{9,11},{10,... | collective-permute-start | bytes 3145736 | tf_op jit(solution)/shard_map/ppermute | solution.py:466
  685.2 42.8 %collective-permute-start.43 = (bf16[2,128,2048]{2,1,0:T(8,128)(2,1)}, bf16[2,128,2048]{2,1,0:T(8,128)(2,1)}, u32[]{:S(2)}, u32[]{:S(2)}) collective-permute-start(bf16[2,128,2048]{2,1,0:T(8,128)(2,1)} %get-tuple-element.224), channel_id=1, source_target_pairs={{0,4},{4,0},{8,12},{12,8},{16,20},{20,16},{24,28},{28,24},{1,5},{5... | collective-permute-start | bytes 3145736 | tf_op jit(solution)/shard_map/ppermute | solution.py:466
  723.7 63.4 %collective-permute-start.61 = (bf16[2,2,256,2048]{3,2,1,0:T(8,128)(2,1)}, bf16[2,2,256,2048]{3,2,1,0:T(8,128)(2,1)}, u32[]{:S(2)}, u32[]{:S(2)}) collective-permute-start(bf16[2,2,256,2048]{3,2,1,0:T(8,128)(2,1)} %get-tuple-element.252), channel_id=1, source_target_pairs={{0,1},{1,0},{2,3},{3,2},{4,5},{5,4},{6,7},{7,6},{8,9},{9,8},{10,11... | collective-permute-start | bytes 12582920 | tf_op jit(solution)/shard_map/ppermute | solution.py:466
  740.7 41.0 %collective-permute-start.53 = (bf16[2,128,2048]{2,1,0:T(8,128)(2,1)}, bf16[2,128,2048]{2,1,0:T(8,128)(2,1)}, u32[]{:S(2)}, u32[]{:S(2)}) collective-permute-start(bf16[2,128,2048]{2,1,0:T(8,128)(2,1)} %fusion.66), channel_id=1, source_target_pairs={{0,2},{1,3},{2,0},{3,1},{4,6},{5,7},{6,4},{7,5},{8,10},{9,11},{10,... | collective-permute-start | bytes 3145736 | tf_op jit(solution)/shard_map/ppermute | solution.py:466
  742.1 42.3 %collective-permute-start.54 = (bf16[2,128,2048]{2,1,0:T(8,128)(2,1)}, bf16[2,128,2048]{2,1,0:T(8,128)(2,1)}, u32[]{:S(2)}, u32[]{:S(2)}) collective-permute-start(bf16[2,128,2048]{2,1,0:T(8,128)(2,1)} %get-tuple-element.242), channel_id=1, source_target_pairs={{0,4},{4,0},{8,12},{12,8},{16,20},{20,16},{24,28},{28,24},{1,5},{5... | collective-permute-start | bytes 3145736 | tf_op jit(solution)/shard_map/ppermute | solution.py:466
  871.7 422.9 %reduce-scatter.5.cloned.1.call-start = ((), (), s32[]{:S(2)}) async-start(), calls=%async_computation.4 | async-start | bytes 5242880 | tf_op jit(solution)/shard_map/reduce_scatter | solution.py:841
  874.5 64.5 %collective-permute-start.69 = (bf16[2,128,2048]{2,1,0:T(8,128)(2,1)}, bf16[2,128,2048]{2,1,0:T(8,128)(2,1)S(1)}, u32[]{:S(2)}, u32[]{:S(2)}) collective-permute-start(bf16[2,128,2048]{2,1,0:T(8,128)(2,1)} %get-tuple-element.274), channel_id=1, source_target_pairs={{0,4},{4,0},{8,12},{12,8},{16,20},{20,16},{24,28},{28,24},{1,5},{5... | collective-permute-start | bytes 3145736 | tf_op jit(solution)/shard_map/ppermute | solution.py:466
  874.9 65.7 %collective-permute-start.67 = (bf16[2,128,2048]{2,1,0:T(8,128)(2,1)}, bf16[2,128,2048]{2,1,0:T(8,128)(2,1)S(1)}, u32[]{:S(2)}, u32[]{:S(2)}) collective-permute-start(bf16[2,128,2048]{2,1,0:T(8,128)(2,1)} %fusion.70), channel_id=1, source_target_pairs={{0,2},{1,3},{2,0},{3,1},{4,6},{5,7},{6,4},{7,5},{8,10},{9,11},{10,... | collective-permute-start | bytes 3145736 | tf_op jit(solution)/shard_map/ppermute | solution.py:466
  900.4 65.8 %collective-permute-start.66 = (bf16[256,2048]{1,0:T(8,128)(2,1)S(1)}, bf16[256,2048]{1,0:T(8,128)(2,1)S(1)}, u32[]{:S(2)}, u32[]{:S(2)}) collective-permute-start(bf16[256,2048]{1,0:T(8,128)(2,1)S(1)} %add_convert_fusion.6), channel_id=1, source_target_pairs={{0,8},{4,12},{8,16},{12,20},{16,24},{20,28},{24,0},{28,4},{1,9},{5... | collective-permute-start | bytes 3145736 | tf_op jit(solution)/shard_map/ppermute | solution.py:483
  999.6 59.4 %collective-permute-start.72 = (bf16[256,2048]{1,0:T(8,128)(2,1)S(1)}, bf16[256,2048]{1,0:T(8,128)(2,1)}, u32[]{:S(2)}, u32[]{:S(2)}) collective-permute-start(bf16[256,2048]{1,0:T(8,128)(2,1)S(1)} %fusion.94.refs_0_), channel_id=1, source_target_pairs={{0,1},{1,0},{2,3},{3,2},{4,5},{5,4},{6,7},{7,6},{8,9},{9,8},{10,11... | collective-permute-start | bytes 3145736 | tf_op jit(solution)/shard_map/ppermute | solution.py:466
  1122.6 54.6 %collective-permute-start.76 = (bf16[256,2048]{1,0:T(8,128)(2,1)}, bf16[256,2048]{1,0:T(8,128)(2,1)}, u32[]{:S(2)}, u32[]{:S(2)}) collective-permute-start(bf16[256,2048]{1,0:T(8,128)(2,1)} %get-tuple-element.365), channel_id=1, source_target_pairs={{0,1},{1,0},{2,3},{3,2},{4,5},{5,4},{6,7},{7,6},{8,9},{9,8},{10,11... | collective-permute-start | bytes 3145736 | tf_op jit(solution)/shard_map/ppermute | solution.py:466
  1144.2 87.4 %collective-permute-start.75 = (bf16[256,2048]{1,0:T(8,128)(2,1)}, bf16[256,2048]{1,0:T(8,128)(2,1)}, u32[]{:S(2)}, u32[]{:S(2)}) collective-permute-start(bf16[256,2048]{1,0:T(8,128)(2,1)} %get-tuple-element.364), channel_id=1, source_target_pairs={{0,1},{1,0},{2,3},{3,2},{4,5},{5,4},{6,7},{7,6},{8,9},{9,8},{10,11... | collective-permute-start | bytes 3145736 | tf_op jit(solution)/shard_map/ppermute | solution.py:466
  1144.6 55.0 %collective-permute-start.90 = (bf16[256,1536]{1,0:T(8,128)(2,1)}, bf16[256,1536]{1,0:T(8,128)(2,1)}, u32[]{:S(2)}, u32[]{:S(2)}) collective-permute-start(bf16[256,1536]{1,0:T(8,128)(2,1)} %get-tuple-element.360), channel_id=1, source_target_pairs={{0,4},{4,0},{8,12},{12,8},{16,20},{20,16},{24,28},{28,24},{1,5},{5... | collective-permute-start | bytes 2359304 | tf_op jit(solution)/shard_map/ppermute | solution.py:466
  1182.1 51.0 %collective-permute-start.77 = (bf16[256,2048]{1,0:T(8,128)(2,1)}, bf16[256,2048]{1,0:T(8,128)(2,1)S(1)}, u32[]{:S(2)}, u32[]{:S(2)}) collective-permute-start(bf16[256,2048]{1,0:T(8,128)(2,1)} %fusion.25), channel_id=1, source_target_pairs={{0,2},{1,3},{2,0},{3,1},{4,6},{5,7},{6,4},{7,5},{8,10},{9,11},{10,... | collective-permute-start | bytes 3145736 | tf_op jit(solution)/shard_map/ppermute | solution.py:466
  1198.1 61.1 %collective-permute-start.92 = (bf16[256,1536]{1,0:T(8,128)(2,1)S(1)}, bf16[256,1536]{1,0:T(8,128)(2,1)S(1)}, u32[]{:S(2)}, u32[]{:S(2)}) collective-permute-start(bf16[256,1536]{1,0:T(8,128)(2,1)S(1)} %copy-done.63), channel_id=1, source_target_pairs={{0,4},{4,0},{8,12},{12,8},{16,20},{20,16},{24,28},{28,24},{1,5},{5... | collective-permute-start | bytes 2359304 | tf_op jit(solution)/shard_map/ppermute | solution.py:466
  1222.1 69.5 %collective-permute-start.94 = (bf16[256,1536]{1,0:T(8,128)(2,1)}, bf16[256,1536]{1,0:T(8,128)(2,1)}, u32[]{:S(2)}, u32[]{:S(2)}) collective-permute-start(bf16[256,1536]{1,0:T(8,128)(2,1)} %get-tuple-element.358), channel_id=1, source_target_pairs={{0,4},{4,0},{8,12},{12,8},{16,20},{20,16},{24,28},{28,24},{1,5},{5... | collective-permute-start | bytes 2359304 | tf_op jit(solution)/shard_map/ppermute | solution.py:466
  (185 other events, 3250.2 us)
Sparse Core Ops, SparseCore 0:
  105.8 214.6 all-gather.1
  871.8 213.8 reduce-scatter.2
  1130.3 94.6 reduce-scatter.4

commit v7 on v6

--- a/solution.py
+++ b/solution.py
@@ -278,8 +278,9 @@
             slots_to_rows(pick.at[pack], grads, rows_own, rows_other, pack)
 
 
-def mix_kernel(packs, steps, capacity, table, places, gates, hidden, down, *refs):
-    rows_own, rows_other, results, pick = refs[-4:]
+def mix_kernel(
+    packs, steps, capacity, table, places, gates, hidden, down, rows_own, rows_other, results, pick
+):
     step = pl.program_id(0)
 
     @pl.when(step < steps)
@@ -291,8 +292,7 @@
     @pl.when(step >= steps)
     def _():
         select_rows(places, gates, pick, capacity)
-        pack = (step - steps) ^ table[1]
-        slots_to_rows(pick, results, rows_own.at[0], rows_other.at[0], pack)
+        slots_to_rows(pick, results, rows_own, rows_other, (step - steps) ^ table[0])
 
 
 def weight_kernel(planes, *refs):
@@ -407,25 +407,22 @@
     )(places, own, other, both, grad_hidden)
 
 
-def mix_rows(table, places, gates, hidden, down, planes, capacity, earlier=()):
+def mix_rows(table, places, gates, hidden, down, capacity):
     packs, _, seq_len = places.shape
     experts, hidden_width, width = down.shape
     group = math.gcd(experts, GROUP)
     steps = experts // group
     first, last = staged(0, steps), staged(steps, packs)
-    part = shape_of((planes, packs, 2, seq_len // 4, width), jnp.bfloat16)
-    out_spec = pl.BlockSpec(
-        (1, 1) + part.shape[2:], lambda step, numbers: (numbers[0], last(step), 0, 0, 0)
-    )
+    listed = lambda step, numbers: numbers[1] * steps + first(step)
+    part = shape_of((packs, 2, seq_len // 4, width), jnp.bfloat16)
     return call(
         functools.partial(mix_kernel, packs, steps, capacity),
         packs + steps,
         [
             block(places.shape, last), block(gates.shape, last),
-            block(hidden.shape, first, group), block(down.shape, first, group),
-        ]
-        + [pl.BlockSpec(memory_space=pl.ANY)] * len(earlier),
-        [out_spec] * 2,
+            block(hidden.shape, listed, group), block(down.shape, first, group),
+        ],
+        [block(part.shape, last)] * 2,
         [part, part],
         [
             pltpu.VMEM((experts, packs, capacity, width), jnp.bfloat16),
@@ -433,8 +430,7 @@
         ],
         2 * experts * packs * capacity * width * (seq_len + hidden_width),
         1,
-        aliases={5 + index: index for index in range(len(earlier))},
-    )(table, places, gates, hidden, down, *earlier)
+    )(table, places, gates, hidden, down)
 
 
 def weight_grads(first, count, slots, hidden, grads, above, earlier=()):
@@ -483,15 +479,36 @@
     return lax.ppermute(values, DP, [(i, (i + 2) % count) for i in range(count)])
 
 
-def spread_plane(values, beside):
+def spread_all(values, small, work):
+    planes = lax.axis_size("plane")
     half_rows = values.shape[0] // 2
-    upper, lower = values[:half_rows], values[half_rows:]
-    near_upper = jnp.stack([upper, far_pack(upper)])
-    near_lower = jnp.stack([lower, far_side(lower)])
-    near, made = beside((near_upper, near_lower))
-    own = jnp.concatenate([*near, far_side(near[0]), far_pack(near[1])])
-    own, made = lax.optimization_barrier((own, made))
-    return own, far_core(own), made
+    first = lambda rows: (far_pack(rows[:half_rows]), far_side(rows[half_rows:]))
+    small, values = tied(small, values)
+    (across_pack, across_side), following = lax.optimization_barrier(
+        (first(values), next_plane(values))
+    )
+    pieces, made = [], []
+    for plane in range(planes):
+        upper = jnp.stack([values[:half_rows], across_pack])
+        lower = jnp.stack([values[half_rows:], across_side])
+        small, (upper, lower, values) = tied(small, (upper, lower, following))
+        moved = [
+            far_side(upper),
+            far_pack(lower),
+            first(values) if plane + 1 < planes else ((), ()),
+            next_plane(values) if plane + 2 < planes else (),
+            far_core(pieces[-1]) if plane else (),
+            work(plane, small),
+        ]
+        upper_far, lower_far, (across_pack, across_side), following, other, result = (
+            lax.optimization_barrier(moved)
+        )
+        if plane:
+            pieces[-1] = (pieces[-1], other)
+        made.append(result)
+        pieces.append(jnp.concatenate([upper, lower, upper_far, lower_far]))
+    pieces[-1] = (pieces[-1], far_core(pieces[-1]))
+    return pieces, made
 
 
 def plane_order():
@@ -538,17 +555,6 @@
     )(order, *pieces)
 
 
-def gather_packs(values, by_column=False):
-    pieces = []
-    planes = lax.axis_size("plane")
-    for plane in range(planes):
-        moved = [far_pack(values), next_plane(values) if plane + 1 < planes else ()]
-        across, following = lax.optimization_barrier(moved)
-        pieces += [values, across]
-        values = following
-    return laid(pieces, plane_order(), by_column)
-
-
 def fold_packs(values):
     order = plane_order()
     take = lambda index: lax.dynamic_index_in_dim(values, order[index], 0, keepdims=False)
@@ -579,20 +585,49 @@
     return added(near, far_side(far), jnp.float32)
 
 
-def gather_both(weights, rows):
-    pieces, row_pieces, values = [], [rows], weights
+def fold_both(weights, rows):
+    order = plane_order()
+    planes = weights.shape[0] // 2
+    take = lambda index: lax.dynamic_index_in_dim(weights, order[index], 0, keepdims=False)
+    split = rows.astype(jnp.bfloat16).reshape((4, -1) + rows.shape[1:])
+    mine = lax.axis_index(TENSOR)
+    pick = lambda bits: lax.dynamic_index_in_dim(split, mine ^ bits, 0, keepdims=False)
+    summed, total = None, None
+    for turn, plane in enumerate([*range(1, planes), 0]):
+        moved = [far_pack(take(2 * plane + 1)), () if summed is None else next_plane(summed)]
+        if turn == 0:
+            moved += [far_core(pick(3)), far_core(pick(1))]
+        if turn == 1:
+            moved += [far_side(far)]
+        across, passed, *arrived = lax.optimization_barrier(moved)
+        if turn == 0:
+            far, close = added(pick(2), arrived[0]), added(pick(0), arrived[1])
+        if turn == 1:
+            total = added(close, arrived[0], jnp.float32)
+        near = added(take(2 * plane), across)
+        kind = jnp.float32 if turn + 1 == planes else jnp.bfloat16
+        summed = near if turn == 0 else added(passed, near, kind)
+    return summed, total
+
+
+def gather_both(weights, outer, rows):
+    pieces, outer_pieces, row_pieces, values = [], [], [rows], (weights, outer)
     planes = lax.axis_size("plane")
     for plane in range(planes):
-        moved = [far_pack(values), next_plane(values) if plane + 1 < planes else ()]
+        moved = [tuple(far_pack(value) for value in values), ()]
+        if plane + 1 < planes:
+            moved[1] = tuple(next_plane(value) for value in values)
         if plane == 0:
             moved += [far_core(rows), far_side(rows)]
         if plane == 1:
             moved += [far_core(row_pieces[2])]
         across, following, *arrived = lax.optimization_barrier(moved)
-        pieces += [values, across]
+        pieces += [values[0], across[0]]
+        outer_pieces += [values[1], across[1]]
         row_pieces += arrived
         values = following
-    return laid(pieces, plane_order()), laid_sides(row_pieces)
+    order = plane_order()
+    return laid(pieces, order), laid(outer_pieces, order, True), laid_sides(row_pieces)
 
 
 def sum_everywhere(values):
@@ -616,18 +651,6 @@
         added(own[0, :, lower], arrived[0, :, lower]),
         added(own[:, 1, upper], arrived[:, 1, upper]),
         added(own[1, :, lower], arrived[1, :, lower]),
-    )
-
-
-def fold_second(upper, lower, upper_far, lower_far):
-    upper = added(upper, far_side(upper_far))
-    lower = added(lower, far_pack(lower_far))
-    return upper[0], lower[0], upper[1], lower[1]
-
-
-def fold_third(upper, lower, upper_far, lower_far):
-    return jnp.concatenate(
-        [added(upper, far_pack(upper_far)), added(lower, far_side(lower_far))]
     )
 
 
@@ -747,45 +770,54 @@
 
 class Folding:
     def __init__(self, order):
-        self.order, self.waiting, self.fresh = order, {}, {}
+        self.order, self.planes, self.ready = order, {}, {}
         self.summed, self.count = None, 0
 
     def begin(self, plane, own, other):
-        self.fresh[plane] = (0, (own, far_core(other)))
-
-    def step(self, small):
-        made = {}
-        for plane, (stage, values) in self.waiting.items():
-            if stage < 3:
-                made[plane] = (fold_first, fold_second, fold_third)[stage](*values)
-        ready = {plane: values for plane, (stage, values) in self.waiting.items() if stage == 3}
-        passed = None
-        if self.order[self.count] in ready:
-            passed = self.passed_on(ready[self.order[self.count]])
-            del self.waiting[self.order[self.count]]
+        self.planes[plane] = (0, (own, other))
+
+    def turn(self, small, work):
+        small, (planes, summed) = tied(
+            small, ({plane: values for plane, (_, values) in self.planes.items()}, self.summed)
+        )
+        sent = {}
+        for plane, values in planes.items():
+            stage = self.planes[plane][0]
+            if stage == 0:
+                sent[plane] = (far_core(values[1]),)
+            elif stage == 1:
+                sent[plane] = (far_side(values[2]), far_pack(values[3]))
+            else:
+                sent[plane] = (far_pack(values[2]), far_side(values[3]))
+        passed = None if summed is None else next_plane(summed)
+        sent, passed, result = lax.optimization_barrier((sent, passed, work(small)))
+        for plane, values in planes.items():
+            stage, arrived = self.planes[plane][0], sent[plane]
+            if stage == 0:
+                made = fold_first(values[0], *arrived)
+            elif stage == 1:
+                upper, lower = added(values[0], arrived[0]), added(values[1], arrived[1])
+                made = (upper[0], lower[0], upper[1], lower[1])
+            else:
+                self.ready[plane] = jnp.concatenate(
+                    [added(values[0], arrived[0]), added(values[1], arrived[1])]
+                )
+            if stage < 2:
+                self.planes[plane] = (stage + 1, made)
+            else:
+                del self.planes[plane]
+        following = self.order[self.count] if self.count < len(self.order) else None
+        if following in self.ready:
+            last = self.count + 1 == len(self.order)
+            self.summed = self.ready[following]
+            if passed is not None:
+                kind = jnp.float32 if last else jnp.bfloat16
+                self.summed = added(passed, self.summed, kind)
             self.count += 1
-        small, (made, passed) = tied(small, (made, passed))
-        self.waiting.update(self.fresh)
-        self.fresh = {}
-        for plane, values in made.items():
-            self.waiting[plane] = (self.waiting[plane][0] + 1, values)
-        if passed is not None:
-            self.summed = passed
-        return small
-
-    def passed_on(self, values):
-        kind = jnp.float32 if self.count + 1 == len(self.order) else jnp.bfloat16
-        return values if self.summed is None else added(next_plane(self.summed), values, kind)
-
-    def finish(self):
-        self.waiting.update(self.fresh)
-        for plane in self.order[self.count :]:
-            stage, values = self.waiting[plane]
-            for fold in (fold_first, fold_second, fold_third)[stage:]:
-                values = fold(*values)
-            self.summed = self.passed_on(values)
-            self.count += 1
-        return self.summed
+        return result
+
+    def done(self):
+        return self.count == len(self.order)
 
 
 def experts_by_gather(second_in, all_cot, places, gates, w_gate, w_up, w_down, capacity):
@@ -802,44 +834,85 @@
         return split.reshape(values.shape)
 
     near_places = as_met(places, pack_order, quarter_order)
-    plane_index = pack_order[::2] // 2
-    whole_order = (plane_index[:, None] * 2 + jnp.arange(2, dtype=jnp.int32)).reshape(-1)
     core_order = lax.axis_index("core") ^ jnp.arange(tensor_count, dtype=jnp.int32)
-    mix_places = as_met(places, whole_order, core_order)
-    mix_gates = as_met(gates, whole_order, core_order)
+    mix_places = as_met(places, jnp.arange(packs, dtype=jnp.int32), core_order)
+    mix_gates = as_met(gates, jnp.arange(packs, dtype=jnp.int32), core_order)
     w_both = jnp.concatenate([w_gate, w_up], axis=2)
-    pieces, travelling = [], second_in
+    pairs = [slice(plane * 2, plane * 2 + 2) for plane in range(planes)]
+
+    def cot_work(plane, order):
+        return cot_slots(order[pairs[plane]], places, gates, all_cot, w_down, capacity)
+
+    pieces, made = spread_all(second_in, pack_order, cot_work)
+    order = [*range(1, planes), 0]
+    kept, parts, folding = {}, {}, Folding(order)
+
+    def row_work(plane, near):
+        return row_slots(near, *pieces[plane], w_both, made[plane][1], capacity)
+
     for plane in range(planes):
-        travelling = next_plane(travelling) if plane else travelling
-
-        def beside(near, listed=pack_order[plane * 2 : plane * 2 + 2]):
-            listed, near = tied(listed, near)
-            return near, cot_slots(listed, places, gates, all_cot, w_down, capacity)
-
-        pieces.append(spread_plane(travelling, beside))
-    pairs = [slice(plane * 2, plane * 2 + 2) for plane in range(planes)]
-    order = [*range(1, planes), 0]
-    kept, folding = {}, Folding(order)
-    for plane in range(planes):
+        near = near_places[pairs[plane]]
+        if plane:
+            result = folding.turn(near, functools.partial(row_work, plane))
+        else:
+            result = row_work(plane, near)
+        slots, hidden, above, *part = result
+        folding.begin(plane, *part)
+        kept[plane] = (slots, hidden, made[plane][0], above)
+    hidden_all = jnp.concatenate([kept[plane][1] for plane in range(planes)])
+    tables = jnp.stack(
+        [
+            jnp.stack([lax.axis_index("pack"), (lax.axis_index("plane") + planes - plane) % planes])
+            for plane in range(planes)
+        ]
+    )
+
+    def mix_work(plane, table):
         pair = pairs[plane]
-        own, other, (grad_slots, grad_hidden) = pieces[plane]
-        near = folding.step(near_places[pair]) if plane else near_places[pair]
-        slots, hidden, above, *part = row_slots(near, own, other, w_both, grad_hidden, capacity)
-        folding.begin(plane, *part)
-        kept[plane] = (slots, hidden, grad_slots, above)
-    mixed = ()
-    for index, plane in enumerate(order):
-        pair = pairs[plane]
-        near = mix_places[pair] if index % 2 else folding.step(mix_places[pair])
-        table = jnp.stack([plane_index[plane], lax.axis_index("pack")])
-        mixed = mix_rows(
-            table, near, mix_gates[pair], kept[plane][1], w_down, planes, capacity, mixed
-        )
-    own, other = mixed
-    whole = added(own, far_core(other)).reshape(planes, -1, own.shape[-1])
-    whole = lax.psum_scatter(whole, ("pack", "side"), scatter_dimension=1, tiled=True)
-    whole = lax.psum_scatter(whole, "plane", scatter_dimension=0, tiled=True)
-    return folding.finish(), whole[0].astype(jnp.float32), [kept[plane] for plane in range(planes)]
+        return mix_rows(table[plane], mix_places[pair], mix_gates[pair], hidden_all, w_down, capacity)
+
+    def cross():
+        return [far_core(parts[plane][1]) for plane in parts if plane not in crossed]
+
+    def mix_turn(some, table):
+        return [mix_work(plane, table) for plane in some], cross()
+
+    crossed = {}
+    for start in range(0, planes, 2):
+        some = order[start : start + 2]
+        waiting = [plane for plane in parts if plane not in crossed]
+        results, arrived = folding.turn(tables, functools.partial(mix_turn, some))
+        crossed.update(zip(waiting, arrived))
+        parts.update(zip(some, results))
+    kept = [kept[plane] for plane in range(planes)]
+    weight_parts, next_expert = (), 0
+    part_size = math.gcd(local_experts, GROUP)
+
+    def weight_turn(count, small):
+        state, (held, weights) = next_expert, small
+        for _ in range(count):
+            if state < local_experts:
+                weights = weight_grads(state, part_size, *zip(*held), weights)
+                state += part_size
+        return weights, cross()
+
+    for count in (2, 1, *[0] * planes):
+        if folding.done():
+            break
+        waiting = [plane for plane in parts if plane not in crossed]
+        weight_parts, arrived = folding.turn(
+            (kept, weight_parts), functools.partial(weight_turn, count)
+        )
+        next_expert = min(next_expert + count * part_size, local_experts)
+        crossed.update(zip(waiting, arrived))
+        if len(crossed) == planes and waiting:
+            whole = jnp.stack(
+                [added(parts[plane][0], crossed[plane]) for plane in range(planes)]
+            )
+            whole = whole.reshape(planes, -1, whole.shape[-1])
+            whole = lax.psum_scatter(whole, ("pack", "side"), scatter_dimension=1, tiled=True)
+    rest = (kept, weight_parts, next_expert, part_size)
+    return folding.summed, whole, rest
 
 
 def shards(
@@ -888,15 +961,14 @@
         side_sum, side_gather = fold_sides, gather_sides
         local_width = w_query.shape[1]
         w_in = jnp.concatenate([w_query, w_key, w_value], axis=1)
-        full_in, pack_in = gather_both(w_in, first_in)
-        full_in, cotangent, w_output = lax.optimization_barrier((full_in, cotangent, w_output))
+        full_in, full_output, pack_in = gather_both(w_in, w_output, first_in)
+        full_in, cotangent = tied(full_in, cotangent)
         all_cot = lax.all_gather(cotangent, axes, axis=0, tiled=True)
         all_cot = all_cot.reshape(data_count, seq_len, model_width)
         full_in = full_in.reshape(model_width, -1)
         full_query, full_key, full_value = (
             full_in[:, index * local_width : (index + 1) * local_width] for index in range(3)
         )
-        full_output = gather_packs(w_output, True)
     else:
         side_sum, side_gather = lambda term: row_sum(lambda *_: term, tok_rows), gather_rows
         segments = lax.all_gather(segment_ids, TENSOR, axis=1, tiled=True)[0]
@@ -943,7 +1015,7 @@
     normed_two, factor_two = norm_parts(middle)
     second_in = (normed_two * ffn_gain).astype(jnp.bfloat16)
     if by_gather:
-        grad_second, mixed, kept = experts_by_gather(
+        grad_second, mixed, rest = experts_by_gather(
             second_in, all_cot, places, gates, w_gate, w_up, w_down, capacity
         )
     else:
@@ -956,12 +1028,15 @@
     )
     grad_attended = grad_middle.astype(jnp.bfloat16)
     if by_gather:
-        kept, grad_attended = tied(kept, grad_attended)
-        part_size = math.gcd(local_experts, GROUP)
-        weight_parts = ()
-        for first in range(0, local_experts // 2, part_size):
+        kept, weight_parts, next_expert, part_size = rest
+        (kept, weight_parts), grad_attended = tied((kept, weight_parts), grad_attended)
+        moved = [far_core(grad_attended), far_side(grad_attended)]
+        for first in range(next_expert, local_experts, part_size):
             weight_parts = weight_grads(first, part_size, *zip(*kept), weight_parts)
-        weight_parts, pack_grad = tied(weight_parts, side_gather(grad_attended))
+        grad_w_gate, grad_w_up, grad_w_down = weight_parts
+        near, across, weight_parts = lax.optimization_barrier((*moved, weight_parts))
+        grad_w_gate, grad_w_up, grad_w_down = weight_parts
+        pack_grad = laid_sides([grad_attended, near, across, far_core(across)])
     else:
         pack_grad = side_gather(grad_attended)
     output_part = contract_first(mixture, pack_grad)
@@ -1022,23 +1097,26 @@
 
     total_term = contract_last(grad_query_pre, full_query)
     total_term = total_term + contract_last(grad_key_pre, full_key)
-    grad_first = side_sum(total_term + contract_last(grad_value_low, full_value))
+    total_term = total_term + contract_last(grad_value_low, full_value)
+    if by_gather:
+        by_column = output_part.astype(jnp.bfloat16).reshape(local_width, data_count, -1)
+        grad_w_output = fold_packs(by_column.transpose(1, 0, 2))
+        in_part = jnp.concatenate([query_part, key_part, value_part], axis=1)
+        in_part = in_part.astype(jnp.bfloat16).reshape(data_count, -1, 3 * local_width)
+        mixed, in_part = tied(mixed, in_part)
+        mixed = lax.psum_scatter(mixed, "plane", scatter_dimension=0, tiled=True)
+        grad_in, grad_first = fold_both(in_part, total_term)
+        mixed, grad_in = tied(mixed, grad_in)
+    else:
+        grad_first = side_sum(total_term)
     attn_gain_part = jnp.sum(grad_first * normed_one, axis=0)
     grad_inputs = grad_middle + norm_back(grad_first, normed_one, factor_one, attn_gain)
     gain_parts = (attn_gain_part, ffn_gain_part, query_gain_part, key_gain_part)
     if by_gather:
-        in_part = jnp.concatenate([query_part, key_part, value_part], axis=1)
-        grad_in = fold_packs(in_part.astype(jnp.bfloat16).reshape(data_count, -1, 3 * local_width))
         grad_w_query, grad_w_key, grad_w_value = (
             grad_in[:, index * local_width : (index + 1) * local_width] for index in range(3)
         )
-        by_column = output_part.astype(jnp.bfloat16).reshape(local_width, data_count, -1)
-        grad_w_output = fold_packs(by_column.transpose(1, 0, 2))
-        kept, _ = tied(kept, in_part)
-        for first in range(local_experts // 2 // part_size * part_size, local_experts, part_size):
-            weight_parts = weight_grads(first, part_size, *zip(*kept), weight_parts)
-        grad_w_gate, grad_w_up, grad_w_down = weight_parts
-        outputs = middle + mixed
+        outputs = middle + mixed[0].astype(jnp.float32)
         late = sum_everywhere(attn_gain_part)
         early = sum_everywhere(jnp.concatenate(gain_parts[1:]))
         splits = (model_width, model_width + head_size)

time: 1320 us -> 1280 us (0.970)
  waiting for transfers between devices: 508 us -> 417 us
  starting transfers between devices: 83.3 us -> 110 us
  local copies, waits for them, and re-layouts: 91.8 us -> 117 us
    ppermute x84 -> x87, waiting for transfers between devices: 397 us -> 225 us  [swapped(): return lax.ppermute(values, axis, [(i, i ^ bit) for i in range(count)])]
    all_gather x1, waiting for transfers between devices: 0.01 us -> 69.2 us  [shards(): all_cot = lax.all_gather(cotangent, axes, axis=0, tiled=True)]
    ppermute x18, starting transfers between devices: 14.6 us -> 35.8 us  [next_plane(): lax.ppermute(values, DP, [(i, (i + 2) % count) for i in range(count)])]
    reduce_scatter x1, waiting for transfers between devices: 0.01 us -> 20.7 us  [experts_by_gather(): lax.psum_scatter(whole, ('pack', 'side'), scatter_dimension=1, tiled=True)]
    unnamed x236 -> x287, local copies, waits for them, and re-layouts: 27.5 us -> 44 us
    concatenate x6 -> x1, other arithmetic: 14.7 us -> 1.05 us  [turn(): jnp.concatenate([added(values[0], arrived[0]), added(values[1], arrived[1...]
    ppermute x84 -> x87, starting transfers between devices: 68.6 us -> 73.8 us  [swapped(): return lax.ppermute(values, axis, [(i, i ^ bit) for i in range(count)])]
    convert_element_type x39 -> x42, other arithmetic: 78 us -> 79.8 us  [added(): return (left.astype(jnp.float32) + right.astype(jnp.float32)).astype(kind)]
  transfers between devices with their start and end apart: 105 -> 108, of which waited for: 44 -> 34; matrix products, arithmetic and copies ran while one was open for 21% -> 22% of each run, Pallas kernels for 26% -> 29%
where the time goes in v7:
time: 1280 us; the launch traced here: 1270 us
  waiting for transfers between devices  417 us (33%)
  Pallas kernels  377 us (29%)
  other arithmetic  151 us (12%)
  local copies, waits for them, and re-layouts  117 us (9%)
  starting transfers between devices  110 us (9%)
  matrix products  83.8 us (7%)
  between operations  16.9 us (1%)
    ppermute x87, waiting for transfers between devices, swapped(): return lax.ppermute(values, axis, [(i, i ^ bit) for i in range(count)])  225 us
    pallas_call x4, Pallas kernels, row_slots(): call(functools.partial(row_kernel, packs, steps, capacity), 2 * packs + s...  152 us
    ppermute x18, waiting for transfers between devices, next_plane(): lax.ppermute(values, DP, [(i, (i + 2) % count) for i in range(count)])  102 us
    pallas_call x4, Pallas kernels, cot_slots(): call(functools.partial(cot_kernel, packs, steps, capacity), packs + steps...  81.6 us
    convert_element_type x42, other arithmetic, added(): return (left.astype(jnp.float32) + right.astype(jnp.float32)).astype(kind)  79.8 us
    ppermute x87, starting transfers between devices, swapped(): return lax.ppermute(values, axis, [(i, i ^ bit) for i in range(count)])  73.8 us
    pallas_call x4, Pallas kernels, mix_rows(): call(functools.partial(mix_kernel, packs, steps, capacity), packs + steps...  70.9 us
    all_gather x1, waiting for transfers between devices, shards(): all_cot = lax.all_gather(cotangent, axes, axis=0, tiled=True)  69.2 us
  transfers between devices with their start and end apart: 108, of which 34 were waited for; matrix products, arithmetic and copies ran while one was open for 22% of the time, Pallas kernels for 29%

profile of v7, /device:TPU:0, one launch (start us, length us, event | category | flops | bytes accessed | tf_op | source)
XLA Modules:
  0.0 1272.4 jit_solution(2311843341563035723)
XLA Ops:
  19.0 23.3 %collective-permute-done.1.refs_1_ = bf16[512,256]{1,0:T(8,128)(2,1)S(1)} collective-permute-done((bf16[512,256]{1,0:T(8,128)(2,1)S(1)}, bf16[512,256]{1,0:T(8,128)(2,1)S(1)}, u32[]{:S(2)}, u32[]{:S(2)}) %collective-permute-start.1) | collective-permute-done | bytes 262176 | tf_op jit(solution)/shard_map/ppermute | solution.py:462
  56.2 24.0 %collective-permute-done.9.refs_4_ = bf16[512,256]{1,0:T(8,128)(2,1)S(1)} collective-permute-done((bf16[512,256]{1,0:T(8,128)(2,1)S(1)}, bf16[512,256]{1,0:T(8,128)(2,1)S(1)}, u32[]{:S(2)}, u32[]{:S(2)}) %collective-permute-start.9) | collective-permute-done | bytes 262176 | tf_op jit(solution)/shard_map/ppermute | solution.py:479
  84.0 23.7 %collective-permute-done.14.refs_6_ = bf16[512,256]{1,0:T(8,128)(2,1)} collective-permute-done((bf16[512,256]{1,0:T(8,128)(2,1)S(1)}, bf16[512,256]{1,0:T(8,128)(2,1)}, u32[]{:S(2)}, u32[]{:S(2)}) %collective-permute-start.14) | collective-permute-done | bytes 262176 | tf_op jit(solution)/shard_map/ppermute | solution.py:479
  111.0 21.0 %collective-permute-done.16.refs_7_ = bf16[512,256]{1,0:T(8,128)(2,1)} collective-permute-done((bf16[512,256]{1,0:T(8,128)(2,1)}, bf16[512,256]{1,0:T(8,128)(2,1)}, u32[]{:S(2)}, u32[]{:S(2)}) %collective-permute-start.16) | collective-permute-done | bytes 262176 | tf_op jit(solution)/shard_map/ppermute | solution.py:462
  214.9 17.3 %collective-permute-done.24 = bf16[16,17,256]{2,0,1:T(8,128)(2,1)S(1)} collective-permute-done((bf16[16,17,256]{2,0,1:T(8,128)(2,1)S(1)}, bf16[16,17,256]{2,0,1:T(8,128)(2,1)S(1)}, u32[]{:S(2)}, u32[]{:S(2)}) %collective-permute-start.24) | collective-permute-done | bytes 139296 | tf_op jit(solution)/shard_map/ppermute | solution.py:462
  241.7 17.9 %collective-permute-done.26 = bf16[128,2048]{1,0:T(8,128)(2,1)S(1)} collective-permute-done((bf16[128,2048]{1,0:T(8,128)(2,1)S(1)}, bf16[128,2048]{1,0:T(8,128)(2,1)S(1)}, u32[]{:S(2)}, u32[]{:S(2)}) %collective-permute-start.26) | collective-permute-done | bytes 524320 | tf_op jit(solution)/shard_map/ppermute | solution.py:462
  261.1 22.0 %collective-permute-done.27 = bf16[256,2048]{1,0:T(8,128)(2,1)} collective-permute-done((bf16[256,2048]{1,0:T(8,128)(2,1)S(1)}, bf16[256,2048]{1,0:T(8,128)(2,1)}, u32[]{:S(2)}, u32[]{:S(2)}) %collective-permute-start.27) | collective-permute-done | bytes 1048608 | tf_op jit(solution)/shard_map/ppermute | solution.py:479
  284.8 16.9 %collective-permute-start.32 = (bf16[256,2048]{1,0:T(8,128)(2,1)}, bf16[256,2048]{1,0:T(8,128)(2,1)}, u32[]{:S(2)}, u32[]{:S(2)}) collective-permute-start(bf16[256,2048]{1,0:T(8,128)(2,1)} %collective-permute-done.27), channel_id=1, source_target_pairs={{0,8},{4,12},{8,16},{12,20},{16,24},{20,28},{24,0},{28,4},{1,9},{5... | collective-permute-start | bytes 3145736 | tf_op jit(solution)/shard_map/ppermute | solution.py:479
  309.6 69.2 %all-gather.2.cloned.1.call-done = bf16[8192,2048]{1,0:T(8,128)(2,1)} async-done(((bf16[256,2048]{1,0:T(8,128)(2,1)}), bf16[8192,2048]{1,0:T(8,128)(2,1)}) %all-gather.2.cloned.1.call-update) | async-done | bytes 33554448 | tf_op jit(solution)/shard_map/all_gather | solution.py:966
  378.8 20.4 %shard_map.258 = (bf16[8,256,2048]{2,1,0:T(8,128)(2,1)}, f32[8,256,256]{2,1,0:T(8,128)}) custom-call(s32[2]{0:T(128)} %bitcast.425, bf16[8,8,1024]{2,1,0:T(8,128)(2,1)} %get-tuple-element.727.places, bf16[8,8,1024]{2,1,0:T(8,128)(2,1)} %fusion.17.gates, bf16[8,1024,2048]{2,1,0:T(8,128)(2,1)} %bitcast.342, bf16[8,256,2048]{2,1,0:T(8,128)(2,1)} %down.15), custom_call_target="tpu_custom_call" | custom-call | flops 10737418240 | bytes 21474836 | tf_op jit(solution)/shard_map/pallas_call | solution.py:357
  440.5 20.4 %shard_map.259 = (bf16[8,256,2048]{2,1,0:T(8,128)(2,1)}, f32[8,256,256]{2,1,0:T(8,128)}) custom-call(s32[2]{0:T(128)} %slice.386.table, bf16[8,8,1024]{2,1,0:T(8,128)(2,1)} %get-tuple-element.727.places, bf16[8,8,1024]{2,1,0:T(8,128)(2,1)} %fusion.17.gates, bf16[8,1024,2048]{2,1,0:T(8,128)(2,1)} %bitcast.343, bf16[8,256,2048]{2,1,0:T(8,128)(2,1)} %down.15), custom_call_target="tpu_custom_call" | custom-call | flops 10737418240 | bytes 21474836 | tf_op jit(solution)/shard_map/pallas_call | solution.py:357
  480.8 37.8 %shard_map.260 = (bf16[8,256,2048]{2,1,0:T(8,128)(2,1)}, bf16[8,256,256]{2,1,0:T(8,128)(2,1)}, bf16[8,256,512]{2,1,0:T(8,128)(2,1)}, bf16[2,2,256,2048]{3,2,1,0:T(8,128)(2,1)}, bf16[2,2,256,2048]{3,2,1,0:T(8,128)(2,1)}) custom-call(bf16[2,8,1024]{2,1,0:T(8,128)(2,1)} %bitcast.413, bf16[8,128,2048]{2,1,0:T(8,128)(2,1)} %constant_dynamic-update-slice_fusion.3.own, ...), custom_call_target="tpu_custom_call" | custom-call | flops 25769803776 | bytes 51539608 | tf_op jit(solution)/shard_map/pallas_call | solution.py:390
  518.7 20.4 %shard_map.261 = (bf16[8,256,2048]{2,1,0:T(8,128)(2,1)}, f32[8,256,256]{2,1,0:T(8,128)}) custom-call(s32[2]{0:T(128)} %slice.390.table, bf16[8,8,1024]{2,1,0:T(8,128)(2,1)} %get-tuple-element.727.places, bf16[8,8,1024]{2,1,0:T(8,128)(2,1)} %fusion.17.gates, bf16[8,1024,2048]{2,1,0:T(8,128)(2,1)} %bitcast.344, bf16[8,256,2048]{2,1,0:T(8,128)(2,1)} %down.15), custom_call_target="tpu_custom_call" | custom-call | flops 10737418240 | bytes 21474836 | tf_op jit(solution)/shard_map/pallas_call | solution.py:357
  548.7 38.2 %shard_map.262 = (bf16[8,256,2048]{2,1,0:T(8,128)(2,1)}, bf16[8,256,256]{2,1,0:T(8,128)(2,1)}, bf16[8,256,512]{2,1,0:T(8,128)(2,1)}, bf16[2,2,256,2048]{3,2,1,0:T(8,128)(2,1)}, bf16[2,2,256,2048]{3,2,1,0:T(8,128)(2,1)}) custom-call(bf16[2,8,1024]{2,1,0:T(8,128)(2,1)} %bitcast.412, bf16[8,128,2048]{2,1,0:T(8,128)(2,1)} %constant_dynamic-update-slice_fusion.9.own, ...), custom_call_target="tpu_custom_call" | custom-call | flops 25769803776 | bytes 51539608 | tf_op jit(solution)/shard_map/pallas_call | solution.py:390
  602.7 20.4 %shard_map.263 = (bf16[8,256,2048]{2,1,0:T(8,128)(2,1)}, f32[8,256,256]{2,1,0:T(8,128)}) custom-call(s32[2]{0:T(128)} %slice.398.table, bf16[8,8,1024]{2,1,0:T(8,128)(2,1)} %get-tuple-element.727.places, bf16[8,8,1024]{2,1,0:T(8,128)(2,1)} %fusion.17.gates, bf16[8,1024,2048]{2,1,0:T(8,128)(2,1)} %bitcast.345, bf16[8,256,2048]{2,1,0:T(8,128)(2,1)} %down.15), custom_call_target="tpu_custom_call" | custom-call | flops 10737418240 | bytes 21474836 | tf_op jit(solution)/shard_map/pallas_call | solution.py:357
  628.6 38.1 %shard_map.264 = (bf16[8,256,2048]{2,1,0:T(8,128)(2,1)}, bf16[8,256,256]{2,1,0:T(8,128)(2,1)}, bf16[8,256,512]{2,1,0:T(8,128)(2,1)}, bf16[2,2,256,2048]{3,2,1,0:T(8,128)(2,1)}, bf16[2,2,256,2048]{3,2,1,0:T(8,128)(2,1)}) custom-call(bf16[2,8,1024]{2,1,0:T(8,128)(2,1)} %bitcast.411, bf16[8,128,2048]{2,1,0:T(8,128)(2,1)} %constant_dynamic-update-slice_fusion.13.own, ...), custom_call_target="tpu_custom_call" | custom-call | flops 25769803776 | bytes 51539608 | tf_op jit(solution)/shard_map/pallas_call | solution.py:390
  683.5 38.2 %shard_map.265 = (bf16[8,256,2048]{2,1,0:T(8,128)(2,1)}, bf16[8,256,256]{2,1,0:T(8,128)(2,1)}, bf16[8,256,512]{2,1,0:T(8,128)(2,1)}, bf16[2,2,256,2048]{3,2,1,0:T(8,128)(2,1)}, bf16[2,2,256,2048]{3,2,1,0:T(8,128)(2,1)}) custom-call(bf16[2,8,1024]{2,1,0:T(8,128)(2,1)} %bitcast.410, bf16[8,128,2048]{2,1,0:T(8,128)(2,1)} %constant_dynamic-update-slice_fusion.17.own, ...), custom_call_target="tpu_custom_call" | custom-call | flops 25769803776 | bytes 51539608 | tf_op jit(solution)/shard_map/pallas_call | solution.py:390
  752.6 17.7 %shard_map.267 = (bf16[2,2,256,2048]{3,2,1,0:T(8,128)(2,1)}, bf16[2,2,256,2048]{3,2,1,0:T(8,128)(2,1)}) custom-call(s32[2]{0:T(128)} %get-tuple-element.711.table, bf16[2,8,1024]{2,1,0:T(8,128)(2,1)} %bitcast.420, bf16[2,8,1024]{2,1,0:T(8,128)(2,1)} %bitcast.415, bf16[32,256,256]{2,1,0:T(8,128)(2,1)} %copy-done.97, bf16[8,256,2048]{2,1,0:T(8,128)(2,1)} %down.15), custom_call_target="tpu_custom_call" | custom-call | flops 10737418240 | bytes 21474836 | tf_op jit(solution)/shard_map/pallas_call | solution.py:418
  770.3 17.9 %shard_map.266 = (bf16[2,2,256,2048]{3,2,1,0:T(8,128)(2,1)}, bf16[2,2,256,2048]{3,2,1,0:T(8,128)(2,1)}) custom-call(s32[2]{0:T(128)} %get-tuple-element.712.table, bf16[2,8,1024]{2,1,0:T(8,128)(2,1)} %bitcast.417, bf16[2,8,1024]{2,1,0:T(8,128)(2,1)} %bitcast.414, bf16[32,256,256]{2,1,0:T(8,128)(2,1)} %copy-done.97, bf16[8,256,2048]{2,1,0:T(8,128)(2,1)} %down.15), custom_call_target="tpu_custom_call" | custom-call | flops 10737418240 | bytes 21474836 | tf_op jit(solution)/shard_map/pallas_call | solution.py:418
  817.8 17.6 %shard_map.269 = (bf16[2,2,256,2048]{3,2,1,0:T(8,128)(2,1)}, bf16[2,2,256,2048]{3,2,1,0:T(8,128)(2,1)}) custom-call(s32[2]{0:T(128)} %get-tuple-element.709.table, bf16[2,8,1024]{2,1,0:T(8,128)(2,1)} %bitcast.421, bf16[2,8,1024]{2,1,0:T(8,128)(2,1)} %bitcast.419, bf16[32,256,256]{2,1,0:T(8,128)(2,1)} %copy-done.97, bf16[8,256,2048]{2,1,0:T(8,128)(2,1)} %down.15), custom_call_target="tpu_custom_call" | custom-call | flops 10737418240 | bytes 21474836 | tf_op jit(solution)/shard_map/pallas_call | solution.py:418
  835.5 17.7 %shard_map.268 = (bf16[2,2,256,2048]{3,2,1,0:T(8,128)(2,1)}, bf16[2,2,256,2048]{3,2,1,0:T(8,128)(2,1)}) custom-call(s32[2]{0:T(128)} %get-tuple-element.710.table, bf16[2,8,1024]{2,1,0:T(8,128)(2,1)} %bitcast.418, bf16[2,8,1024]{2,1,0:T(8,128)(2,1)} %bitcast.416, bf16[32,256,256]{2,1,0:T(8,128)(2,1)} %copy-done.97, bf16[8,256,2048]{2,1,0:T(8,128)(2,1)} %down.15), custom_call_target="tpu_custom_call" | custom-call | flops 10737418240 | bytes 21474836 | tf_op jit(solution)/shard_map/pallas_call | solution.py:418
  876.9 13.1 %shard_map.270 = (f32[8,2048,256]{2,1,0:T(8,128)}, f32[8,2048,256]{2,1,0:T(8,128)}, f32[8,256,2048]{2,1,0:T(8,128)}) custom-call(bf16[8,256,2048]{2,1,0:T(8,128)(2,1)} %get-tuple-element.558.refs_0_, bf16[8,256,2048]{2,1,0:T(8,128)(2,1)} %get-tuple-element.559.refs_1_, bf16[8,256,2048]{2,1,0:T(8,128)(2,1)} %get-tuple-element.560.refs_2_, ...), custom_call_target="tpu_custom_call" | custom-call | flops 6442450944 | bytes 12884901 | tf_op jit(solution)/shard_map/pallas_call | solution.py:447
  890.0 13.1 %shard_map.271 = (f32[8,2048,256]{2,1,0:T(8,128)}, f32[8,2048,256]{2,1,0:T(8,128)}, f32[8,256,2048]{2,1,0:T(8,128)}) custom-call(bf16[8,256,2048]{2,1,0:T(8,128)(2,1)} %get-tuple-element.558.refs_0_, bf16[8,256,2048]{2,1,0:T(8,128)(2,1)} %get-tuple-element.559.refs_1_, ...), custom_call_target="tpu_custom_call", output_to_operand_aliasing={{0}: (16, {}), {1}: (17, {}), {2}: (18, {})} | custom-call | flops 6442450944 | bytes 12884901 | tf_op jit(solution)/shard_map/pallas_call | solution.py:447
  931.2 13.4 %shard_map.272 = (f32[8,2048,256]{2,1,0:T(8,128)}, f32[8,2048,256]{2,1,0:T(8,128)}, f32[8,256,2048]{2,1,0:T(8,128)}) custom-call(bf16[8,256,2048]{2,1,0:T(8,128)(2,1)} %get-tuple-element.558.refs_0_, bf16[8,256,2048]{2,1,0:T(8,128)(2,1)} %get-tuple-element.559.refs_1_, ...), custom_call_target="tpu_custom_call", output_to_operand_aliasing={{0}: (16, {}), {1}: (17, {}), {2}: (18, {})} | custom-call | flops 6442450944 | bytes 12884901 | tf_op jit(solution)/shard_map/pallas_call | solution.py:447
  961.6 13.3 %shard_map.273 = (f32[8,2048,256]{2,1,0:T(8,128)}, f32[8,2048,256]{2,1,0:T(8,128)}, f32[8,256,2048]{2,1,0:T(8,128)}) custom-call(bf16[8,256,2048]{2,1,0:T(8,128)(2,1)} %get-tuple-element.558.refs_0_, bf16[8,256,2048]{2,1,0:T(8,128)(2,1)} %get-tuple-element.559.refs_1_, ...), custom_call_target="tpu_custom_call", output_to_operand_aliasing={{0}: (16, {}), {1}: (17, {}), {2}: (18, {})} | custom-call | flops 6442450944 | bytes 12884901 | tf_op jit(solution)/shard_map/pallas_call | solution.py:447
  974.9 33.0 %collective-permute-done.76.refs_2_ = bf16[256,2048]{1,0:T(8,128)(2,1)S(1)} collective-permute-done((bf16[256,2048]{1,0:T(8,128)(2,1)}, bf16[256,2048]{1,0:T(8,128)(2,1)S(1)}, u32[]{:S(2)}, u32[]{:S(2)}) %collective-permute-start.76) | collective-permute-done | bytes 1048608 | tf_op jit(solution)/shard_map/ppermute | solution.py:462
  1078.4 20.7 %reduce-scatter.3.cloned.1.call-done = bf16[4,256,2048]{2,1,0:T(8,128)(2,1)} async-done(((bf16[4,1024,2048]{2,1,0:T(8,128)(2,1)}), bf16[4,256,2048]{2,1,0:T(8,128)(2,1)}) %reduce-scatter.3.cloned.1.call-update) | async-done | bytes 4194320 | tf_op jit(solution)/shard_map/reduce_scatter | solution.py:913
  1138.5 13.1 %collective-permute-done.98 = bf16[512,256]{1,0:T(8,128)(2,1)S(1)} collective-permute-done((bf16[512,256]{1,0:T(8,128)(2,1)S(1)}, bf16[512,256]{1,0:T(8,128)(2,1)S(1)}, u32[]{:S(2)}, u32[]{:S(2)}) %collective-permute-start.98) | collective-permute-done | bytes 262176 | tf_op jit(solution)/shard_map/ppermute | solution.py:462
  1160.4 9.5 collective-permute-done.99
  1172.2 25.6 %collective-permute-done.96 = f32[2304]{0:T(1024)S(1)} collective-permute-done((f32[2304]{0:T(1024)S(1)}, f32[2304]{0:T(1024)S(1)}, u32[]{:S(2)}, u32[]{:S(2)}) %collective-permute-start.96) | collective-permute-done | bytes 9248 | tf_op jit(solution)/shard_map/ppermute | solution.py:462
  1214.2 16.9 %collective-permute-done.97 = f32[2304]{0:T(1024)S(1)} collective-permute-done((f32[2304]{0:T(1024)S(1)}, f32[2304]{0:T(1024)S(1)}, u32[]{:S(2)}, u32[]{:S(2)}) %collective-permute-start.97) | collective-permute-done | bytes 9248 | tf_op jit(solution)/shard_map/ppermute | solution.py:462
  1246.2 13.3 %collective-permute-done.92 = f32[2048]{0:T(1024)S(1)} collective-permute-done((f32[2048]{0:T(1024)S(1)}, f32[2048]{0:T(1024)S(1)}, u32[]{:S(2)}, u32[]{:S(2)}) %collective-permute-start.92) | collective-permute-done | bytes 8224 | tf_op jit(solution)/shard_map/ppermute | solution.py:462
  (725 shorter events, 530.5 us)
Async XLA Ops:
  7.2 371.6 %all-gather.2.cloned.1.call-start = ((), (), s32[]{:S(2)}) async-start(), calls=%async_computation.2 | async-start | bytes 34603008 | tf_op jit(solution)/shard_map/all_gather | solution.py:966
  138.3 960.8 %reduce-scatter.3.cloned.1.call-start = ((), (), s32[]{:S(2)}) async-start(), calls=%async_computation.3 | async-start | bytes 20971520 | tf_op jit(solution)/shard_map/reduce_scatter | solution.py:913
  236.2 46.9 %collective-permute-start.27 = (bf16[256,2048]{1,0:T(8,128)(2,1)S(1)}, bf16[256,2048]{1,0:T(8,128)(2,1)}, u32[]{:S(2)}, u32[]{:S(2)}) collective-permute-start(bf16[256,2048]{1,0:T(8,128)(2,1)S(1)} %multiply_convert_fusion.4), channel_id=1, source_target_pairs={{0,8},{4,12},{8,16},{12,20},{16,24},{20,28},{24,0},{28,4},{1,9},{5... | collective-permute-start | bytes 3145736 | tf_op jit(solution)/shard_map/ppermute | solution.py:479
  283.4 115.8 %collective-permute-start.28 = (bf16[2,128,2048]{2,1,0:T(8,128)(2,1)S(1)}, bf16[2,128,2048]{2,1,0:T(8,128)(2,1)}, u32[]{:S(2)}, u32[]{:S(2)}) collective-permute-start(bf16[2,128,2048]{2,1,0:T(8,128)(2,1)S(1)} %pad_maximum_fusion.7), channel_id=1, source_target_pairs={{0,2},{1,3},{2,0},{3,1},{4,6},{5,7},{6,4},{7,5},{8,10},{9,11},{10,... | collective-permute-start | bytes 3145736 | tf_op jit(solution)/shard_map/ppermute | solution.py:462
  283.4 115.8 %collective-permute-start.29 = (bf16[2,128,2048]{2,1,0:T(8,128)(2,1)S(1)}, bf16[2,128,2048]{2,1,0:T(8,128)(2,1)}, u32[]{:S(2)}, u32[]{:S(2)}) collective-permute-start(bf16[2,128,2048]{2,1,0:T(8,128)(2,1)S(1)} %pad_maximum_fusion.8), channel_id=1, source_target_pairs={{0,4},{4,0},{8,12},{12,8},{16,20},{20,16},{24,28},{28,24},{1,5},{5... | collective-permute-start | bytes 3145736 | tf_op jit(solution)/shard_map/ppermute | solution.py:462
  284.8 114.4 %collective-permute-start.32 = (bf16[256,2048]{1,0:T(8,128)(2,1)}, bf16[256,2048]{1,0:T(8,128)(2,1)}, u32[]{:S(2)}, u32[]{:S(2)}) collective-permute-start(bf16[256,2048]{1,0:T(8,128)(2,1)} %collective-permute-done.27), channel_id=1, source_target_pairs={{0,8},{4,12},{8,16},{12,20},{16,24},{20,28},{24,0},{28,4},{1,9},{5... | collective-permute-start | bytes 3145736 | tf_op jit(solution)/shard_map/ppermute | solution.py:479
  304.1 95.1 %collective-permute-start.31 = (bf16[128,2048]{1,0:T(8,128)(2,1)}, bf16[128,2048]{1,0:T(8,128)(2,1)}, u32[]{:S(2)}, u32[]{:S(2)}) collective-permute-start(bf16[128,2048]{1,0:T(8,128)(2,1)} %get-tuple-element.677), channel_id=1, source_target_pairs={{0,2},{1,3},{2,0},{3,1},{4,6},{5,7},{6,4},{7,5},{8,10},{9,11},{10,... | collective-permute-start | bytes 1572872 | tf_op jit(solution)/shard_map/ppermute | solution.py:462
  306.0 93.2 %collective-permute-start.30 = (bf16[128,2048]{1,0:T(8,128)(2,1)}, bf16[128,2048]{1,0:T(8,128)(2,1)}, u32[]{:S(2)}, u32[]{:S(2)}) collective-permute-start(bf16[128,2048]{1,0:T(8,128)(2,1)} %get-tuple-element.678), channel_id=1, source_target_pairs={{0,4},{4,0},{8,12},{12,8},{16,20},{20,16},{24,28},{28,24},{1,5},{5... | collective-permute-start | bytes 1572872 | tf_op jit(solution)/shard_map/ppermute | solution.py:462
  403.8 62.1 %collective-permute-start.38 = (bf16[8,128,2048]{2,1,0:T(8,128)(2,1)}, bf16[8,128,2048]{2,1,0:T(8,128)(2,1)}, u32[]{:S(2)}, u32[]{:S(2)}) collective-permute-start(bf16[8,128,2048]{2,1,0:T(8,128)(2,1)} %constant_dynamic-update-slice_fusion.3.own), channel_id=1, source_target_pairs={{0,1},{1,0},{2,3},{3,2},{4,5},{5,4},{6,7},{7,6},{8,9},{9,8},{10,11... | collective-permute-start | bytes 12582920 | tf_op jit(solution)/shard_map/ppermute | solution.py:462
  474.3 67.0 %collective-permute-start.44 = (bf16[8,128,2048]{2,1,0:T(8,128)(2,1)}, bf16[8,128,2048]{2,1,0:T(8,128)(2,1)}, u32[]{:S(2)}, u32[]{:S(2)}) collective-permute-start(bf16[8,128,2048]{2,1,0:T(8,128)(2,1)} %constant_dynamic-update-slice_fusion.9.own), channel_id=1, source_target_pairs={{0,1},{1,0},{2,3},{3,2},{4,5},{5,4},{6,7},{7,6},{8,9},{9,8},{10,11... | collective-permute-start | bytes 12582920 | tf_op jit(solution)/shard_map/ppermute | solution.py:462
  477.0 64.3 %collective-permute-start.42 = (bf16[128,2048]{1,0:T(8,128)(2,1)}, bf16[128,2048]{1,0:T(8,128)(2,1)}, u32[]{:S(2)}, u32[]{:S(2)}) collective-permute-start(bf16[128,2048]{1,0:T(8,128)(2,1)} %get-tuple-element.670), channel_id=1, source_target_pairs={{0,4},{4,0},{8,12},{12,8},{16,20},{20,16},{24,28},{28,24},{1,5},{5... | collective-permute-start | bytes 1572872 | tf_op jit(solution)/shard_map/ppermute | solution.py:462
  478.2 63.0 %collective-permute-start.40 = (bf16[2,128,2048]{2,1,0:T(8,128)(2,1)S(1)}, bf16[2,128,2048]{2,1,0:T(8,128)(2,1)}, u32[]{:S(2)}, u32[]{:S(2)}) collective-permute-start(bf16[2,128,2048]{2,1,0:T(8,128)(2,1)S(1)} %pad_maximum_fusion.11), channel_id=1, source_target_pairs={{0,2},{1,3},{2,0},{3,1},{4,6},{5,7},{6,4},{7,5},{8,10},{9,11},{10,... | collective-permute-start | bytes 3145736 | tf_op jit(solution)/shard_map/ppermute | solution.py:462
  480.0 61.3 %collective-permute-start.41 = (bf16[2,128,2048]{2,1,0:T(8,128)(2,1)S(1)}, bf16[2,128,2048]{2,1,0:T(8,128)(2,1)}, u32[]{:S(2)}, u32[]{:S(2)}) collective-permute-start(bf16[2,128,2048]{2,1,0:T(8,128)(2,1)S(1)} %pad_maximum_fusion.12), channel_id=1, source_target_pairs={{0,4},{4,0},{8,12},{12,8},{16,20},{20,16},{24,28},{28,24},{1,5},{5... | collective-permute-start | bytes 3145736 | tf_op jit(solution)/shard_map/ppermute | solution.py:462
  518.6 68.3 %collective-permute-start.39 = (bf16[2,2,256,2048]{3,2,1,0:T(8,128)(2,1)}, bf16[2,2,256,2048]{3,2,1,0:T(8,128)(2,1)}, u32[]{:S(2)}, u32[]{:S(2)}) collective-permute-start(bf16[2,2,256,2048]{3,2,1,0:T(8,128)(2,1)} %get-tuple-element.353), channel_id=1, source_target_pairs={{0,1},{1,0},{2,3},{3,2},{4,5},{5,4},{6,7},{7,6},{8,9},{9,8},{10,11... | collective-permute-start | bytes 12582920 | tf_op jit(solution)/shard_map/ppermute | solution.py:462
  543.5 79.6 %collective-permute-start.48 = (bf16[2,128,2048]{2,1,0:T(8,128)(2,1)}, bf16[2,128,2048]{2,1,0:T(8,128)(2,1)}, u32[]{:S(2)}, u32[]{:S(2)}) collective-permute-start(bf16[2,128,2048]{2,1,0:T(8,128)(2,1)} %pad_maximum_fusion.13), channel_id=1, source_target_pairs={{0,2},{1,3},{2,0},{3,1},{4,6},{5,7},{6,4},{7,5},{8,10},{9,11},{10,... | collective-permute-start | bytes 3145736 | tf_op jit(solution)/shard_map/ppermute | solution.py:462
  548.5 75.4 %collective-permute-start.50 = (bf16[8,128,2048]{2,1,0:T(8,128)(2,1)}, bf16[8,128,2048]{2,1,0:T(8,128)(2,1)}, u32[]{:S(2)}, u32[]{:S(2)}) collective-permute-start(bf16[8,128,2048]{2,1,0:T(8,128)(2,1)} %constant_dynamic-update-slice_fusion.13.own), channel_id=1, source_target_pairs={{0,1},{1,0},{2,3},{3,2},{4,5},{5,4},{6,7},{7,6},{8,9},{9,8},{10,11... | collective-permute-start | bytes 12582920 | tf_op jit(solution)/shard_map/ppermute | solution.py:462
  595.3 71.4 %collective-permute-start.47 = (bf16[2,2,256,2048]{3,2,1,0:T(8,128)(2,1)}, bf16[2,2,256,2048]{3,2,1,0:T(8,128)(2,1)}, u32[]{:S(2)}, u32[]{:S(2)}) collective-permute-start(bf16[2,2,256,2048]{3,2,1,0:T(8,128)(2,1)} %get-tuple-element.379), channel_id=1, source_target_pairs={{0,1},{1,0},{2,3},{3,2},{4,5},{5,4},{6,7},{7,6},{8,9},{9,8},{10,11... | collective-permute-start | bytes 12582920 | tf_op jit(solution)/shard_map/ppermute | solution.py:462
  601.0 65.8 %collective-permute-start.45 = (bf16[2,128,2048]{2,1,0:T(8,128)(2,1)}, bf16[2,128,2048]{2,1,0:T(8,128)(2,1)}, u32[]{:S(2)}, u32[]{:S(2)}) collective-permute-start(bf16[2,128,2048]{2,1,0:T(8,128)(2,1)} %fusion.58), channel_id=1, source_target_pairs={{0,2},{1,3},{2,0},{3,1},{4,6},{5,7},{6,4},{7,5},{8,10},{9,11},{10,... | collective-permute-start | bytes 3145736 | tf_op jit(solution)/shard_map/ppermute | solution.py:462
  623.1 43.6 %collective-permute-start.46 = (bf16[2,128,2048]{2,1,0:T(8,128)(2,1)}, bf16[2,128,2048]{2,1,0:T(8,128)(2,1)}, u32[]{:S(2)}, u32[]{:S(2)}) collective-permute-start(bf16[2,128,2048]{2,1,0:T(8,128)(2,1)} %get-tuple-element.378), channel_id=1, source_target_pairs={{0,4},{4,0},{8,12},{12,8},{16,20},{20,16},{24,28},{28,24},{1,5},{5... | collective-permute-start | bytes 3145736 | tf_op jit(solution)/shard_map/ppermute | solution.py:462
  628.6 54.1 %collective-permute-start.56 = (bf16[8,128,2048]{2,1,0:T(8,128)(2,1)}, bf16[8,128,2048]{2,1,0:T(8,128)(2,1)}, u32[]{:S(2)}, u32[]{:S(2)}) collective-permute-start(bf16[8,128,2048]{2,1,0:T(8,128)(2,1)} %constant_dynamic-update-slice_fusion.17.own), channel_id=1, source_target_pairs={{0,1},{1,0},{2,3},{3,2},{4,5},{5,4},{6,7},{7,6},{8,9},{9,8},{10,11... | collective-permute-start | bytes 12582920 | tf_op jit(solution)/shard_map/ppermute | solution.py:462
  736.9 51.3 %collective-permute-start.61 = (bf16[2,2,256,2048]{3,2,1,0:T(8,128)(2,1)}, bf16[2,2,256,2048]{3,2,1,0:T(8,128)(2,1)}, u32[]{:S(2)}, u32[]{:S(2)}) collective-permute-start(bf16[2,2,256,2048]{3,2,1,0:T(8,128)(2,1)} %get-tuple-element.431), channel_id=1, source_target_pairs={{0,1},{1,0},{2,3},{3,2},{4,5},{5,4},{6,7},{7,6},{8,9},{9,8},{10,11... | collective-permute-start | bytes 12582920 | tf_op jit(solution)/shard_map/ppermute | solution.py:462
  789.9 63.3 %collective-permute-start.67 = (bf16[2,2,256,2048]{3,2,1,0:T(8,128)(2,1)}, bf16[2,2,256,2048]{3,2,1,0:T(8,128)(2,1)}, u32[]{:S(2)}, u32[]{:S(2)}) collective-permute-start(bf16[2,2,256,2048]{3,2,1,0:T(8,128)(2,1)} %get-tuple-element.460), channel_id=1, source_target_pairs={{0,1},{1,0},{2,3},{3,2},{4,5},{5,4},{6,7},{7,6},{8,9},{9,8},{10,11... | collective-permute-start | bytes 12582920 | tf_op jit(solution)/shard_map/ppermute | solution.py:462
  790.0 63.2 %collective-permute-start.68 = (bf16[2,2,256,2048]{3,2,1,0:T(8,128)(2,1)}, bf16[2,2,256,2048]{3,2,1,0:T(8,128)(2,1)}, u32[]{:S(2)}, u32[]{:S(2)}) collective-permute-start(bf16[2,2,256,2048]{3,2,1,0:T(8,128)(2,1)} %get-tuple-element.461), channel_id=1, source_target_pairs={{0,1},{1,0},{2,3},{3,2},{4,5},{5,4},{6,7},{7,6},{8,9},{9,8},{10,11... | collective-permute-start | bytes 12582920 | tf_op jit(solution)/shard_map/ppermute | solution.py:462
  804.7 48.4 %collective-permute-start.64 = (bf16[2,128,2048]{2,1,0:T(8,128)(2,1)}, bf16[2,128,2048]{2,1,0:T(8,128)(2,1)}, u32[]{:S(2)}, u32[]{:S(2)}) collective-permute-start(bf16[2,128,2048]{2,1,0:T(8,128)(2,1)} %fusion.70), channel_id=1, source_target_pairs={{0,2},{1,3},{2,0},{3,1},{4,6},{5,7},{6,4},{7,5},{8,10},{9,11},{10,... | collective-permute-start | bytes 3145736 | tf_op jit(solution)/shard_map/ppermute | solution.py:462
  858.3 44.9 %collective-permute-start.72 = (bf16[2,2,256,2048]{3,2,1,0:T(8,128)(2,1)}, bf16[2,2,256,2048]{3,2,1,0:T(8,128)(2,1)}, u32[]{:S(2)}, u32[]{:S(2)}) collective-permute-start(bf16[2,2,256,2048]{3,2,1,0:T(8,128)(2,1)} %get-tuple-element.509), channel_id=1, source_target_pairs={{0,1},{1,0},{2,3},{3,2},{4,5},{5,4},{6,7},{7,6},{8,9},{9,8},{10,11... | collective-permute-start | bytes 12582920 | tf_op jit(solution)/shard_map/ppermute | solution.py:462
  858.3 44.9 %collective-permute-start.73 = (bf16[2,2,256,2048]{3,2,1,0:T(8,128)(2,1)}, bf16[2,2,256,2048]{3,2,1,0:T(8,128)(2,1)}, u32[]{:S(2)}, u32[]{:S(2)}) collective-permute-start(bf16[2,2,256,2048]{3,2,1,0:T(8,128)(2,1)} %get-tuple-element.510), channel_id=1, source_target_pairs={{0,1},{1,0},{2,3},{3,2},{4,5},{5,4},{6,7},{7,6},{8,9},{9,8},{10,11... | collective-permute-start | bytes 12582920 | tf_op jit(solution)/shard_map/ppermute | solution.py:462
  921.7 339.8 %reduce-scatter.5.cloned.1.call-start = ((), (), s32[]{:S(2)}) async-start(), calls=%async_computation.4 | async-start | bytes 5242880 | tf_op jit(solution)/shard_map/reduce_scatter | solution.py:1107
  960.0 47.9 %collective-permute-start.76 = (bf16[256,2048]{1,0:T(8,128)(2,1)}, bf16[256,2048]{1,0:T(8,128)(2,1)S(1)}, u32[]{:S(2)}, u32[]{:S(2)}) collective-permute-start(bf16[256,2048]{1,0:T(8,128)(2,1)} %get-tuple-element.557.refs_0_), channel_id=1, source_target_pairs={{0,2},{1,3},{2,0},{3,1},{4,6},{5,7},{6,4},{7,5},{8,10},{9,11},{10,... | collective-permute-start | bytes 3145736 | tf_op jit(solution)/shard_map/ppermute | solution.py:462
  961.6 46.3 %collective-permute-start.75 = (bf16[256,2048]{1,0:T(8,128)(2,1)}, bf16[256,2048]{1,0:T(8,128)(2,1)}, u32[]{:S(2)}, u32[]{:S(2)}) collective-permute-start(bf16[256,2048]{1,0:T(8,128)(2,1)} %get-tuple-element.557.refs_0_), channel_id=1, source_target_pairs={{0,1},{1,0},{2,3},{3,2},{4,5},{5,4},{6,7},{7,6},{8,9},{9,8},{10,11... | collective-permute-start | bytes 3145736 | tf_op jit(solution)/shard_map/ppermute | solution.py:462
  1154.5 54.9 %collective-permute-start.80 = (bf16[256,1536]{1,0:T(8,128)(2,1)S(1)}, bf16[256,1536]{1,0:T(8,128)(2,1)S(1)}, u32[]{:S(2)}, u32[]{:S(2)}) collective-permute-start(bf16[256,1536]{1,0:T(8,128)(2,1)S(1)} %get-tuple-element.621), channel_id=1, source_target_pairs={{0,4},{4,0},{8,12},{12,8},{16,20},{20,16},{24,28},{28,24},{1,5},{5... | collective-permute-start | bytes 2359304 | tf_op jit(solution)/shard_map/ppermute | solution.py:462
  1155.6 55.9 %collective-permute-start.85 = (bf16[256,2048]{1,0:T(8,128)(2,1)S(1)}, bf16[256,2048]{1,0:T(8,128)(2,1)S(1)}, u32[]{:S(2)}, u32[]{:S(2)}) collective-permute-start(bf16[256,2048]{1,0:T(8,128)(2,1)S(1)} %fusion.26), channel_id=1, source_target_pairs={{0,2},{1,3},{2,0},{3,1},{4,6},{5,7},{6,4},{7,5},{8,10},{9,11},{10,... | collective-permute-start | bytes 3145736 | tf_op jit(solution)/shard_map/ppermute | solution.py:462
  1157.5 52.5 %collective-permute-start.84 = (bf16[256,1536]{1,0:T(8,128)(2,1)S(1)}, bf16[256,1536]{1,0:T(8,128)(2,1)S(1)}, u32[]{:S(2)}, u32[]{:S(2)}) collective-permute-start(bf16[256,1536]{1,0:T(8,128)(2,1)S(1)} %fusion.43), channel_id=1, source_target_pairs={{0,8},{4,12},{8,16},{12,20},{16,24},{20,28},{24,0},{28,4},{1,9},{5... | collective-permute-start | bytes 2359304 | tf_op jit(solution)/shard_map/ppermute | solution.py:479
  (206 other events, 3552.0 us)
Sparse Core Ops, SparseCore 0:
  138.4 240.3 all-gather.1
  921.8 177.2 reduce-scatter.2
  1101.4 97.3 reduce-scatter.4

commit v8 on v7

--- a/solution.py
+++ b/solution.py
@@ -498,14 +498,15 @@
             first(values) if plane + 1 < planes else ((), ()),
             next_plane(values) if plane + 2 < planes else (),
             far_core(pieces[-1]) if plane else (),
-            work(plane, small),
+            work(plane - 2, small) if plane > 1 else (),
         ]
         upper_far, lower_far, (across_pack, across_side), following, other, result = (
             lax.optimization_barrier(moved)
         )
         if plane:
             pieces[-1] = (pieces[-1], other)
-        made.append(result)
+        if plane > 1:
+            made.append(result)
         pieces.append(jnp.concatenate([upper, lower, upper_far, lower_far]))
     pieces[-1] = (pieces[-1], far_core(pieces[-1]))
     return pieces, made
@@ -555,14 +556,37 @@
     )(order, *pieces)
 
 
-def fold_packs(values):
-    order = plane_order()
-    take = lambda index: lax.dynamic_index_in_dim(values, order[index], 0, keepdims=False)
-    near = [added(take(2 * i), far_pack(take(2 * i + 1))) for i in range(values.shape[0] // 2)]
-    summed = near[1]
-    for part in near[2:]:
-        summed = added(next_plane(summed), part)
-    return added(next_plane(summed), near[0], jnp.float32)
+class FoldPacks:
+    def __init__(self, values):
+        order = plane_order()
+        take = lambda index: lax.dynamic_index_in_dim(values, order[index], 0, keepdims=False)
+        planes = values.shape[0] // 2
+        self.turns = [*range(1, planes), 0]
+        self.near = {plane: take(2 * plane) for plane in self.turns}
+        self.moving = {plane: far_pack(take(2 * plane + 1)) for plane in self.turns}
+        self.summed, self.count = None, 0
+
+    def step(self, other):
+        if self.count >= len(self.turns):
+            return other
+        self.moving, other = tied(self.moving, other)
+        if self.summed is None:
+            self.near = {plane: added(self.near[plane], self.moving[plane]) for plane in self.turns}
+            self.summed = self.near[self.turns[0]]
+        else:
+            kind = jnp.float32 if self.count + 1 == len(self.turns) else jnp.bfloat16
+            self.summed = added(self.moving, self.near[self.turns[self.count]], kind)
+        self.count += 1
+        if self.count < len(self.turns):
+            self.moving = next_plane(self.summed)
+        return other
+
+    def finish(self):
+        for plane in self.turns[self.count :]:
+            kind = jnp.float32 if plane == 0 else jnp.bfloat16
+            self.summed = added(self.moving, self.near[plane], kind)
+            self.moving = next_plane(self.summed) if plane else None
+        return self.summed
 
 
 def laid_sides(pieces):
@@ -610,7 +634,7 @@
     return summed, total
 
 
-def gather_both(weights, outer, rows):
+def gather_both(weights, outer, rows, gate, up):
     pieces, outer_pieces, row_pieces, values = [], [], [rows], (weights, outer)
     planes = lax.axis_size("plane")
     for plane in range(planes):
@@ -621,13 +645,17 @@
             moved += [far_core(rows), far_side(rows)]
         if plane == 1:
             moved += [far_core(row_pieces[2])]
+        if plane == 0:
+            moved.insert(2, jnp.concatenate([gate, up], axis=2))
         across, following, *arrived = lax.optimization_barrier(moved)
+        if plane == 0:
+            joined = arrived.pop(0)
         pieces += [values[0], across[0]]
         outer_pieces += [values[1], across[1]]
         row_pieces += arrived
         values = following
     order = plane_order()
-    return laid(pieces, order), laid(outer_pieces, order, True), laid_sides(row_pieces)
+    return laid(pieces, order), laid(outer_pieces, order, True), laid_sides(row_pieces), joined
 
 
 def sum_everywhere(values):
@@ -820,7 +848,7 @@
         return self.count == len(self.order)
 
 
-def experts_by_gather(second_in, all_cot, places, gates, w_gate, w_up, w_down, capacity):
+def experts_by_gather(second_in, all_cot, places, gates, w_both, w_down, capacity):
     packs, local_experts, seq_len = places.shape
     tensor_count = lax.axis_size(TENSOR)
     planes = packs // 2
@@ -837,11 +865,19 @@
     core_order = lax.axis_index("core") ^ jnp.arange(tensor_count, dtype=jnp.int32)
     mix_places = as_met(places, jnp.arange(packs, dtype=jnp.int32), core_order)
     mix_gates = as_met(gates, jnp.arange(packs, dtype=jnp.int32), core_order)
-    w_both = jnp.concatenate([w_gate, w_up], axis=2)
     pairs = [slice(plane * 2, plane * 2 + 2) for plane in range(planes)]
+    tables = [
+        jnp.stack([lax.axis_index("pack"), (lax.axis_index("plane") + planes - plane) % planes])
+        for plane in range(planes)
+    ]
+    prepared = [
+        [table[pair] for pair in pairs] for table in (near_places, mix_places, mix_gates, pack_order)
+    ]
+    prepared, second_in = tied((prepared, tables, places, gates), second_in)
+    (near_places, mix_places, mix_gates, pack_order), tables, places, gates = prepared
 
     def cot_work(plane, order):
-        return cot_slots(order[pairs[plane]], places, gates, all_cot, w_down, capacity)
+        return cot_slots(order[plane], places, gates, all_cot, w_down, capacity)
 
     pieces, made = spread_all(second_in, pack_order, cot_work)
     order = [*range(1, planes), 0]
@@ -851,25 +887,20 @@
         return row_slots(near, *pieces[plane], w_both, made[plane][1], capacity)
 
     for plane in range(planes):
-        near = near_places[pairs[plane]]
         if plane:
-            result = folding.turn(near, functools.partial(row_work, plane))
+            result = folding.turn(near_places[plane], functools.partial(row_work, plane))
         else:
-            result = row_work(plane, near)
+            result = row_work(plane, near_places[plane])
         slots, hidden, above, *part = result
         folding.begin(plane, *part)
         kept[plane] = (slots, hidden, made[plane][0], above)
+        if len(made) < planes:
+            made.append(folding.turn(pack_order, functools.partial(cot_work, len(made))))
     hidden_all = jnp.concatenate([kept[plane][1] for plane in range(planes)])
-    tables = jnp.stack(
-        [
-            jnp.stack([lax.axis_index("pack"), (lax.axis_index("plane") + planes - plane) % planes])
-            for plane in range(planes)
-        ]
-    )
-
     def mix_work(plane, table):
-        pair = pairs[plane]
-        return mix_rows(table[plane], mix_places[pair], mix_gates[pair], hidden_all, w_down, capacity)
+        return mix_rows(
+            table[plane], mix_places[plane], mix_gates[plane], hidden_all, w_down, capacity
+        )
 
     def cross():
         return [far_core(parts[plane][1]) for plane in parts if plane not in crossed]
@@ -961,7 +992,9 @@
         side_sum, side_gather = fold_sides, gather_sides
         local_width = w_query.shape[1]
         w_in = jnp.concatenate([w_query, w_key, w_value], axis=1)
-        full_in, full_output, pack_in = gather_both(w_in, w_output, first_in)
+        full_in, full_output, pack_in, w_both = gather_both(
+            w_in, w_output, first_in, w_gate, w_up
+        )
         full_in, cotangent = tied(full_in, cotangent)
         all_cot = lax.all_gather(cotangent, axes, axis=0, tiled=True)
         all_cot = all_cot.reshape(data_count, seq_len, model_width)
@@ -1016,7 +1049,7 @@
     second_in = (normed_two * ffn_gain).astype(jnp.bfloat16)
     if by_gather:
         grad_second, mixed, rest = experts_by_gather(
-            second_in, all_cot, places, gates, w_gate, w_up, w_down, capacity
+            second_in, all_cot, places, gates, w_both, w_down, capacity
         )
     else:
         outputs, grad_second, grad_w_gate, grad_w_up, grad_w_down = experts_by_exchange(
@@ -1040,6 +1073,11 @@
     else:
         pack_grad = side_gather(grad_attended)
     output_part = contract_first(mixture, pack_grad)
+    fold_step = lambda other: other
+    if by_gather:
+        by_column = output_part.astype(jnp.bfloat16).reshape(local_width, data_count, -1)
+        folded = FoldPacks(by_column.transpose(1, 0, 2))
+        fold_step = folded.step
     grad_mixture = (
         contract_last(pack_grad, full_output)
         .astype(jnp.bfloat16)
@@ -1051,6 +1089,8 @@
     for block_index in range(block_total):
         offset = block_index * block_rows
         query_block = query_low[offset : offset + block_rows]
+        if block_index:
+            query_block = fold_step(query_block)
         grad_block = grad_mixture[offset : offset + block_rows]
         scores = block_scores(query_block, key_low, masks[block_index], inv_root)
         prob_rows = jnp.exp(scores - lse_parts[block_index])
@@ -1078,6 +1118,8 @@
         )
     grad_query_norm = rotate_back(jnp.concatenate(grad_query_parts, axis=0), cosine, sine_tab)
     grad_key_norm = rotate_back(grad_key_sum, cosine, sine_tab)
+    grad_query_norm = fold_step(grad_query_norm)
+    grad_key_norm = fold_step(grad_key_norm)
     query_gain_part = jnp.sum(grad_query_norm * query_norm, axis=(0, 1))
     key_gain_part = jnp.sum(grad_key_norm * key_norm, axis=(0, 1))
     grad_query_pre = (
@@ -1099,10 +1141,10 @@
     total_term = total_term + contract_last(grad_key_pre, full_key)
     total_term = total_term + contract_last(grad_value_low, full_value)
     if by_gather:
-        by_column = output_part.astype(jnp.bfloat16).reshape(local_width, data_count, -1)
-        grad_w_output = fold_packs(by_column.transpose(1, 0, 2))
         in_part = jnp.concatenate([query_part, key_part, value_part], axis=1)
         in_part = in_part.astype(jnp.bfloat16).reshape(data_count, -1, 3 * local_width)
+        in_part = fold_step(in_part)
+        grad_w_output = folded.finish()
         mixed, in_part = tied(mixed, in_part)
         mixed = lax.psum_scatter(mixed, "plane", scatter_dimension=0, tiled=True)
         grad_in, grad_first = fold_both(in_part, total_term)
@@ -1117,10 +1159,8 @@
             grad_in[:, index * local_width : (index + 1) * local_width] for index in range(3)
         )
         outputs = middle + mixed[0].astype(jnp.float32)
-        late = sum_everywhere(attn_gain_part)
-        early = sum_everywhere(jnp.concatenate(gain_parts[1:]))
-        splits = (model_width, model_width + head_size)
-        gain_sums = (late, *jnp.split(early, splits))
+        splits = (model_width, 2 * model_width, 2 * model_width + head_size)
+        gain_sums = jnp.split(sum_everywhere(jnp.concatenate(gain_parts)), splits)
     else:
         grad_w_query, grad_w_key, grad_w_value, grad_w_output = (
             lax.psum_scatter(

time: 1280 us -> 1250 us (0.977)
  local copies, waits for them, and re-layouts: 117 us -> 90.7 us
    all_gather x1, waiting for transfers between devices: 69.2 us -> 0.01 us  [shards(): all_cot = lax.all_gather(cotangent, axes, axis=0, tiled=True)]
    ppermute x87 -> x82, waiting for transfers between devices: 225 us -> 293 us  [swapped(): return lax.ppermute(values, axis, [(i, i ^ bit) for i in range(count)])]
    reduce_scatter x1, waiting for transfers between devices: 20.7 us -> 0.01 us  [experts_by_gather(): lax.psum_scatter(whole, ('pack', 'side'), scatter_dimension=1, tiled=True)]
    ppermute x18, waiting for transfers between devices: 102 us -> 120 us  [next_plane(): lax.ppermute(values, DP, [(i, (i + 2) % count) for i in range(count)])]
    concatenate x1 -> x5, other arithmetic: 0.01 us -> 14.1 us  [the longest x1 13.7 us: gather_both(): moved.insert(2, jnp.concatenate([gate, up], axis=2))]
    unnamed x287 -> x292, local copies, waits for them, and re-layouts: 44 us -> 32.4 us
    ppermute x87 -> x82, starting transfers between devices: 73.8 us -> 64.2 us  [swapped(): return lax.ppermute(values, axis, [(i, i ^ bit) for i in range(count)])]
  transfers between devices with their start and end apart: 108 -> 103, of which waited for: 34 -> 33; matrix products, arithmetic and copies ran while one was open for 22% -> 22% of each run, Pallas kernels for 29% -> 27%
where the time goes in v8:
time: 1250 us; the launch traced here: 1240 us
  waiting for transfers between devices  413 us (33%)
  Pallas kernels  378 us (30%)
  other arithmetic  158 us (13%)
  starting transfers between devices  106 us (8%)
  local copies, waits for them, and re-layouts  90.7 us (7%)
  matrix products  82.4 us (7%)
  between operations  17.1 us (1%)
    ppermute x82, waiting for transfers between devices, swapped(): return lax.ppermute(values, axis, [(i, i ^ bit) for i in range(count)])  293 us
    pallas_call x4, Pallas kernels, row_slots(): call(functools.partial(row_kernel, packs, steps, capacity), 2 * packs + s...  152 us
    ppermute x18, waiting for transfers between devices, next_plane(): lax.ppermute(values, DP, [(i, (i + 2) % count) for i in range(count)])  120 us
    convert_element_type x42, other arithmetic, added(): return (left.astype(jnp.float32) + right.astype(jnp.float32)).astype(kind)  81.9 us
    pallas_call x4, Pallas kernels, cot_slots(): call(functools.partial(cot_kernel, packs, steps, capacity), packs + steps...  81.7 us
    pallas_call x4, Pallas kernels, mix_rows(): call(functools.partial(mix_kernel, packs, steps, capacity), packs + steps...  71.1 us
    ppermute x82, starting transfers between devices, swapped(): return lax.ppermute(values, axis, [(i, i ^ bit) for i in range(count)])  64.2 us
    pallas_call x4, Pallas kernels, weight_grads(): call(functools.partial(weight_kernel, planes), count, [block(operand.shap...  53 us
  transfers between devices with their start and end apart: 103, of which 33 were waited for; matrix products, arithmetic and copies ran while one was open for 22% of the time, Pallas kernels for 27%

profile of v8, /device:TPU:0, one launch (start us, length us, event | category | flops | bytes accessed | tf_op | source)
XLA Modules:
  0.0 1244.8 jit_solution(16318996832664233020)
XLA Ops:
  21.5 13.7 %pad_maximum_fusion.both = bf16[8,2048,512]{2,1,0:T(8,128)(2,1)} fusion(bf16[8,2048,256]{2,1,0:T(8,128)(2,1)} %param.33, bf16[8,2048,256]{2,1,0:T(8,128)(2,1)} %param.32), kind=kLoop, calls=%fused_computation.8 | loop fusion | flops 33554432 | bytes 33554432 | tf_op jit(solution)/shard_map/concatenate | solution.py:649
  48.8 23.4 %collective-permute-done.9.refs_4_ = bf16[512,256]{1,0:T(8,128)(2,1)S(1)} collective-permute-done((bf16[512,256]{1,0:T(8,128)(2,1)S(1)}, bf16[512,256]{1,0:T(8,128)(2,1)S(1)}, u32[]{:S(2)}, u32[]{:S(2)}) %collective-permute-start.9) | collective-permute-done | bytes 262176 | tf_op jit(solution)/shard_map/ppermute | solution.py:479
  75.6 23.3 %collective-permute-done.14.refs_6_ = bf16[512,256]{1,0:T(8,128)(2,1)S(1)} collective-permute-done((bf16[512,256]{1,0:T(8,128)(2,1)S(1)}, bf16[512,256]{1,0:T(8,128)(2,1)S(1)}, u32[]{:S(2)}, u32[]{:S(2)}) %collective-permute-start.14) | collective-permute-done | bytes 262176 | tf_op jit(solution)/shard_map/ppermute | solution.py:479
  102.1 21.1 %collective-permute-done.16.refs_7_ = bf16[512,256]{1,0:T(8,128)(2,1)} collective-permute-done((bf16[512,256]{1,0:T(8,128)(2,1)S(1)}, bf16[512,256]{1,0:T(8,128)(2,1)}, u32[]{:S(2)}, u32[]{:S(2)}) %collective-permute-start.16) | collective-permute-done | bytes 262176 | tf_op jit(solution)/shard_map/ppermute | solution.py:462
  156.3 13.5 %collective-permute-done.24 = bf16[16,17,256]{2,0,1:T(8,128)(2,1)S(1)} collective-permute-done((bf16[16,17,256]{2,0,1:T(8,128)(2,1)S(1)}, bf16[16,17,256]{2,0,1:T(8,128)(2,1)S(1)}, u32[]{:S(2)}, u32[]{:S(2)}) %collective-permute-start.24) | collective-permute-done | bytes 139296 | tf_op jit(solution)/shard_map/ppermute | solution.py:462
  245.8 34.2 %collective-permute-done.21 = bf16[256,2048]{1,0:T(8,128)(2,1)} collective-permute-done((bf16[256,2048]{1,0:T(8,128)(2,1)S(1)}, bf16[256,2048]{1,0:T(8,128)(2,1)}, u32[]{:S(2)}, u32[]{:S(2)}) %collective-permute-start.21) | collective-permute-done | bytes 1048608 | tf_op jit(solution)/shard_map/ppermute | solution.py:462
  287.2 22.0 %collective-permute-done.26 = bf16[128,2048]{1,0:T(8,128)(2,1)S(1)} collective-permute-done((bf16[128,2048]{1,0:T(8,128)(2,1)S(1)}, bf16[128,2048]{1,0:T(8,128)(2,1)S(1)}, u32[]{:S(2)}, u32[]{:S(2)}) %collective-permute-start.26) | collective-permute-done | bytes 524320 | tf_op jit(solution)/shard_map/ppermute | solution.py:462
  309.2 11.7 collective-permute-done.27
  326.1 33.0 %collective-permute-done.31 = bf16[128,2048]{1,0:T(8,128)(2,1)S(1)} collective-permute-done((bf16[128,2048]{1,0:T(8,128)(2,1)S(1)}, bf16[128,2048]{1,0:T(8,128)(2,1)S(1)}, u32[]{:S(2)}, u32[]{:S(2)}) %collective-permute-start.31) | collective-permute-done | bytes 524320 | tf_op jit(solution)/shard_map/ppermute | solution.py:462
  385.6 21.3 %collective-permute-done.35 = bf16[128,2048]{1,0:T(8,128)(2,1)S(1)} collective-permute-done((bf16[128,2048]{1,0:T(8,128)(2,1)S(1)}, bf16[128,2048]{1,0:T(8,128)(2,1)S(1)}, u32[]{:S(2)}, u32[]{:S(2)}) %collective-permute-start.35) | collective-permute-done | bytes 524320 | tf_op jit(solution)/shard_map/ppermute | solution.py:462
  415.3 20.4 %shard_map.258 = (bf16[8,256,2048]{2,1,0:T(8,128)(2,1)}, f32[8,256,256]{2,1,0:T(8,128)}) custom-call(s32[2]{0:T(128)} %get-tuple-element.412.table, bf16[8,8,1024]{2,1,0:T(8,128)(2,1)} %get-tuple-element.413.places, bf16[8,8,1024]{2,1,0:T(8,128)(2,1)} %copy-done.26, bf16[8,1024,2048]{2,1,0:T(8,128)(2,1)} %bitcast.328, bf16[8,256,2048]{2,1,0:T(8,128)(2,1)} %down.15), custom_call_target="tpu_custom_call" | custom-call | flops 10737418240 | bytes 21474836 | tf_op jit(solution)/shard_map/pallas_call | solution.py:357
  447.6 38.1 %shard_map.259 = (bf16[8,256,2048]{2,1,0:T(8,128)(2,1)}, bf16[8,256,256]{2,1,0:T(8,128)(2,1)}, bf16[8,256,512]{2,1,0:T(8,128)(2,1)}, bf16[2,2,256,2048]{3,2,1,0:T(8,128)(2,1)}, bf16[2,2,256,2048]{3,2,1,0:T(8,128)(2,1)}) custom-call(bf16[2,8,1024]{2,1,0:T(8,128)(2,1)} %bitcast.403, bf16[8,128,2048]{2,1,0:T(8,128)(2,1)} %copy-done.99, ...), custom_call_target="tpu_custom_call" | custom-call | flops 25769803776 | bytes 51539608 | tf_op jit(solution)/shard_map/pallas_call | solution.py:390
  496.8 20.4 %shard_map.260 = (bf16[8,256,2048]{2,1,0:T(8,128)(2,1)}, f32[8,256,256]{2,1,0:T(8,128)}) custom-call(s32[2]{0:T(128)} %get-tuple-element.423.table, bf16[8,8,1024]{2,1,0:T(8,128)(2,1)} %get-tuple-element.413.places, bf16[8,8,1024]{2,1,0:T(8,128)(2,1)} %copy-done.26, bf16[8,1024,2048]{2,1,0:T(8,128)(2,1)} %bitcast.329, bf16[8,256,2048]{2,1,0:T(8,128)(2,1)} %down.15), custom_call_target="tpu_custom_call" | custom-call | flops 10737418240 | bytes 21474836 | tf_op jit(solution)/shard_map/pallas_call | solution.py:357
  517.2 20.4 %shard_map.261 = (bf16[8,256,2048]{2,1,0:T(8,128)(2,1)}, f32[8,256,256]{2,1,0:T(8,128)}) custom-call(s32[2]{0:T(128)} %get-tuple-element.439.table, bf16[8,8,1024]{2,1,0:T(8,128)(2,1)} %get-tuple-element.413.places, bf16[8,8,1024]{2,1,0:T(8,128)(2,1)} %copy-done.26, bf16[8,1024,2048]{2,1,0:T(8,128)(2,1)} %bitcast.330, bf16[8,256,2048]{2,1,0:T(8,128)(2,1)} %down.15), custom_call_target="tpu_custom_call" | custom-call | flops 10737418240 | bytes 21474836 | tf_op jit(solution)/shard_map/pallas_call | solution.py:357
  549.1 38.2 %shard_map.262 = (bf16[8,256,2048]{2,1,0:T(8,128)(2,1)}, bf16[8,256,256]{2,1,0:T(8,128)(2,1)}, bf16[8,256,512]{2,1,0:T(8,128)(2,1)}, bf16[2,2,256,2048]{3,2,1,0:T(8,128)(2,1)}, bf16[2,2,256,2048]{3,2,1,0:T(8,128)(2,1)}) custom-call(bf16[2,8,1024]{2,1,0:T(8,128)(2,1)} %bitcast.402, bf16[8,128,2048]{2,1,0:T(8,128)(2,1)} %constant_dynamic-update-slice_fusion.7.own, ...), custom_call_target="tpu_custom_call" | custom-call | flops 25769803776 | bytes 51539608 | tf_op jit(solution)/shard_map/pallas_call | solution.py:390
  601.6 20.4 %shard_map.263 = (bf16[8,256,2048]{2,1,0:T(8,128)(2,1)}, f32[8,256,256]{2,1,0:T(8,128)}) custom-call(s32[2]{0:T(128)} %get-tuple-element.457.table, bf16[8,8,1024]{2,1,0:T(8,128)(2,1)} %get-tuple-element.413.places, bf16[8,8,1024]{2,1,0:T(8,128)(2,1)} %copy-done.26, bf16[8,1024,2048]{2,1,0:T(8,128)(2,1)} %bitcast.331, bf16[8,256,2048]{2,1,0:T(8,128)(2,1)} %down.15), custom_call_target="tpu_custom_call" | custom-call | flops 10737418240 | bytes 21474836 | tf_op jit(solution)/shard_map/pallas_call | solution.py:357
  634.6 37.8 %shard_map.264 = (bf16[8,256,2048]{2,1,0:T(8,128)(2,1)}, bf16[8,256,256]{2,1,0:T(8,128)(2,1)}, bf16[8,256,512]{2,1,0:T(8,128)(2,1)}, bf16[2,2,256,2048]{3,2,1,0:T(8,128)(2,1)}, bf16[2,2,256,2048]{3,2,1,0:T(8,128)(2,1)}) custom-call(bf16[2,8,1024]{2,1,0:T(8,128)(2,1)} %bitcast.401, bf16[8,128,2048]{2,1,0:T(8,128)(2,1)} %constant_dynamic-update-slice_fusion.11.own, ...), custom_call_target="tpu_custom_call" | custom-call | flops 25769803776 | bytes 51539608 | tf_op jit(solution)/shard_map/pallas_call | solution.py:390
  676.2 38.2 %shard_map.265 = (bf16[8,256,2048]{2,1,0:T(8,128)(2,1)}, bf16[8,256,256]{2,1,0:T(8,128)(2,1)}, bf16[8,256,512]{2,1,0:T(8,128)(2,1)}, bf16[2,2,256,2048]{3,2,1,0:T(8,128)(2,1)}, bf16[2,2,256,2048]{3,2,1,0:T(8,128)(2,1)}) custom-call(bf16[2,8,1024]{2,1,0:T(8,128)(2,1)} %bitcast.400, bf16[8,128,2048]{2,1,0:T(8,128)(2,1)} %constant_dynamic-update-slice_fusion.15.own, ...), custom_call_target="tpu_custom_call" | custom-call | flops 25769803776 | bytes 51539608 | tf_op jit(solution)/shard_map/pallas_call | solution.py:390
  732.4 17.7 %shard_map.266 = (bf16[2,2,256,2048]{3,2,1,0:T(8,128)(2,1)}, bf16[2,2,256,2048]{3,2,1,0:T(8,128)(2,1)}) custom-call(s32[2]{0:T(128)} %get-tuple-element.501.table, bf16[2,8,1024]{2,1,0:T(8,128)(2,1)} %bitcast.399, bf16[2,8,1024]{2,1,0:T(8,128)(2,1)} %bitcast.397, bf16[32,256,256]{2,1,0:T(8,128)(2,1)} %constant_dynamic-update-slice_fusion.19.hidden, ...), custom_call_target="tpu_custom_call" | custom-call | flops 10737418240 | bytes 21474836 | tf_op jit(solution)/shard_map/pallas_call | solution.py:418
  750.1 18.1 %shard_map.267 = (bf16[2,2,256,2048]{3,2,1,0:T(8,128)(2,1)}, bf16[2,2,256,2048]{3,2,1,0:T(8,128)(2,1)}) custom-call(s32[2]{0:T(128)} %get-tuple-element.510.table, bf16[2,8,1024]{2,1,0:T(8,128)(2,1)} %bitcast.398, bf16[2,8,1024]{2,1,0:T(8,128)(2,1)} %bitcast.396, bf16[32,256,256]{2,1,0:T(8,128)(2,1)} %constant_dynamic-update-slice_fusion.19.hidden, ...), custom_call_target="tpu_custom_call" | custom-call | flops 10737418240 | bytes 21474836 | tf_op jit(solution)/shard_map/pallas_call | solution.py:418
  801.2 17.7 %shard_map.268 = (bf16[2,2,256,2048]{3,2,1,0:T(8,128)(2,1)}, bf16[2,2,256,2048]{3,2,1,0:T(8,128)(2,1)}) custom-call(s32[2]{0:T(128)} %get-tuple-element.525.table, bf16[2,8,1024]{2,1,0:T(8,128)(2,1)} %bitcast.394, bf16[2,8,1024]{2,1,0:T(8,128)(2,1)} %bitcast.392, bf16[32,256,256]{2,1,0:T(8,128)(2,1)} %constant_dynamic-update-slice_fusion.19.hidden, ...), custom_call_target="tpu_custom_call" | custom-call | flops 10737418240 | bytes 21474836 | tf_op jit(solution)/shard_map/pallas_call | solution.py:418
  818.9 17.6 %shard_map.269 = (bf16[2,2,256,2048]{3,2,1,0:T(8,128)(2,1)}, bf16[2,2,256,2048]{3,2,1,0:T(8,128)(2,1)}) custom-call(s32[2]{0:T(128)} %get-tuple-element.530.table, bf16[2,8,1024]{2,1,0:T(8,128)(2,1)} %bitcast.395, bf16[2,8,1024]{2,1,0:T(8,128)(2,1)} %bitcast.393, bf16[32,256,256]{2,1,0:T(8,128)(2,1)} %constant_dynamic-update-slice_fusion.19.hidden, ...), custom_call_target="tpu_custom_call" | custom-call | flops 10737418240 | bytes 21474836 | tf_op jit(solution)/shard_map/pallas_call | solution.py:418
  862.8 13.1 %shard_map.270 = (f32[8,2048,256]{2,1,0:T(8,128)}, f32[8,2048,256]{2,1,0:T(8,128)}, f32[8,256,2048]{2,1,0:T(8,128)}) custom-call(bf16[8,256,2048]{2,1,0:T(8,128)(2,1)} %get-tuple-element.633.refs_0_, bf16[8,256,2048]{2,1,0:T(8,128)(2,1)} %get-tuple-element.634.refs_1_, bf16[8,256,2048]{2,1,0:T(8,128)(2,1)} %get-tuple-element.635.refs_2_, ...), custom_call_target="tpu_custom_call" | custom-call | flops 6442450944 | bytes 12884901 | tf_op jit(solution)/shard_map/pallas_call | solution.py:447
  875.9 13.1 %shard_map.271 = (f32[8,2048,256]{2,1,0:T(8,128)}, f32[8,2048,256]{2,1,0:T(8,128)}, f32[8,256,2048]{2,1,0:T(8,128)}) custom-call(bf16[8,256,2048]{2,1,0:T(8,128)(2,1)} %get-tuple-element.633.refs_0_, bf16[8,256,2048]{2,1,0:T(8,128)(2,1)} %get-tuple-element.634.refs_1_, ...), custom_call_target="tpu_custom_call", output_to_operand_aliasing={{0}: (16, {}), {1}: (17, {}), {2}: (18, {})} | custom-call | flops 6442450944 | bytes 12884901 | tf_op jit(solution)/shard_map/pallas_call | solution.py:447
  913.9 13.5 %shard_map.272 = (f32[8,2048,256]{2,1,0:T(8,128)}, f32[8,2048,256]{2,1,0:T(8,128)}, f32[8,256,2048]{2,1,0:T(8,128)}) custom-call(bf16[8,256,2048]{2,1,0:T(8,128)(2,1)} %get-tuple-element.633.refs_0_, bf16[8,256,2048]{2,1,0:T(8,128)(2,1)} %get-tuple-element.634.refs_1_, ...), custom_call_target="tpu_custom_call", output_to_operand_aliasing={{0}: (16, {}), {1}: (17, {}), {2}: (18, {})} | custom-call | flops 6442450944 | bytes 12884901 | tf_op jit(solution)/shard_map/pallas_call | solution.py:447
  927.4 12.4 collective-permute-done.74
  946.3 13.3 %shard_map.273 = (f32[8,2048,256]{2,1,0:T(8,128)}, f32[8,2048,256]{2,1,0:T(8,128)}, f32[8,256,2048]{2,1,0:T(8,128)}) custom-call(bf16[8,256,2048]{2,1,0:T(8,128)(2,1)} %get-tuple-element.633.refs_0_, bf16[8,256,2048]{2,1,0:T(8,128)(2,1)} %get-tuple-element.634.refs_1_, ...), custom_call_target="tpu_custom_call", output_to_operand_aliasing={{0}: (16, {}), {1}: (17, {}), {2}: (18, {})} | custom-call | flops 6442450944 | bytes 12884901 | tf_op jit(solution)/shard_map/pallas_call | solution.py:447
  959.6 33.9 %collective-permute-done.76.refs_2_ = bf16[256,2048]{1,0:T(8,128)(2,1)S(1)} collective-permute-done((bf16[256,2048]{1,0:T(8,128)(2,1)}, bf16[256,2048]{1,0:T(8,128)(2,1)S(1)}, u32[]{:S(2)}, u32[]{:S(2)}) %collective-permute-start.76) | collective-permute-done | bytes 1048608 | tf_op jit(solution)/shard_map/ppermute | solution.py:462
  1119.5 17.0 %collective-permute-done.88 = bf16[256,1536]{1,0:T(8,128)(2,1)S(1)} collective-permute-done((bf16[256,1536]{1,0:T(8,128)(2,1)S(1)}, bf16[256,1536]{1,0:T(8,128)(2,1)S(1)}, u32[]{:S(2)}, u32[]{:S(2)}) %collective-permute-start.88) | collective-permute-done | bytes 786464 | tf_op jit(solution)/shard_map/ppermute | solution.py:462
  1153.4 22.6 %collective-permute-done.91 = bf16[256,1536]{1,0:T(8,128)(2,1)S(1)} collective-permute-done((bf16[256,1536]{1,0:T(8,128)(2,1)S(1)}, bf16[256,1536]{1,0:T(8,128)(2,1)S(1)}, u32[]{:S(2)}, u32[]{:S(2)}) %collective-permute-start.91) | collective-permute-done | bytes 786464 | tf_op jit(solution)/shard_map/ppermute | solution.py:479
  1176.3 12.1 collective-permute-start.93
  1216.4 15.9 %collective-permute-done.94 = bf16[256,1536]{1,0:T(8,128)(2,1)S(1)} collective-permute-done((bf16[256,1536]{1,0:T(8,128)(2,1)S(1)}, bf16[256,1536]{1,0:T(8,128)(2,1)S(1)}, u32[]{:S(2)}, u32[]{:S(2)}) %collective-permute-start.94) | collective-permute-done | bytes 786464 | tf_op jit(solution)/shard_map/ppermute | solution.py:479
  (714 shorter events, 538.5 us)
Async XLA Ops:
  7.2 408.1 %all-gather.2.cloned.1.call-start = ((), (), s32[]{:S(2)}) async-start(), calls=%async_computation.2 | async-start | bytes 34603008 | tf_op jit(solution)/shard_map/all_gather | solution.py:999
  129.4 968.8 %reduce-scatter.3.cloned.1.call-start = ((), (), s32[]{:S(2)}) async-start(), calls=%async_computation.3 | async-start | bytes 20971520 | tf_op jit(solution)/shard_map/reduce_scatter | solution.py:944
  231.4 48.6 %collective-permute-start.21 = (bf16[256,2048]{1,0:T(8,128)(2,1)S(1)}, bf16[256,2048]{1,0:T(8,128)(2,1)}, u32[]{:S(2)}, u32[]{:S(2)}) collective-permute-start(bf16[256,2048]{1,0:T(8,128)(2,1)S(1)} %fusion.31), channel_id=1, source_target_pairs={{0,2},{1,3},{2,0},{3,1},{4,6},{5,7},{6,4},{7,5},{8,10},{9,11},{10,... | collective-permute-start | bytes 3145736 | tf_op jit(solution)/shard_map/ppermute | solution.py:462
  325.4 42.4 %collective-permute-start.32 = (bf16[256,2048]{1,0:T(8,128)(2,1)S(1)}, bf16[256,2048]{1,0:T(8,128)(2,1)S(1)}, u32[]{:S(2)}, u32[]{:S(2)}) collective-permute-start(bf16[256,2048]{1,0:T(8,128)(2,1)S(1)} %collective-permute-done.27), channel_id=1, source_target_pairs={{0,8},{4,12},{8,16},{12,20},{16,24},{20,28},{24,0},{28,4},{1,9},{5... | collective-permute-start | bytes 3145736 | tf_op jit(solution)/shard_map/ppermute | solution.py:479
  485.7 51.9 %collective-permute-start.44 = (bf16[2,2,256,2048]{3,2,1,0:T(8,128)(2,1)}, bf16[2,2,256,2048]{3,2,1,0:T(8,128)(2,1)}, u32[]{:S(2)}, u32[]{:S(2)}) collective-permute-start(bf16[2,2,256,2048]{3,2,1,0:T(8,128)(2,1)} %get-tuple-element.422), channel_id=1, source_target_pairs={{0,1},{1,0},{2,3},{3,2},{4,5},{5,4},{6,7},{7,6},{8,9},{9,8},{10,11... | collective-permute-start | bytes 12582920 | tf_op jit(solution)/shard_map/ppermute | solution.py:462
  492.6 56.6 %collective-permute-start.49 = (bf16[8,128,2048]{2,1,0:T(8,128)(2,1)}, bf16[8,128,2048]{2,1,0:T(8,128)(2,1)}, u32[]{:S(2)}, u32[]{:S(2)}) collective-permute-start(bf16[8,128,2048]{2,1,0:T(8,128)(2,1)} %constant_dynamic-update-slice_fusion.11.own), channel_id=1, source_target_pairs={{0,1},{1,0},{2,3},{3,2},{4,5},{5,4},{6,7},{7,6},{8,9},{9,8},{10,11... | collective-permute-start | bytes 12582920 | tf_op jit(solution)/shard_map/ppermute | solution.py:462
  495.4 53.8 %collective-permute-start.47 = (bf16[2,128,2048]{2,1,0:T(8,128)(2,1)S(1)}, bf16[2,128,2048]{2,1,0:T(8,128)(2,1)}, u32[]{:S(2)}, u32[]{:S(2)}) collective-permute-start(bf16[2,128,2048]{2,1,0:T(8,128)(2,1)S(1)} %pad_maximum_fusion.14), channel_id=1, source_target_pairs={{0,2},{1,3},{2,0},{3,1},{4,6},{5,7},{6,4},{7,5},{8,10},{9,11},{10,... | collective-permute-start | bytes 3145736 | tf_op jit(solution)/shard_map/ppermute | solution.py:462
  496.5 52.6 %collective-permute-start.48 = (bf16[2,128,2048]{2,1,0:T(8,128)(2,1)S(1)}, bf16[2,128,2048]{2,1,0:T(8,128)(2,1)}, u32[]{:S(2)}, u32[]{:S(2)}) collective-permute-start(bf16[2,128,2048]{2,1,0:T(8,128)(2,1)S(1)} %pad_maximum_fusion.15), channel_id=1, source_target_pairs={{0,4},{4,0},{8,12},{12,8},{16,20},{20,16},{24,28},{28,24},{1,5},{5... | collective-permute-start | bytes 3145736 | tf_op jit(solution)/shard_map/ppermute | solution.py:462
  546.4 41.0 %collective-permute-start.45 = (bf16[2,128,2048]{2,1,0:T(8,128)(2,1)}, bf16[2,128,2048]{2,1,0:T(8,128)(2,1)}, u32[]{:S(2)}, u32[]{:S(2)}) collective-permute-start(bf16[2,128,2048]{2,1,0:T(8,128)(2,1)} %fusion.62), channel_id=1, source_target_pairs={{0,2},{1,3},{2,0},{3,1},{4,6},{5,7},{6,4},{7,5},{8,10},{9,11},{10,... | collective-permute-start | bytes 3145736 | tf_op jit(solution)/shard_map/ppermute | solution.py:462
  547.4 40.0 %collective-permute-start.46 = (bf16[2,128,2048]{2,1,0:T(8,128)(2,1)}, bf16[2,128,2048]{2,1,0:T(8,128)(2,1)}, u32[]{:S(2)}, u32[]{:S(2)}) collective-permute-start(bf16[2,128,2048]{2,1,0:T(8,128)(2,1)} %get-tuple-element.429), channel_id=1, source_target_pairs={{0,4},{4,0},{8,12},{12,8},{16,20},{20,16},{24,28},{28,24},{1,5},{5... | collective-permute-start | bytes 3145736 | tf_op jit(solution)/shard_map/ppermute | solution.py:462
  599.8 76.4 %collective-permute-start.58 = (bf16[8,128,2048]{2,1,0:T(8,128)(2,1)}, bf16[8,128,2048]{2,1,0:T(8,128)(2,1)}, u32[]{:S(2)}, u32[]{:S(2)}) collective-permute-start(bf16[8,128,2048]{2,1,0:T(8,128)(2,1)} %constant_dynamic-update-slice_fusion.15.own), channel_id=1, source_target_pairs={{0,1},{1,0},{2,3},{3,2},{4,5},{5,4},{6,7},{7,6},{8,9},{9,8},{10,11... | collective-permute-start | bytes 12582920 | tf_op jit(solution)/shard_map/ppermute | solution.py:462
  631.9 40.5 %collective-permute-start.53 = (bf16[2,128,2048]{2,1,0:T(8,128)(2,1)}, bf16[2,128,2048]{2,1,0:T(8,128)(2,1)S(1)}, u32[]{:S(2)}, u32[]{:S(2)}) collective-permute-start(bf16[2,128,2048]{2,1,0:T(8,128)(2,1)} %fusion.66), channel_id=1, source_target_pairs={{0,2},{1,3},{2,0},{3,1},{4,6},{5,7},{6,4},{7,5},{8,10},{9,11},{10,... | collective-permute-start | bytes 3145736 | tf_op jit(solution)/shard_map/ppermute | solution.py:462
  632.9 39.6 %collective-permute-start.54 = (bf16[2,128,2048]{2,1,0:T(8,128)(2,1)}, bf16[2,128,2048]{2,1,0:T(8,128)(2,1)}, u32[]{:S(2)}, u32[]{:S(2)}) collective-permute-start(bf16[2,128,2048]{2,1,0:T(8,128)(2,1)} %get-tuple-element.463), channel_id=1, source_target_pairs={{0,4},{4,0},{8,12},{12,8},{16,20},{20,16},{24,28},{28,24},{1,5},{5... | collective-permute-start | bytes 3145736 | tf_op jit(solution)/shard_map/ppermute | solution.py:462
  674.7 39.8 %collective-permute-start.57 = (bf16[2,2,256,2048]{3,2,1,0:T(8,128)(2,1)}, bf16[2,2,256,2048]{3,2,1,0:T(8,128)(2,1)}, u32[]{:S(2)}, u32[]{:S(2)}) collective-permute-start(bf16[2,2,256,2048]{3,2,1,0:T(8,128)(2,1)} %get-tuple-element.480), channel_id=1, source_target_pairs={{0,1},{1,0},{2,3},{3,2},{4,5},{5,4},{6,7},{7,6},{8,9},{9,8},{10,11... | collective-permute-start | bytes 12582920 | tf_op jit(solution)/shard_map/ppermute | solution.py:462
  674.7 39.7 %collective-permute-start.55 = (bf16[128,2048]{1,0:T(8,128)(2,1)S(1)}, bf16[128,2048]{1,0:T(8,128)(2,1)S(1)}, u32[]{:S(2)}, u32[]{:S(2)}) collective-permute-start(bf16[128,2048]{1,0:T(8,128)(2,1)S(1)} %get-tuple-element.478), channel_id=1, source_target_pairs={{0,4},{4,0},{8,12},{12,8},{16,20},{20,16},{24,28},{28,24},{1,5},{5... | collective-permute-start | bytes 1572872 | tf_op jit(solution)/shard_map/ppermute | solution.py:462
  675.1 39.3 %collective-permute-start.56 = (bf16[128,2048]{1,0:T(8,128)(2,1)S(1)}, bf16[128,2048]{1,0:T(8,128)(2,1)S(1)}, u32[]{:S(2)}, u32[]{:S(2)}) collective-permute-start(bf16[128,2048]{1,0:T(8,128)(2,1)S(1)} %get-tuple-element.479), channel_id=1, source_target_pairs={{0,2},{1,3},{2,0},{3,1},{4,6},{5,7},{6,4},{7,5},{8,10},{9,11},{10,... | collective-permute-start | bytes 1572872 | tf_op jit(solution)/shard_map/ppermute | solution.py:462
  725.5 42.7 %collective-permute-start.61 = (bf16[2,2,256,2048]{3,2,1,0:T(8,128)(2,1)}, bf16[2,2,256,2048]{3,2,1,0:T(8,128)(2,1)}, u32[]{:S(2)}, u32[]{:S(2)}) collective-permute-start(bf16[2,2,256,2048]{3,2,1,0:T(8,128)(2,1)} %get-tuple-element.500), channel_id=1, source_target_pairs={{0,1},{1,0},{2,3},{3,2},{4,5},{5,4},{6,7},{7,6},{8,9},{9,8},{10,11... | collective-permute-start | bytes 12582920 | tf_op jit(solution)/shard_map/ppermute | solution.py:462
  728.6 39.5 %collective-permute-start.59 = (bf16[2,128,2048]{2,1,0:T(8,128)(2,1)}, bf16[2,128,2048]{2,1,0:T(8,128)(2,1)S(1)}, u32[]{:S(2)}, u32[]{:S(2)}) collective-permute-start(bf16[2,128,2048]{2,1,0:T(8,128)(2,1)} %fusion.70), channel_id=1, source_target_pairs={{0,2},{1,3},{2,0},{3,1},{4,6},{5,7},{6,4},{7,5},{8,10},{9,11},{10,... | collective-permute-start | bytes 3145736 | tf_op jit(solution)/shard_map/ppermute | solution.py:462
  769.9 66.6 %collective-permute-start.67 = (bf16[2,2,256,2048]{3,2,1,0:T(8,128)(2,1)}, bf16[2,2,256,2048]{3,2,1,0:T(8,128)(2,1)}, u32[]{:S(2)}, u32[]{:S(2)}) collective-permute-start(bf16[2,2,256,2048]{3,2,1,0:T(8,128)(2,1)} %get-tuple-element.535), channel_id=1, source_target_pairs={{0,1},{1,0},{2,3},{3,2},{4,5},{5,4},{6,7},{7,6},{8,9},{9,8},{10,11... | collective-permute-start | bytes 12582920 | tf_op jit(solution)/shard_map/ppermute | solution.py:462
  770.0 66.6 %collective-permute-start.68 = (bf16[2,2,256,2048]{3,2,1,0:T(8,128)(2,1)}, bf16[2,2,256,2048]{3,2,1,0:T(8,128)(2,1)}, u32[]{:S(2)}, u32[]{:S(2)}) collective-permute-start(bf16[2,2,256,2048]{3,2,1,0:T(8,128)(2,1)} %get-tuple-element.536), channel_id=1, source_target_pairs={{0,1},{1,0},{2,3},{3,2},{4,5},{5,4},{6,7},{7,6},{8,9},{9,8},{10,11... | collective-permute-start | bytes 12582920 | tf_op jit(solution)/shard_map/ppermute | solution.py:462
  780.9 55.6 %collective-permute-start.64 = (bf16[2,128,2048]{2,1,0:T(8,128)(2,1)}, bf16[2,128,2048]{2,1,0:T(8,128)(2,1)}, u32[]{:S(2)}, u32[]{:S(2)}) collective-permute-start(bf16[2,128,2048]{2,1,0:T(8,128)(2,1)} %fusion.74), channel_id=1, source_target_pairs={{0,2},{1,3},{2,0},{3,1},{4,6},{5,7},{6,4},{7,5},{8,10},{9,11},{10,... | collective-permute-start | bytes 3145736 | tf_op jit(solution)/shard_map/ppermute | solution.py:462
  793.3 43.2 %collective-permute-start.65 = (bf16[2,128,2048]{2,1,0:T(8,128)(2,1)}, bf16[2,128,2048]{2,1,0:T(8,128)(2,1)}, u32[]{:S(2)}, u32[]{:S(2)}) collective-permute-start(bf16[2,128,2048]{2,1,0:T(8,128)(2,1)} %get-tuple-element.523), channel_id=1, source_target_pairs={{0,4},{4,0},{8,12},{12,8},{16,20},{20,16},{24,28},{28,24},{1,5},{5... | collective-permute-start | bytes 3145736 | tf_op jit(solution)/shard_map/ppermute | solution.py:462
  794.8 41.7 %collective-permute-start.66 = (bf16[256,2048]{1,0:T(8,128)(2,1)}, bf16[256,2048]{1,0:T(8,128)(2,1)}, u32[]{:S(2)}, u32[]{:S(2)}) collective-permute-start(bf16[256,2048]{1,0:T(8,128)(2,1)} %pad_maximum_fusion.16), channel_id=1, source_target_pairs={{0,8},{4,12},{8,16},{12,20},{16,24},{20,28},{24,0},{28,4},{1,9},{5... | collective-permute-start | bytes 3145736 | tf_op jit(solution)/shard_map/ppermute | solution.py:479
  841.7 47.4 %collective-permute-start.72 = (bf16[2,2,256,2048]{3,2,1,0:T(8,128)(2,1)}, bf16[2,2,256,2048]{3,2,1,0:T(8,128)(2,1)}, u32[]{:S(2)}, u32[]{:S(2)}) collective-permute-start(bf16[2,2,256,2048]{3,2,1,0:T(8,128)(2,1)} %get-tuple-element.584), channel_id=1, source_target_pairs={{0,1},{1,0},{2,3},{3,2},{4,5},{5,4},{6,7},{7,6},{8,9},{9,8},{10,11... | collective-permute-start | bytes 12582920 | tf_op jit(solution)/shard_map/ppermute | solution.py:462
  841.7 47.4 %collective-permute-start.73 = (bf16[2,2,256,2048]{3,2,1,0:T(8,128)(2,1)}, bf16[2,2,256,2048]{3,2,1,0:T(8,128)(2,1)}, u32[]{:S(2)}, u32[]{:S(2)}) collective-permute-start(bf16[2,2,256,2048]{3,2,1,0:T(8,128)(2,1)} %get-tuple-element.585), channel_id=1, source_target_pairs={{0,1},{1,0},{2,3},{3,2},{4,5},{5,4},{6,7},{7,6},{8,9},{9,8},{10,11... | collective-permute-start | bytes 12582920 | tf_op jit(solution)/shard_map/ppermute | solution.py:462
  845.2 43.8 %collective-permute-start.69 = (bf16[128,2048]{1,0:T(8,128)(2,1)}, bf16[128,2048]{1,0:T(8,128)(2,1)S(1)}, u32[]{:S(2)}, u32[]{:S(2)}) collective-permute-start(bf16[128,2048]{1,0:T(8,128)(2,1)} %get-tuple-element.559), channel_id=1, source_target_pairs={{0,4},{4,0},{8,12},{12,8},{16,20},{20,16},{24,28},{28,24},{1,5},{5... | collective-permute-start | bytes 1572872 | tf_op jit(solution)/shard_map/ppermute | solution.py:462
  845.6 43.4 %collective-permute-start.70 = (bf16[128,2048]{1,0:T(8,128)(2,1)}, bf16[128,2048]{1,0:T(8,128)(2,1)S(1)}, u32[]{:S(2)}, u32[]{:S(2)}) collective-permute-start(bf16[128,2048]{1,0:T(8,128)(2,1)} %get-tuple-element.560), channel_id=1, source_target_pairs={{0,2},{1,3},{2,0},{3,1},{4,6},{5,7},{6,4},{7,5},{8,10},{9,11},{10,... | collective-permute-start | bytes 1572872 | tf_op jit(solution)/shard_map/ppermute | solution.py:462
  846.0 43.1 %collective-permute-start.71 = (bf16[256,2048]{1,0:T(8,128)(2,1)S(1)}, bf16[256,2048]{1,0:T(8,128)(2,1)S(1)}, u32[]{:S(2)}, u32[]{:S(2)}) collective-permute-start(bf16[256,2048]{1,0:T(8,128)(2,1)S(1)} %add_convert_fusion.7), channel_id=1, source_target_pairs={{0,8},{4,12},{8,16},{12,20},{16,24},{20,28},{24,0},{28,4},{1,9},{5... | collective-permute-start | bytes 3145736 | tf_op jit(solution)/shard_map/ppermute | solution.py:479
  907.6 326.1 %reduce-scatter.5.cloned.1.call-start = ((), (), s32[]{:S(2)}) async-start(), calls=%async_computation.4 | async-start | bytes 5242880 | tf_op jit(solution)/shard_map/reduce_scatter | solution.py:1149
  945.8 47.7 %collective-permute-start.76 = (bf16[256,2048]{1,0:T(8,128)(2,1)}, bf16[256,2048]{1,0:T(8,128)(2,1)S(1)}, u32[]{:S(2)}, u32[]{:S(2)}) collective-permute-start(bf16[256,2048]{1,0:T(8,128)(2,1)} %get-tuple-element.632.refs_0_), channel_id=1, source_target_pairs={{0,2},{1,3},{2,0},{3,1},{4,6},{5,7},{6,4},{7,5},{8,10},{9,11},{10,... | collective-permute-start | bytes 3145736 | tf_op jit(solution)/shard_map/ppermute | solution.py:462
  946.3 47.3 %collective-permute-start.75 = (bf16[256,2048]{1,0:T(8,128)(2,1)}, bf16[256,2048]{1,0:T(8,128)(2,1)}, u32[]{:S(2)}, u32[]{:S(2)}) collective-permute-start(bf16[256,2048]{1,0:T(8,128)(2,1)} %get-tuple-element.632.refs_0_), channel_id=1, source_target_pairs={{0,1},{1,0},{2,3},{3,2},{4,5},{5,4},{6,7},{7,6},{8,9},{9,8},{10,11... | collective-permute-start | bytes 3145736 | tf_op jit(solution)/shard_map/ppermute | solution.py:462
  1141.9 69.2 %collective-permute-start.86 = (bf16[256,1536]{1,0:T(8,128)(2,1)S(1)}, bf16[256,1536]{1,0:T(8,128)(2,1)S(1)}, u32[]{:S(2)}, u32[]{:S(2)}) collective-permute-start(bf16[256,1536]{1,0:T(8,128)(2,1)S(1)} %get-tuple-element.708), channel_id=1, source_target_pairs={{0,4},{4,0},{8,12},{12,8},{16,20},{20,16},{24,28},{28,24},{1,5},{5... | collective-permute-start | bytes 2359304 | tf_op jit(solution)/shard_map/ppermute | solution.py:462
  (204 other events, 3576.0 us)
Sparse Core Ops, SparseCore 0:
  129.5 256.1 all-gather.1
  907.7 183.7 reduce-scatter.2
  1098.3 94.0 reduce-scatter.4

commit v9 on v8

--- a/solution.py
+++ b/solution.py
@@ -278,9 +278,8 @@
             slots_to_rows(pick.at[pack], grads, rows_own, rows_other, pack)
 
 
-def mix_kernel(
-    packs, steps, capacity, table, places, gates, hidden, down, rows_own, rows_other, results, pick
-):
+def mix_kernel(packs, steps, capacity, table, places, gates, hidden, down, *refs):
+    rows, results, pick = refs[-3:]
     step = pl.program_id(0)
 
     @pl.when(step < steps)
@@ -292,7 +291,11 @@
     @pl.when(step >= steps)
     def _():
         select_rows(places, gates, pick, capacity)
-        slots_to_rows(pick, results, rows_own, rows_other, (step - steps) ^ table[0])
+        pack = (step - steps) ^ table[0]
+        for start in range(0, rows.shape[3], COLUMN_CHUNK):
+            columns = slice(start, start + COLUMN_CHUNK)
+            slots = results[:, pack, :, columns].reshape(-1, COLUMN_CHUNK)
+            rows[0, 0, :, columns] = contract_first(pick[...], slots).astype(rows.dtype)
 
 
 def weight_kernel(planes, *refs):
@@ -407,30 +410,31 @@
     )(places, own, other, both, grad_hidden)
 
 
-def mix_rows(table, places, gates, hidden, down, capacity):
+def mix_rows(plane, planes, table, places, gates, hidden, down, capacity, earlier=()):
     packs, _, seq_len = places.shape
     experts, hidden_width, width = down.shape
     group = math.gcd(experts, GROUP)
     steps = experts // group
     first, last = staged(0, steps), staged(steps, packs)
     listed = lambda step, numbers: numbers[1] * steps + first(step)
-    part = shape_of((packs, 2, seq_len // 4, width), jnp.bfloat16)
     return call(
         functools.partial(mix_kernel, packs, steps, capacity),
         packs + steps,
         [
             block(places.shape, last), block(gates.shape, last),
             block(hidden.shape, listed, group), block(down.shape, first, group),
-        ],
-        [block(part.shape, last)] * 2,
-        [part, part],
+        ]
+        + [pl.BlockSpec(memory_space=pl.ANY)] * len(earlier),
+        [pl.BlockSpec((1, 1, seq_len, width), lambda step, numbers: (plane, last(step), 0, 0))],
+        [shape_of((planes, packs, seq_len, width), jnp.bfloat16)],
         [
             pltpu.VMEM((experts, packs, capacity, width), jnp.bfloat16),
             pltpu.VMEM((experts * capacity, seq_len), jnp.bfloat16),
         ],
         2 * experts * packs * capacity * width * (seq_len + hidden_width),
         1,
-    )(table, places, gates, hidden, down)
+        aliases={5 + index: index for index in range(len(earlier))},
+    )(table, places, gates, hidden, down, *earlier)
 
 
 def weight_grads(first, count, slots, hidden, grads, above, earlier=()):
@@ -634,7 +638,8 @@
     return summed, total
 
 
-def gather_both(weights, outer, rows, gate, up):
+def gather_both(weights, outer, rows, gate, up, tables):
+    hops = table_hops()
     pieces, outer_pieces, row_pieces, values = [], [], [rows], (weights, outer)
     planes = lax.axis_size("plane")
     for plane in range(planes):
@@ -647,7 +652,10 @@
             moved += [far_core(row_pieces[2])]
         if plane == 0:
             moved.insert(2, jnp.concatenate([gate, up], axis=2))
-        across, following, *arrived = lax.optimization_barrier(moved)
+        moved.insert(2, swapped(tables, *hops[plane]) if plane < len(hops) else ())
+        across, following, more, *arrived = lax.optimization_barrier(moved)
+        if plane < len(hops):
+            tables = jnp.concatenate([tables, more])
         if plane == 0:
             joined = arrived.pop(0)
         pieces += [values[0], across[0]]
@@ -655,7 +663,10 @@
         row_pieces += arrived
         values = following
     order = plane_order()
-    return laid(pieces, order), laid(outer_pieces, order, True), laid_sides(row_pieces), joined
+    for hop in hops[planes:]:
+        tables = jnp.concatenate([tables, swapped(tables, *hop)])
+    laid_rows = laid_sides(row_pieces)
+    return laid(pieces, order), laid(outer_pieces, order, True), laid_rows, joined, tables
 
 
 def sum_everywhere(values):
@@ -686,21 +697,21 @@
     return lax.optimization_barrier((small, values))
 
 
-def gather_tables(expert_ids, gate_values, segment_ids):
-    top_count = expert_ids.shape[1]
-    tables = jnp.concatenate(
-        [expert_ids.T.astype(jnp.bfloat16), gate_values.T, segment_ids.astype(jnp.bfloat16)]
-    )[None]
+def table_hops():
+    hops = []
     for axis in (TENSOR, DP):
         bit = 1
         while bit < lax.axis_size(axis):
-            tables = jnp.concatenate([tables, swapped(tables, axis, bit)])
+            hops.append((axis, bit))
             bit *= 2
-        if axis == TENSOR:
-            sides = jnp.arange(tables.shape[0], dtype=jnp.int32) ^ lax.axis_index(TENSOR)
-            segments = jnp.take(tables[:, -1], sides, axis=0).reshape(-1)
+    return hops
+
+
+def read_tables(tables, top_count):
+    own = lax.axis_index(DP) * lax.axis_size(TENSOR) + lax.axis_index(TENSOR)
+    sides = jnp.arange(lax.axis_size(TENSOR), dtype=jnp.int32) ^ lax.axis_index(TENSOR)
+    segments = jnp.take(tables[: sides.shape[0], -1], sides, axis=0).reshape(-1)
     devices = jnp.arange(tables.shape[0], dtype=jnp.int32)
-    own = lax.axis_index(DP) * lax.axis_size(TENSOR) + lax.axis_index(TENSOR)
     tables = jnp.take(tables, devices ^ own, axis=0)
     all_ids, all_gates = tables[:, :top_count], tables[:, top_count : 2 * top_count]
     return all_ids.astype(jnp.int32), all_gates, segments.astype(jnp.int32)
@@ -799,7 +810,7 @@
 class Folding:
     def __init__(self, order):
         self.order, self.planes, self.ready = order, {}, {}
-        self.summed, self.count = None, 0
+        self.summed, self.passed, self.count = None, None, 0
 
     def begin(self, plane, own, other):
         self.planes[plane] = (0, (own, other))
@@ -817,8 +828,11 @@
                 sent[plane] = (far_side(values[2]), far_pack(values[3]))
             else:
                 sent[plane] = (far_pack(values[2]), far_side(values[3]))
-        passed = None if summed is None else next_plane(summed)
+        passed = self.passed
+        if passed is None and summed is not None and not self.done():
+            passed = next_plane(summed)
         sent, passed, result = lax.optimization_barrier((sent, passed, work(small)))
+        self.passed = passed
         for plane, values in planes.items():
             stage, arrived = self.planes[plane][0], sent[plane]
             if stage == 0:
@@ -841,6 +855,7 @@
             if passed is not None:
                 kind = jnp.float32 if last else jnp.bfloat16
                 self.summed = added(passed, self.summed, kind)
+            self.passed = None
             self.count += 1
         return result
 
@@ -862,16 +877,13 @@
         return split.reshape(values.shape)
 
     near_places = as_met(places, pack_order, quarter_order)
-    core_order = lax.axis_index("core") ^ jnp.arange(tensor_count, dtype=jnp.int32)
-    mix_places = as_met(places, jnp.arange(packs, dtype=jnp.int32), core_order)
-    mix_gates = as_met(gates, jnp.arange(packs, dtype=jnp.int32), core_order)
     pairs = [slice(plane * 2, plane * 2 + 2) for plane in range(planes)]
     tables = [
         jnp.stack([lax.axis_index("pack"), (lax.axis_index("plane") + planes - plane) % planes])
         for plane in range(planes)
     ]
     prepared = [
-        [table[pair] for pair in pairs] for table in (near_places, mix_places, mix_gates, pack_order)
+        [table[pair] for pair in pairs] for table in (near_places, places, gates, pack_order)
     ]
     prepared, second_in = tied((prepared, tables, places, gates), second_in)
     (near_places, mix_places, mix_gates, pack_order), tables, places, gates = prepared
@@ -881,13 +893,13 @@
 
     pieces, made = spread_all(second_in, pack_order, cot_work)
     order = [*range(1, planes), 0]
-    kept, parts, folding = {}, {}, Folding(order)
+    kept, folding = {}, Folding(order)
 
     def row_work(plane, near):
         return row_slots(near, *pieces[plane], w_both, made[plane][1], capacity)
 
-    for plane in range(planes):
-        if plane:
+    for plane in order:
+        if folding.planes:
             result = folding.turn(near_places[plane], functools.partial(row_work, plane))
         else:
             result = row_work(plane, near_places[plane])
@@ -897,24 +909,24 @@
         if len(made) < planes:
             made.append(folding.turn(pack_order, functools.partial(cot_work, len(made))))
     hidden_all = jnp.concatenate([kept[plane][1] for plane in range(planes)])
-    def mix_work(plane, table):
-        return mix_rows(
-            table[plane], mix_places[plane], mix_gates[plane], hidden_all, w_down, capacity
-        )
-
-    def cross():
-        return [far_core(parts[plane][1]) for plane in parts if plane not in crossed]
-
-    def mix_turn(some, table):
-        return [mix_work(plane, table) for plane in some], cross()
-
-    crossed = {}
+
+    def mix_turn(some, given):
+        table, mixed = given
+        for plane in some:
+            mixed = mix_rows(
+                plane, planes, table[plane], mix_places[plane], mix_gates[plane], hidden_all, w_down,
+                capacity, mixed,
+            )
+        return mixed
+
+    mixed = ()
     for start in range(0, planes, 2):
-        some = order[start : start + 2]
-        waiting = [plane for plane in parts if plane not in crossed]
-        results, arrived = folding.turn(tables, functools.partial(mix_turn, some))
-        crossed.update(zip(waiting, arrived))
-        parts.update(zip(some, results))
+        some = range(start, start + 2)
+        mixed = folding.turn((tables, mixed), functools.partial(mix_turn, some))
+    whole = mixed[0].reshape(planes, -1, mixed[0].shape[-1])
+    whole = lax.psum_scatter(
+        whole, ("pack", "side", "core"), scatter_dimension=1, tiled=True
+    )
     kept = [kept[plane] for plane in range(planes)]
     weight_parts, next_expert = (), 0
     part_size = math.gcd(local_experts, GROUP)
@@ -925,23 +937,13 @@
             if state < local_experts:
                 weights = weight_grads(state, part_size, *zip(*held), weights)
                 state += part_size
-        return weights, cross()
+        return weights
 
     for count in (2, 1, *[0] * planes):
         if folding.done():
             break
-        waiting = [plane for plane in parts if plane not in crossed]
-        weight_parts, arrived = folding.turn(
-            (kept, weight_parts), functools.partial(weight_turn, count)
-        )
+        weight_parts = folding.turn((kept, weight_parts), functools.partial(weight_turn, count))
         next_expert = min(next_expert + count * part_size, local_experts)
-        crossed.update(zip(waiting, arrived))
-        if len(crossed) == planes and waiting:
-            whole = jnp.stack(
-                [added(parts[plane][0], crossed[plane]) for plane in range(planes)]
-            )
-            whole = whole.reshape(planes, -1, whole.shape[-1])
-            whole = lax.psum_scatter(whole, ("pack", "side"), scatter_dimension=1, tiled=True)
     rest = (kept, weight_parts, next_expert, part_size)
     return folding.summed, whole, rest
 
@@ -983,8 +985,9 @@
     )
     if by_gather:
         axes = (*DP, *TENSOR)
-        all_ids, all_gates, segments = gather_tables(expert_ids, gate_values, segment_ids)
-        places, gates = routing(all_ids, all_gates, local_experts, capacity)
+        tables = jnp.concatenate(
+            [expert_ids.T.astype(jnp.bfloat16), gate_values.T, segment_ids.astype(jnp.bfloat16)]
+        )[None]
     inputs_f32 = inputs.astype(jnp.float32)
     normed_one, factor_one = norm_parts(inputs_f32)
     first_in = (normed_one * attn_gain).astype(jnp.bfloat16)
@@ -992,9 +995,11 @@
         side_sum, side_gather = fold_sides, gather_sides
         local_width = w_query.shape[1]
         w_in = jnp.concatenate([w_query, w_key, w_value], axis=1)
-        full_in, full_output, pack_in, w_both = gather_both(
-            w_in, w_output, first_in, w_gate, w_up
-        )
+        full_in, full_output, pack_in, w_both, tables = gather_both(
+            w_in, w_output, first_in, w_gate, w_up, tables
+        )
+        all_ids, all_gates, segments = read_tables(tables, top_count)
+        places, gates = routing(all_ids, all_gates, local_experts, capacity)
         full_in, cotangent = tied(full_in, cotangent)
         all_cot = lax.all_gather(cotangent, axes, axis=0, tiled=True)
         all_cot = all_cot.reshape(data_count, seq_len, model_width)

time: 1250 us -> 1220 us (0.976)
  starting transfers between devices: 106 us -> 153 us
  waiting for transfers between devices: 413 us -> 376 us
  other arithmetic: 158 us -> 123 us
    ppermute x18, starting transfers between devices: 41.2 us -> 88.5 us  [next_plane(): lax.ppermute(values, DP, [(i, (i + 2) % count) for i in range(count)])]
    ppermute x82 -> x78, waiting for transfers between devices: 293 us -> 255 us  [swapped(): return lax.ppermute(values, axis, [(i, i ^ bit) for i in range(count)])]
    convert_element_type x42 -> x38, other arithmetic: 81.9 us -> 60.1 us  [added(): return (left.astype(jnp.float32) + right.astype(jnp.float32)).astype(kind)]
    reduce_scatter x1, waiting for transfers between devices: 0.01 us -> 20.5 us  [experts_by_gather(): lax.psum_scatter(whole, ('pack', 'side', 'core'), scatter_dimension=1, ti...]
    ppermute x18, waiting for transfers between devices: 120 us -> 101 us  [next_plane(): lax.ppermute(values, DP, [(i, (i + 2) % count) for i in range(count)])]
    unnamed x292 -> x260, local copies, waits for them, and re-layouts: 32.4 us -> 33.8 us
    ppermute x82 -> x78, starting transfers between devices: 64.2 us -> 64.1 us  [swapped(): return lax.ppermute(values, axis, [(i, i ^ bit) for i in range(count)])]
  transfers between devices with their start and end apart: 103 -> 99, of which waited for: 33 -> 37; matrix products, arithmetic and copies ran while one was open for 22% -> 18% of each run, Pallas kernels for 27% -> 28%
where the time goes in v9:
time: 1220 us
  Pallas kernels  387 us (32%)
  waiting for transfers between devices  376 us (31%)
  starting transfers between devices  153 us (13%)
  other arithmetic  123 us (10%)
  local copies, waits for them, and re-layouts  85 us (7%)
  matrix products  74.6 us (6%)
  between operations  16.7 us (1%)
    ppermute x78, waiting for transfers between devices, swapped(): return lax.ppermute(values, axis, [(i, i ^ bit) for i in range(count)])  255 us
    pallas_call x4, Pallas kernels, row_slots(): call(functools.partial(row_kernel, packs, steps, capacity), 2 * packs + s...  152 us
    ppermute x18, waiting for transfers between devices, next_plane(): lax.ppermute(values, DP, [(i, (i + 2) % count) for i in range(count)])  101 us
    ppermute x18, starting transfers between devices, next_plane(): lax.ppermute(values, DP, [(i, (i + 2) % count) for i in range(count)])  88.5 us
    pallas_call x4, Pallas kernels, cot_slots(): call(functools.partial(cot_kernel, packs, steps, capacity), packs + steps...  81.6 us
    pallas_call x4, Pallas kernels, mix_rows(): call(functools.partial(mix_kernel, packs, steps, capacity), packs + steps...  70.9 us
    ppermute x78, starting transfers between devices, swapped(): return lax.ppermute(values, axis, [(i, i ^ bit) for i in range(count)])  64.1 us
    pallas_call x4, Pallas kernels, weight_grads(): call(functools.partial(weight_kernel, planes), count, [block(operand.shap...  62.7 us
  transfers between devices with their start and end apart: 99, of which 37 were waited for; matrix products, arithmetic and copies ran while one was open for 18% of the time, Pallas kernels for 28%

profile of v9, /device:TPU:0, one launch (start us, length us, event | category | flops | bytes accessed | tf_op | source)
XLA Modules:
  0.0 1215.5 jit_solution(12164271424915163072)
XLA Ops:
  21.8 13.7 %pad_maximum_fusion.both = bf16[8,2048,512]{2,1,0:T(8,128)(2,1)} fusion(bf16[8,2048,256]{2,1,0:T(8,128)(2,1)} %param.29, bf16[8,2048,256]{2,1,0:T(8,128)(2,1)} %param.28), kind=kLoop, calls=%fused_computation.4 | loop fusion | flops 33554432 | bytes 33554432 | tf_op jit(solution)/shard_map/concatenate | solution.py:654
  53.9 19.9 %collective-permute-done.10.refs_4_ = bf16[512,256]{1,0:T(8,128)(2,1)S(1)} collective-permute-done((bf16[512,256]{1,0:T(8,128)(2,1)S(1)}, bf16[512,256]{1,0:T(8,128)(2,1)S(1)}, u32[]{:S(2)}, u32[]{:S(2)}) %collective-permute-start.10) | collective-permute-done | bytes 262176 | tf_op jit(solution)/shard_map/ppermute | solution.py:483
  78.9 20.7 %collective-permute-done.17 = bf16[4,17,256]{2,0,1:T(4,128)(2,1)S(1)} collective-permute-done((bf16[4,17,256]{2,0,1:T(4,128)(2,1)S(1)}, bf16[4,17,256]{2,0,1:T(4,128)(2,1)S(1)}, u32[]{:S(2)}, u32[]{:S(2)}) %collective-permute-start.17) | collective-permute-done | bytes 34848 | tf_op jit(solution)/shard_map/ppermute | solution.py:466
  107.8 17.2 %collective-permute-done.19.refs_7_ = bf16[512,256]{1,0:T(8,128)(2,1)} collective-permute-done((bf16[512,256]{1,0:T(8,128)(2,1)}, bf16[512,256]{1,0:T(8,128)(2,1)}, u32[]{:S(2)}, u32[]{:S(2)}) %collective-permute-start.19) | collective-permute-done | bytes 262176 | tf_op jit(solution)/shard_map/ppermute | solution.py:466
  207.5 24.6 %collective-permute-done.23 = bf16[256,2048]{1,0:T(8,128)(2,1)S(1)} collective-permute-done((bf16[256,2048]{1,0:T(8,128)(2,1)S(1)}, bf16[256,2048]{1,0:T(8,128)(2,1)S(1)}, u32[]{:S(2)}, u32[]{:S(2)}) %collective-permute-start.23) | collective-permute-done | bytes 1048608 | tf_op jit(solution)/shard_map/ppermute | solution.py:466
  238.5 22.6 %collective-permute-done.26 = bf16[128,2048]{1,0:T(8,128)(2,1)S(1)} collective-permute-done((bf16[128,2048]{1,0:T(8,128)(2,1)S(1)}, bf16[128,2048]{1,0:T(8,128)(2,1)S(1)}, u32[]{:S(2)}, u32[]{:S(2)}) %collective-permute-start.26) | collective-permute-done | bytes 524320 | tf_op jit(solution)/shard_map/ppermute | solution.py:466
  261.5 20.4 %collective-permute-done.27 = bf16[256,2048]{1,0:T(8,128)(2,1)S(1)} collective-permute-done((bf16[256,2048]{1,0:T(8,128)(2,1)S(1)}, bf16[256,2048]{1,0:T(8,128)(2,1)S(1)}, u32[]{:S(2)}, u32[]{:S(2)}) %collective-permute-start.27) | collective-permute-done | bytes 1048608 | tf_op jit(solution)/shard_map/ppermute | solution.py:483
  282.1 23.3 %collective-permute-start.32 = (bf16[256,2048]{1,0:T(8,128)(2,1)S(1)}, bf16[256,2048]{1,0:T(8,128)(2,1)S(1)}, u32[]{:S(2)}, u32[]{:S(2)}) collective-permute-start(bf16[256,2048]{1,0:T(8,128)(2,1)S(1)} %collective-permute-done.27), channel_id=1, source_target_pairs={{0,8},{4,12},{8,16},{12,20},{16,24},{20,28},{24,0},{28,4},{1,9},{5... | collective-permute-start | bytes 3145736 | tf_op jit(solution)/shard_map/ppermute | solution.py:483
  310.0 33.5 %collective-permute-done.31 = bf16[128,2048]{1,0:T(8,128)(2,1)S(1)} collective-permute-done((bf16[128,2048]{1,0:T(8,128)(2,1)S(1)}, bf16[128,2048]{1,0:T(8,128)(2,1)S(1)}, u32[]{:S(2)}, u32[]{:S(2)}) %collective-permute-start.31) | collective-permute-done | bytes 524320 | tf_op jit(solution)/shard_map/ppermute | solution.py:466
  356.5 22.1 %collective-permute-start.37 = (bf16[256,2048]{1,0:T(8,128)(2,1)S(1)}, bf16[256,2048]{1,0:T(8,128)(2,1)S(1)}, u32[]{:S(2)}, u32[]{:S(2)}) collective-permute-start(bf16[256,2048]{1,0:T(8,128)(2,1)S(1)} %collective-permute-done.32), channel_id=1, source_target_pairs={{0,8},{4,12},{8,16},{12,20},{16,24},{20,28},{24,0},{28,4},{1,9},{5... | collective-permute-start | bytes 3145736 | tf_op jit(solution)/shard_map/ppermute | solution.py:483
  413.1 20.4 %shard_map.258 = (bf16[8,256,2048]{2,1,0:T(8,128)(2,1)}, f32[8,256,256]{2,1,0:T(8,128)}) custom-call(s32[2]{0:T(128)} %get-tuple-element.379.table, bf16[8,8,1024]{2,1,0:T(8,128)(2,1)} %copy-done.43, bf16[8,8,1024]{2,1,0:T(8,128)(2,1)} %copy-done.25, bf16[8,1024,2048]{2,1,0:T(8,128)(2,1)} %bitcast.323, bf16[8,256,2048]{2,1,0:T(8,128)(2,1)} %down.15), custom_call_target="tpu_custom_call" | custom-call | flops 10737418240 | bytes 21474836 | tf_op jit(solution)/shard_map/pallas_call | solution.py:360
  453.4 20.4 %shard_map.259 = (bf16[8,256,2048]{2,1,0:T(8,128)(2,1)}, f32[8,256,256]{2,1,0:T(8,128)}) custom-call(s32[2]{0:T(128)} %get-tuple-element.394.table, bf16[8,8,1024]{2,1,0:T(8,128)(2,1)} %copy-done.43, bf16[8,8,1024]{2,1,0:T(8,128)(2,1)} %copy-done.25, bf16[8,1024,2048]{2,1,0:T(8,128)(2,1)} %bitcast.324, bf16[8,256,2048]{2,1,0:T(8,128)(2,1)} %down.15), custom_call_target="tpu_custom_call" | custom-call | flops 10737418240 | bytes 21474836 | tf_op jit(solution)/shard_map/pallas_call | solution.py:360
  478.2 38.1 %shard_map.260 = (bf16[8,256,2048]{2,1,0:T(8,128)(2,1)}, bf16[8,256,256]{2,1,0:T(8,128)(2,1)}, bf16[8,256,512]{2,1,0:T(8,128)(2,1)}, bf16[2,2,256,2048]{3,2,1,0:T(8,128)(2,1)}, bf16[2,2,256,2048]{3,2,1,0:T(8,128)(2,1)}) custom-call(bf16[2,8,1024]{2,1,0:T(8,128)(2,1)} %bitcast.385, bf16[8,128,2048]{2,1,0:T(8,128)(2,1)} %constant_dynamic-update-slice_fusion.7.own, ...), custom_call_target="tpu_custom_call" | custom-call | flops 25769803776 | bytes 51539608 | tf_op jit(solution)/shard_map/pallas_call | solution.py:393
  516.4 20.4 %shard_map.261 = (bf16[8,256,2048]{2,1,0:T(8,128)(2,1)}, f32[8,256,256]{2,1,0:T(8,128)}) custom-call(s32[2]{0:T(128)} %get-tuple-element.402.table, bf16[8,8,1024]{2,1,0:T(8,128)(2,1)} %copy-done.43, bf16[8,8,1024]{2,1,0:T(8,128)(2,1)} %copy-done.25, bf16[8,1024,2048]{2,1,0:T(8,128)(2,1)} %bitcast.325, bf16[8,256,2048]{2,1,0:T(8,128)(2,1)} %down.15), custom_call_target="tpu_custom_call" | custom-call | flops 10737418240 | bytes 21474836 | tf_op jit(solution)/shard_map/pallas_call | solution.py:360
  546.4 38.2 %shard_map.262 = (bf16[8,256,2048]{2,1,0:T(8,128)(2,1)}, bf16[8,256,256]{2,1,0:T(8,128)(2,1)}, bf16[8,256,512]{2,1,0:T(8,128)(2,1)}, bf16[2,2,256,2048]{3,2,1,0:T(8,128)(2,1)}, bf16[2,2,256,2048]{3,2,1,0:T(8,128)(2,1)}) custom-call(bf16[2,8,1024]{2,1,0:T(8,128)(2,1)} %bitcast.384, bf16[8,128,2048]{2,1,0:T(8,128)(2,1)} %constant_dynamic-update-slice_fusion.11.own, ...), custom_call_target="tpu_custom_call" | custom-call | flops 25769803776 | bytes 51539608 | tf_op jit(solution)/shard_map/pallas_call | solution.py:393
  598.4 20.4 %shard_map.263 = (bf16[8,256,2048]{2,1,0:T(8,128)(2,1)}, f32[8,256,256]{2,1,0:T(8,128)}) custom-call(s32[2]{0:T(128)} %get-tuple-element.426.table, bf16[8,8,1024]{2,1,0:T(8,128)(2,1)} %copy-done.43, bf16[8,8,1024]{2,1,0:T(8,128)(2,1)} %copy-done.25, bf16[8,1024,2048]{2,1,0:T(8,128)(2,1)} %bitcast.326, bf16[8,256,2048]{2,1,0:T(8,128)(2,1)} %down.15), custom_call_target="tpu_custom_call" | custom-call | flops 10737418240 | bytes 21474836 | tf_op jit(solution)/shard_map/pallas_call | solution.py:360
  640.0 37.8 %shard_map.264 = (bf16[8,256,2048]{2,1,0:T(8,128)(2,1)}, bf16[8,256,256]{2,1,0:T(8,128)(2,1)}, bf16[8,256,512]{2,1,0:T(8,128)(2,1)}, bf16[2,2,256,2048]{3,2,1,0:T(8,128)(2,1)}, bf16[2,2,256,2048]{3,2,1,0:T(8,128)(2,1)}) custom-call(bf16[2,8,1024]{2,1,0:T(8,128)(2,1)} %bitcast.383, bf16[8,128,2048]{2,1,0:T(8,128)(2,1)} %constant_dynamic-update-slice_fusion.15.own, ...), custom_call_target="tpu_custom_call" | custom-call | flops 25769803776 | bytes 51539608 | tf_op jit(solution)/shard_map/pallas_call | solution.py:393
  684.0 38.1 %shard_map.265 = (bf16[8,256,2048]{2,1,0:T(8,128)(2,1)}, bf16[8,256,256]{2,1,0:T(8,128)(2,1)}, bf16[8,256,512]{2,1,0:T(8,128)(2,1)}, bf16[2,2,256,2048]{3,2,1,0:T(8,128)(2,1)}, bf16[2,2,256,2048]{3,2,1,0:T(8,128)(2,1)}) custom-call(bf16[2,8,1024]{2,1,0:T(8,128)(2,1)} %bitcast.382, bf16[8,128,2048]{2,1,0:T(8,128)(2,1)} %copy-done.89, ...), custom_call_target="tpu_custom_call" | custom-call | flops 25769803776 | bytes 51539608 | tf_op jit(solution)/shard_map/pallas_call | solution.py:393
  743.3 17.7 %shard_map.266.refs_0_ = bf16[4,2,1024,2048]{3,2,1,0:T(8,128)(2,1)} custom-call(s32[2]{0:T(128)} %get-tuple-element.484.table, bf16[2,8,1024]{2,1,0:T(8,128)(2,1)} %get-tuple-element.485.places, bf16[2,8,1024]{2,1,0:T(8,128)(2,1)} %get-tuple-element.486.gates, bf16[32,256,256]{2,1,0:T(8,128)(2,1)} %constant_dynamic-update-slice_fusion.19.hidden, ...), custom_call_target="tpu_custom_call" | custom-call | flops 10737418240 | bytes 21474836 | tf_op jit(solution)/shard_map/pallas_call | solution.py:420
  761.0 17.6 %shard_map.267.refs_0_ = bf16[4,2,1024,2048]{3,2,1,0:T(8,128)(2,1)} custom-call(s32[2]{0:T(128)} %get-tuple-element.477.table, bf16[2,8,1024]{2,1,0:T(8,128)(2,1)} %get-tuple-element.478.places, bf16[2,8,1024]{2,1,0:T(8,128)(2,1)} %get-tuple-element.479.gates, ...), custom_call_target="tpu_custom_call", output_to_operand_aliasing={{}: (5, {})} | custom-call | flops 10737418240 | bytes 21474836 | tf_op jit(solution)/shard_map/pallas_call | solution.py:420
  795.2 17.9 %shard_map.268.refs_0_ = bf16[4,2,1024,2048]{3,2,1,0:T(8,128)(2,1)} custom-call(s32[2]{0:T(128)} %get-tuple-element.502.table, bf16[2,8,1024]{2,1,0:T(8,128)(2,1)} %get-tuple-element.503.places, bf16[2,8,1024]{2,1,0:T(8,128)(2,1)} %get-tuple-element.504.gates, ...), custom_call_target="tpu_custom_call", output_to_operand_aliasing={{}: (5, {})} | custom-call | flops 10737418240 | bytes 21474836 | tf_op jit(solution)/shard_map/pallas_call | solution.py:420
  813.1 17.6 %shard_map.269 = bf16[4,2,1024,2048]{3,2,1,0:T(8,128)(2,1)} custom-call(s32[2]{0:T(128)} %get-tuple-element.499.table, bf16[2,8,1024]{2,1,0:T(8,128)(2,1)} %get-tuple-element.500.places, bf16[2,8,1024]{2,1,0:T(8,128)(2,1)} %get-tuple-element.501.gates, ...), custom_call_target="tpu_custom_call", output_to_operand_aliasing={{}: (5, {})} | custom-call | flops 10737418240 | bytes 21474836 | tf_op jit(solution)/shard_map/pallas_call | solution.py:420
  842.2 18.2 %shard_map.270 = (f32[8,2048,256]{2,1,0:T(8,128)}, f32[8,2048,256]{2,1,0:T(8,128)}, f32[8,256,2048]{2,1,0:T(8,128)}) custom-call(bf16[8,256,2048]{2,1,0:T(8,128)(2,1)} %get-tuple-element.562.refs_0_, bf16[8,256,2048]{2,1,0:T(8,128)(2,1)} %get-tuple-element.563.refs_1_, bf16[8,256,2048]{2,1,0:T(8,128)(2,1)} %get-tuple-element.564.refs_2_, ...), custom_call_target="tpu_custom_call" | custom-call | flops 6442450944 | bytes 12884901 | tf_op jit(solution)/shard_map/pallas_call | solution.py:451
  860.5 17.4 %shard_map.271 = (f32[8,2048,256]{2,1,0:T(8,128)}, f32[8,2048,256]{2,1,0:T(8,128)}, f32[8,256,2048]{2,1,0:T(8,128)}) custom-call(bf16[8,256,2048]{2,1,0:T(8,128)(2,1)} %get-tuple-element.562.refs_0_, bf16[8,256,2048]{2,1,0:T(8,128)(2,1)} %get-tuple-element.563.refs_1_, ...), custom_call_target="tpu_custom_call", output_to_operand_aliasing={{0}: (16, {}), {1}: (17, {}), {2}: (18, {})} | custom-call | flops 6442450944 | bytes 12884901 | tf_op jit(solution)/shard_map/pallas_call | solution.py:451
  884.0 13.8 %shard_map.272 = (f32[8,2048,256]{2,1,0:T(8,128)}, f32[8,2048,256]{2,1,0:T(8,128)}, f32[8,256,2048]{2,1,0:T(8,128)}) custom-call(bf16[8,256,2048]{2,1,0:T(8,128)(2,1)} %get-tuple-element.562.refs_0_, bf16[8,256,2048]{2,1,0:T(8,128)(2,1)} %get-tuple-element.563.refs_1_, ...), custom_call_target="tpu_custom_call", output_to_operand_aliasing={{0}: (16, {}), {1}: (17, {}), {2}: (18, {})} | custom-call | flops 6442450944 | bytes 12884901 | tf_op jit(solution)/shard_map/pallas_call | solution.py:451
  897.8 13.3 %shard_map.273 = (f32[8,2048,256]{2,1,0:T(8,128)}, f32[8,2048,256]{2,1,0:T(8,128)}, f32[8,256,2048]{2,1,0:T(8,128)}) custom-call(bf16[8,256,2048]{2,1,0:T(8,128)(2,1)} %get-tuple-element.562.refs_0_, bf16[8,256,2048]{2,1,0:T(8,128)(2,1)} %get-tuple-element.563.refs_1_, ...), custom_call_target="tpu_custom_call", output_to_operand_aliasing={{0}: (16, {}), {1}: (17, {}), {2}: (18, {})} | custom-call | flops 6442450944 | bytes 12884901 | tf_op jit(solution)/shard_map/pallas_call | solution.py:451
  911.0 15.7 %collective-permute-done.72.refs_2_ = bf16[256,2048]{1,0:T(8,128)(2,1)S(1)} collective-permute-done((bf16[256,2048]{1,0:T(8,128)(2,1)S(1)}, bf16[256,2048]{1,0:T(8,128)(2,1)S(1)}, u32[]{:S(2)}, u32[]{:S(2)}) %collective-permute-start.72) | collective-permute-done | bytes 1048608 | tf_op jit(solution)/shard_map/ppermute | solution.py:466
  1046.9 20.5 %reduce-scatter.3.cloned.1.call-done = bf16[4,256,2048]{2,1,0:T(8,128)(2,1)} async-done(((bf16[4,2048,2048]{2,1,0:T(8,128)(2,1)}), bf16[4,256,2048]{2,1,0:T(8,128)(2,1)}) %reduce-scatter.3.cloned.1.call-update) | async-done | bytes 4194320 | tf_op jit(solution)/shard_map/reduce_scatter | solution.py:927
  1083.8 17.0 %collective-permute-done.84 = bf16[256,1536]{1,0:T(8,128)(2,1)S(1)} collective-permute-done((bf16[256,1536]{1,0:T(8,128)(2,1)S(1)}, bf16[256,1536]{1,0:T(8,128)(2,1)S(1)}, u32[]{:S(2)}, u32[]{:S(2)}) %collective-permute-start.84) | collective-permute-done | bytes 786464 | tf_op jit(solution)/shard_map/ppermute | solution.py:466
  1117.7 23.2 %collective-permute-done.87 = bf16[256,1536]{1,0:T(8,128)(2,1)S(1)} collective-permute-done((bf16[256,1536]{1,0:T(8,128)(2,1)S(1)}, bf16[256,1536]{1,0:T(8,128)(2,1)S(1)}, u32[]{:S(2)}, u32[]{:S(2)}) %collective-permute-start.87) | collective-permute-done | bytes 786464 | tf_op jit(solution)/shard_map/ppermute | solution.py:483
  1141.2 15.8 %collective-permute-start.89 = (bf16[256,1536]{1,0:T(8,128)(2,1)S(1)}, bf16[256,1536]{1,0:T(8,128)(2,1)S(1)}, u32[]{:S(2)}, u32[]{:S(2)}) collective-permute-start(bf16[256,1536]{1,0:T(8,128)(2,1)S(1)} %add_convert_fusion.29), channel_id=1, source_target_pairs={{0,8},{4,12},{8,16},{12,20},{16,24},{20,28},{24,0},{28,4},{1,9},{5... | collective-permute-start | bytes 2359304 | tf_op jit(solution)/shard_map/ppermute | solution.py:483
  1187.4 15.9 %collective-permute-done.90 = bf16[256,1536]{1,0:T(8,128)(2,1)S(1)} collective-permute-done((bf16[256,1536]{1,0:T(8,128)(2,1)S(1)}, bf16[256,1536]{1,0:T(8,128)(2,1)S(1)}, u32[]{:S(2)}, u32[]{:S(2)}) %collective-permute-start.90) | collective-permute-done | bytes 786464 | tf_op jit(solution)/shard_map/ppermute | solution.py:483
  (650 shorter events, 505.3 us)
Async XLA Ops:
  7.2 405.9 %all-gather.2.cloned.1.call-start = ((), (), s32[]{:S(2)}) async-start(), calls=%async_computation.2 | async-start | bytes 34603008 | tf_op jit(solution)/shard_map/all_gather | solution.py:1004
  131.2 936.2 %reduce-scatter.3.cloned.1.call-start = ((), (), s32[]{:S(2)}) async-start(), calls=%async_computation.3 | async-start | bytes 37748736 | tf_op jit(solution)/shard_map/reduce_scatter | solution.py:927
  143.3 52.4 %collective-permute-start.24 = (bf16[16,17,256]{2,0,1:T(8,128)(2,1)S(1)}, bf16[16,17,256]{2,0,1:T(8,128)(2,1)S(1)}, u32[]{:S(2)}, u32[]{:S(2)}) collective-permute-start(bf16[16,17,256]{2,0,1:T(8,128)(2,1)S(1)} %concatenate.117), channel_id=1, source_target_pairs={{0,16},{4,20},{8,24},{12,28},{16,0},{20,4},{24,8},{28,12},{1,17},{... | collective-permute-start | bytes 417800 | tf_op jit(solution)/shard_map/ppermute | solution.py:466
  234.6 47.3 %collective-permute-start.27 = (bf16[256,2048]{1,0:T(8,128)(2,1)S(1)}, bf16[256,2048]{1,0:T(8,128)(2,1)S(1)}, u32[]{:S(2)}, u32[]{:S(2)}) collective-permute-start(bf16[256,2048]{1,0:T(8,128)(2,1)S(1)} %multiply_convert_fusion.4), channel_id=1, source_target_pairs={{0,8},{4,12},{8,16},{12,20},{16,24},{20,28},{24,0},{28,4},{1,9},{5... | collective-permute-start | bytes 3145736 | tf_op jit(solution)/shard_map/ppermute | solution.py:483
  282.1 68.4 %collective-permute-start.32 = (bf16[256,2048]{1,0:T(8,128)(2,1)S(1)}, bf16[256,2048]{1,0:T(8,128)(2,1)S(1)}, u32[]{:S(2)}, u32[]{:S(2)}) collective-permute-start(bf16[256,2048]{1,0:T(8,128)(2,1)S(1)} %collective-permute-done.27), channel_id=1, source_target_pairs={{0,8},{4,12},{8,16},{12,20},{16,24},{20,28},{24,0},{28,4},{1,9},{5... | collective-permute-start | bytes 3145736 | tf_op jit(solution)/shard_map/ppermute | solution.py:483
  305.4 45.0 %collective-permute-start.28 = (bf16[2,128,2048]{2,1,0:T(8,128)(2,1)S(1)}, bf16[2,128,2048]{2,1,0:T(8,128)(2,1)S(1)}, u32[]{:S(2)}, u32[]{:S(2)}) collective-permute-start(bf16[2,128,2048]{2,1,0:T(8,128)(2,1)S(1)} %pad_maximum_fusion.7), channel_id=1, source_target_pairs={{0,2},{1,3},{2,0},{3,1},{4,6},{5,7},{6,4},{7,5},{8,10},{9,11},{10,... | collective-permute-start | bytes 3145736 | tf_op jit(solution)/shard_map/ppermute | solution.py:466
  305.4 45.0 %collective-permute-start.29 = (bf16[2,128,2048]{2,1,0:T(8,128)(2,1)S(1)}, bf16[2,128,2048]{2,1,0:T(8,128)(2,1)S(1)}, u32[]{:S(2)}, u32[]{:S(2)}) collective-permute-start(bf16[2,128,2048]{2,1,0:T(8,128)(2,1)S(1)} %pad_maximum_fusion.8), channel_id=1, source_target_pairs={{0,4},{4,0},{8,12},{12,8},{16,20},{20,16},{24,28},{28,24},{1,5},{5... | collective-permute-start | bytes 3145736 | tf_op jit(solution)/shard_map/ppermute | solution.py:466
  350.7 52.1 %collective-permute-start.38 = (bf16[8,128,2048]{2,1,0:T(8,128)(2,1)S(1)}, bf16[8,128,2048]{2,1,0:T(8,128)(2,1)S(1)}, u32[]{:S(2)}, u32[]{:S(2)}) collective-permute-start(bf16[8,128,2048]{2,1,0:T(8,128)(2,1)S(1)} %constant_dynamic-update-slice_fusion.3.own), channel_id=1, source_target_pairs={{0,1},{1,0},{2,3},{3,2},{4,5},{5,4},{6,7},{7,6},{8,9},{9,8},{10,11... | collective-permute-start | bytes 12582920 | tf_op jit(solution)/shard_map/ppermute | solution.py:466
  356.5 46.3 %collective-permute-start.37 = (bf16[256,2048]{1,0:T(8,128)(2,1)S(1)}, bf16[256,2048]{1,0:T(8,128)(2,1)S(1)}, u32[]{:S(2)}, u32[]{:S(2)}) collective-permute-start(bf16[256,2048]{1,0:T(8,128)(2,1)S(1)} %collective-permute-done.32), channel_id=1, source_target_pairs={{0,8},{4,12},{8,16},{12,20},{16,24},{20,28},{24,0},{28,4},{1,9},{5... | collective-permute-start | bytes 3145736 | tf_op jit(solution)/shard_map/ppermute | solution.py:483
  545.5 39.1 %collective-permute-start.48 = (bf16[2,128,2048]{2,1,0:T(8,128)(2,1)}, bf16[2,128,2048]{2,1,0:T(8,128)(2,1)}, u32[]{:S(2)}, u32[]{:S(2)}) collective-permute-start(bf16[2,128,2048]{2,1,0:T(8,128)(2,1)} %fusion.62), channel_id=1, source_target_pairs={{0,2},{1,3},{2,0},{3,1},{4,6},{5,7},{6,4},{7,5},{8,10},{9,11},{10,... | collective-permute-start | bytes 3145736 | tf_op jit(solution)/shard_map/ppermute | solution.py:466
  545.9 38.8 %collective-permute-start.49 = (bf16[2,128,2048]{2,1,0:T(8,128)(2,1)}, bf16[2,128,2048]{2,1,0:T(8,128)(2,1)}, u32[]{:S(2)}, u32[]{:S(2)}) collective-permute-start(bf16[2,128,2048]{2,1,0:T(8,128)(2,1)} %get-tuple-element.408), channel_id=1, source_target_pairs={{0,4},{4,0},{8,12},{12,8},{16,20},{20,16},{24,28},{28,24},{1,5},{5... | collective-permute-start | bytes 3145736 | tf_op jit(solution)/shard_map/ppermute | solution.py:466
  594.8 45.3 %collective-permute-start.56 = (bf16[8,128,2048]{2,1,0:T(8,128)(2,1)}, bf16[8,128,2048]{2,1,0:T(8,128)(2,1)}, u32[]{:S(2)}, u32[]{:S(2)}) collective-permute-start(bf16[8,128,2048]{2,1,0:T(8,128)(2,1)} %constant_dynamic-update-slice_fusion.15.own), channel_id=1, source_target_pairs={{0,1},{1,0},{2,3},{3,2},{4,5},{5,4},{6,7},{7,6},{8,9},{9,8},{10,11... | collective-permute-start | bytes 12582920 | tf_op jit(solution)/shard_map/ppermute | solution.py:466
  628.9 48.9 %collective-permute-start.53 = (bf16[2,128,2048]{2,1,0:T(8,128)(2,1)}, bf16[2,128,2048]{2,1,0:T(8,128)(2,1)}, u32[]{:S(2)}, u32[]{:S(2)}) collective-permute-start(bf16[2,128,2048]{2,1,0:T(8,128)(2,1)} %fusion.66), channel_id=1, source_target_pairs={{0,2},{1,3},{2,0},{3,1},{4,6},{5,7},{6,4},{7,5},{8,10},{9,11},{10,... | collective-permute-start | bytes 3145736 | tf_op jit(solution)/shard_map/ppermute | solution.py:466
  629.3 48.6 %collective-permute-start.54 = (bf16[2,128,2048]{2,1,0:T(8,128)(2,1)}, bf16[2,128,2048]{2,1,0:T(8,128)(2,1)}, u32[]{:S(2)}, u32[]{:S(2)}) collective-permute-start(bf16[2,128,2048]{2,1,0:T(8,128)(2,1)} %get-tuple-element.436), channel_id=1, source_target_pairs={{0,4},{4,0},{8,12},{12,8},{16,20},{20,16},{24,28},{28,24},{1,5},{5... | collective-permute-start | bytes 3145736 | tf_op jit(solution)/shard_map/ppermute | solution.py:466
  629.8 48.0 %collective-permute-start.55 = (bf16[256,2048]{1,0:T(8,128)(2,1)}, bf16[256,2048]{1,0:T(8,128)(2,1)S(1)}, u32[]{:S(2)}, u32[]{:S(2)}) collective-permute-start(bf16[256,2048]{1,0:T(8,128)(2,1)} %pad_maximum_fusion.15), channel_id=1, source_target_pairs={{0,8},{4,12},{8,16},{12,20},{16,24},{20,28},{24,0},{28,4},{1,9},{5... | collective-permute-start | bytes 3145736 | tf_op jit(solution)/shard_map/ppermute | solution.py:483
  682.1 40.1 %collective-permute-start.59 = (bf16[2,2,256,2048]{3,2,1,0:T(8,128)(2,1)}, bf16[2,2,256,2048]{3,2,1,0:T(8,128)(2,1)}, u32[]{:S(2)}, u32[]{:S(2)}) collective-permute-start(bf16[2,2,256,2048]{3,2,1,0:T(8,128)(2,1)} %get-tuple-element.454), channel_id=1, source_target_pairs={{0,1},{1,0},{2,3},{3,2},{4,5},{5,4},{6,7},{7,6},{8,9},{9,8},{10,11... | collective-permute-start | bytes 12582920 | tf_op jit(solution)/shard_map/ppermute | solution.py:466
  682.1 40.0 %collective-permute-start.57 = (bf16[128,2048]{1,0:T(8,128)(2,1)}, bf16[128,2048]{1,0:T(8,128)(2,1)S(1)}, u32[]{:S(2)}, u32[]{:S(2)}) collective-permute-start(bf16[128,2048]{1,0:T(8,128)(2,1)} %get-tuple-element.452), channel_id=1, source_target_pairs={{0,4},{4,0},{8,12},{12,8},{16,20},{20,16},{24,28},{28,24},{1,5},{5... | collective-permute-start | bytes 1572872 | tf_op jit(solution)/shard_map/ppermute | solution.py:466
  682.6 39.5 %collective-permute-start.58 = (bf16[128,2048]{1,0:T(8,128)(2,1)S(1)}, bf16[128,2048]{1,0:T(8,128)(2,1)S(1)}, u32[]{:S(2)}, u32[]{:S(2)}) collective-permute-start(bf16[128,2048]{1,0:T(8,128)(2,1)S(1)} %get-tuple-element.453), channel_id=1, source_target_pairs={{0,2},{1,3},{2,0},{3,1},{4,6},{5,7},{6,4},{7,5},{8,10},{9,11},{10,... | collective-permute-start | bytes 1572872 | tf_op jit(solution)/shard_map/ppermute | solution.py:466
  734.5 44.2 %collective-permute-start.60 = (bf16[2,2,256,2048]{3,2,1,0:T(8,128)(2,1)}, bf16[2,2,256,2048]{3,2,1,0:T(8,128)(2,1)}, u32[]{:S(2)}, u32[]{:S(2)}) collective-permute-start(bf16[2,2,256,2048]{3,2,1,0:T(8,128)(2,1)} %get-tuple-element.473), channel_id=1, source_target_pairs={{0,1},{1,0},{2,3},{3,2},{4,5},{5,4},{6,7},{7,6},{8,9},{9,8},{10,11... | collective-permute-start | bytes 12582920 | tf_op jit(solution)/shard_map/ppermute | solution.py:466
  734.5 44.1 %collective-permute-start.61 = (bf16[2,128,2048]{2,1,0:T(8,128)(2,1)}, bf16[2,128,2048]{2,1,0:T(8,128)(2,1)}, u32[]{:S(2)}, u32[]{:S(2)}) collective-permute-start(bf16[2,128,2048]{2,1,0:T(8,128)(2,1)} %fusion.70), channel_id=1, source_target_pairs={{0,2},{1,3},{2,0},{3,1},{4,6},{5,7},{6,4},{7,5},{8,10},{9,11},{10,... | collective-permute-start | bytes 3145736 | tf_op jit(solution)/shard_map/ppermute | solution.py:466
  735.2 43.5 %collective-permute-start.62 = (bf16[2,128,2048]{2,1,0:T(8,128)(2,1)}, bf16[2,128,2048]{2,1,0:T(8,128)(2,1)S(1)}, u32[]{:S(2)}, u32[]{:S(2)}) collective-permute-start(bf16[2,128,2048]{2,1,0:T(8,128)(2,1)} %get-tuple-element.475), channel_id=1, source_target_pairs={{0,4},{4,0},{8,12},{12,8},{16,20},{20,16},{24,28},{28,24},{1,5},{5... | collective-permute-start | bytes 3145736 | tf_op jit(solution)/shard_map/ppermute | solution.py:466
  736.6 42.0 %collective-permute-start.63 = (bf16[256,2048]{1,0:T(8,128)(2,1)}, bf16[256,2048]{1,0:T(8,128)(2,1)S(1)}, u32[]{:S(2)}, u32[]{:S(2)}) collective-permute-start(bf16[256,2048]{1,0:T(8,128)(2,1)} %add_convert_fusion.11), channel_id=1, source_target_pairs={{0,8},{4,12},{8,16},{12,20},{16,24},{20,28},{24,0},{28,4},{1,9},{5... | collective-permute-start | bytes 3145736 | tf_op jit(solution)/shard_map/ppermute | solution.py:483
  791.1 39.6 %collective-permute-start.66 = (bf16[128,2048]{1,0:T(8,128)(2,1)S(1)}, bf16[128,2048]{1,0:T(8,128)(2,1)}, u32[]{:S(2)}, u32[]{:S(2)}) collective-permute-start(bf16[128,2048]{1,0:T(8,128)(2,1)S(1)} %get-tuple-element.496), channel_id=1, source_target_pairs={{0,4},{4,0},{8,12},{12,8},{16,20},{20,16},{24,28},{28,24},{1,5},{5... | collective-permute-start | bytes 1572872 | tf_op jit(solution)/shard_map/ppermute | solution.py:466
  791.7 39.1 %collective-permute-start.67 = (bf16[128,2048]{1,0:T(8,128)(2,1)}, bf16[128,2048]{1,0:T(8,128)(2,1)}, u32[]{:S(2)}, u32[]{:S(2)}) collective-permute-start(bf16[128,2048]{1,0:T(8,128)(2,1)} %get-tuple-element.497), channel_id=1, source_target_pairs={{0,2},{1,3},{2,0},{3,1},{4,6},{5,7},{6,4},{7,5},{8,10},{9,11},{10,... | collective-permute-start | bytes 1572872 | tf_op jit(solution)/shard_map/ppermute | solution.py:466
  830.8 373.9 %reduce-scatter.5.cloned.1.call-start = ((), (), s32[]{:S(2)}) async-start(), calls=%async_computation.4 | async-start | bytes 5242880 | tf_op jit(solution)/shard_map/reduce_scatter | solution.py:1154
  839.2 38.7 %collective-permute-start.68 = (bf16[128,2048]{1,0:T(8,128)(2,1)}, bf16[128,2048]{1,0:T(8,128)(2,1)S(1)}, u32[]{:S(2)}, u32[]{:S(2)}) collective-permute-start(bf16[128,2048]{1,0:T(8,128)(2,1)} %get-tuple-element.528), channel_id=1, source_target_pairs={{0,4},{4,0},{8,12},{12,8},{16,20},{20,16},{24,28},{28,24},{1,5},{5... | collective-permute-start | bytes 1572872 | tf_op jit(solution)/shard_map/ppermute | solution.py:466
  883.2 43.5 %collective-permute-start.72 = (bf16[256,2048]{1,0:T(8,128)(2,1)S(1)}, bf16[256,2048]{1,0:T(8,128)(2,1)S(1)}, u32[]{:S(2)}, u32[]{:S(2)}) collective-permute-start(bf16[256,2048]{1,0:T(8,128)(2,1)S(1)} %get-tuple-element.561.refs_0_), channel_id=1, source_target_pairs={{0,2},{1,3},{2,0},{3,1},{4,6},{5,7},{6,4},{7,5},{8,10},{9,11},{10,... | collective-permute-start | bytes 3145736 | tf_op jit(solution)/shard_map/ppermute | solution.py:466
  884.0 42.8 %collective-permute-start.71 = (bf16[256,2048]{1,0:T(8,128)(2,1)S(1)}, bf16[256,2048]{1,0:T(8,128)(2,1)S(1)}, u32[]{:S(2)}, u32[]{:S(2)}) collective-permute-start(bf16[256,2048]{1,0:T(8,128)(2,1)S(1)} %get-tuple-element.561.refs_0_), channel_id=1, source_target_pairs={{0,1},{1,0},{2,3},{3,2},{4,5},{5,4},{6,7},{7,6},{8,9},{9,8},{10,11... | collective-permute-start | bytes 3145736 | tf_op jit(solution)/shard_map/ppermute | solution.py:466
  957.7 44.4 %collective-permute-start.77 = (bf16[512,256]{1,0:T(8,128)(2,1)}, bf16[512,256]{1,0:T(8,128)(2,1)}, u32[]{:S(2)}, u32[]{:S(2)}) collective-permute-start(bf16[512,256]{1,0:T(8,128)(2,1)} %bitcast.318), channel_id=1, source_target_pairs={{0,4},{4,0},{8,12},{12,8},{16,20},{20,16},{24,28},{28,24},{1,5},{5... | collective-permute-start | bytes 786440 | tf_op jit(solution)/shard_map/ppermute | solution.py:466
  1101.2 39.6 %collective-permute-start.88 = (bf16[256,2048]{1,0:T(8,128)(2,1)S(1)}, bf16[256,2048]{1,0:T(8,128)(2,1)S(1)}, u32[]{:S(2)}, u32[]{:S(2)}) collective-permute-start(bf16[256,2048]{1,0:T(8,128)(2,1)S(1)} %fusion.30), channel_id=1, source_target_pairs={{0,2},{1,3},{2,0},{3,1},{4,6},{5,7},{6,4},{7,5},{8,10},{9,11},{10,... | collective-permute-start | bytes 3145736 | tf_op jit(solution)/shard_map/ppermute | solution.py:466
  1104.1 78.1 %collective-permute-start.82 = (bf16[256,1536]{1,0:T(8,128)(2,1)S(1)}, bf16[256,1536]{1,0:T(8,128)(2,1)S(1)}, u32[]{:S(2)}, u32[]{:S(2)}) collective-permute-start(bf16[256,1536]{1,0:T(8,128)(2,1)S(1)} %get-tuple-element.640), channel_id=1, source_target_pairs={{0,4},{4,0},{8,12},{12,8},{16,20},{20,16},{24,28},{28,24},{1,5},{5... | collective-permute-start | bytes 2359304 | tf_op jit(solution)/shard_map/ppermute | solution.py:466
  1141.2 40.9 %collective-permute-start.89 = (bf16[256,1536]{1,0:T(8,128)(2,1)S(1)}, bf16[256,1536]{1,0:T(8,128)(2,1)S(1)}, u32[]{:S(2)}, u32[]{:S(2)}) collective-permute-start(bf16[256,1536]{1,0:T(8,128)(2,1)S(1)} %add_convert_fusion.29), channel_id=1, source_target_pairs={{0,8},{4,12},{8,16},{12,20},{16,24},{20,28},{24,0},{28,4},{1,9},{5... | collective-permute-start | bytes 2359304 | tf_op jit(solution)/shard_map/ppermute | solution.py:483
  (184 other events, 2829.6 us)
Sparse Core Ops, SparseCore 0:
  131.3 246.4 all-gather.1
  830.9 236.4 reduce-scatter.2
  1069.8 96.6 reduce-scatter.4

commit v10 on v9

--- a/solution.py
+++ b/solution.py
@@ -502,14 +502,14 @@
             first(values) if plane + 1 < planes else ((), ()),
             next_plane(values) if plane + 2 < planes else (),
             far_core(pieces[-1]) if plane else (),
-            work(plane - 2, small) if plane > 1 else (),
+            work(plane - 1, small) if plane else (),
         ]
         upper_far, lower_far, (across_pack, across_side), following, other, result = (
             lax.optimization_barrier(moved)
         )
         if plane:
             pieces[-1] = (pieces[-1], other)
-        if plane > 1:
+        if plane:
             made.append(result)
         pieces.append(jnp.concatenate([upper, lower, upper_far, lower_far]))
     pieces[-1] = (pieces[-1], far_core(pieces[-1]))
@@ -613,7 +613,7 @@
     return added(near, far_side(far), jnp.float32)
 
 
-def fold_both(weights, rows):
+def fold_both(weights, rows, mixed):
     order = plane_order()
     planes = weights.shape[0] // 2
     take = lambda index: lax.dynamic_index_in_dim(weights, order[index], 0, keepdims=False)
@@ -630,12 +630,14 @@
         across, passed, *arrived = lax.optimization_barrier(moved)
         if turn == 0:
             far, close = added(pick(2), arrived[0]), added(pick(0), arrived[1])
+            mixed, far = tied(mixed, far)
+            mixed = lax.psum_scatter(mixed, "plane", scatter_dimension=0, tiled=True)
         if turn == 1:
             total = added(close, arrived[0], jnp.float32)
         near = added(take(2 * plane), across)
         kind = jnp.float32 if turn + 1 == planes else jnp.bfloat16
         summed = near if turn == 0 else added(passed, near, kind)
-    return summed, total
+    return summed, total, mixed
 
 
 def gather_both(weights, outer, rows, gate, up, tables):
@@ -1094,8 +1096,6 @@
     for block_index in range(block_total):
         offset = block_index * block_rows
         query_block = query_low[offset : offset + block_rows]
-        if block_index:
-            query_block = fold_step(query_block)
         grad_block = grad_mixture[offset : offset + block_rows]
         scores = block_scores(query_block, key_low, masks[block_index], inv_root)
         prob_rows = jnp.exp(scores - lse_parts[block_index])
@@ -1124,7 +1124,6 @@
     grad_query_norm = rotate_back(jnp.concatenate(grad_query_parts, axis=0), cosine, sine_tab)
     grad_key_norm = rotate_back(grad_key_sum, cosine, sine_tab)
     grad_query_norm = fold_step(grad_query_norm)
-    grad_key_norm = fold_step(grad_key_norm)
     query_gain_part = jnp.sum(grad_query_norm * query_norm, axis=(0, 1))
     key_gain_part = jnp.sum(grad_key_norm * key_norm, axis=(0, 1))
     grad_query_pre = (
@@ -1150,9 +1149,7 @@
         in_part = in_part.astype(jnp.bfloat16).reshape(data_count, -1, 3 * local_width)
         in_part = fold_step(in_part)
         grad_w_output = folded.finish()
-        mixed, in_part = tied(mixed, in_part)
-        mixed = lax.psum_scatter(mixed, "plane", scatter_dimension=0, tiled=True)
-        grad_in, grad_first = fold_both(in_part, total_term)
+        grad_in, grad_first, mixed = fold_both(in_part, total_term, mixed)
         mixed, grad_in = tied(mixed, grad_in)
     else:
         grad_first = side_sum(total_term)

time: 1220 us -> 1230 us (level)
  local copies, waits for them, and re-layouts: 85 us -> 101 us
  waiting for transfers between devices: 376 us -> 360 us
    ppermute x78, waiting for transfers between devices: 255 us -> 231 us  [swapped(): return lax.ppermute(values, axis, [(i, i ^ bit) for i in range(count)])]
    unnamed x260 -> x308, local copies, waits for them, and re-layouts: 33.8 us -> 41.9 us
  transfers between devices with their start and end apart: 99 -> 99, of which waited for: 37 -> 30; matrix products, arithmetic and copies ran while one was open for 18% -> 20% of each run, Pallas kernels for 28% -> 28%
where the time goes in v10:
time: 1230 us; the launch traced here: 1220 us
  Pallas kernels  387 us (31%)
  waiting for transfers between devices  360 us (29%)
  starting transfers between devices  154 us (13%)
  other arithmetic  133 us (11%)
  local copies, waits for them, and re-layouts  101 us (8%)
  matrix products  73.4 us (6%)
  between operations  16.6 us (1%)
    ppermute x78, waiting for transfers between devices, swapped(): return lax.ppermute(values, axis, [(i, i ^ bit) for i in range(count)])  231 us
    pallas_call x4, Pallas kernels, row_slots(): call(functools.partial(row_kernel, packs, steps, capacity), 2 * packs + s...  152 us
    ppermute x18, waiting for transfers between devices, next_plane(): lax.ppermute(values, DP, [(i, (i + 2) % count) for i in range(count)])  109 us
    pallas_call x4, Pallas kernels, cot_slots(): call(functools.partial(cot_kernel, packs, steps, capacity), packs + steps...  81.5 us
    ppermute x18, starting transfers between devices, next_plane(): lax.ppermute(values, DP, [(i, (i + 2) % count) for i in range(count)])  79.9 us
    ppermute x78, starting transfers between devices, swapped(): return lax.ppermute(values, axis, [(i, i ^ bit) for i in range(count)])  73.3 us
    pallas_call x4, Pallas kernels, mix_rows(): call(functools.partial(mix_kernel, packs, steps, capacity), packs + steps...  70.8 us
    convert_element_type x38, other arithmetic, added(): return (left.astype(jnp.float32) + right.astype(jnp.float32)).astype(kind)  62.6 us
  transfers between devices with their start and end apart: 99, of which 30 were waited for; matrix products, arithmetic and copies ran while one was open for 20% of the time, Pallas kernels for 28%

profile of v10, /device:TPU:0, one launch (start us, length us, event | category | flops | bytes accessed | tf_op | source)
XLA Modules:
  0.0 1224.2 jit_solution(11544406303694132350)
XLA Ops:
  21.8 13.7 %pad_maximum_fusion.both = bf16[8,2048,512]{2,1,0:T(8,128)(2,1)} fusion(bf16[8,2048,256]{2,1,0:T(8,128)(2,1)} %param.29, bf16[8,2048,256]{2,1,0:T(8,128)(2,1)} %param.28), kind=kLoop, calls=%fused_computation.4 | loop fusion | flops 33554432 | bytes 33554432 | tf_op jit(solution)/shard_map/concatenate | solution.py:656
  53.9 19.9 %collective-permute-done.10.refs_4_ = bf16[512,256]{1,0:T(8,128)(2,1)S(1)} collective-permute-done((bf16[512,256]{1,0:T(8,128)(2,1)S(1)}, bf16[512,256]{1,0:T(8,128)(2,1)S(1)}, u32[]{:S(2)}, u32[]{:S(2)}) %collective-permute-start.10) | collective-permute-done | bytes 262176 | tf_op jit(solution)/shard_map/ppermute | solution.py:483
  78.9 20.7 %collective-permute-done.17 = bf16[4,17,256]{2,0,1:T(4,128)(2,1)S(1)} collective-permute-done((bf16[4,17,256]{2,0,1:T(4,128)(2,1)S(1)}, bf16[4,17,256]{2,0,1:T(4,128)(2,1)S(1)}, u32[]{:S(2)}, u32[]{:S(2)}) %collective-permute-start.17) | collective-permute-done | bytes 34848 | tf_op jit(solution)/shard_map/ppermute | solution.py:466
  108.5 16.5 %collective-permute-done.19.refs_7_ = bf16[512,256]{1,0:T(8,128)(2,1)} collective-permute-done((bf16[512,256]{1,0:T(8,128)(2,1)}, bf16[512,256]{1,0:T(8,128)(2,1)}, u32[]{:S(2)}, u32[]{:S(2)}) %collective-permute-start.19) | collective-permute-done | bytes 262176 | tf_op jit(solution)/shard_map/ppermute | solution.py:466
  208.9 23.2 %collective-permute-done.23 = bf16[256,2048]{1,0:T(8,128)(2,1)S(1)} collective-permute-done((bf16[256,2048]{1,0:T(8,128)(2,1)S(1)}, bf16[256,2048]{1,0:T(8,128)(2,1)S(1)}, u32[]{:S(2)}, u32[]{:S(2)}) %collective-permute-start.23) | collective-permute-done | bytes 1048608 | tf_op jit(solution)/shard_map/ppermute | solution.py:466
  238.6 23.2 %collective-permute-done.26 = bf16[128,2048]{1,0:T(8,128)(2,1)S(1)} collective-permute-done((bf16[128,2048]{1,0:T(8,128)(2,1)S(1)}, bf16[128,2048]{1,0:T(8,128)(2,1)S(1)}, u32[]{:S(2)}, u32[]{:S(2)}) %collective-permute-start.26) | collective-permute-done | bytes 524320 | tf_op jit(solution)/shard_map/ppermute | solution.py:466
  262.4 20.9 %collective-permute-done.27 = bf16[256,2048]{1,0:T(8,128)(2,1)S(1)} collective-permute-done((bf16[256,2048]{1,0:T(8,128)(2,1)S(1)}, bf16[256,2048]{1,0:T(8,128)(2,1)S(1)}, u32[]{:S(2)}, u32[]{:S(2)}) %collective-permute-start.27) | collective-permute-done | bytes 1048608 | tf_op jit(solution)/shard_map/ppermute | solution.py:483
  283.5 22.3 %collective-permute-start.32 = (bf16[256,2048]{1,0:T(8,128)(2,1)S(1)}, bf16[256,2048]{1,0:T(8,128)(2,1)}, u32[]{:S(2)}, u32[]{:S(2)}) collective-permute-start(bf16[256,2048]{1,0:T(8,128)(2,1)S(1)} %collective-permute-done.27), channel_id=1, source_target_pairs={{0,8},{4,12},{8,16},{12,20},{16,24},{20,28},{24,0},{28,4},{1,9},{5... | collective-permute-start | bytes 3145736 | tf_op jit(solution)/shard_map/ppermute | solution.py:483
  312.4 31.2 %collective-permute-done.31 = bf16[128,2048]{1,0:T(8,128)(2,1)S(1)} collective-permute-done((bf16[128,2048]{1,0:T(8,128)(2,1)S(1)}, bf16[128,2048]{1,0:T(8,128)(2,1)S(1)}, u32[]{:S(2)}, u32[]{:S(2)}) %collective-permute-start.31) | collective-permute-done | bytes 524320 | tf_op jit(solution)/shard_map/ppermute | solution.py:466
  357.7 20.0 %collective-permute-start.37 = (bf16[256,2048]{1,0:T(8,128)(2,1)}, bf16[256,2048]{1,0:T(8,128)(2,1)}, u32[]{:S(2)}, u32[]{:S(2)}) collective-permute-start(bf16[256,2048]{1,0:T(8,128)(2,1)} %collective-permute-done.32), channel_id=1, source_target_pairs={{0,8},{4,12},{8,16},{12,20},{16,24},{20,28},{24,0},{28,4},{1,9},{5... | collective-permute-start | bytes 3145736 | tf_op jit(solution)/shard_map/ppermute | solution.py:483
  383.4 20.4 %shard_map.258 = (bf16[8,256,2048]{2,1,0:T(8,128)(2,1)}, f32[8,256,256]{2,1,0:T(8,128)}) custom-call(s32[2]{0:T(128)} %get-tuple-element.368.table, bf16[8,8,1024]{2,1,0:T(8,128)(2,1)} %copy-done.50, bf16[8,8,1024]{2,1,0:T(8,128)(2,1)} %copy-done.20, bf16[8,1024,2048]{2,1,0:T(8,128)(2,1)} %bitcast.320, bf16[8,256,2048]{2,1,0:T(8,128)(2,1)} %down.15), custom_call_target="tpu_custom_call" | custom-call | flops 10737418240 | bytes 21474836 | tf_op jit(solution)/shard_map/pallas_call | solution.py:360
  428.8 20.4 %shard_map.259 = (bf16[8,256,2048]{2,1,0:T(8,128)(2,1)}, f32[8,256,256]{2,1,0:T(8,128)}) custom-call(s32[2]{0:T(128)} %get-tuple-element.384.table, bf16[8,8,1024]{2,1,0:T(8,128)(2,1)} %copy-done.50, bf16[8,8,1024]{2,1,0:T(8,128)(2,1)} %copy-done.20, bf16[8,1024,2048]{2,1,0:T(8,128)(2,1)} %bitcast.321, bf16[8,256,2048]{2,1,0:T(8,128)(2,1)} %down.15), custom_call_target="tpu_custom_call" | custom-call | flops 10737418240 | bytes 21474836 | tf_op jit(solution)/shard_map/pallas_call | solution.py:360
  459.4 38.1 %shard_map.260 = (bf16[8,256,2048]{2,1,0:T(8,128)(2,1)}, bf16[8,256,256]{2,1,0:T(8,128)(2,1)}, bf16[8,256,512]{2,1,0:T(8,128)(2,1)}, bf16[2,2,256,2048]{3,2,1,0:T(8,128)(2,1)}, bf16[2,2,256,2048]{3,2,1,0:T(8,128)(2,1)}) custom-call(bf16[2,8,1024]{2,1,0:T(8,128)(2,1)} %bitcast.382, bf16[8,128,2048]{2,1,0:T(8,128)(2,1)} %constant_dynamic-update-slice_fusion.7.own, ...), custom_call_target="tpu_custom_call" | custom-call | flops 25769803776 | bytes 51539608 | tf_op jit(solution)/shard_map/pallas_call | solution.py:393
  513.4 20.3 %shard_map.261 = (bf16[8,256,2048]{2,1,0:T(8,128)(2,1)}, f32[8,256,256]{2,1,0:T(8,128)}) custom-call(s32[2]{0:T(128)} %get-tuple-element.394.table, bf16[8,8,1024]{2,1,0:T(8,128)(2,1)} %copy-done.50, bf16[8,8,1024]{2,1,0:T(8,128)(2,1)} %copy-done.20, bf16[8,1024,2048]{2,1,0:T(8,128)(2,1)} %bitcast.322, bf16[8,256,2048]{2,1,0:T(8,128)(2,1)} %down.15), custom_call_target="tpu_custom_call" | custom-call | flops 10737418240 | bytes 21474836 | tf_op jit(solution)/shard_map/pallas_call | solution.py:360
  533.7 20.4 %shard_map.262 = (bf16[8,256,2048]{2,1,0:T(8,128)(2,1)}, f32[8,256,256]{2,1,0:T(8,128)}) custom-call(s32[2]{0:T(128)} %get-tuple-element.409.table, bf16[8,8,1024]{2,1,0:T(8,128)(2,1)} %copy-done.50, bf16[8,8,1024]{2,1,0:T(8,128)(2,1)} %copy-done.20, bf16[8,1024,2048]{2,1,0:T(8,128)(2,1)} %bitcast.323, bf16[8,256,2048]{2,1,0:T(8,128)(2,1)} %down.15), custom_call_target="tpu_custom_call" | custom-call | flops 10737418240 | bytes 21474836 | tf_op jit(solution)/shard_map/pallas_call | solution.py:360
  568.2 37.8 %shard_map.263 = (bf16[8,256,2048]{2,1,0:T(8,128)(2,1)}, bf16[8,256,256]{2,1,0:T(8,128)(2,1)}, bf16[8,256,512]{2,1,0:T(8,128)(2,1)}, bf16[2,2,256,2048]{3,2,1,0:T(8,128)(2,1)}, bf16[2,2,256,2048]{3,2,1,0:T(8,128)(2,1)}) custom-call(bf16[2,8,1024]{2,1,0:T(8,128)(2,1)} %bitcast.381, bf16[8,128,2048]{2,1,0:T(8,128)(2,1)} %constant_dynamic-update-slice_fusion.11.own, ...), custom_call_target="tpu_custom_call" | custom-call | flops 25769803776 | bytes 51539608 | tf_op jit(solution)/shard_map/pallas_call | solution.py:393
  611.9 38.0 %shard_map.264 = (bf16[8,256,2048]{2,1,0:T(8,128)(2,1)}, bf16[8,256,256]{2,1,0:T(8,128)(2,1)}, bf16[8,256,512]{2,1,0:T(8,128)(2,1)}, bf16[2,2,256,2048]{3,2,1,0:T(8,128)(2,1)}, bf16[2,2,256,2048]{3,2,1,0:T(8,128)(2,1)}) custom-call(bf16[2,8,1024]{2,1,0:T(8,128)(2,1)} %bitcast.380, bf16[8,128,2048]{2,1,0:T(8,128)(2,1)} %constant_dynamic-update-slice_fusion.15.own, ...), custom_call_target="tpu_custom_call" | custom-call | flops 25769803776 | bytes 51539608 | tf_op jit(solution)/shard_map/pallas_call | solution.py:393
  664.3 38.2 %shard_map.265 = (bf16[8,256,2048]{2,1,0:T(8,128)(2,1)}, bf16[8,256,256]{2,1,0:T(8,128)(2,1)}, bf16[8,256,512]{2,1,0:T(8,128)(2,1)}, bf16[2,2,256,2048]{3,2,1,0:T(8,128)(2,1)}, bf16[2,2,256,2048]{3,2,1,0:T(8,128)(2,1)}) custom-call(bf16[2,8,1024]{2,1,0:T(8,128)(2,1)} %bitcast.379, bf16[8,128,2048]{2,1,0:T(8,128)(2,1)} %constant_dynamic-update-slice_fusion.3.own, ...), custom_call_target="tpu_custom_call" | custom-call | flops 25769803776 | bytes 51539608 | tf_op jit(solution)/shard_map/pallas_call | solution.py:393
  725.7 17.7 %shard_map.266.refs_0_ = bf16[4,2,1024,2048]{3,2,1,0:T(8,128)(2,1)} custom-call(s32[2]{0:T(128)} %get-tuple-element.477.table, bf16[2,8,1024]{2,1,0:T(8,128)(2,1)} %get-tuple-element.478.places, bf16[2,8,1024]{2,1,0:T(8,128)(2,1)} %get-tuple-element.479.gates, bf16[32,256,256]{2,1,0:T(8,128)(2,1)} %constant_dynamic-update-slice_fusion.19.hidden, ...), custom_call_target="tpu_custom_call" | custom-call | flops 10737418240 | bytes 21474836 | tf_op jit(solution)/shard_map/pallas_call | solution.py:420
  743.3 17.8 %shard_map.267.refs_0_ = bf16[4,2,1024,2048]{3,2,1,0:T(8,128)(2,1)} custom-call(s32[2]{0:T(128)} %get-tuple-element.470.table, bf16[2,8,1024]{2,1,0:T(8,128)(2,1)} %get-tuple-element.471.places, bf16[2,8,1024]{2,1,0:T(8,128)(2,1)} %get-tuple-element.472.gates, ...), custom_call_target="tpu_custom_call", output_to_operand_aliasing={{}: (5, {})} | custom-call | flops 10737418240 | bytes 21474836 | tf_op jit(solution)/shard_map/pallas_call | solution.py:420
  783.0 17.7 %shard_map.268.refs_0_ = bf16[4,2,1024,2048]{3,2,1,0:T(8,128)(2,1)} custom-call(s32[2]{0:T(128)} %get-tuple-element.500.table, bf16[2,8,1024]{2,1,0:T(8,128)(2,1)} %get-tuple-element.501.places, bf16[2,8,1024]{2,1,0:T(8,128)(2,1)} %get-tuple-element.502.gates, ...), custom_call_target="tpu_custom_call", output_to_operand_aliasing={{}: (5, {})} | custom-call | flops 10737418240 | bytes 21474836 | tf_op jit(solution)/shard_map/pallas_call | solution.py:420
  800.7 17.7 %shard_map.269 = bf16[4,2,1024,2048]{3,2,1,0:T(8,128)(2,1)} custom-call(s32[2]{0:T(128)} %get-tuple-element.497.table, bf16[2,8,1024]{2,1,0:T(8,128)(2,1)} %get-tuple-element.498.places, bf16[2,8,1024]{2,1,0:T(8,128)(2,1)} %get-tuple-element.499.gates, ...), custom_call_target="tpu_custom_call", output_to_operand_aliasing={{}: (5, {})} | custom-call | flops 10737418240 | bytes 21474836 | tf_op jit(solution)/shard_map/pallas_call | solution.py:420
  831.2 17.5 %shard_map.270 = (f32[8,2048,256]{2,1,0:T(8,128)}, f32[8,2048,256]{2,1,0:T(8,128)}, f32[8,256,2048]{2,1,0:T(8,128)}) custom-call(bf16[8,256,2048]{2,1,0:T(8,128)(2,1)} %get-tuple-element.560.refs_0_, bf16[8,256,2048]{2,1,0:T(8,128)(2,1)} %get-tuple-element.561.refs_1_, bf16[8,256,2048]{2,1,0:T(8,128)(2,1)} %get-tuple-element.562.refs_2_, ...), custom_call_target="tpu_custom_call" | custom-call | flops 6442450944 | bytes 12884901 | tf_op jit(solution)/shard_map/pallas_call | solution.py:451
  848.7 17.7 %shard_map.271 = (f32[8,2048,256]{2,1,0:T(8,128)}, f32[8,2048,256]{2,1,0:T(8,128)}, f32[8,256,2048]{2,1,0:T(8,128)}) custom-call(bf16[8,256,2048]{2,1,0:T(8,128)(2,1)} %get-tuple-element.560.refs_0_, bf16[8,256,2048]{2,1,0:T(8,128)(2,1)} %get-tuple-element.561.refs_1_, ...), custom_call_target="tpu_custom_call", output_to_operand_aliasing={{0}: (16, {}), {1}: (17, {}), {2}: (18, {})} | custom-call | flops 6442450944 | bytes 12884901 | tf_op jit(solution)/shard_map/pallas_call | solution.py:451
  873.1 13.5 %shard_map.272 = (f32[8,2048,256]{2,1,0:T(8,128)}, f32[8,2048,256]{2,1,0:T(8,128)}, f32[8,256,2048]{2,1,0:T(8,128)}) custom-call(bf16[8,256,2048]{2,1,0:T(8,128)(2,1)} %get-tuple-element.560.refs_0_, bf16[8,256,2048]{2,1,0:T(8,128)(2,1)} %get-tuple-element.561.refs_1_, ...), custom_call_target="tpu_custom_call", output_to_operand_aliasing={{0}: (16, {}), {1}: (17, {}), {2}: (18, {})} | custom-call | flops 6442450944 | bytes 12884901 | tf_op jit(solution)/shard_map/pallas_call | solution.py:451
  886.6 13.3 %shard_map.273 = (f32[8,2048,256]{2,1,0:T(8,128)}, f32[8,2048,256]{2,1,0:T(8,128)}, f32[8,256,2048]{2,1,0:T(8,128)}) custom-call(bf16[8,256,2048]{2,1,0:T(8,128)(2,1)} %get-tuple-element.560.refs_0_, bf16[8,256,2048]{2,1,0:T(8,128)(2,1)} %get-tuple-element.561.refs_1_, ...), custom_call_target="tpu_custom_call", output_to_operand_aliasing={{0}: (16, {}), {1}: (17, {}), {2}: (18, {})} | custom-call | flops 6442450944 | bytes 12884901 | tf_op jit(solution)/shard_map/pallas_call | solution.py:451
  899.8 14.2 %collective-permute-done.72.refs_2_ = bf16[256,2048]{1,0:T(8,128)(2,1)S(1)} collective-permute-done((bf16[256,2048]{1,0:T(8,128)(2,1)S(1)}, bf16[256,2048]{1,0:T(8,128)(2,1)S(1)}, u32[]{:S(2)}, u32[]{:S(2)}) %collective-permute-start.72) | collective-permute-done | bytes 1048608 | tf_op jit(solution)/shard_map/ppermute | solution.py:466
  1016.3 36.4 %collective-permute-done.79 = bf16[256,1536]{1,0:T(8,128)(2,1)S(1)} collective-permute-done((bf16[256,1536]{1,0:T(8,128)(2,1)S(1)}, bf16[256,1536]{1,0:T(8,128)(2,1)S(1)}, u32[]{:S(2)}, u32[]{:S(2)}) %collective-permute-start.79) | collective-permute-done | bytes 786464 | tf_op jit(solution)/shard_map/ppermute | solution.py:466
  1053.2 20.1 %reduce-scatter.3.cloned.1.call-done = bf16[4,256,2048]{2,1,0:T(8,128)(2,1)} async-done(((bf16[4,2048,2048]{2,1,0:T(8,128)(2,1)}), bf16[4,256,2048]{2,1,0:T(8,128)(2,1)}) %reduce-scatter.3.cloned.1.call-update) | async-done | bytes 4194320 | tf_op jit(solution)/shard_map/reduce_scatter | solution.py:929
  1082.4 39.7 %collective-permute-done.94 = bf16[512,256]{1,0:T(8,128)(2,1)S(1)} collective-permute-done((bf16[512,256]{1,0:T(8,128)(2,1)S(1)}, bf16[512,256]{1,0:T(8,128)(2,1)S(1)}, u32[]{:S(2)}, u32[]{:S(2)}) %collective-permute-start.94) | collective-permute-done | bytes 262176 | tf_op jit(solution)/shard_map/ppermute | solution.py:483
  1123.3 16.5 %collective-permute-start.95 = (bf16[512,256]{1,0:T(8,128)(2,1)S(1)}, bf16[512,256]{1,0:T(8,128)(2,1)S(1)}, u32[]{:S(2)}, u32[]{:S(2)}) collective-permute-start(bf16[512,256]{1,0:T(8,128)(2,1)S(1)} %add_convert_fusion.40), channel_id=1, source_target_pairs={{0,8},{4,12},{8,16},{12,20},{16,24},{20,28},{24,0},{28,4},{1,9},{5... | collective-permute-start | bytes 786440 | tf_op jit(solution)/shard_map/ppermute | solution.py:483
  1197.3 13.5 %collective-permute-done.88 = bf16[256,1536]{1,0:T(8,128)(2,1)S(1)} collective-permute-done((bf16[256,1536]{1,0:T(8,128)(2,1)S(1)}, bf16[256,1536]{1,0:T(8,128)(2,1)S(1)}, u32[]{:S(2)}, u32[]{:S(2)}) %collective-permute-start.88) | collective-permute-done | bytes 786464 | tf_op jit(solution)/shard_map/ppermute | solution.py:483
  (696 shorter events, 489.0 us)
Async XLA Ops:
  7.2 376.2 %all-gather.2.cloned.1.call-start = ((), (), s32[]{:S(2)}) async-start(), calls=%async_computation.2 | async-start | bytes 34603008 | tf_op jit(solution)/shard_map/all_gather | solution.py:1006
  131.2 942.1 %reduce-scatter.3.cloned.1.call-start = ((), (), s32[]{:S(2)}) async-start(), calls=%async_computation.3 | async-start | bytes 37748736 | tf_op jit(solution)/shard_map/reduce_scatter | solution.py:929
  148.4 48.5 %collective-permute-start.24 = (bf16[16,17,256]{2,0,1:T(8,128)(2,1)}, bf16[16,17,256]{2,0,1:T(8,128)(2,1)}, u32[]{:S(2)}, u32[]{:S(2)}) collective-permute-start(bf16[16,17,256]{2,0,1:T(8,128)(2,1)} %concatenate.117), channel_id=1, source_target_pairs={{0,16},{4,20},{8,24},{12,28},{16,0},{20,4},{24,8},{28,12},{1,17},{... | collective-permute-start | bytes 417800 | tf_op jit(solution)/shard_map/ppermute | solution.py:466
  234.7 48.7 %collective-permute-start.27 = (bf16[256,2048]{1,0:T(8,128)(2,1)S(1)}, bf16[256,2048]{1,0:T(8,128)(2,1)S(1)}, u32[]{:S(2)}, u32[]{:S(2)}) collective-permute-start(bf16[256,2048]{1,0:T(8,128)(2,1)S(1)} %multiply_convert_fusion.4), channel_id=1, source_target_pairs={{0,8},{4,12},{8,16},{12,20},{16,24},{20,28},{24,0},{28,4},{1,9},{5... | collective-permute-start | bytes 3145736 | tf_op jit(solution)/shard_map/ppermute | solution.py:483
  283.5 69.6 %collective-permute-start.32 = (bf16[256,2048]{1,0:T(8,128)(2,1)S(1)}, bf16[256,2048]{1,0:T(8,128)(2,1)}, u32[]{:S(2)}, u32[]{:S(2)}) collective-permute-start(bf16[256,2048]{1,0:T(8,128)(2,1)S(1)} %collective-permute-done.27), channel_id=1, source_target_pairs={{0,8},{4,12},{8,16},{12,20},{16,24},{20,28},{24,0},{28,4},{1,9},{5... | collective-permute-start | bytes 3145736 | tf_op jit(solution)/shard_map/ppermute | solution.py:483
  305.9 47.3 %collective-permute-start.28 = (bf16[2,128,2048]{2,1,0:T(8,128)(2,1)S(1)}, bf16[2,128,2048]{2,1,0:T(8,128)(2,1)S(1)}, u32[]{:S(2)}, u32[]{:S(2)}) collective-permute-start(bf16[2,128,2048]{2,1,0:T(8,128)(2,1)S(1)} %pad_maximum_fusion.7), channel_id=1, source_target_pairs={{0,2},{1,3},{2,0},{3,1},{4,6},{5,7},{6,4},{7,5},{8,10},{9,11},{10,... | collective-permute-start | bytes 3145736 | tf_op jit(solution)/shard_map/ppermute | solution.py:466
  306.6 46.5 %collective-permute-start.29 = (bf16[2,128,2048]{2,1,0:T(8,128)(2,1)S(1)}, bf16[2,128,2048]{2,1,0:T(8,128)(2,1)S(1)}, u32[]{:S(2)}, u32[]{:S(2)}) collective-permute-start(bf16[2,128,2048]{2,1,0:T(8,128)(2,1)S(1)} %pad_maximum_fusion.8), channel_id=1, source_target_pairs={{0,4},{4,0},{8,12},{12,8},{16,20},{20,16},{24,28},{28,24},{1,5},{5... | collective-permute-start | bytes 3145736 | tf_op jit(solution)/shard_map/ppermute | solution.py:466
  355.2 60.1 %collective-permute-start.38 = (bf16[8,128,2048]{2,1,0:T(8,128)(2,1)}, bf16[8,128,2048]{2,1,0:T(8,128)(2,1)}, u32[]{:S(2)}, u32[]{:S(2)}) collective-permute-start(bf16[8,128,2048]{2,1,0:T(8,128)(2,1)} %constant_dynamic-update-slice_fusion.3.own), channel_id=1, source_target_pairs={{0,1},{1,0},{2,3},{3,2},{4,5},{5,4},{6,7},{7,6},{8,9},{9,8},{10,11... | collective-permute-start | bytes 12582920 | tf_op jit(solution)/shard_map/ppermute | solution.py:466
  357.7 57.6 %collective-permute-start.37 = (bf16[256,2048]{1,0:T(8,128)(2,1)}, bf16[256,2048]{1,0:T(8,128)(2,1)}, u32[]{:S(2)}, u32[]{:S(2)}) collective-permute-start(bf16[256,2048]{1,0:T(8,128)(2,1)} %collective-permute-done.32), channel_id=1, source_target_pairs={{0,8},{4,12},{8,16},{12,20},{16,24},{20,28},{24,0},{28,4},{1,9},{5... | collective-permute-start | bytes 3145736 | tf_op jit(solution)/shard_map/ppermute | solution.py:483
  497.5 56.6 %collective-permute-start.44 = (bf16[2,2,256,2048]{3,2,1,0:T(8,128)(2,1)}, bf16[2,2,256,2048]{3,2,1,0:T(8,128)(2,1)}, u32[]{:S(2)}, u32[]{:S(2)}) collective-permute-start(bf16[2,2,256,2048]{3,2,1,0:T(8,128)(2,1)} %get-tuple-element.393), channel_id=1, source_target_pairs={{0,1},{1,0},{2,3},{3,2},{4,5},{5,4},{6,7},{7,6},{8,9},{9,8},{10,11... | collective-permute-start | bytes 12582920 | tf_op jit(solution)/shard_map/ppermute | solution.py:466
  503.2 59.4 %collective-permute-start.49 = (bf16[8,128,2048]{2,1,0:T(8,128)(2,1)}, bf16[8,128,2048]{2,1,0:T(8,128)(2,1)}, u32[]{:S(2)}, u32[]{:S(2)}) collective-permute-start(bf16[8,128,2048]{2,1,0:T(8,128)(2,1)} %constant_dynamic-update-slice_fusion.11.own), channel_id=1, source_target_pairs={{0,1},{1,0},{2,3},{3,2},{4,5},{5,4},{6,7},{7,6},{8,9},{9,8},{10,11... | collective-permute-start | bytes 12582920 | tf_op jit(solution)/shard_map/ppermute | solution.py:466
  506.9 55.6 %collective-permute-start.47 = (bf16[2,128,2048]{2,1,0:T(8,128)(2,1)S(1)}, bf16[2,128,2048]{2,1,0:T(8,128)(2,1)}, u32[]{:S(2)}, u32[]{:S(2)}) collective-permute-start(bf16[2,128,2048]{2,1,0:T(8,128)(2,1)S(1)} %pad_maximum_fusion.13), channel_id=1, source_target_pairs={{0,2},{1,3},{2,0},{3,1},{4,6},{5,7},{6,4},{7,5},{8,10},{9,11},{10,... | collective-permute-start | bytes 3145736 | tf_op jit(solution)/shard_map/ppermute | solution.py:466
  508.5 54.0 %collective-permute-start.48 = (bf16[2,128,2048]{2,1,0:T(8,128)(2,1)}, bf16[2,128,2048]{2,1,0:T(8,128)(2,1)}, u32[]{:S(2)}, u32[]{:S(2)}) collective-permute-start(bf16[2,128,2048]{2,1,0:T(8,128)(2,1)} %pad_maximum_fusion.14), channel_id=1, source_target_pairs={{0,4},{4,0},{8,12},{12,8},{16,20},{20,16},{24,28},{28,24},{1,5},{5... | collective-permute-start | bytes 3145736 | tf_op jit(solution)/shard_map/ppermute | solution.py:466
  562.5 43.6 %collective-permute-start.45 = (bf16[2,128,2048]{2,1,0:T(8,128)(2,1)}, bf16[2,128,2048]{2,1,0:T(8,128)(2,1)S(1)}, u32[]{:S(2)}, u32[]{:S(2)}) collective-permute-start(bf16[2,128,2048]{2,1,0:T(8,128)(2,1)} %fusion.58), channel_id=1, source_target_pairs={{0,2},{1,3},{2,0},{3,1},{4,6},{5,7},{6,4},{7,5},{8,10},{9,11},{10,... | collective-permute-start | bytes 3145736 | tf_op jit(solution)/shard_map/ppermute | solution.py:466
  563.1 43.0 %collective-permute-start.46 = (bf16[2,128,2048]{2,1,0:T(8,128)(2,1)}, bf16[2,128,2048]{2,1,0:T(8,128)(2,1)}, u32[]{:S(2)}, u32[]{:S(2)}) collective-permute-start(bf16[2,128,2048]{2,1,0:T(8,128)(2,1)} %get-tuple-element.400), channel_id=1, source_target_pairs={{0,4},{4,0},{8,12},{12,8},{16,20},{20,16},{24,28},{28,24},{1,5},{5... | collective-permute-start | bytes 3145736 | tf_op jit(solution)/shard_map/ppermute | solution.py:466
  568.2 43.6 %collective-permute-start.53 = (bf16[8,128,2048]{2,1,0:T(8,128)(2,1)}, bf16[8,128,2048]{2,1,0:T(8,128)(2,1)}, u32[]{:S(2)}, u32[]{:S(2)}) collective-permute-start(bf16[8,128,2048]{2,1,0:T(8,128)(2,1)} %constant_dynamic-update-slice_fusion.15.own), channel_id=1, source_target_pairs={{0,1},{1,0},{2,3},{3,2},{4,5},{5,4},{6,7},{7,6},{8,9},{9,8},{10,11... | collective-permute-start | bytes 12582920 | tf_op jit(solution)/shard_map/ppermute | solution.py:466
  717.5 43.7 %collective-permute-start.58 = (bf16[2,2,256,2048]{3,2,1,0:T(8,128)(2,1)}, bf16[2,2,256,2048]{3,2,1,0:T(8,128)(2,1)}, u32[]{:S(2)}, u32[]{:S(2)}) collective-permute-start(bf16[2,2,256,2048]{3,2,1,0:T(8,128)(2,1)} %get-tuple-element.464), channel_id=1, source_target_pairs={{0,1},{1,0},{2,3},{3,2},{4,5},{5,4},{6,7},{7,6},{8,9},{9,8},{10,11... | collective-permute-start | bytes 12582920 | tf_op jit(solution)/shard_map/ppermute | solution.py:466
  717.5 43.7 %collective-permute-start.59 = (bf16[128,2048]{1,0:T(8,128)(2,1)}, bf16[128,2048]{1,0:T(8,128)(2,1)}, u32[]{:S(2)}, u32[]{:S(2)}) collective-permute-start(bf16[128,2048]{1,0:T(8,128)(2,1)} %get-tuple-element.465), channel_id=1, source_target_pairs={{0,4},{4,0},{8,12},{12,8},{16,20},{20,16},{24,28},{28,24},{1,5},{5... | collective-permute-start | bytes 1572872 | tf_op jit(solution)/shard_map/ppermute | solution.py:466
  818.4 394.9 %reduce-scatter.5.cloned.1.call-start = ((), (), s32[]{:S(2)}) async-start(), calls=%async_computation.4 | async-start | bytes 5242880 | tf_op jit(solution)/shard_map/reduce_scatter | solution.py:634
  941.2 46.6 %collective-permute-start.74 = (bf16[512,256]{1,0:T(8,128)(2,1)}, bf16[512,256]{1,0:T(8,128)(2,1)}, u32[]{:S(2)}, u32[]{:S(2)}) collective-permute-start(bf16[512,256]{1,0:T(8,128)(2,1)} %bitcast.318), channel_id=1, source_target_pairs={{0,4},{4,0},{8,12},{12,8},{16,20},{20,16},{24,28},{28,24},{1,5},{5... | collective-permute-start | bytes 786440 | tf_op jit(solution)/shard_map/ppermute | solution.py:466
  941.4 46.3 %collective-permute-start.75 = (bf16[512,256]{1,0:T(8,128)(2,1)}, bf16[512,256]{1,0:T(8,128)(2,1)}, u32[]{:S(2)}, u32[]{:S(2)}) collective-permute-start(bf16[512,256]{1,0:T(8,128)(2,1)} %bitcast.317), channel_id=1, source_target_pairs={{0,4},{4,0},{8,12},{12,8},{16,20},{20,16},{24,28},{28,24},{1,5},{5... | collective-permute-start | bytes 786440 | tf_op jit(solution)/shard_map/ppermute | solution.py:466
  943.2 44.6 %collective-permute-start.76 = (bf16[512,256]{1,0:T(8,128)(2,1)}, bf16[512,256]{1,0:T(8,128)(2,1)}, u32[]{:S(2)}, u32[]{:S(2)}) collective-permute-start(bf16[512,256]{1,0:T(8,128)(2,1)} %bitcast.316), channel_id=1, source_target_pairs={{0,4},{4,0},{8,12},{12,8},{16,20},{20,16},{24,28},{28,24},{1,5},{5... | collective-permute-start | bytes 786440 | tf_op jit(solution)/shard_map/ppermute | solution.py:466
  943.5 46.1 %collective-permute-start.77 = (bf16[512,256]{1,0:T(8,128)(2,1)}, bf16[512,256]{1,0:T(8,128)(2,1)}, u32[]{:S(2)}, u32[]{:S(2)}) collective-permute-start(bf16[512,256]{1,0:T(8,128)(2,1)} %bitcast.315), channel_id=1, source_target_pairs={{0,4},{4,0},{8,12},{12,8},{16,20},{20,16},{24,28},{28,24},{1,5},{5... | collective-permute-start | bytes 786440 | tf_op jit(solution)/shard_map/ppermute | solution.py:466
  1004.7 48.1 %collective-permute-start.81 = (bf16[256,2048]{1,0:T(8,128)(2,1)S(1)}, bf16[256,2048]{1,0:T(8,128)(2,1)S(1)}, u32[]{:S(2)}, u32[]{:S(2)}) collective-permute-start(bf16[256,2048]{1,0:T(8,128)(2,1)S(1)} %get-tuple-element.638), channel_id=1, source_target_pairs={{0,1},{1,0},{2,3},{3,2},{4,5},{5,4},{6,7},{7,6},{8,9},{9,8},{10,11... | collective-permute-start | bytes 3145736 | tf_op jit(solution)/shard_map/ppermute | solution.py:466
  1004.8 48.0 %collective-permute-start.80 = (bf16[256,2048]{1,0:T(8,128)(2,1)S(1)}, bf16[256,2048]{1,0:T(8,128)(2,1)S(1)}, u32[]{:S(2)}, u32[]{:S(2)}) collective-permute-start(bf16[256,2048]{1,0:T(8,128)(2,1)S(1)} %get-tuple-element.639), channel_id=1, source_target_pairs={{0,1},{1,0},{2,3},{3,2},{4,5},{5,4},{6,7},{7,6},{8,9},{9,8},{10,11... | collective-permute-start | bytes 3145736 | tf_op jit(solution)/shard_map/ppermute | solution.py:466
  1073.4 66.4 %collective-permute-start.84 = (bf16[256,1536]{1,0:T(8,128)(2,1)}, bf16[256,1536]{1,0:T(8,128)(2,1)S(1)}, u32[]{:S(2)}, u32[]{:S(2)}) collective-permute-start(bf16[256,1536]{1,0:T(8,128)(2,1)} %get-tuple-element.632), channel_id=1, source_target_pairs={{0,4},{4,0},{8,12},{12,8},{16,20},{20,16},{24,28},{28,24},{1,5},{5... | collective-permute-start | bytes 2359304 | tf_op jit(solution)/shard_map/ppermute | solution.py:466
  1073.7 66.0 %collective-permute-start.86 = (bf16[256,2048]{1,0:T(8,128)(2,1)S(1)}, bf16[256,2048]{1,0:T(8,128)(2,1)S(1)}, u32[]{:S(2)}, u32[]{:S(2)}) collective-permute-start(bf16[256,2048]{1,0:T(8,128)(2,1)S(1)} %fusion.26), channel_id=1, source_target_pairs={{0,2},{1,3},{2,0},{3,1},{4,6},{5,7},{6,4},{7,5},{8,10},{9,11},{10,... | collective-permute-start | bytes 3145736 | tf_op jit(solution)/shard_map/ppermute | solution.py:466
  1076.8 63.0 %collective-permute-start.85 = (bf16[256,1536]{1,0:T(8,128)(2,1)S(1)}, bf16[256,1536]{1,0:T(8,128)(2,1)S(1)}, u32[]{:S(2)}, u32[]{:S(2)}) collective-permute-start(bf16[256,1536]{1,0:T(8,128)(2,1)S(1)} %fusion.43), channel_id=1, source_target_pairs={{0,8},{4,12},{8,16},{12,20},{16,24},{20,28},{24,0},{28,4},{1,9},{5... | collective-permute-start | bytes 2359304 | tf_op jit(solution)/shard_map/ppermute | solution.py:483
  1079.4 42.7 %collective-permute-start.94 = (bf16[512,256]{1,0:T(8,128)(2,1)S(1)}, bf16[512,256]{1,0:T(8,128)(2,1)S(1)}, u32[]{:S(2)}, u32[]{:S(2)}) collective-permute-start(bf16[512,256]{1,0:T(8,128)(2,1)S(1)} %add_convert_fusion.41), channel_id=1, source_target_pairs={{0,8},{4,12},{8,16},{12,20},{16,24},{20,28},{24,0},{28,4},{1,9},{5... | collective-permute-start | bytes 786440 | tf_op jit(solution)/shard_map/ppermute | solution.py:483
  1081.0 109.1 %collective-permute-start.83 = (bf16[256,1536]{1,0:T(8,128)(2,1)S(1)}, bf16[256,1536]{1,0:T(8,128)(2,1)S(1)}, u32[]{:S(2)}, u32[]{:S(2)}) collective-permute-start(bf16[256,1536]{1,0:T(8,128)(2,1)S(1)} %copy-done.89), channel_id=1, source_target_pairs={{0,4},{4,0},{8,12},{12,8},{16,20},{20,16},{24,28},{28,24},{1,5},{5... | collective-permute-start | bytes 2359304 | tf_op jit(solution)/shard_map/ppermute | solution.py:466
  1141.2 48.8 %collective-permute-start.87 = (bf16[256,1536]{1,0:T(8,128)(2,1)S(1)}, bf16[256,1536]{1,0:T(8,128)(2,1)S(1)}, u32[]{:S(2)}, u32[]{:S(2)}) collective-permute-start(bf16[256,1536]{1,0:T(8,128)(2,1)S(1)} %add_convert_fusion.29), channel_id=1, source_target_pairs={{0,8},{4,12},{8,16},{12,20},{16,24},{20,28},{24,0},{28,4},{1,9},{5... | collective-permute-start | bytes 2359304 | tf_op jit(solution)/shard_map/ppermute | solution.py:483
  1148.6 48.6 %collective-permute-start.82 = (bf16[256,1536]{1,0:T(8,128)(2,1)S(1)}, bf16[256,1536]{1,0:T(8,128)(2,1)S(1)}, u32[]{:S(2)}, u32[]{:S(2)}) collective-permute-start(bf16[256,1536]{1,0:T(8,128)(2,1)S(1)} %copy-done.88), channel_id=1, source_target_pairs={{0,4},{4,0},{8,12},{12,8},{16,20},{20,16},{24,28},{28,24},{1,5},{5... | collective-permute-start | bytes 2359304 | tf_op jit(solution)/shard_map/ppermute | solution.py:466
  (208 other events, 3160.5 us)
Sparse Core Ops, SparseCore 0:
  131.4 246.5 all-gather.1
  818.6 254.7 reduce-scatter.2
  1075.7 119.3 reduce-scatter.4

commit v11 on v10

--- a/solution.py
+++ b/solution.py
@@ -631,6 +631,7 @@
         if turn == 0:
             far, close = added(pick(2), arrived[0]), added(pick(0), arrived[1])
             mixed, far = tied(mixed, far)
+            mixed = jnp.concatenate(mixed)
             mixed = lax.psum_scatter(mixed, "plane", scatter_dimension=0, tiled=True)
         if turn == 1:
             total = added(close, arrived[0], jnp.float32)
@@ -912,23 +913,22 @@
             made.append(folding.turn(pack_order, functools.partial(cot_work, len(made))))
     hidden_all = jnp.concatenate([kept[plane][1] for plane in range(planes)])
 
-    def mix_turn(some, given):
-        table, mixed = given
-        for plane in some:
+    def mix_turn(start, table):
+        mixed = ()
+        for index in range(2):
+            plane = start + index
             mixed = mix_rows(
-                plane, planes, table[plane], mix_places[plane], mix_gates[plane], hidden_all, w_down,
+                index, 2, table[plane], mix_places[plane], mix_gates[plane], hidden_all, w_down,
                 capacity, mixed,
             )
-        return mixed
-
-    mixed = ()
+        return mixed[0].reshape(2, -1, mixed[0].shape[-1])
+
+    mixed = []
     for start in range(0, planes, 2):
-        some = range(start, start + 2)
-        mixed = folding.turn((tables, mixed), functools.partial(mix_turn, some))
-    whole = mixed[0].reshape(planes, -1, mixed[0].shape[-1])
-    whole = lax.psum_scatter(
-        whole, ("pack", "side", "core"), scatter_dimension=1, tiled=True
-    )
+        part = folding.turn(tables, functools.partial(mix_turn, start))
+        mixed.append(
+            lax.psum_scatter(part, ("pack", "side", "core"), scatter_dimension=1, tiled=True)
+        )
     kept = [kept[plane] for plane in range(planes)]
     weight_parts, next_expert = (), 0
     part_size = math.gcd(local_experts, GROUP)
@@ -947,7 +947,7 @@
         weight_parts = folding.turn((kept, weight_parts), functools.partial(weight_turn, count))
         next_expert = min(next_expert + count * part_size, local_experts)
     rest = (kept, weight_parts, next_expert, part_size)
-    return folding.summed, whole, rest
+    return folding.summed, mixed, rest
 
 
 def shards(

time: 1230 us -> 1230 us (level)
    ppermute x78, waiting for transfers between devices: 231 us -> 255 us  [swapped(): return lax.ppermute(values, axis, [(i, i ^ bit) for i in range(count)])]
    reduce_scatter x1 -> x2, waiting for transfers between devices: 20.1 us -> 6.43 us  [experts_by_gather(): lax.psum_scatter(part, ('pack', 'side', 'core'), scatter_dimension=1, til...]
    unnamed x308 -> x296, local copies, waits for them, and re-layouts: 41.9 us -> 40.7 us
  transfers between devices with their start and end apart: 99 -> 100, of which waited for: 30 -> 30; matrix products, arithmetic and copies ran while one was open for 20% -> 21% of each run, Pallas kernels for 28% -> 27%
where the time goes in v11:
time: 1230 us; the launch traced here: 1220 us
  Pallas kernels  379 us (31%)
  waiting for transfers between devices  360 us (29%)
  starting transfers between devices  154 us (13%)
  other arithmetic  137 us (11%)
  local copies, waits for them, and re-layouts  98.9 us (8%)
  matrix products  74.6 us (6%)
  between operations  16.6 us (1%)
    ppermute x78, waiting for transfers between devices, swapped(): return lax.ppermute(values, axis, [(i, i ^ bit) for i in range(count)])  255 us
    pallas_call x4, Pallas kernels, row_slots(): call(functools.partial(row_kernel, packs, steps, capacity), 2 * packs + s...  152 us
    ppermute x18, waiting for transfers between devices, next_plane(): lax.ppermute(values, DP, [(i, (i + 2) % count) for i in range(count)])  98.5 us
    ppermute x18, starting transfers between devices, next_plane(): lax.ppermute(values, DP, [(i, (i + 2) % count) for i in range(count)])  82.2 us
    pallas_call x4, Pallas kernels, cot_slots(): call(functools.partial(cot_kernel, packs, steps, capacity), packs + steps...  81.5 us
    ppermute x78, starting transfers between devices, swapped(): return lax.ppermute(values, axis, [(i, i ^ bit) for i in range(count)])  71.4 us
    pallas_call x4, Pallas kernels, mix_rows(): call(functools.partial(mix_kernel, packs, steps, capacity), packs + steps...  71.1 us
    convert_element_type x38, other arithmetic, added(): return (left.astype(jnp.float32) + right.astype(jnp.float32)).astype(kind)  62.7 us
  transfers between devices with their start and end apart: 100, of which 30 were waited for; matrix products, arithmetic and copies ran while one was open for 21% of the time, Pallas kernels for 27%

profile of v11, /device:TPU:0, one launch (start us, length us, event | category | flops | bytes accessed | tf_op | source)
XLA Modules:
  0.0 1221.0 jit_solution(15929526220994369253)
XLA Ops:
  21.8 13.7 %pad_maximum_fusion.both = bf16[8,2048,512]{2,1,0:T(8,128)(2,1)} fusion(bf16[8,2048,256]{2,1,0:T(8,128)(2,1)} %param.29, bf16[8,2048,256]{2,1,0:T(8,128)(2,1)} %param.28), kind=kLoop, calls=%fused_computation.4 | loop fusion | flops 33554432 | bytes 33554432 | tf_op jit(solution)/shard_map/concatenate | solution.py:657
  53.9 19.9 %collective-permute-done.10.refs_4_ = bf16[512,256]{1,0:T(8,128)(2,1)S(1)} collective-permute-done((bf16[512,256]{1,0:T(8,128)(2,1)S(1)}, bf16[512,256]{1,0:T(8,128)(2,1)S(1)}, u32[]{:S(2)}, u32[]{:S(2)}) %collective-permute-start.10) | collective-permute-done | bytes 262176 | tf_op jit(solution)/shard_map/ppermute | solution.py:483
  78.9 20.7 %collective-permute-done.17 = bf16[4,17,256]{2,0,1:T(4,128)(2,1)S(1)} collective-permute-done((bf16[4,17,256]{2,0,1:T(4,128)(2,1)S(1)}, bf16[4,17,256]{2,0,1:T(4,128)(2,1)S(1)}, u32[]{:S(2)}, u32[]{:S(2)}) %collective-permute-start.17) | collective-permute-done | bytes 34848 | tf_op jit(solution)/shard_map/ppermute | solution.py:466
  108.5 16.5 %collective-permute-done.19.refs_7_ = bf16[512,256]{1,0:T(8,128)(2,1)} collective-permute-done((bf16[512,256]{1,0:T(8,128)(2,1)}, bf16[512,256]{1,0:T(8,128)(2,1)}, u32[]{:S(2)}, u32[]{:S(2)}) %collective-permute-start.19) | collective-permute-done | bytes 262176 | tf_op jit(solution)/shard_map/ppermute | solution.py:466
  208.8 23.3 %collective-permute-done.23 = bf16[256,2048]{1,0:T(8,128)(2,1)S(1)} collective-permute-done((bf16[256,2048]{1,0:T(8,128)(2,1)S(1)}, bf16[256,2048]{1,0:T(8,128)(2,1)S(1)}, u32[]{:S(2)}, u32[]{:S(2)}) %collective-permute-start.23) | collective-permute-done | bytes 1048608 | tf_op jit(solution)/shard_map/ppermute | solution.py:466
  238.5 23.1 %collective-permute-done.26 = bf16[128,2048]{1,0:T(8,128)(2,1)S(1)} collective-permute-done((bf16[128,2048]{1,0:T(8,128)(2,1)S(1)}, bf16[128,2048]{1,0:T(8,128)(2,1)S(1)}, u32[]{:S(2)}, u32[]{:S(2)}) %collective-permute-start.26) | collective-permute-done | bytes 524320 | tf_op jit(solution)/shard_map/ppermute | solution.py:466
  262.3 21.0 %collective-permute-done.27 = bf16[256,2048]{1,0:T(8,128)(2,1)S(1)} collective-permute-done((bf16[256,2048]{1,0:T(8,128)(2,1)S(1)}, bf16[256,2048]{1,0:T(8,128)(2,1)S(1)}, u32[]{:S(2)}, u32[]{:S(2)}) %collective-permute-start.27) | collective-permute-done | bytes 1048608 | tf_op jit(solution)/shard_map/ppermute | solution.py:483
  283.5 22.3 %collective-permute-start.32 = (bf16[256,2048]{1,0:T(8,128)(2,1)S(1)}, bf16[256,2048]{1,0:T(8,128)(2,1)}, u32[]{:S(2)}, u32[]{:S(2)}) collective-permute-start(bf16[256,2048]{1,0:T(8,128)(2,1)S(1)} %collective-permute-done.27), channel_id=1, source_target_pairs={{0,8},{4,12},{8,16},{12,20},{16,24},{20,28},{24,0},{28,4},{1,9},{5... | collective-permute-start | bytes 3145736 | tf_op jit(solution)/shard_map/ppermute | solution.py:483
  312.4 31.2 %collective-permute-done.31 = bf16[128,2048]{1,0:T(8,128)(2,1)S(1)} collective-permute-done((bf16[128,2048]{1,0:T(8,128)(2,1)S(1)}, bf16[128,2048]{1,0:T(8,128)(2,1)S(1)}, u32[]{:S(2)}, u32[]{:S(2)}) %collective-permute-start.31) | collective-permute-done | bytes 524320 | tf_op jit(solution)/shard_map/ppermute | solution.py:466
  357.6 20.1 %collective-permute-start.37 = (bf16[256,2048]{1,0:T(8,128)(2,1)}, bf16[256,2048]{1,0:T(8,128)(2,1)}, u32[]{:S(2)}, u32[]{:S(2)}) collective-permute-start(bf16[256,2048]{1,0:T(8,128)(2,1)} %collective-permute-done.32), channel_id=1, source_target_pairs={{0,8},{4,12},{8,16},{12,20},{16,24},{20,28},{24,0},{28,4},{1,9},{5... | collective-permute-start | bytes 3145736 | tf_op jit(solution)/shard_map/ppermute | solution.py:483
  383.4 20.4 %shard_map.258 = (bf16[8,256,2048]{2,1,0:T(8,128)(2,1)}, f32[8,256,256]{2,1,0:T(8,128)}) custom-call(s32[2]{0:T(128)} %get-tuple-element.368.table, bf16[8,8,1024]{2,1,0:T(8,128)(2,1)} %copy-done.50, bf16[8,8,1024]{2,1,0:T(8,128)(2,1)} %copy-done.20, bf16[8,1024,2048]{2,1,0:T(8,128)(2,1)} %bitcast.320, bf16[8,256,2048]{2,1,0:T(8,128)(2,1)} %down.15), custom_call_target="tpu_custom_call" | custom-call | flops 10737418240 | bytes 21474836 | tf_op jit(solution)/shard_map/pallas_call | solution.py:360
  428.8 20.4 %shard_map.259 = (bf16[8,256,2048]{2,1,0:T(8,128)(2,1)}, f32[8,256,256]{2,1,0:T(8,128)}) custom-call(s32[2]{0:T(128)} %get-tuple-element.384.table, bf16[8,8,1024]{2,1,0:T(8,128)(2,1)} %copy-done.50, bf16[8,8,1024]{2,1,0:T(8,128)(2,1)} %copy-done.20, bf16[8,1024,2048]{2,1,0:T(8,128)(2,1)} %bitcast.321, bf16[8,256,2048]{2,1,0:T(8,128)(2,1)} %down.15), custom_call_target="tpu_custom_call" | custom-call | flops 10737418240 | bytes 21474836 | tf_op jit(solution)/shard_map/pallas_call | solution.py:360
  459.4 38.2 %shard_map.260 = (bf16[8,256,2048]{2,1,0:T(8,128)(2,1)}, bf16[8,256,256]{2,1,0:T(8,128)(2,1)}, bf16[8,256,512]{2,1,0:T(8,128)(2,1)}, bf16[2,2,256,2048]{3,2,1,0:T(8,128)(2,1)}, bf16[2,2,256,2048]{3,2,1,0:T(8,128)(2,1)}) custom-call(bf16[2,8,1024]{2,1,0:T(8,128)(2,1)} %bitcast.384, bf16[8,128,2048]{2,1,0:T(8,128)(2,1)} %constant_dynamic-update-slice_fusion.7.own, ...), custom_call_target="tpu_custom_call" | custom-call | flops 25769803776 | bytes 51539608 | tf_op jit(solution)/shard_map/pallas_call | solution.py:393
  513.4 20.4 %shard_map.261 = (bf16[8,256,2048]{2,1,0:T(8,128)(2,1)}, f32[8,256,256]{2,1,0:T(8,128)}) custom-call(s32[2]{0:T(128)} %get-tuple-element.394.table, bf16[8,8,1024]{2,1,0:T(8,128)(2,1)} %copy-done.50, bf16[8,8,1024]{2,1,0:T(8,128)(2,1)} %copy-done.20, bf16[8,1024,2048]{2,1,0:T(8,128)(2,1)} %bitcast.322, bf16[8,256,2048]{2,1,0:T(8,128)(2,1)} %down.15), custom_call_target="tpu_custom_call" | custom-call | flops 10737418240 | bytes 21474836 | tf_op jit(solution)/shard_map/pallas_call | solution.py:360
  533.8 20.4 %shard_map.262 = (bf16[8,256,2048]{2,1,0:T(8,128)(2,1)}, f32[8,256,256]{2,1,0:T(8,128)}) custom-call(s32[2]{0:T(128)} %get-tuple-element.409.table, bf16[8,8,1024]{2,1,0:T(8,128)(2,1)} %copy-done.50, bf16[8,8,1024]{2,1,0:T(8,128)(2,1)} %copy-done.20, bf16[8,1024,2048]{2,1,0:T(8,128)(2,1)} %bitcast.323, bf16[8,256,2048]{2,1,0:T(8,128)(2,1)} %down.15), custom_call_target="tpu_custom_call" | custom-call | flops 10737418240 | bytes 21474836 | tf_op jit(solution)/shard_map/pallas_call | solution.py:360
  568.3 37.8 %shard_map.263 = (bf16[8,256,2048]{2,1,0:T(8,128)(2,1)}, bf16[8,256,256]{2,1,0:T(8,128)(2,1)}, bf16[8,256,512]{2,1,0:T(8,128)(2,1)}, bf16[2,2,256,2048]{3,2,1,0:T(8,128)(2,1)}, bf16[2,2,256,2048]{3,2,1,0:T(8,128)(2,1)}) custom-call(bf16[2,8,1024]{2,1,0:T(8,128)(2,1)} %bitcast.383, bf16[8,128,2048]{2,1,0:T(8,128)(2,1)} %constant_dynamic-update-slice_fusion.11.own, ...), custom_call_target="tpu_custom_call" | custom-call | flops 25769803776 | bytes 51539608 | tf_op jit(solution)/shard_map/pallas_call | solution.py:393
  611.9 37.9 %shard_map.264 = (bf16[8,256,2048]{2,1,0:T(8,128)(2,1)}, bf16[8,256,256]{2,1,0:T(8,128)(2,1)}, bf16[8,256,512]{2,1,0:T(8,128)(2,1)}, bf16[2,2,256,2048]{3,2,1,0:T(8,128)(2,1)}, bf16[2,2,256,2048]{3,2,1,0:T(8,128)(2,1)}) custom-call(bf16[2,8,1024]{2,1,0:T(8,128)(2,1)} %bitcast.382, bf16[8,128,2048]{2,1,0:T(8,128)(2,1)} %constant_dynamic-update-slice_fusion.15.own, ...), custom_call_target="tpu_custom_call" | custom-call | flops 25769803776 | bytes 51539608 | tf_op jit(solution)/shard_map/pallas_call | solution.py:393
  663.5 38.2 %shard_map.265 = (bf16[8,256,2048]{2,1,0:T(8,128)(2,1)}, bf16[8,256,256]{2,1,0:T(8,128)(2,1)}, bf16[8,256,512]{2,1,0:T(8,128)(2,1)}, bf16[2,2,256,2048]{3,2,1,0:T(8,128)(2,1)}, bf16[2,2,256,2048]{3,2,1,0:T(8,128)(2,1)}) custom-call(bf16[2,8,1024]{2,1,0:T(8,128)(2,1)} %bitcast.381, bf16[8,128,2048]{2,1,0:T(8,128)(2,1)} %constant_dynamic-update-slice_fusion.3.own, ...), custom_call_target="tpu_custom_call" | custom-call | flops 25769803776 | bytes 51539608 | tf_op jit(solution)/shard_map/pallas_call | solution.py:393
  722.5 17.7 %shard_map.266.refs_0_ = bf16[2,2,1024,2048]{3,2,1,0:T(8,128)(2,1)} custom-call(s32[2]{0:T(128)} %get-tuple-element.477.table, bf16[2,8,1024]{2,1,0:T(8,128)(2,1)} %get-tuple-element.478.places, bf16[2,8,1024]{2,1,0:T(8,128)(2,1)} %get-tuple-element.479.gates, bf16[32,256,256]{2,1,0:T(8,128)(2,1)} %constant_dynamic-update-slice_fusion.19.hidden, ...), custom_call_target="tpu_custom_call" | custom-call | flops 10737418240 | bytes 21474836 | tf_op jit(solution)/shard_map/pallas_call | solution.py:420
  740.2 17.7 %shard_map.267 = bf16[2,2,1024,2048]{3,2,1,0:T(8,128)(2,1)} custom-call(s32[2]{0:T(128)} %get-tuple-element.470.table, bf16[2,8,1024]{2,1,0:T(8,128)(2,1)} %get-tuple-element.471.places, bf16[2,8,1024]{2,1,0:T(8,128)(2,1)} %get-tuple-element.472.gates, ...), custom_call_target="tpu_custom_call", output_to_operand_aliasing={{}: (5, {})} | custom-call | flops 10737418240 | bytes 21474836 | tf_op jit(solution)/shard_map/pallas_call | solution.py:420
  782.0 17.9 %shard_map.268.refs_0_ = bf16[2,2,1024,2048]{3,2,1,0:T(8,128)(2,1)} custom-call(s32[2]{0:T(128)} %get-tuple-element.500.table, bf16[2,8,1024]{2,1,0:T(8,128)(2,1)} %get-tuple-element.501.places, bf16[2,8,1024]{2,1,0:T(8,128)(2,1)} %get-tuple-element.502.gates, bf16[32,256,256]{2,1,0:T(8,128)(2,1)} %constant_dynamic-update-slice_fusion.19.hidden, ...), custom_call_target="tpu_custom_call" | custom-call | flops 10737418240 | bytes 21474836 | tf_op jit(solution)/shard_map/pallas_call | solution.py:420
  799.9 17.8 %shard_map.269 = bf16[2,2,1024,2048]{3,2,1,0:T(8,128)(2,1)} custom-call(s32[2]{0:T(128)} %get-tuple-element.497.table, bf16[2,8,1024]{2,1,0:T(8,128)(2,1)} %get-tuple-element.498.places, bf16[2,8,1024]{2,1,0:T(8,128)(2,1)} %get-tuple-element.499.gates, ...), custom_call_target="tpu_custom_call", output_to_operand_aliasing={{}: (5, {})} | custom-call | flops 10737418240 | bytes 21474836 | tf_op jit(solution)/shard_map/pallas_call | solution.py:420
  817.7 16.3 %collective-permute-done.63 = bf16[2,128,2048]{2,1,0:T(8,128)(2,1)} collective-permute-done((bf16[2,128,2048]{2,1,0:T(8,128)(2,1)}, bf16[2,128,2048]{2,1,0:T(8,128)(2,1)}, u32[]{:S(2)}, u32[]{:S(2)}) %collective-permute-start.63) | collective-permute-done | bytes 1048608 | tf_op jit(solution)/shard_map/ppermute | solution.py:466
  846.1 13.3 %shard_map.270 = (f32[8,2048,256]{2,1,0:T(8,128)}, f32[8,2048,256]{2,1,0:T(8,128)}, f32[8,256,2048]{2,1,0:T(8,128)}) custom-call(bf16[8,256,2048]{2,1,0:T(8,128)(2,1)} %get-tuple-element.559.refs_0_, bf16[8,256,2048]{2,1,0:T(8,128)(2,1)} %get-tuple-element.560.refs_1_, bf16[8,256,2048]{2,1,0:T(8,128)(2,1)} %get-tuple-element.561.refs_2_, ...), custom_call_target="tpu_custom_call" | custom-call | flops 6442450944 | bytes 12884901 | tf_op jit(solution)/shard_map/pallas_call | solution.py:451
  859.4 13.1 %shard_map.271 = (f32[8,2048,256]{2,1,0:T(8,128)}, f32[8,2048,256]{2,1,0:T(8,128)}, f32[8,256,2048]{2,1,0:T(8,128)}) custom-call(bf16[8,256,2048]{2,1,0:T(8,128)(2,1)} %get-tuple-element.559.refs_0_, bf16[8,256,2048]{2,1,0:T(8,128)(2,1)} %get-tuple-element.560.refs_1_, ...), custom_call_target="tpu_custom_call", output_to_operand_aliasing={{0}: (16, {}), {1}: (17, {}), {2}: (18, {})} | custom-call | flops 6442450944 | bytes 12884901 | tf_op jit(solution)/shard_map/pallas_call | solution.py:451
  877.8 13.4 %shard_map.272 = (f32[8,2048,256]{2,1,0:T(8,128)}, f32[8,2048,256]{2,1,0:T(8,128)}, f32[8,256,2048]{2,1,0:T(8,128)}) custom-call(bf16[8,256,2048]{2,1,0:T(8,128)(2,1)} %get-tuple-element.559.refs_0_, bf16[8,256,2048]{2,1,0:T(8,128)(2,1)} %get-tuple-element.560.refs_1_, ...), custom_call_target="tpu_custom_call", output_to_operand_aliasing={{0}: (16, {}), {1}: (17, {}), {2}: (18, {})} | custom-call | flops 6442450944 | bytes 12884901 | tf_op jit(solution)/shard_map/pallas_call | solution.py:451
  891.3 13.5 %shard_map.273 = (f32[8,2048,256]{2,1,0:T(8,128)}, f32[8,2048,256]{2,1,0:T(8,128)}, f32[8,256,2048]{2,1,0:T(8,128)}) custom-call(bf16[8,256,2048]{2,1,0:T(8,128)(2,1)} %get-tuple-element.559.refs_0_, bf16[8,256,2048]{2,1,0:T(8,128)(2,1)} %get-tuple-element.560.refs_1_, ...), custom_call_target="tpu_custom_call", output_to_operand_aliasing={{0}: (16, {}), {1}: (17, {}), {2}: (18, {})} | custom-call | flops 6442450944 | bytes 12884901 | tf_op jit(solution)/shard_map/pallas_call | solution.py:451
  904.8 13.9 %collective-permute-done.72.refs_2_ = bf16[256,2048]{1,0:T(8,128)(2,1)S(1)} collective-permute-done((bf16[256,2048]{1,0:T(8,128)(2,1)S(1)}, bf16[256,2048]{1,0:T(8,128)(2,1)S(1)}, u32[]{:S(2)}, u32[]{:S(2)}) %collective-permute-start.72) | collective-permute-done | bytes 1048608 | tf_op jit(solution)/shard_map/ppermute | solution.py:466
  1023.2 33.7 %collective-permute-done.79 = bf16[256,1536]{1,0:T(8,128)(2,1)S(1)} collective-permute-done((bf16[256,1536]{1,0:T(8,128)(2,1)S(1)}, bf16[256,1536]{1,0:T(8,128)(2,1)S(1)}, u32[]{:S(2)}, u32[]{:S(2)}) %collective-permute-start.79) | collective-permute-done | bytes 786464 | tf_op jit(solution)/shard_map/ppermute | solution.py:466
  1076.9 42.9 %collective-permute-done.94 = bf16[512,256]{1,0:T(8,128)(2,1)S(1)} collective-permute-done((bf16[512,256]{1,0:T(8,128)(2,1)S(1)}, bf16[512,256]{1,0:T(8,128)(2,1)S(1)}, u32[]{:S(2)}, u32[]{:S(2)}) %collective-permute-start.94) | collective-permute-done | bytes 262176 | tf_op jit(solution)/shard_map/ppermute | solution.py:483
  1121.0 18.9 %collective-permute-start.95 = (bf16[512,256]{1,0:T(8,128)(2,1)S(1)}, bf16[512,256]{1,0:T(8,128)(2,1)S(1)}, u32[]{:S(2)}, u32[]{:S(2)}) collective-permute-start(bf16[512,256]{1,0:T(8,128)(2,1)S(1)} %add_convert_fusion.40), channel_id=1, source_target_pairs={{0,8},{4,12},{8,16},{12,20},{16,24},{20,28},{24,0},{28,4},{1,9},{5... | collective-permute-start | bytes 786440 | tf_op jit(solution)/shard_map/ppermute | solution.py:483
  1171.4 12.8 %collective-permute-done.92 = f32[4352]{0:T(1024)S(1)} collective-permute-done((f32[4352]{0:T(1024)S(1)}, f32[4352]{0:T(1024)S(1)}, u32[]{:S(2)}, u32[]{:S(2)}) %collective-permute-start.92) | collective-permute-done | bytes 17440 | tf_op jit(solution)/shard_map/ppermute | solution.py:466
  (688 shorter events, 496.1 us)
Async XLA Ops:
  7.2 376.2 %all-gather.2.cloned.1.call-start = ((), (), s32[]{:S(2)}) async-start(), calls=%async_computation.3 | async-start | bytes 34603008 | tf_op jit(solution)/shard_map/all_gather | solution.py:1006
  131.2 926.1 %reduce-scatter.4.cloned.1.call-start = ((), (), s32[]{:S(2)}) async-start(), calls=%async_computation.4 | async-start | bytes 18874368 | tf_op jit(solution)/shard_map/reduce_scatter | solution.py:930
  148.3 48.5 %collective-permute-start.24 = (bf16[16,17,256]{2,0,1:T(8,128)(2,1)}, bf16[16,17,256]{2,0,1:T(8,128)(2,1)}, u32[]{:S(2)}, u32[]{:S(2)}) collective-permute-start(bf16[16,17,256]{2,0,1:T(8,128)(2,1)} %concatenate.120), channel_id=1, source_target_pairs={{0,16},{4,20},{8,24},{12,28},{16,0},{20,4},{24,8},{28,12},{1,17},{... | collective-permute-start | bytes 417800 | tf_op jit(solution)/shard_map/ppermute | solution.py:466
  234.6 48.7 %collective-permute-start.27 = (bf16[256,2048]{1,0:T(8,128)(2,1)S(1)}, bf16[256,2048]{1,0:T(8,128)(2,1)S(1)}, u32[]{:S(2)}, u32[]{:S(2)}) collective-permute-start(bf16[256,2048]{1,0:T(8,128)(2,1)S(1)} %multiply_convert_fusion.4), channel_id=1, source_target_pairs={{0,8},{4,12},{8,16},{12,20},{16,24},{20,28},{24,0},{28,4},{1,9},{5... | collective-permute-start | bytes 3145736 | tf_op jit(solution)/shard_map/ppermute | solution.py:483
  283.5 69.5 %collective-permute-start.32 = (bf16[256,2048]{1,0:T(8,128)(2,1)S(1)}, bf16[256,2048]{1,0:T(8,128)(2,1)}, u32[]{:S(2)}, u32[]{:S(2)}) collective-permute-start(bf16[256,2048]{1,0:T(8,128)(2,1)S(1)} %collective-permute-done.27), channel_id=1, source_target_pairs={{0,8},{4,12},{8,16},{12,20},{16,24},{20,28},{24,0},{28,4},{1,9},{5... | collective-permute-start | bytes 3145736 | tf_op jit(solution)/shard_map/ppermute | solution.py:483
  305.8 47.2 %collective-permute-start.28 = (bf16[2,128,2048]{2,1,0:T(8,128)(2,1)S(1)}, bf16[2,128,2048]{2,1,0:T(8,128)(2,1)S(1)}, u32[]{:S(2)}, u32[]{:S(2)}) collective-permute-start(bf16[2,128,2048]{2,1,0:T(8,128)(2,1)S(1)} %pad_maximum_fusion.8), channel_id=1, source_target_pairs={{0,2},{1,3},{2,0},{3,1},{4,6},{5,7},{6,4},{7,5},{8,10},{9,11},{10,... | collective-permute-start | bytes 3145736 | tf_op jit(solution)/shard_map/ppermute | solution.py:466
  306.5 46.5 %collective-permute-start.29 = (bf16[2,128,2048]{2,1,0:T(8,128)(2,1)S(1)}, bf16[2,128,2048]{2,1,0:T(8,128)(2,1)S(1)}, u32[]{:S(2)}, u32[]{:S(2)}) collective-permute-start(bf16[2,128,2048]{2,1,0:T(8,128)(2,1)S(1)} %pad_maximum_fusion.9), channel_id=1, source_target_pairs={{0,4},{4,0},{8,12},{12,8},{16,20},{20,16},{24,28},{28,24},{1,5},{5... | collective-permute-start | bytes 3145736 | tf_op jit(solution)/shard_map/ppermute | solution.py:466
  355.1 60.2 %collective-permute-start.38 = (bf16[8,128,2048]{2,1,0:T(8,128)(2,1)}, bf16[8,128,2048]{2,1,0:T(8,128)(2,1)}, u32[]{:S(2)}, u32[]{:S(2)}) collective-permute-start(bf16[8,128,2048]{2,1,0:T(8,128)(2,1)} %constant_dynamic-update-slice_fusion.3.own), channel_id=1, source_target_pairs={{0,1},{1,0},{2,3},{3,2},{4,5},{5,4},{6,7},{7,6},{8,9},{9,8},{10,11... | collective-permute-start | bytes 12582920 | tf_op jit(solution)/shard_map/ppermute | solution.py:466
  357.6 57.7 %collective-permute-start.37 = (bf16[256,2048]{1,0:T(8,128)(2,1)}, bf16[256,2048]{1,0:T(8,128)(2,1)}, u32[]{:S(2)}, u32[]{:S(2)}) collective-permute-start(bf16[256,2048]{1,0:T(8,128)(2,1)} %collective-permute-done.32), channel_id=1, source_target_pairs={{0,8},{4,12},{8,16},{12,20},{16,24},{20,28},{24,0},{28,4},{1,9},{5... | collective-permute-start | bytes 3145736 | tf_op jit(solution)/shard_map/ppermute | solution.py:483
  497.6 56.6 %collective-permute-start.44 = (bf16[2,2,256,2048]{3,2,1,0:T(8,128)(2,1)}, bf16[2,2,256,2048]{3,2,1,0:T(8,128)(2,1)}, u32[]{:S(2)}, u32[]{:S(2)}) collective-permute-start(bf16[2,2,256,2048]{3,2,1,0:T(8,128)(2,1)} %get-tuple-element.393), channel_id=1, source_target_pairs={{0,1},{1,0},{2,3},{3,2},{4,5},{5,4},{6,7},{7,6},{8,9},{9,8},{10,11... | collective-permute-start | bytes 12582920 | tf_op jit(solution)/shard_map/ppermute | solution.py:466
  503.2 59.4 %collective-permute-start.49 = (bf16[8,128,2048]{2,1,0:T(8,128)(2,1)}, bf16[8,128,2048]{2,1,0:T(8,128)(2,1)}, u32[]{:S(2)}, u32[]{:S(2)}) collective-permute-start(bf16[8,128,2048]{2,1,0:T(8,128)(2,1)} %constant_dynamic-update-slice_fusion.11.own), channel_id=1, source_target_pairs={{0,1},{1,0},{2,3},{3,2},{4,5},{5,4},{6,7},{7,6},{8,9},{9,8},{10,11... | collective-permute-start | bytes 12582920 | tf_op jit(solution)/shard_map/ppermute | solution.py:466
  507.0 55.6 %collective-permute-start.47 = (bf16[2,128,2048]{2,1,0:T(8,128)(2,1)S(1)}, bf16[2,128,2048]{2,1,0:T(8,128)(2,1)}, u32[]{:S(2)}, u32[]{:S(2)}) collective-permute-start(bf16[2,128,2048]{2,1,0:T(8,128)(2,1)S(1)} %pad_maximum_fusion.14), channel_id=1, source_target_pairs={{0,2},{1,3},{2,0},{3,1},{4,6},{5,7},{6,4},{7,5},{8,10},{9,11},{10,... | collective-permute-start | bytes 3145736 | tf_op jit(solution)/shard_map/ppermute | solution.py:466
  508.5 54.0 %collective-permute-start.48 = (bf16[2,128,2048]{2,1,0:T(8,128)(2,1)}, bf16[2,128,2048]{2,1,0:T(8,128)(2,1)}, u32[]{:S(2)}, u32[]{:S(2)}) collective-permute-start(bf16[2,128,2048]{2,1,0:T(8,128)(2,1)} %pad_maximum_fusion.15), channel_id=1, source_target_pairs={{0,4},{4,0},{8,12},{12,8},{16,20},{20,16},{24,28},{28,24},{1,5},{5... | collective-permute-start | bytes 3145736 | tf_op jit(solution)/shard_map/ppermute | solution.py:466
  714.3 43.6 %collective-permute-start.58 = (bf16[2,2,256,2048]{3,2,1,0:T(8,128)(2,1)}, bf16[2,2,256,2048]{3,2,1,0:T(8,128)(2,1)}, u32[]{:S(2)}, u32[]{:S(2)}) collective-permute-start(bf16[2,2,256,2048]{3,2,1,0:T(8,128)(2,1)} %get-tuple-element.464), channel_id=1, source_target_pairs={{0,1},{1,0},{2,3},{3,2},{4,5},{5,4},{6,7},{7,6},{8,9},{9,8},{10,11... | collective-permute-start | bytes 12582920 | tf_op jit(solution)/shard_map/ppermute | solution.py:466
  714.3 43.6 %collective-permute-start.59 = (bf16[128,2048]{1,0:T(8,128)(2,1)S(1)}, bf16[128,2048]{1,0:T(8,128)(2,1)}, u32[]{:S(2)}, u32[]{:S(2)}) collective-permute-start(bf16[128,2048]{1,0:T(8,128)(2,1)S(1)} %get-tuple-element.465), channel_id=1, source_target_pairs={{0,4},{4,0},{8,12},{12,8},{16,20},{20,16},{24,28},{28,24},{1,5},{5... | collective-permute-start | bytes 1572872 | tf_op jit(solution)/shard_map/ppermute | solution.py:466
  758.0 305.8 %reduce-scatter.6.cloned.1.call-start = ((), (), s32[]{:S(2)}) async-start(), calls=%async_computation.5 | async-start | bytes 18874368 | tf_op jit(solution)/shard_map/reduce_scatter | solution.py:930
  779.7 54.3 %collective-permute-start.63 = (bf16[2,128,2048]{2,1,0:T(8,128)(2,1)}, bf16[2,128,2048]{2,1,0:T(8,128)(2,1)}, u32[]{:S(2)}, u32[]{:S(2)}) collective-permute-start(bf16[2,128,2048]{2,1,0:T(8,128)(2,1)} %fusion.70), channel_id=1, source_target_pairs={{0,2},{1,3},{2,0},{3,1},{4,6},{5,7},{6,4},{7,5},{8,10},{9,11},{10,... | collective-permute-start | bytes 3145736 | tf_op jit(solution)/shard_map/ppermute | solution.py:466
  780.0 54.0 %collective-permute-start.64 = (bf16[2,128,2048]{2,1,0:T(8,128)(2,1)}, bf16[2,128,2048]{2,1,0:T(8,128)(2,1)}, u32[]{:S(2)}, u32[]{:S(2)}) collective-permute-start(bf16[2,128,2048]{2,1,0:T(8,128)(2,1)} %get-tuple-element.493), channel_id=1, source_target_pairs={{0,4},{4,0},{8,12},{12,8},{16,20},{20,16},{24,28},{28,24},{1,5},{5... | collective-permute-start | bytes 3145736 | tf_op jit(solution)/shard_map/ppermute | solution.py:466
  780.5 53.4 %collective-permute-start.67 = (bf16[256,2048]{1,0:T(8,128)(2,1)}, bf16[256,2048]{1,0:T(8,128)(2,1)}, u32[]{:S(2)}, u32[]{:S(2)}) collective-permute-start(bf16[256,2048]{1,0:T(8,128)(2,1)} %add_convert_fusion.5), channel_id=1, source_target_pairs={{0,8},{4,12},{8,16},{12,20},{16,24},{20,28},{24,0},{28,4},{1,9},{5... | collective-permute-start | bytes 3145736 | tf_op jit(solution)/shard_map/ppermute | solution.py:483
  834.0 376.1 %reduce-scatter.8.cloned.1.call-start = ((), (), s32[]{:S(2)}) async-start(), calls=%async_computation.6 | async-start | bytes 5242880 | tf_op jit(solution)/shard_map/reduce_scatter | solution.py:635
  947.3 46.3 %collective-permute-start.74 = (bf16[512,256]{1,0:T(8,128)(2,1)}, bf16[512,256]{1,0:T(8,128)(2,1)}, u32[]{:S(2)}, u32[]{:S(2)}) collective-permute-start(bf16[512,256]{1,0:T(8,128)(2,1)} %bitcast.319), channel_id=1, source_target_pairs={{0,4},{4,0},{8,12},{12,8},{16,20},{20,16},{24,28},{28,24},{1,5},{5... | collective-permute-start | bytes 786440 | tf_op jit(solution)/shard_map/ppermute | solution.py:466
  948.5 45.2 %collective-permute-start.75 = (bf16[512,256]{1,0:T(8,128)(2,1)}, bf16[512,256]{1,0:T(8,128)(2,1)}, u32[]{:S(2)}, u32[]{:S(2)}) collective-permute-start(bf16[512,256]{1,0:T(8,128)(2,1)} %bitcast.318), channel_id=1, source_target_pairs={{0,4},{4,0},{8,12},{12,8},{16,20},{20,16},{24,28},{28,24},{1,5},{5... | collective-permute-start | bytes 786440 | tf_op jit(solution)/shard_map/ppermute | solution.py:466
  949.3 44.3 %collective-permute-start.76 = (bf16[512,256]{1,0:T(8,128)(2,1)}, bf16[512,256]{1,0:T(8,128)(2,1)}, u32[]{:S(2)}, u32[]{:S(2)}) collective-permute-start(bf16[512,256]{1,0:T(8,128)(2,1)} %bitcast.317), channel_id=1, source_target_pairs={{0,4},{4,0},{8,12},{12,8},{16,20},{20,16},{24,28},{28,24},{1,5},{5... | collective-permute-start | bytes 786440 | tf_op jit(solution)/shard_map/ppermute | solution.py:466
  1010.3 46.7 %collective-permute-start.81 = (bf16[256,2048]{1,0:T(8,128)(2,1)S(1)}, bf16[256,2048]{1,0:T(8,128)(2,1)S(1)}, u32[]{:S(2)}, u32[]{:S(2)}) collective-permute-start(bf16[256,2048]{1,0:T(8,128)(2,1)S(1)} %get-tuple-element.638), channel_id=1, source_target_pairs={{0,1},{1,0},{2,3},{3,2},{4,5},{5,4},{6,7},{7,6},{8,9},{9,8},{10,11... | collective-permute-start | bytes 3145736 | tf_op jit(solution)/shard_map/ppermute | solution.py:466
  1010.3 46.6 %collective-permute-start.80 = (bf16[256,2048]{1,0:T(8,128)(2,1)S(1)}, bf16[256,2048]{1,0:T(8,128)(2,1)S(1)}, u32[]{:S(2)}, u32[]{:S(2)}) collective-permute-start(bf16[256,2048]{1,0:T(8,128)(2,1)S(1)} %get-tuple-element.639), channel_id=1, source_target_pairs={{0,1},{1,0},{2,3},{3,2},{4,5},{5,4},{6,7},{7,6},{8,9},{9,8},{10,11... | collective-permute-start | bytes 3145736 | tf_op jit(solution)/shard_map/ppermute | solution.py:466
  1068.4 71.5 %collective-permute-start.84 = (bf16[256,1536]{1,0:T(8,128)(2,1)}, bf16[256,1536]{1,0:T(8,128)(2,1)S(1)}, u32[]{:S(2)}, u32[]{:S(2)}) collective-permute-start(bf16[256,1536]{1,0:T(8,128)(2,1)} %get-tuple-element.632), channel_id=1, source_target_pairs={{0,4},{4,0},{8,12},{12,8},{16,20},{20,16},{24,28},{28,24},{1,5},{5... | collective-permute-start | bytes 2359304 | tf_op jit(solution)/shard_map/ppermute | solution.py:466
  1069.6 70.3 %collective-permute-start.86 = (bf16[256,2048]{1,0:T(8,128)(2,1)S(1)}, bf16[256,2048]{1,0:T(8,128)(2,1)S(1)}, u32[]{:S(2)}, u32[]{:S(2)}) collective-permute-start(bf16[256,2048]{1,0:T(8,128)(2,1)S(1)} %fusion.26), channel_id=1, source_target_pairs={{0,2},{1,3},{2,0},{3,1},{4,6},{5,7},{6,4},{7,5},{8,10},{9,11},{10,... | collective-permute-start | bytes 3145736 | tf_op jit(solution)/shard_map/ppermute | solution.py:466
  1071.8 68.1 %collective-permute-start.85 = (bf16[256,1536]{1,0:T(8,128)(2,1)S(1)}, bf16[256,1536]{1,0:T(8,128)(2,1)S(1)}, u32[]{:S(2)}, u32[]{:S(2)}) collective-permute-start(bf16[256,1536]{1,0:T(8,128)(2,1)S(1)} %fusion.43), channel_id=1, source_target_pairs={{0,8},{4,12},{8,16},{12,20},{16,24},{20,28},{24,0},{28,4},{1,9},{5... | collective-permute-start | bytes 2359304 | tf_op jit(solution)/shard_map/ppermute | solution.py:483
  1073.3 46.6 %collective-permute-start.94 = (bf16[512,256]{1,0:T(8,128)(2,1)S(1)}, bf16[512,256]{1,0:T(8,128)(2,1)S(1)}, u32[]{:S(2)}, u32[]{:S(2)}) collective-permute-start(bf16[512,256]{1,0:T(8,128)(2,1)S(1)} %add_convert_fusion.41), channel_id=1, source_target_pairs={{0,8},{4,12},{8,16},{12,20},{16,24},{20,28},{24,0},{28,4},{1,9},{5... | collective-permute-start | bytes 786440 | tf_op jit(solution)/shard_map/ppermute | solution.py:483
  1075.3 113.6 %collective-permute-start.83 = (bf16[256,1536]{1,0:T(8,128)(2,1)S(1)}, bf16[256,1536]{1,0:T(8,128)(2,1)S(1)}, u32[]{:S(2)}, u32[]{:S(2)}) collective-permute-start(bf16[256,1536]{1,0:T(8,128)(2,1)S(1)} %copy-done.87), channel_id=1, source_target_pairs={{0,4},{4,0},{8,12},{12,8},{16,20},{20,16},{24,28},{28,24},{1,5},{5... | collective-permute-start | bytes 2359304 | tf_op jit(solution)/shard_map/ppermute | solution.py:466
  1141.4 47.6 %collective-permute-start.87 = (bf16[256,1536]{1,0:T(8,128)(2,1)S(1)}, bf16[256,1536]{1,0:T(8,128)(2,1)S(1)}, u32[]{:S(2)}, u32[]{:S(2)}) collective-permute-start(bf16[256,1536]{1,0:T(8,128)(2,1)S(1)} %add_convert_fusion.29), channel_id=1, source_target_pairs={{0,8},{4,12},{8,16},{12,20},{16,24},{20,28},{24,0},{28,4},{1,9},{5... | collective-permute-start | bytes 2359304 | tf_op jit(solution)/shard_map/ppermute | solution.py:483
  1150.1 57.3 %collective-permute-start.82 = (bf16[256,1536]{1,0:T(8,128)(2,1)S(1)}, bf16[256,1536]{1,0:T(8,128)(2,1)S(1)}, u32[]{:S(2)}, u32[]{:S(2)}) collective-permute-start(bf16[256,1536]{1,0:T(8,128)(2,1)S(1)} %copy-done.86), channel_id=1, source_target_pairs={{0,4},{4,0},{8,12},{12,8},{16,20},{20,16},{24,28},{28,24},{1,5},{5... | collective-permute-start | bytes 2359304 | tf_op jit(solution)/shard_map/ppermute | solution.py:466
  (203 other events, 3189.2 us)
Sparse Core Ops, SparseCore 0:
  131.4 246.4 all-gather.1
  758.1 160.4 reduce-scatter.3
  922.1 141.6 reduce-scatter.5
  1068.5 121.5 reduce-scatter.7

commit v12 on v11

--- a/solution.py
+++ b/solution.py
@@ -1096,6 +1096,8 @@
     for block_index in range(block_total):
         offset = block_index * block_rows
         query_block = query_low[offset : offset + block_rows]
+        if block_index:
+            query_block = fold_step(query_block)
         grad_block = grad_mixture[offset : offset + block_rows]
         scores = block_scores(query_block, key_low, masks[block_index], inv_root)
         prob_rows = jnp.exp(scores - lse_parts[block_index])
@@ -1124,6 +1126,7 @@
     grad_query_norm = rotate_back(jnp.concatenate(grad_query_parts, axis=0), cosine, sine_tab)
     grad_key_norm = rotate_back(grad_key_sum, cosine, sine_tab)
     grad_query_norm = fold_step(grad_query_norm)
+    grad_key_norm = fold_step(grad_key_norm)
     query_gain_part = jnp.sum(grad_query_norm * query_norm, axis=(0, 1))
     key_gain_part = jnp.sum(grad_key_norm * key_norm, axis=(0, 1))
     grad_query_pre = (

time: 1230 us -> 1210 us (0.984)
  waiting for transfers between devices: 360 us -> 329 us
  starting transfers between devices: 154 us -> 174 us
    ppermute x18, waiting for transfers between devices: 98.5 us -> 78.1 us  [next_plane(): lax.ppermute(values, DP, [(i, (i + 2) % count) for i in range(count)])]
    ppermute x78, starting transfers between devices: 71.4 us -> 91 us  [swapped(): return lax.ppermute(values, axis, [(i, i ^ bit) for i in range(count)])]
    unnamed x296 -> x264, local copies, waits for them, and re-layouts: 40.7 us -> 40.9 us
  transfers between devices with their start and end apart: 100 -> 100, of which waited for: 30 -> 33; matrix products, arithmetic and copies ran while one was open for 21% -> 21% of each run, Pallas kernels for 27% -> 28%
where the time goes in v12:
time: 1210 us
  Pallas kernels  379 us (31%)
  waiting for transfers between devices  329 us (27%)
  starting transfers between devices  174 us (14%)
  other arithmetic  134 us (11%)
  local copies, waits for them, and re-layouts  97.9 us (8%)
  matrix products  75.8 us (6%)
  between operations  16.7 us (1%)
    ppermute x78, waiting for transfers between devices, swapped(): return lax.ppermute(values, axis, [(i, i ^ bit) for i in range(count)])  251 us
    pallas_call x4, Pallas kernels, row_slots(): call(functools.partial(row_kernel, packs, steps, capacity), 2 * packs + s...  152 us
    ppermute x78, starting transfers between devices, swapped(): return lax.ppermute(values, axis, [(i, i ^ bit) for i in range(count)])  91 us
    ppermute x18, starting transfers between devices, next_plane(): lax.ppermute(values, DP, [(i, (i + 2) % count) for i in range(count)])  82.6 us
    pallas_call x4, Pallas kernels, cot_slots(): call(functools.partial(cot_kernel, packs, steps, capacity), packs + steps...  81.8 us
    ppermute x18, waiting for transfers between devices, next_plane(): lax.ppermute(values, DP, [(i, (i + 2) % count) for i in range(count)])  78.1 us
    pallas_call x4, Pallas kernels, mix_rows(): call(functools.partial(mix_kernel, packs, steps, capacity), packs + steps...  71.3 us
    convert_element_type x38, other arithmetic, added(): return (left.astype(jnp.float32) + right.astype(jnp.float32)).astype(kind)  65.2 us
  transfers between devices with their start and end apart: 100, of which 33 were waited for; matrix products, arithmetic and copies ran while one was open for 21% of the time, Pallas kernels for 28%

profile of v12, /device:TPU:0, one launch (start us, length us, event | category | flops | bytes accessed | tf_op | source)
XLA Modules:
  0.0 1205.7 jit_solution(1372006343096983006)
XLA Ops:
  21.8 13.7 %pad_maximum_fusion.both = bf16[8,2048,512]{2,1,0:T(8,128)(2,1)} fusion(bf16[8,2048,256]{2,1,0:T(8,128)(2,1)} %param.29, bf16[8,2048,256]{2,1,0:T(8,128)(2,1)} %param.28), kind=kLoop, calls=%fused_computation.4 | loop fusion | flops 33554432 | bytes 33554432 | tf_op jit(solution)/shard_map/concatenate | solution.py:657
  53.9 19.9 %collective-permute-done.10.refs_4_ = bf16[512,256]{1,0:T(8,128)(2,1)S(1)} collective-permute-done((bf16[512,256]{1,0:T(8,128)(2,1)S(1)}, bf16[512,256]{1,0:T(8,128)(2,1)S(1)}, u32[]{:S(2)}, u32[]{:S(2)}) %collective-permute-start.10) | collective-permute-done | bytes 262176 | tf_op jit(solution)/shard_map/ppermute | solution.py:483
  78.9 20.7 %collective-permute-done.17 = bf16[4,17,256]{2,0,1:T(4,128)(2,1)S(1)} collective-permute-done((bf16[4,17,256]{2,0,1:T(4,128)(2,1)S(1)}, bf16[4,17,256]{2,0,1:T(4,128)(2,1)S(1)}, u32[]{:S(2)}, u32[]{:S(2)}) %collective-permute-start.17) | collective-permute-done | bytes 34848 | tf_op jit(solution)/shard_map/ppermute | solution.py:466
  107.7 17.3 %collective-permute-done.19.refs_7_ = bf16[512,256]{1,0:T(8,128)(2,1)} collective-permute-done((bf16[512,256]{1,0:T(8,128)(2,1)}, bf16[512,256]{1,0:T(8,128)(2,1)}, u32[]{:S(2)}, u32[]{:S(2)}) %collective-permute-start.19) | collective-permute-done | bytes 262176 | tf_op jit(solution)/shard_map/ppermute | solution.py:466
  207.2 24.9 %collective-permute-done.23 = bf16[256,2048]{1,0:T(8,128)(2,1)S(1)} collective-permute-done((bf16[256,2048]{1,0:T(8,128)(2,1)S(1)}, bf16[256,2048]{1,0:T(8,128)(2,1)S(1)}, u32[]{:S(2)}, u32[]{:S(2)}) %collective-permute-start.23) | collective-permute-done | bytes 1048608 | tf_op jit(solution)/shard_map/ppermute | solution.py:466
  238.6 22.2 %collective-permute-done.26 = bf16[128,2048]{1,0:T(8,128)(2,1)S(1)} collective-permute-done((bf16[128,2048]{1,0:T(8,128)(2,1)S(1)}, bf16[128,2048]{1,0:T(8,128)(2,1)S(1)}, u32[]{:S(2)}, u32[]{:S(2)}) %collective-permute-start.26) | collective-permute-done | bytes 524320 | tf_op jit(solution)/shard_map/ppermute | solution.py:466
  261.5 20.1 %collective-permute-done.27 = bf16[256,2048]{1,0:T(8,128)(2,1)S(1)} collective-permute-done((bf16[256,2048]{1,0:T(8,128)(2,1)S(1)}, bf16[256,2048]{1,0:T(8,128)(2,1)S(1)}, u32[]{:S(2)}, u32[]{:S(2)}) %collective-permute-start.27) | collective-permute-done | bytes 1048608 | tf_op jit(solution)/shard_map/ppermute | solution.py:483
  281.8 23.1 %collective-permute-start.32 = (bf16[256,2048]{1,0:T(8,128)(2,1)S(1)}, bf16[256,2048]{1,0:T(8,128)(2,1)}, u32[]{:S(2)}, u32[]{:S(2)}) collective-permute-start(bf16[256,2048]{1,0:T(8,128)(2,1)S(1)} %collective-permute-done.27), channel_id=1, source_target_pairs={{0,8},{4,12},{8,16},{12,20},{16,24},{20,28},{24,0},{28,4},{1,9},{5... | collective-permute-start | bytes 3145736 | tf_op jit(solution)/shard_map/ppermute | solution.py:483
  311.5 32.0 %collective-permute-done.31 = bf16[128,2048]{1,0:T(8,128)(2,1)S(1)} collective-permute-done((bf16[128,2048]{1,0:T(8,128)(2,1)S(1)}, bf16[128,2048]{1,0:T(8,128)(2,1)S(1)}, u32[]{:S(2)}, u32[]{:S(2)}) %collective-permute-start.31) | collective-permute-done | bytes 524320 | tf_op jit(solution)/shard_map/ppermute | solution.py:466
  354.7 23.1 %collective-permute-start.37 = (bf16[256,2048]{1,0:T(8,128)(2,1)}, bf16[256,2048]{1,0:T(8,128)(2,1)}, u32[]{:S(2)}, u32[]{:S(2)}) collective-permute-start(bf16[256,2048]{1,0:T(8,128)(2,1)} %collective-permute-done.32), channel_id=1, source_target_pairs={{0,8},{4,12},{8,16},{12,20},{16,24},{20,28},{24,0},{28,4},{1,9},{5... | collective-permute-start | bytes 3145736 | tf_op jit(solution)/shard_map/ppermute | solution.py:483
  383.4 20.4 %shard_map.258 = (bf16[8,256,2048]{2,1,0:T(8,128)(2,1)}, f32[8,256,256]{2,1,0:T(8,128)}) custom-call(s32[2]{0:T(128)} %get-tuple-element.372.table, bf16[8,8,1024]{2,1,0:T(8,128)(2,1)} %copy-done.46, bf16[8,8,1024]{2,1,0:T(8,128)(2,1)} %copy-done.27, bf16[8,1024,2048]{2,1,0:T(8,128)(2,1)} %bitcast.323, bf16[8,256,2048]{2,1,0:T(8,128)(2,1)} %down.15), custom_call_target="tpu_custom_call" | custom-call | flops 10737418240 | bytes 21474836 | tf_op jit(solution)/shard_map/pallas_call | solution.py:360
  428.7 20.4 %shard_map.259 = (bf16[8,256,2048]{2,1,0:T(8,128)(2,1)}, f32[8,256,256]{2,1,0:T(8,128)}) custom-call(s32[2]{0:T(128)} %get-tuple-element.388.table, bf16[8,8,1024]{2,1,0:T(8,128)(2,1)} %copy-done.46, bf16[8,8,1024]{2,1,0:T(8,128)(2,1)} %copy-done.27, bf16[8,1024,2048]{2,1,0:T(8,128)(2,1)} %bitcast.324, bf16[8,256,2048]{2,1,0:T(8,128)(2,1)} %down.15), custom_call_target="tpu_custom_call" | custom-call | flops 10737418240 | bytes 21474836 | tf_op jit(solution)/shard_map/pallas_call | solution.py:360
  459.5 38.1 %shard_map.260 = (bf16[8,256,2048]{2,1,0:T(8,128)(2,1)}, bf16[8,256,256]{2,1,0:T(8,128)(2,1)}, bf16[8,256,512]{2,1,0:T(8,128)(2,1)}, bf16[2,2,256,2048]{3,2,1,0:T(8,128)(2,1)}, bf16[2,2,256,2048]{3,2,1,0:T(8,128)(2,1)}) custom-call(bf16[2,8,1024]{2,1,0:T(8,128)(2,1)} %bitcast.385, bf16[8,128,2048]{2,1,0:T(8,128)(2,1)} %constant_dynamic-update-slice_fusion.7.own, ...), custom_call_target="tpu_custom_call" | custom-call | flops 25769803776 | bytes 51539608 | tf_op jit(solution)/shard_map/pallas_call | solution.py:393
  513.3 20.5 %shard_map.261 = (bf16[8,256,2048]{2,1,0:T(8,128)(2,1)}, f32[8,256,256]{2,1,0:T(8,128)}) custom-call(s32[2]{0:T(128)} %get-tuple-element.398.table, bf16[8,8,1024]{2,1,0:T(8,128)(2,1)} %copy-done.46, bf16[8,8,1024]{2,1,0:T(8,128)(2,1)} %copy-done.27, bf16[8,1024,2048]{2,1,0:T(8,128)(2,1)} %bitcast.325, bf16[8,256,2048]{2,1,0:T(8,128)(2,1)} %down.15), custom_call_target="tpu_custom_call" | custom-call | flops 10737418240 | bytes 21474836 | tf_op jit(solution)/shard_map/pallas_call | solution.py:360
  533.8 20.5 %shard_map.262 = (bf16[8,256,2048]{2,1,0:T(8,128)(2,1)}, f32[8,256,256]{2,1,0:T(8,128)}) custom-call(s32[2]{0:T(128)} %get-tuple-element.413.table, bf16[8,8,1024]{2,1,0:T(8,128)(2,1)} %copy-done.46, bf16[8,8,1024]{2,1,0:T(8,128)(2,1)} %copy-done.27, bf16[8,1024,2048]{2,1,0:T(8,128)(2,1)} %bitcast.326, bf16[8,256,2048]{2,1,0:T(8,128)(2,1)} %down.15), custom_call_target="tpu_custom_call" | custom-call | flops 10737418240 | bytes 21474836 | tf_op jit(solution)/shard_map/pallas_call | solution.py:360
  568.6 38.0 %shard_map.263 = (bf16[8,256,2048]{2,1,0:T(8,128)(2,1)}, bf16[8,256,256]{2,1,0:T(8,128)(2,1)}, bf16[8,256,512]{2,1,0:T(8,128)(2,1)}, bf16[2,2,256,2048]{3,2,1,0:T(8,128)(2,1)}, bf16[2,2,256,2048]{3,2,1,0:T(8,128)(2,1)}) custom-call(bf16[2,8,1024]{2,1,0:T(8,128)(2,1)} %bitcast.384, bf16[8,128,2048]{2,1,0:T(8,128)(2,1)} %constant_dynamic-update-slice_fusion.11.own, ...), custom_call_target="tpu_custom_call" | custom-call | flops 25769803776 | bytes 51539608 | tf_op jit(solution)/shard_map/pallas_call | solution.py:393
  612.2 37.7 %shard_map.264 = (bf16[8,256,2048]{2,1,0:T(8,128)(2,1)}, bf16[8,256,256]{2,1,0:T(8,128)(2,1)}, bf16[8,256,512]{2,1,0:T(8,128)(2,1)}, bf16[2,2,256,2048]{3,2,1,0:T(8,128)(2,1)}, bf16[2,2,256,2048]{3,2,1,0:T(8,128)(2,1)}) custom-call(bf16[2,8,1024]{2,1,0:T(8,128)(2,1)} %bitcast.383, bf16[8,128,2048]{2,1,0:T(8,128)(2,1)} %constant_dynamic-update-slice_fusion.15.own, ...), custom_call_target="tpu_custom_call" | custom-call | flops 25769803776 | bytes 51539608 | tf_op jit(solution)/shard_map/pallas_call | solution.py:393
  664.0 38.2 %shard_map.265 = (bf16[8,256,2048]{2,1,0:T(8,128)(2,1)}, bf16[8,256,256]{2,1,0:T(8,128)(2,1)}, bf16[8,256,512]{2,1,0:T(8,128)(2,1)}, bf16[2,2,256,2048]{3,2,1,0:T(8,128)(2,1)}, bf16[2,2,256,2048]{3,2,1,0:T(8,128)(2,1)}) custom-call(bf16[2,8,1024]{2,1,0:T(8,128)(2,1)} %bitcast.382, bf16[8,128,2048]{2,1,0:T(8,128)(2,1)} %constant_dynamic-update-slice_fusion.3.own, ...), custom_call_target="tpu_custom_call" | custom-call | flops 25769803776 | bytes 51539608 | tf_op jit(solution)/shard_map/pallas_call | solution.py:393
  722.9 17.7 %shard_map.266.refs_0_ = bf16[2,2,1024,2048]{3,2,1,0:T(8,128)(2,1)} custom-call(s32[2]{0:T(128)} %get-tuple-element.481.table, bf16[2,8,1024]{2,1,0:T(8,128)(2,1)} %get-tuple-element.482.places, bf16[2,8,1024]{2,1,0:T(8,128)(2,1)} %get-tuple-element.483.gates, bf16[32,256,256]{2,1,0:T(8,128)(2,1)} %constant_dynamic-update-slice_fusion.19.hidden, ...), custom_call_target="tpu_custom_call" | custom-call | flops 10737418240 | bytes 21474836 | tf_op jit(solution)/shard_map/pallas_call | solution.py:420
  740.6 17.6 %shard_map.267 = bf16[2,2,1024,2048]{3,2,1,0:T(8,128)(2,1)} custom-call(s32[2]{0:T(128)} %get-tuple-element.474.table, bf16[2,8,1024]{2,1,0:T(8,128)(2,1)} %get-tuple-element.475.places, bf16[2,8,1024]{2,1,0:T(8,128)(2,1)} %get-tuple-element.476.gates, ...), custom_call_target="tpu_custom_call", output_to_operand_aliasing={{}: (5, {})} | custom-call | flops 10737418240 | bytes 21474836 | tf_op jit(solution)/shard_map/pallas_call | solution.py:420
  781.1 18.2 %shard_map.268.refs_0_ = bf16[2,2,1024,2048]{3,2,1,0:T(8,128)(2,1)} custom-call(s32[2]{0:T(128)} %get-tuple-element.504.table, bf16[2,8,1024]{2,1,0:T(8,128)(2,1)} %get-tuple-element.505.places, bf16[2,8,1024]{2,1,0:T(8,128)(2,1)} %get-tuple-element.506.gates, bf16[32,256,256]{2,1,0:T(8,128)(2,1)} %constant_dynamic-update-slice_fusion.19.hidden, ...), custom_call_target="tpu_custom_call" | custom-call | flops 10737418240 | bytes 21474836 | tf_op jit(solution)/shard_map/pallas_call | solution.py:420
  799.3 17.8 %shard_map.269 = bf16[2,2,1024,2048]{3,2,1,0:T(8,128)(2,1)} custom-call(s32[2]{0:T(128)} %get-tuple-element.501.table, bf16[2,8,1024]{2,1,0:T(8,128)(2,1)} %get-tuple-element.502.places, bf16[2,8,1024]{2,1,0:T(8,128)(2,1)} %get-tuple-element.503.gates, ...), custom_call_target="tpu_custom_call", output_to_operand_aliasing={{}: (5, {})} | custom-call | flops 10737418240 | bytes 21474836 | tf_op jit(solution)/shard_map/pallas_call | solution.py:420
  817.1 14.1 %collective-permute-done.63 = bf16[2,128,2048]{2,1,0:T(8,128)(2,1)} collective-permute-done((bf16[2,128,2048]{2,1,0:T(8,128)(2,1)}, bf16[2,128,2048]{2,1,0:T(8,128)(2,1)}, u32[]{:S(2)}, u32[]{:S(2)}) %collective-permute-start.63) | collective-permute-done | bytes 1048608 | tf_op jit(solution)/shard_map/ppermute | solution.py:466
  844.6 13.1 %shard_map.270 = (f32[8,2048,256]{2,1,0:T(8,128)}, f32[8,2048,256]{2,1,0:T(8,128)}, f32[8,256,2048]{2,1,0:T(8,128)}) custom-call(bf16[8,256,2048]{2,1,0:T(8,128)(2,1)} %get-tuple-element.563.refs_0_, bf16[8,256,2048]{2,1,0:T(8,128)(2,1)} %get-tuple-element.564.refs_1_, bf16[8,256,2048]{2,1,0:T(8,128)(2,1)} %get-tuple-element.565.refs_2_, ...), custom_call_target="tpu_custom_call" | custom-call | flops 6442450944 | bytes 12884901 | tf_op jit(solution)/shard_map/pallas_call | solution.py:451
  857.6 13.2 %shard_map.271 = (f32[8,2048,256]{2,1,0:T(8,128)}, f32[8,2048,256]{2,1,0:T(8,128)}, f32[8,256,2048]{2,1,0:T(8,128)}) custom-call(bf16[8,256,2048]{2,1,0:T(8,128)(2,1)} %get-tuple-element.563.refs_0_, bf16[8,256,2048]{2,1,0:T(8,128)(2,1)} %get-tuple-element.564.refs_1_, ...), custom_call_target="tpu_custom_call", output_to_operand_aliasing={{0}: (16, {}), {1}: (17, {}), {2}: (18, {})} | custom-call | flops 6442450944 | bytes 12884901 | tf_op jit(solution)/shard_map/pallas_call | solution.py:451
  876.3 13.4 %shard_map.272 = (f32[8,2048,256]{2,1,0:T(8,128)}, f32[8,2048,256]{2,1,0:T(8,128)}, f32[8,256,2048]{2,1,0:T(8,128)}) custom-call(bf16[8,256,2048]{2,1,0:T(8,128)(2,1)} %get-tuple-element.563.refs_0_, bf16[8,256,2048]{2,1,0:T(8,128)(2,1)} %get-tuple-element.564.refs_1_, ...), custom_call_target="tpu_custom_call", output_to_operand_aliasing={{0}: (16, {}), {1}: (17, {}), {2}: (18, {})} | custom-call | flops 6442450944 | bytes 12884901 | tf_op jit(solution)/shard_map/pallas_call | solution.py:451
  889.8 13.5 %shard_map.273 = (f32[8,2048,256]{2,1,0:T(8,128)}, f32[8,2048,256]{2,1,0:T(8,128)}, f32[8,256,2048]{2,1,0:T(8,128)}) custom-call(bf16[8,256,2048]{2,1,0:T(8,128)(2,1)} %get-tuple-element.563.refs_0_, bf16[8,256,2048]{2,1,0:T(8,128)(2,1)} %get-tuple-element.564.refs_1_, ...), custom_call_target="tpu_custom_call", output_to_operand_aliasing={{0}: (16, {}), {1}: (17, {}), {2}: (18, {})} | custom-call | flops 6442450944 | bytes 12884901 | tf_op jit(solution)/shard_map/pallas_call | solution.py:451
  1045.5 16.6 %collective-permute-done.81 = bf16[256,1536]{1,0:T(8,128)(2,1)S(1)} collective-permute-done((bf16[256,1536]{1,0:T(8,128)(2,1)S(1)}, bf16[256,1536]{1,0:T(8,128)(2,1)S(1)}, u32[]{:S(2)}, u32[]{:S(2)}) %collective-permute-start.81) | collective-permute-done | bytes 786464 | tf_op jit(solution)/shard_map/ppermute | solution.py:466
  1073.7 14.3 %collective-permute-done.86 = bf16[256,1536]{1,0:T(8,128)(2,1)S(1)} collective-permute-done((bf16[256,1536]{1,0:T(8,128)(2,1)}, bf16[256,1536]{1,0:T(8,128)(2,1)S(1)}, u32[]{:S(2)}, u32[]{:S(2)}) %collective-permute-start.86) | collective-permute-done | bytes 786464 | tf_op jit(solution)/shard_map/ppermute | solution.py:466
  1088.0 18.0 %collective-permute-done.87 = bf16[256,1536]{1,0:T(8,128)(2,1)S(1)} collective-permute-done((bf16[256,1536]{1,0:T(8,128)(2,1)S(1)}, bf16[256,1536]{1,0:T(8,128)(2,1)S(1)}, u32[]{:S(2)}, u32[]{:S(2)}) %collective-permute-start.87) | collective-permute-done | bytes 786464 | tf_op jit(solution)/shard_map/ppermute | solution.py:483
  1130.9 13.0 %collective-permute-done.93 = f32[4352]{0:T(1024)S(1)} collective-permute-done((f32[4352]{0:T(1024)S(1)}, f32[4352]{0:T(1024)S(1)}, u32[]{:S(2)}, u32[]{:S(2)}) %collective-permute-start.93) | collective-permute-done | bytes 17440 | tf_op jit(solution)/shard_map/ppermute | solution.py:466
  1149.7 24.3 %collective-permute-start.95 = (f32[4352]{0:T(1024)S(1)}, f32[4352]{0:T(1024)S(1)}, u32[]{:S(2)}, u32[]{:S(2)}) collective-permute-start(f32[4352]{0:T(1024)S(1)} %add.752), channel_id=1, source_target_pairs={{0,16},{4,20},{8,24},{12,28},{16,0},{20,4},{24,8},{28,12},{1,17},{... | collective-permute-start | bytes 52232 | tf_op jit(solution)/shard_map/ppermute | solution.py:466
  (658 shorter events, 513.3 us)
Async XLA Ops:
  7.2 376.2 %all-gather.2.cloned.1.call-start = ((), (), s32[]{:S(2)}) async-start(), calls=%async_computation.3 | async-start | bytes 34603008 | tf_op jit(solution)/shard_map/all_gather | solution.py:1006
  131.2 931.4 %reduce-scatter.4.cloned.1.call-start = ((), (), s32[]{:S(2)}) async-start(), calls=%async_computation.4 | async-start | bytes 18874368 | tf_op jit(solution)/shard_map/reduce_scatter | solution.py:930
  143.5 52.0 %collective-permute-start.24 = (bf16[16,17,256]{2,0,1:T(8,128)(2,1)S(1)}, bf16[16,17,256]{2,0,1:T(8,128)(2,1)S(1)}, u32[]{:S(2)}, u32[]{:S(2)}) collective-permute-start(bf16[16,17,256]{2,0,1:T(8,128)(2,1)S(1)} %concatenate.120), channel_id=1, source_target_pairs={{0,16},{4,20},{8,24},{12,28},{16,0},{20,4},{24,8},{28,12},{1,17},{... | collective-permute-start | bytes 417800 | tf_op jit(solution)/shard_map/ppermute | solution.py:466
  234.6 47.0 %collective-permute-start.27 = (bf16[256,2048]{1,0:T(8,128)(2,1)S(1)}, bf16[256,2048]{1,0:T(8,128)(2,1)S(1)}, u32[]{:S(2)}, u32[]{:S(2)}) collective-permute-start(bf16[256,2048]{1,0:T(8,128)(2,1)S(1)} %multiply_convert_fusion.4), channel_id=1, source_target_pairs={{0,8},{4,12},{8,16},{12,20},{16,24},{20,28},{24,0},{28,4},{1,9},{5... | collective-permute-start | bytes 3145736 | tf_op jit(solution)/shard_map/ppermute | solution.py:483
  281.8 68.1 %collective-permute-start.32 = (bf16[256,2048]{1,0:T(8,128)(2,1)S(1)}, bf16[256,2048]{1,0:T(8,128)(2,1)}, u32[]{:S(2)}, u32[]{:S(2)}) collective-permute-start(bf16[256,2048]{1,0:T(8,128)(2,1)S(1)} %collective-permute-done.27), channel_id=1, source_target_pairs={{0,8},{4,12},{8,16},{12,20},{16,24},{20,28},{24,0},{28,4},{1,9},{5... | collective-permute-start | bytes 3145736 | tf_op jit(solution)/shard_map/ppermute | solution.py:483
  305.0 44.9 %collective-permute-start.28 = (bf16[2,128,2048]{2,1,0:T(8,128)(2,1)S(1)}, bf16[2,128,2048]{2,1,0:T(8,128)(2,1)S(1)}, u32[]{:S(2)}, u32[]{:S(2)}) collective-permute-start(bf16[2,128,2048]{2,1,0:T(8,128)(2,1)S(1)} %pad_maximum_fusion.8), channel_id=1, source_target_pairs={{0,2},{1,3},{2,0},{3,1},{4,6},{5,7},{6,4},{7,5},{8,10},{9,11},{10,... | collective-permute-start | bytes 3145736 | tf_op jit(solution)/shard_map/ppermute | solution.py:466
  305.0 44.9 %collective-permute-start.29 = (bf16[2,128,2048]{2,1,0:T(8,128)(2,1)S(1)}, bf16[2,128,2048]{2,1,0:T(8,128)(2,1)S(1)}, u32[]{:S(2)}, u32[]{:S(2)}) collective-permute-start(bf16[2,128,2048]{2,1,0:T(8,128)(2,1)S(1)} %pad_maximum_fusion.9), channel_id=1, source_target_pairs={{0,4},{4,0},{8,12},{12,8},{16,20},{20,16},{24,28},{28,24},{1,5},{5... | collective-permute-start | bytes 3145736 | tf_op jit(solution)/shard_map/ppermute | solution.py:466
  352.0 63.3 %collective-permute-start.38 = (bf16[8,128,2048]{2,1,0:T(8,128)(2,1)}, bf16[8,128,2048]{2,1,0:T(8,128)(2,1)}, u32[]{:S(2)}, u32[]{:S(2)}) collective-permute-start(bf16[8,128,2048]{2,1,0:T(8,128)(2,1)} %constant_dynamic-update-slice_fusion.3.own), channel_id=1, source_target_pairs={{0,1},{1,0},{2,3},{3,2},{4,5},{5,4},{6,7},{7,6},{8,9},{9,8},{10,11... | collective-permute-start | bytes 12582920 | tf_op jit(solution)/shard_map/ppermute | solution.py:466
  354.7 60.5 %collective-permute-start.37 = (bf16[256,2048]{1,0:T(8,128)(2,1)}, bf16[256,2048]{1,0:T(8,128)(2,1)}, u32[]{:S(2)}, u32[]{:S(2)}) collective-permute-start(bf16[256,2048]{1,0:T(8,128)(2,1)} %collective-permute-done.32), channel_id=1, source_target_pairs={{0,8},{4,12},{8,16},{12,20},{16,24},{20,28},{24,0},{28,4},{1,9},{5... | collective-permute-start | bytes 3145736 | tf_op jit(solution)/shard_map/ppermute | solution.py:483
  497.7 56.7 %collective-permute-start.44 = (bf16[2,2,256,2048]{3,2,1,0:T(8,128)(2,1)}, bf16[2,2,256,2048]{3,2,1,0:T(8,128)(2,1)}, u32[]{:S(2)}, u32[]{:S(2)}) collective-permute-start(bf16[2,2,256,2048]{3,2,1,0:T(8,128)(2,1)} %get-tuple-element.397), channel_id=1, source_target_pairs={{0,1},{1,0},{2,3},{3,2},{4,5},{5,4},{6,7},{7,6},{8,9},{9,8},{10,11... | collective-permute-start | bytes 12582920 | tf_op jit(solution)/shard_map/ppermute | solution.py:466
  503.3 59.4 %collective-permute-start.49 = (bf16[8,128,2048]{2,1,0:T(8,128)(2,1)}, bf16[8,128,2048]{2,1,0:T(8,128)(2,1)}, u32[]{:S(2)}, u32[]{:S(2)}) collective-permute-start(bf16[8,128,2048]{2,1,0:T(8,128)(2,1)} %constant_dynamic-update-slice_fusion.11.own), channel_id=1, source_target_pairs={{0,1},{1,0},{2,3},{3,2},{4,5},{5,4},{6,7},{7,6},{8,9},{9,8},{10,11... | collective-permute-start | bytes 12582920 | tf_op jit(solution)/shard_map/ppermute | solution.py:466
  507.1 55.6 %collective-permute-start.47 = (bf16[2,128,2048]{2,1,0:T(8,128)(2,1)S(1)}, bf16[2,128,2048]{2,1,0:T(8,128)(2,1)}, u32[]{:S(2)}, u32[]{:S(2)}) collective-permute-start(bf16[2,128,2048]{2,1,0:T(8,128)(2,1)S(1)} %pad_maximum_fusion.14), channel_id=1, source_target_pairs={{0,2},{1,3},{2,0},{3,1},{4,6},{5,7},{6,4},{7,5},{8,10},{9,11},{10,... | collective-permute-start | bytes 3145736 | tf_op jit(solution)/shard_map/ppermute | solution.py:466
  508.4 54.3 %collective-permute-start.48 = (bf16[2,128,2048]{2,1,0:T(8,128)(2,1)}, bf16[2,128,2048]{2,1,0:T(8,128)(2,1)}, u32[]{:S(2)}, u32[]{:S(2)}) collective-permute-start(bf16[2,128,2048]{2,1,0:T(8,128)(2,1)} %pad_maximum_fusion.15), channel_id=1, source_target_pairs={{0,4},{4,0},{8,12},{12,8},{16,20},{20,16},{24,28},{28,24},{1,5},{5... | collective-permute-start | bytes 3145736 | tf_op jit(solution)/shard_map/ppermute | solution.py:466
  562.7 44.0 %collective-permute-start.45 = (bf16[2,128,2048]{2,1,0:T(8,128)(2,1)}, bf16[2,128,2048]{2,1,0:T(8,128)(2,1)S(1)}, u32[]{:S(2)}, u32[]{:S(2)}) collective-permute-start(bf16[2,128,2048]{2,1,0:T(8,128)(2,1)} %fusion.62), channel_id=1, source_target_pairs={{0,2},{1,3},{2,0},{3,1},{4,6},{5,7},{6,4},{7,5},{8,10},{9,11},{10,... | collective-permute-start | bytes 3145736 | tf_op jit(solution)/shard_map/ppermute | solution.py:466
  563.4 43.3 %collective-permute-start.46 = (bf16[2,128,2048]{2,1,0:T(8,128)(2,1)}, bf16[2,128,2048]{2,1,0:T(8,128)(2,1)}, u32[]{:S(2)}, u32[]{:S(2)}) collective-permute-start(bf16[2,128,2048]{2,1,0:T(8,128)(2,1)} %get-tuple-element.404), channel_id=1, source_target_pairs={{0,4},{4,0},{8,12},{12,8},{16,20},{20,16},{24,28},{28,24},{1,5},{5... | collective-permute-start | bytes 3145736 | tf_op jit(solution)/shard_map/ppermute | solution.py:466
  568.6 43.6 %collective-permute-start.53 = (bf16[8,128,2048]{2,1,0:T(8,128)(2,1)}, bf16[8,128,2048]{2,1,0:T(8,128)(2,1)}, u32[]{:S(2)}, u32[]{:S(2)}) collective-permute-start(bf16[8,128,2048]{2,1,0:T(8,128)(2,1)} %constant_dynamic-update-slice_fusion.15.own), channel_id=1, source_target_pairs={{0,1},{1,0},{2,3},{3,2},{4,5},{5,4},{6,7},{7,6},{8,9},{9,8},{10,11... | collective-permute-start | bytes 12582920 | tf_op jit(solution)/shard_map/ppermute | solution.py:466
  608.9 41.1 %collective-permute-start.52 = (bf16[2,2,256,2048]{3,2,1,0:T(8,128)(2,1)}, bf16[2,2,256,2048]{3,2,1,0:T(8,128)(2,1)}, u32[]{:S(2)}, u32[]{:S(2)}) collective-permute-start(bf16[2,2,256,2048]{3,2,1,0:T(8,128)(2,1)} %get-tuple-element.431), channel_id=1, source_target_pairs={{0,1},{1,0},{2,3},{3,2},{4,5},{5,4},{6,7},{7,6},{8,9},{9,8},{10,11... | collective-permute-start | bytes 12582920 | tf_op jit(solution)/shard_map/ppermute | solution.py:466
  660.1 42.1 %collective-permute-start.56 = (bf16[2,2,256,2048]{3,2,1,0:T(8,128)(2,1)}, bf16[2,2,256,2048]{3,2,1,0:T(8,128)(2,1)}, u32[]{:S(2)}, u32[]{:S(2)}) collective-permute-start(bf16[2,2,256,2048]{3,2,1,0:T(8,128)(2,1)} %get-tuple-element.450), channel_id=1, source_target_pairs={{0,1},{1,0},{2,3},{3,2},{4,5},{5,4},{6,7},{7,6},{8,9},{9,8},{10,11... | collective-permute-start | bytes 12582920 | tf_op jit(solution)/shard_map/ppermute | solution.py:466
  660.1 42.0 %collective-permute-start.54 = (bf16[2,128,2048]{2,1,0:T(8,128)(2,1)}, bf16[2,128,2048]{2,1,0:T(8,128)(2,1)}, u32[]{:S(2)}, u32[]{:S(2)}) collective-permute-start(bf16[2,128,2048]{2,1,0:T(8,128)(2,1)} %fusion.66), channel_id=1, source_target_pairs={{0,2},{1,3},{2,0},{3,1},{4,6},{5,7},{6,4},{7,5},{8,10},{9,11},{10,... | collective-permute-start | bytes 3145736 | tf_op jit(solution)/shard_map/ppermute | solution.py:466
  660.8 41.3 %collective-permute-start.55 = (bf16[2,128,2048]{2,1,0:T(8,128)(2,1)}, bf16[2,128,2048]{2,1,0:T(8,128)(2,1)S(1)}, u32[]{:S(2)}, u32[]{:S(2)}) collective-permute-start(bf16[2,128,2048]{2,1,0:T(8,128)(2,1)} %get-tuple-element.449), channel_id=1, source_target_pairs={{0,4},{4,0},{8,12},{12,8},{16,20},{20,16},{24,28},{28,24},{1,5},{5... | collective-permute-start | bytes 3145736 | tf_op jit(solution)/shard_map/ppermute | solution.py:466
  714.7 43.6 %collective-permute-start.58 = (bf16[2,2,256,2048]{3,2,1,0:T(8,128)(2,1)}, bf16[2,2,256,2048]{3,2,1,0:T(8,128)(2,1)}, u32[]{:S(2)}, u32[]{:S(2)}) collective-permute-start(bf16[2,2,256,2048]{3,2,1,0:T(8,128)(2,1)} %get-tuple-element.468), channel_id=1, source_target_pairs={{0,1},{1,0},{2,3},{3,2},{4,5},{5,4},{6,7},{7,6},{8,9},{9,8},{10,11... | collective-permute-start | bytes 12582920 | tf_op jit(solution)/shard_map/ppermute | solution.py:466
  714.7 43.5 %collective-permute-start.59 = (bf16[128,2048]{1,0:T(8,128)(2,1)S(1)}, bf16[128,2048]{1,0:T(8,128)(2,1)}, u32[]{:S(2)}, u32[]{:S(2)}) collective-permute-start(bf16[128,2048]{1,0:T(8,128)(2,1)S(1)} %get-tuple-element.469), channel_id=1, source_target_pairs={{0,4},{4,0},{8,12},{12,8},{16,20},{20,16},{24,28},{28,24},{1,5},{5... | collective-permute-start | bytes 1572872 | tf_op jit(solution)/shard_map/ppermute | solution.py:466
  716.2 42.1 %collective-permute-start.60 = (bf16[128,2048]{1,0:T(8,128)(2,1)}, bf16[128,2048]{1,0:T(8,128)(2,1)}, u32[]{:S(2)}, u32[]{:S(2)}) collective-permute-start(bf16[128,2048]{1,0:T(8,128)(2,1)} %get-tuple-element.470), channel_id=1, source_target_pairs={{0,2},{1,3},{2,0},{3,1},{4,6},{5,7},{6,4},{7,5},{8,10},{9,11},{10,... | collective-permute-start | bytes 1572872 | tf_op jit(solution)/shard_map/ppermute | solution.py:466
  758.3 304.3 %reduce-scatter.6.cloned.1.call-start = ((), (), s32[]{:S(2)}) async-start(), calls=%async_computation.5 | async-start | bytes 18874368 | tf_op jit(solution)/shard_map/reduce_scatter | solution.py:930
  776.0 41.1 %collective-permute-start.65 = (bf16[128,2048]{1,0:T(8,128)(2,1)S(1)}, bf16[128,2048]{1,0:T(8,128)(2,1)}, u32[]{:S(2)}, u32[]{:S(2)}) collective-permute-start(bf16[128,2048]{1,0:T(8,128)(2,1)S(1)} %get-tuple-element.498), channel_id=1, source_target_pairs={{0,4},{4,0},{8,12},{12,8},{16,20},{20,16},{24,28},{28,24},{1,5},{5... | collective-permute-start | bytes 1572872 | tf_op jit(solution)/shard_map/ppermute | solution.py:466
  778.7 52.4 %collective-permute-start.63 = (bf16[2,128,2048]{2,1,0:T(8,128)(2,1)}, bf16[2,128,2048]{2,1,0:T(8,128)(2,1)}, u32[]{:S(2)}, u32[]{:S(2)}) collective-permute-start(bf16[2,128,2048]{2,1,0:T(8,128)(2,1)} %fusion.74), channel_id=1, source_target_pairs={{0,2},{1,3},{2,0},{3,1},{4,6},{5,7},{6,4},{7,5},{8,10},{9,11},{10,... | collective-permute-start | bytes 3145736 | tf_op jit(solution)/shard_map/ppermute | solution.py:466
  779.4 51.8 %collective-permute-start.64 = (bf16[2,128,2048]{2,1,0:T(8,128)(2,1)}, bf16[2,128,2048]{2,1,0:T(8,128)(2,1)}, u32[]{:S(2)}, u32[]{:S(2)}) collective-permute-start(bf16[2,128,2048]{2,1,0:T(8,128)(2,1)} %get-tuple-element.497), channel_id=1, source_target_pairs={{0,4},{4,0},{8,12},{12,8},{16,20},{20,16},{24,28},{28,24},{1,5},{5... | collective-permute-start | bytes 3145736 | tf_op jit(solution)/shard_map/ppermute | solution.py:466
  780.1 51.1 %collective-permute-start.67 = (bf16[256,2048]{1,0:T(8,128)(2,1)}, bf16[256,2048]{1,0:T(8,128)(2,1)}, u32[]{:S(2)}, u32[]{:S(2)}) collective-permute-start(bf16[256,2048]{1,0:T(8,128)(2,1)} %add_convert_fusion.5), channel_id=1, source_target_pairs={{0,8},{4,12},{8,16},{12,20},{16,24},{20,28},{24,0},{28,4},{1,9},{5... | collective-permute-start | bytes 3145736 | tf_op jit(solution)/shard_map/ppermute | solution.py:483
  835.3 359.5 %reduce-scatter.8.cloned.1.call-start = ((), (), s32[]{:S(2)}) async-start(), calls=%async_computation.6 | async-start | bytes 5242880 | tf_op jit(solution)/shard_map/reduce_scatter | solution.py:635
  1072.2 101.8 %collective-permute-start.85 = (bf16[256,1536]{1,0:T(8,128)(2,1)S(1)}, bf16[256,1536]{1,0:T(8,128)(2,1)S(1)}, u32[]{:S(2)}, u32[]{:S(2)}) collective-permute-start(bf16[256,1536]{1,0:T(8,128)(2,1)S(1)} %copy-done.82), channel_id=1, source_target_pairs={{0,4},{4,0},{8,12},{12,8},{16,20},{20,16},{24,28},{28,24},{1,5},{5... | collective-permute-start | bytes 2359304 | tf_op jit(solution)/shard_map/ppermute | solution.py:466
  1107.4 66.6 %collective-permute-start.89 = (bf16[256,1536]{1,0:T(8,128)(2,1)S(1)}, bf16[256,1536]{1,0:T(8,128)(2,1)S(1)}, u32[]{:S(2)}, u32[]{:S(2)}) collective-permute-start(bf16[256,1536]{1,0:T(8,128)(2,1)S(1)} %add_convert_fusion.29), channel_id=1, source_target_pairs={{0,8},{4,12},{8,16},{12,20},{16,24},{20,28},{24,0},{28,4},{1,9},{5... | collective-permute-start | bytes 2359304 | tf_op jit(solution)/shard_map/ppermute | solution.py:483
  1124.1 57.1 %collective-permute-start.84 = (bf16[256,1536]{1,0:T(8,128)(2,1)S(1)}, bf16[256,1536]{1,0:T(8,128)(2,1)S(1)}, u32[]{:S(2)}, u32[]{:S(2)}) collective-permute-start(bf16[256,1536]{1,0:T(8,128)(2,1)S(1)} %copy-done.81), channel_id=1, source_target_pairs={{0,4},{4,0},{8,12},{12,8},{16,20},{20,16},{24,28},{28,24},{1,5},{5... | collective-permute-start | bytes 2359304 | tf_op jit(solution)/shard_map/ppermute | solution.py:466
  (187 other events, 3034.9 us)
Sparse Core Ops, SparseCore 0:
  131.3 246.4 all-gather.1
  758.4 156.6 reduce-scatter.3
  918.7 129.1 reduce-scatter.5
  1067.3 113.7 reduce-scatter.7
